TPU v7x, 32 devices: a whole 2x2x4 slice. The times are simulated.
32 devices in a mesh: stretch: 16 (over z, x, core), chan: 2 (over y).
Axes of the slice: x: 2, y: 2, z: 4, core: 2. Of those that a mesh axis runs over, the one named last changes fastest.
Arguments:
- tokens: bfloat16 [8192, 4096], P('stretch', 'chan'), may hold values from -6 to 6
- in_weight: bfloat16 [4096, 3, 4096], P('stretch', None, 'chan'), may hold values from -0.09375 to 0.09375
- short_weight: bfloat16 [7, 3, 4096], P(None, None, 'chan'), may hold values from -2.390625 to 2.390625
- medium_filter: bfloat16 [128, 256], P(None, 'chan'), may hold values from -1 to 1
- seq_lengths: int32 [8], replicated, may hold values from 1 to 2048, 8192 in all
- stretch_slot: int32 [16], replicated, may hold values from 0 to 15, as said below
Outputs:
- gated_output: bfloat16 [8192, 4096], P('stretch', 'chan')
Inputs may be any that keep to these rules, and one draw needn't show every extreme that they name: stretch_slot is a permutation; stretches 2k and 2k + 1 are held at indices 2k and 2k + 1 in some order, so stretch_slot[c] - stretch_slot[c - 1] is one of -1, 1, 2, 3.
All inputs are finite; a program needn't handle non-finite values.
Results may differ from a plain program's by a relative error of at most 0.007.
Values may be sent and summed in bfloat16 or wider, within the bound.
No kernel may reach another device: no remote copies, remote signals or barrier semaphores. Data moves between devices by JAX's collectives and lax.ppermute only.
A program may use at most 128 MiB of HBM per device.

v0:
```python
import jax
import jax.numpy as jnp
from jax import lax
from jax.sharding import PartitionSpec as P

OFFSETS = (-1, 1, 2, 3)


def from_behind(array, axis, by):
    length = lax.axis_size(axis)
    pairs = [(i, i + by) for i in range(length) if 0 <= i + by < length]
    return lax.ppermute(array, axis, pairs)


def locate(stretch_slot, device):
    stretch_count = stretch_slot.shape[0]
    stretch_order = jnp.arange(stretch_count, dtype=jnp.int32)
    stretch_id = jnp.sum(jnp.where(stretch_slot == device, stretch_order, 0))
    previous = jnp.sum(jnp.where(stretch_order == stretch_id - 1, stretch_slot, 0))
    return (stretch_id, previous)


def in_sequence(places, seq_lengths):
    seq_ends = jnp.cumsum(seq_lengths)
    starts = seq_ends - seq_lengths
    inside = (places[:, None] >= starts[None, :]) & (places[:, None] < seq_ends[None, :])
    return jnp.sum(jnp.where(inside, places[:, None] - starts[None, :], 0), axis=1)


def short_conv(extended, weights, positions):
    tap_count = weights.shape[0]
    row_count = extended.shape[0] - tap_count + 1
    shape_tail = (1,) * (extended.ndim - 1)
    running = jnp.zeros((row_count,) + extended.shape[1:], jnp.float32)
    for lag_index in range(tap_count):
        start_row = tap_count - 1 - lag_index
        window = extended[start_row : start_row + row_count].astype(jnp.float32)
        allowed = (positions >= lag_index).reshape((row_count,) + shape_tail)
        running = running + jnp.where(allowed, window * weights[lag_index].astype(jnp.float32), 0.0)
    return running


def lag_tables(medium_filter):
    span_len = medium_filter.shape[0]
    row_ids = lax.broadcasted_iota(jnp.int32, (span_len, span_len), 0)
    col_ids = lax.broadcasted_iota(jnp.int32, (span_len, span_len), 1)
    lag_grid = row_ids - col_ids
    lag_ids = jnp.arange(span_len, dtype=jnp.int32)
    lower_hot = (lag_grid[:, :, None] == lag_ids).astype(jnp.bfloat16)
    upper_hot = (lag_grid[:, :, None] + span_len == lag_ids).astype(jnp.bfloat16)
    lower_band = jnp.einsum(
        "pqj,jg->gpq", lower_hot, medium_filter, preferred_element_type=jnp.float32
    ).astype(jnp.bfloat16)
    upper_band = jnp.einsum(
        "pqj,jg->gpq", upper_hot, medium_filter, preferred_element_type=jnp.float32
    ).astype(jnp.bfloat16)
    return (lower_band, upper_band, lag_grid)


def medium_conv(extended, medium_filter, positions):
    span_len = medium_filter.shape[0]
    filter_count = medium_filter.shape[1]
    row_count = extended.shape[0] - span_len
    chan_width = extended.shape[1]
    group_size = chan_width // filter_count
    block_count = row_count // span_len
    lower_band, upper_band, lag_grid = lag_tables(medium_filter)
    limits = positions.reshape(block_count, span_len, 1)
    keep_lower = (lag_grid[None] <= limits).astype(jnp.bfloat16)
    keep_upper = (lag_grid[None] + span_len <= limits).astype(jnp.bfloat16)
    lower_masked = lower_band[None] * keep_lower[:, None]
    upper_masked = upper_band[None] * keep_upper[:, None]
    blocks = extended.reshape(block_count + 1, span_len, filter_count, group_size)
    result = jnp.einsum(
        "bgpq,bqgc->bpgc", lower_masked, blocks[1:], preferred_element_type=jnp.float32
    )
    result = result + jnp.einsum(
        "bgpq,bqgc->bpgc", upper_masked, blocks[:-1], preferred_element_type=jnp.float32
    )
    return result.reshape(row_count, chan_width)


def per_device(tokens, in_weight, short_weight, medium_filter, seq_lengths, stretch_slot):
    row_count = tokens.shape[0]
    chan_width = in_weight.shape[2]
    tap_count = short_weight.shape[0]
    span_len = medium_filter.shape[0]
    device = lax.axis_index("stretch")
    stretch_id, previous = locate(stretch_slot, device)
    has_prev = stretch_id > 0
    wanted = device - previous
    first_place = stretch_id * row_count
    positions = in_sequence(first_place + jnp.arange(row_count, dtype=jnp.int32), seq_lengths)
    features = lax.all_gather(tokens, "chan", axis=1, tiled=True)
    full_weight = lax.all_gather(in_weight, "stretch", axis=0, tiled=True)
    projected = jnp.einsum("td,dsc->tsc", features, full_weight, preferred_element_type=jnp.float32)
    projected = projected.astype(jnp.bfloat16)
    parcel = projected[row_count - tap_count + 1 :]
    received = jnp.zeros_like(parcel)
    for by_count in OFFSETS:
        arrived = from_behind(parcel, "stretch", by_count)
        received = jnp.where(wanted == by_count, arrived, received)
    received = jnp.where(has_prev, received, jnp.zeros_like(received))
    short_out = short_conv(jnp.concatenate([received, projected], axis=0), short_weight, positions)
    mixed_in = (short_out[:, 0] * short_out[:, 2]).astype(jnp.bfloat16)
    parcel_mixed = mixed_in[row_count - span_len + 1 :]
    tail_mixed = jnp.zeros_like(parcel_mixed)
    for by_count in OFFSETS:
        arrived = from_behind(parcel_mixed, "stretch", by_count)
        tail_mixed = jnp.where(wanted == by_count, arrived, tail_mixed)
    tail_mixed = jnp.where(has_prev, tail_mixed, jnp.zeros_like(tail_mixed))
    extended = jnp.concatenate(
        [jnp.zeros((1, chan_width), jnp.bfloat16), tail_mixed, mixed_in], axis=0
    )
    medium = medium_conv(extended, medium_filter, positions)
    return (short_out[:, 1] * medium).astype(jnp.bfloat16)


def solution(mesh):
    return jax.shard_map(
        per_device,
        mesh=mesh,
        in_specs=(
            P("stretch", "chan"),
            P("stretch", None, "chan"),
            P(None, None, "chan"),
            P(None, "chan"),
            P(),
            P(),
        ),
        out_specs=P("stretch", "chan"),
        check_vma=False,
    )
```

profile of v0, /device:TPU:0, one launch (start us, length us, event | category | flops | bytes accessed | tf_op | source)
XLA Modules:
  0.0 497.0 jit_solution(15529717255521755702)
XLA Ops:
  6.5 0.0 copy-start
  6.5 0.0 all-gather.3.cloned.1.call-start
  6.5 0.7 all-gather.3.cloned.1.call-update
  7.3 0.0 all-gather.5.cloned.1.call-start
  7.3 0.7 all-gather.5.cloned.1.call-update
  8.0 0.0 copy-start.5
  8.0 1.3 fusion.27
  11.3 0.8 reduce-window.8
  12.1 0.7 bitcast_subtract_fusion
  12.8 0.1 select_reduce_fusion
  12.9 0.1 compare_convert_fusion.1
  13.1 0.0 copy-done
  13.1 5.8 %convert_bitcast_fusion = bf16[128,128,128]{0,2,1:T(8,128)(2,1)} fusion(s32[128,128]{1,0:T(8,128)S(1)} %get-tuple-element.22, bf16[128,128]{1,0:T(8,128)(2,1)S(1)} %copy-done), kind=kOutput, calls=%fused_computation.36 | convolution fusion | flops 541065216 | bytes 4292608 | tf_op jit(solution)/shard_map/pqj,jg->gpq/dot_general | solution.py:54
  18.9 5.7 %convert_bitcast_fusion.1 = bf16[128,128,128]{0,2,1:T(8,128)(2,1)} fusion(s32[128,128]{1,0:T(8,128)S(1)} %get-tuple-element.21, bf16[128,128]{1,0:T(8,128)(2,1)S(1)} %copy-done), kind=kOutput, calls=%fused_computation.38 | convolution fusion | flops 541065216 | bytes 4292608 | tf_op jit(solution)/shard_map/pqj,jg->gpq/dot_general | solution.py:51
  24.6 0.0 copy-done.5
  24.6 0.1 slice_convert_fusion.6
  24.8 0.0 copy-start.7
  24.8 43.6 %all-gather.3.cloned.1.call-done = bf16[512,4096]{1,0:T(8,128)(2,1)} async-done(((bf16[512,2048]{1,0:T(8,128)(2,1)}), bf16[512,4096]{1,0:T(8,128)(2,1)}) %all-gather.3.cloned.1.call-update) | async-done | bytes 4194320 | tf_op jit(solution)/shard_map/all_gather | solution.py:94
  68.4 248.7 %all-gather.5.cloned.1.call-done = bf16[4096,3,2048]{2,0,1:T(8,128)(2,1)} async-done(((bf16[256,3,2048]{2,0,1:T(8,128)(2,1)}), bf16[4096,3,2048]{2,0,1:T(8,128)(2,1)}) %all-gather.5.cloned.1.call-update) | async-done | bytes 50331664 | tf_op jit(solution)/shard_map/all_gather | solution.py:95
  317.1 32.4 %convolution_convert_fusion = bf16[512,3,2048]{2,0,1:T(8,128)(2,1)S(1)} fusion(bf16[4096,3,2048]{2,0,1:T(8,128)(2,1)} %all-gather.5.cloned.1.call-done, bf16[512,4096]{1,0:T(8,128)(2,1)} %all-gather.3.cloned.1.call-done), kind=kOutput, calls=%fused_computation.27 | convolution fusion | flops 25772949504 | bytes 60817408 | tf_op jit(solution)/shard_map/td,dsc->tsc/dot_general | solution.py:96
  349.5 0.0 copy-start.4
  349.5 2.7 copy-done.4
  352.2 2.7 collective-permute-start
  354.9 3.9 collective-permute-start.1
  358.8 1.4 collective-permute-start.2
  360.2 1.3 collective-permute-start.3
  361.5 0.0 copy-done.7
  361.5 0.6 fusion.28
  362.9 0.0 copy-start.6
  362.9 6.7 %copy.20 = bf16[128,128,128]{2,1,0:T(8,128)(2,1)} copy(bf16[128,128,128]{0,2,1:T(8,128)(2,1)} %convert_bitcast_fusion) | data formatting | bytes 8388608 | tf_op jit(solution)/shard_map/convert_element_type | solution.py:56
  369.5 6.7 %copy.17 = bf16[128,128,128]{2,1,0:T(8,128)(2,1)} copy(bf16[128,128,128]{0,2,1:T(8,128)(2,1)} %convert_bitcast_fusion.1) | data formatting | bytes 8388608 | tf_op jit(solution)/shard_map/convert_element_type | solution.py:53
  376.2 0.0 copy-done.6
  376.2 0.0 collective-permute-done
  376.2 0.0 collective-permute-done.1
  376.2 0.0 collective-permute-done.2
  376.3 0.0 collective-permute-done.3
  376.3 28.6 %select_add_fusion = f32[512,3,2048]{2,0,1:T(8,128)S(1)} fusion(bf16[512,3,2048]{2,0,1:T(8,128)(2,1)} %copy-done.4, bf16[6,3,2048]{2,0,1:T(8,128)(2,1)S(1)} %select_select_fusion.1, f32[3,2048]{1,0:T(4,128)S(1)} %get-tuple-element.23, f32[3,2048]{1,0:T(4,128)S(1)} %get-tuple-element.24, f32[3,2048]{1,0:T(4,128)S(1)} %get-tuple-element.25, ...), kind=kLoop, calls=%fused_computation.9 | loop fusion | flops 141557760 | bytes 19123712 | tf_op jit(solution)/shard_map/add | solution.py:39
  404.9 4.5 copy-done.2
  409.4 0.6 fusion.15
  410.0 0.9 slice_bitcast_fusion.1
  411.0 5.8 %collective-permute-start.4 = (bf16[127,2048]{1,0:T(8,128)(2,1)}, bf16[127,2048]{1,0:T(8,128)(2,1)S(1)}, u32[]{:S(2)}, u32[]{:S(2)}) collective-permute-start(bf16[127,2048]{1,0:T(8,128)(2,1)} %slice_bitcast_fusion.1), channel_id=1, source_target_pairs={{0,6},{2,8},{4,10},{6,12},{8,14},{10,16},{12,18},{14,20},{16,22},{... | collective-permute-start | bytes 1560584 | tf_op jit(solution)/shard_map/ppermute | solution.py:12
  416.7 2.9 collective-permute-start.5
  419.6 3.1 collective-permute-start.6
  422.7 1.5 collective-permute-start.7
  424.2 2.5 copy.16
  426.7 2.5 convert_element_type.88
  429.2 0.0 slice-start
  429.2 4.1 fusion.30
  433.3 0.0 collective-permute-done.4
  433.3 10.2 %collective-permute-done.5 = bf16[127,2048]{1,0:T(8,128)(2,1)S(1)} collective-permute-done((bf16[127,2048]{1,0:T(8,128)(2,1)}, bf16[127,2048]{1,0:T(8,128)(2,1)S(1)}, u32[]{:S(2)}, u32[]{:S(2)}) %collective-permute-start.5) | collective-permute-done | bytes 520224 | tf_op jit(solution)/shard_map/ppermute | solution.py:12
  443.5 0.0 collective-permute-done.6
  443.5 0.0 collective-permute-done.7
  443.5 1.1 select_select_fusion
  444.7 1.8 pad_maximum_fusion.1
  446.5 3.9 copy.19
  450.5 4.0 slice.85
  454.4 11.0 %fusion = f32[4,128,16,128]{3,2,1,0:T(8,128)S(1)} fusion(bf16[4,128,128]{2,1,0:T(8,128)(2,1)S(1)} %get-tuple-element.13, bf16[128,128,128]{2,1,0:T(8,128)(2,1)} %copy.20, bf16[4,128,128,16]{1,0,3,2:T(4,128)(2,1)} %slice.85), kind=kOutput, calls=%fused_computation | convolution fusion | flops 276824064 | bytes 10616832 | tf_op jit(solution)/shard_map/bgpq,bqgc->bpgc/dot_general | solution.py:77
  465.4 0.0 copy-done.3
  465.4 8.9 %add_bitcast_fusion = f32[4,128,128,16]{1,3,2,0:T(8,128)S(1)} fusion(f32[4,128,16,128]{3,2,1,0:T(8,128)S(1)} %fusion, bf16[4,128,128]{2,1,0:T(8,128)(2,1)S(1)} %get-tuple-element.12, bf16[128,128,128]{2,1,0:T(8,128)(2,1)S(1)} %copy-done.3, bf16[4,128,128,16]{1,0,3,2:T(4,128)(2,1)S(1)} %convert_element_type.88), kind=kOutput, calls=%fused_computation.35 | convolution fusion | flops 277872640 | bytes 14811136 | tf_op jit(solution)/shard_map/bgpq,bqgc->bpgc/dot_general | solution.py:74
  474.3 2.7 copy.22
  477.0 2.4 copy.44
  479.4 5.4 %copy.23 = f32[512,2048]{1,0:T(8,128)} copy(f32[512,2048]{0,1:T(8,128)} %bitcast.57) | data formatting | bytes 8388608 | tf_op jit(solution)/shard_map/reshape | solution.py:80
  484.8 5.4 %fusion.17 = bf16[512,2048]{1,0:T(8,128)(2,1)} fusion(f32[512,2048]{1,0:T(8,128)} %copy.23, f32[512,3,2048]{2,0,1:T(8,128)} %copy-done.2), kind=kLoop, calls=%fused_computation.33 | loop fusion | flops 2097152 | bytes 10485760 | tf_op jit(solution)/shard_map/convert_element_type | solution.py:116
  490.2 0.0 copy-done.1
  (14 shorter events, 0.2 us)
Async XLA Ops:
  6.5 6.5 %copy-start = (bf16[128,128]{1,0:T(8,128)(2,1)S(1)}, bf16[128,128]{1,0:T(8,128)(2,1)}, u32[]{:S(2)}) copy-start(bf16[128,128]{1,0:T(8,128)(2,1)} %param.9) | copy-start | bytes 98308
  6.5 61.8 %all-gather.3.cloned.1.call-start = ((), (), s32[]{:S(2)}) async-start(), calls=%async_computation | async-start | bytes 6291456 | tf_op jit(solution)/shard_map/all_gather | solution.py:94
  7.3 309.8 %all-gather.5.cloned.1.call-start = ((), (), s32[]{:S(2)}) async-start(), calls=%async_computation.1 | async-start | bytes 53477376 | tf_op jit(solution)/shard_map/all_gather | solution.py:95
  8.0 16.6 %copy-start.5 = (bf16[7,3,2048]{2,0,1:T(8,128)(2,1)S(1)}, bf16[7,3,2048]{2,0,1:T(8,128)(2,1)}, u32[]{:S(2)}) copy-start(bf16[7,3,2048]{2,0,1:T(8,128)(2,1)} %param.8) | copy-start | bytes 258052
  24.8 336.7 %copy-start.7 = (s32[16]{0:T(128)S(1)}, s32[16]{0:T(128)}, u32[]{:S(2)}) copy-start(s32[16]{0:T(128)} %param.11) | copy-start | bytes 196
  349.5 2.7 copy-start.4
  352.2 24.1 %collective-permute-start = (bf16[6,3,2048]{2,0,1:T(8,128)(2,1)S(1)}, bf16[6,3,2048]{2,0,1:T(8,128)(2,1)S(1)}, u32[]{:S(2)}, u32[]{:S(2)}) collective-permute-start(bf16[6,3,2048]{2,0,1:T(8,128)(2,1)S(1)} %slice.86), channel_id=1, source_target_pairs={{0,6},{2,8},{4,10},{6,12},{8,14},{10,16},{12,18},{14,20},{16,22},{... | collective-permute-start | bytes 221192 | tf_op jit(solution)/shard_map/ppermute | solution.py:12
  354.9 21.3 %collective-permute-start.1 = (bf16[6,3,2048]{2,0,1:T(8,128)(2,1)S(1)}, bf16[6,3,2048]{2,0,1:T(8,128)(2,1)S(1)}, u32[]{:S(2)}, u32[]{:S(2)}) collective-permute-start(bf16[6,3,2048]{2,0,1:T(8,128)(2,1)S(1)} %slice.86), channel_id=1, source_target_pairs={{0,4},{2,6},{4,8},{6,10},{8,12},{10,14},{12,16},{14,18},{16,20},{1... | collective-permute-start | bytes 221192 | tf_op jit(solution)/shard_map/ppermute | solution.py:12
  358.8 17.4 %collective-permute-start.2 = (bf16[6,3,2048]{2,0,1:T(8,128)(2,1)S(1)}, bf16[6,3,2048]{2,0,1:T(8,128)(2,1)S(1)}, u32[]{:S(2)}, u32[]{:S(2)}) collective-permute-start(bf16[6,3,2048]{2,0,1:T(8,128)(2,1)S(1)} %slice.86), channel_id=1, source_target_pairs={{0,2},{2,4},{4,6},{6,8},{8,10},{10,12},{12,14},{14,16},{16,18},{18... | collective-permute-start | bytes 221192 | tf_op jit(solution)/shard_map/ppermute | solution.py:12
  360.2 16.0 %collective-permute-start.3 = (bf16[6,3,2048]{2,0,1:T(8,128)(2,1)S(1)}, bf16[6,3,2048]{2,0,1:T(8,128)(2,1)S(1)}, u32[]{:S(2)}, u32[]{:S(2)}) collective-permute-start(bf16[6,3,2048]{2,0,1:T(8,128)(2,1)S(1)} %slice.86), channel_id=1, source_target_pairs={{2,0},{4,2},{6,4},{8,6},{10,8},{12,10},{14,12},{16,14},{18,16},{20... | collective-permute-start | bytes 221192 | tf_op jit(solution)/shard_map/ppermute | solution.py:12
  362.9 13.4 %copy-start.6 = (bf16[640]{0:T(1024)(128)(2,1)}, bf16[640]{0:T(1024)(128)(2,1)S(1)}, u32[]{:S(2)}) copy-start(bf16[640]{0:T(1024)(128)(2,1)S(1)} %pad.clone) | copy-start | bytes 3844
  404.9 4.5 copy-start.2
  411.0 22.4 %collective-permute-start.4 = (bf16[127,2048]{1,0:T(8,128)(2,1)}, bf16[127,2048]{1,0:T(8,128)(2,1)S(1)}, u32[]{:S(2)}, u32[]{:S(2)}) collective-permute-start(bf16[127,2048]{1,0:T(8,128)(2,1)} %slice_bitcast_fusion.1), channel_id=1, source_target_pairs={{0,6},{2,8},{4,10},{6,12},{8,14},{10,16},{12,18},{14,20},{16,22},{... | collective-permute-start | bytes 1560584 | tf_op jit(solution)/shard_map/ppermute | solution.py:12
  416.7 26.8 %collective-permute-start.5 = (bf16[127,2048]{1,0:T(8,128)(2,1)}, bf16[127,2048]{1,0:T(8,128)(2,1)S(1)}, u32[]{:S(2)}, u32[]{:S(2)}) collective-permute-start(bf16[127,2048]{1,0:T(8,128)(2,1)} %slice_bitcast_fusion.1), channel_id=1, source_target_pairs={{0,4},{2,6},{4,8},{6,10},{8,12},{10,14},{12,16},{14,18},{16,20},{1... | collective-permute-start | bytes 1560584 | tf_op jit(solution)/shard_map/ppermute | solution.py:12
  419.6 23.9 %collective-permute-start.6 = (bf16[127,2048]{1,0:T(8,128)(2,1)}, bf16[127,2048]{1,0:T(8,128)(2,1)}, u32[]{:S(2)}, u32[]{:S(2)}) collective-permute-start(bf16[127,2048]{1,0:T(8,128)(2,1)} %slice_bitcast_fusion.1), channel_id=1, source_target_pairs={{0,2},{2,4},{4,6},{6,8},{8,10},{10,12},{12,14},{14,16},{16,18},{18... | collective-permute-start | bytes 1560584 | tf_op jit(solution)/shard_map/ppermute | solution.py:12
  422.7 20.8 %collective-permute-start.7 = (bf16[127,2048]{1,0:T(8,128)(2,1)}, bf16[127,2048]{1,0:T(8,128)(2,1)}, u32[]{:S(2)}, u32[]{:S(2)}) collective-permute-start(bf16[127,2048]{1,0:T(8,128)(2,1)} %slice_bitcast_fusion.1), channel_id=1, source_target_pairs={{2,0},{4,2},{6,4},{8,6},{10,8},{12,10},{14,12},{16,14},{18,16},{20... | collective-permute-start | bytes 1560584 | tf_op jit(solution)/shard_map/ppermute | solution.py:12
  429.2 15.5 %slice-start = ((bf16[640]{0:T(1024)(128)(2,1)}), bf16[512]{0:T(512)(128)(2,1)S(1)}, s32[]{:S(2)}) async-start(bf16[640]{0:T(1024)(128)(2,1)} %copy-done.6), calls=%async_computation.2 | async-start | bytes 2048 | tf_op jit(solution)/shard_map/slice | solution.py:78
  454.4 11.0 %copy-start.3 = (bf16[128,128,128]{2,1,0:T(8,128)(2,1)S(1)}, bf16[128,128,128]{2,1,0:T(8,128)(2,1)}, u32[]{:S(2)}) copy-start(bf16[128,128,128]{2,1,0:T(8,128)(2,1)} %copy.17) | copy-start | bytes 12582916
  479.4 10.8 %copy-start.1 = (bf16[128,128]{1,0:T(8,128)(2,1)S(1)}, bf16[128,128]{1,0:T(8,128)(2,1)}, u32[]{:S(2)}) copy-start(bf16[128,128]{1,0:T(8,128)(2,1)} %param.9) | copy-start | bytes 98308
Sparse Core Ops, SparseCore 0:
  8.9 59.4 all-gather.2
  69.9 247.0 all-gather.4
where the time goes:
time: 504 us; the launch traced here: 497 us
  waiting for transfers between devices  304 us (60%)
  matrix products  63.8 us (13%)
  other arithmetic  45.5 us (9%)
  local copies, waits for them, and re-layouts  45.1 us (9%)
  starting transfers between devices  22.5 us (4%)
  between operations  16.3 us (3%)
    all_gather x1, waiting for transfers between devices, per_device(): full_weight = lax.all_gather(in_weight, 'stretch', axis=0, tiled=True)  249 us
    all_gather x1, waiting for transfers between devices, per_device(): features = lax.all_gather(tokens, 'chan', axis=1, tiled=True)  43.6 us
    dot_general x1, matrix products, per_device(): jnp.einsum('td,dsc->tsc', features, full_weight, preferred_element_type=j...  32.4 us
    add x1, other arithmetic, short_conv(): running + jnp.where(allowed, window * weights[lag_index].astype(jnp.float...  28.6 us
    ppermute x8, starting transfers between devices, from_behind(): return lax.ppermute(array, axis, pairs)  22.5 us
    dot_general x1, matrix products, medium_conv(): jnp.einsum('bgpq,bqgc->bpgc', upper_masked, blocks[:-1], preferred_elemen...  11 us
    ppermute x8, waiting for transfers between devices, from_behind(): return lax.ppermute(array, axis, pairs)  10.2 us
  transfers between devices with their start and end apart: 10, of which 3 were waited for; matrix products, arithmetic and copies ran while one was open for 8% of the time, Pallas kernels for 0%

commit v1 on v0

v1 whole, which is shorter than its diff:
```python
import functools

import jax
import jax.numpy as jnp
from jax import lax
from jax.experimental import pallas as pl
from jax.experimental.pallas import tpu as pltpu
from jax.sharding import PartitionSpec as P

ROW_TILE = 256
CHAN_TILE = 256
LANES = 128


def in_sequence(places, seq_lengths):
    seq_ends = jnp.cumsum(seq_lengths)
    starts = seq_ends - seq_lengths
    inside = (places[:, None] >= starts[None, :]) & (places[:, None] < seq_ends[None, :])
    return jnp.sum(jnp.where(inside, places[:, None] - starts[None, :], 0), axis=1)


def block_kernel(x_ref, w_ref, sw_ref, fr_ref, pos_ref, out_ref, proj, mix, band):
    i = pl.program_id(1)
    taps = sw_ref.shape[1]
    rows, chans = out_ref.shape
    span = band.shape[0] // fr_ref.shape[0]
    groups = fr_ref.shape[0]
    per_lanes = groups * LANES // chans
    width = LANES // per_lanes

    @pl.when(i == 0)
    def _():
        proj[:, :8, :] = jnp.zeros((3, 8, chans), jnp.float32)
        mix[:span, :] = jnp.zeros((span, chans), mix.dtype)
        for g in range(groups):
            row = jnp.broadcast_to(fr_ref[g : g + 1, :], (span, 2 * span))
            band[g * span : (g + 1) * span, :] = pltpu.roll(
                row, 0, 1, stride=1, stride_axis=0
            ).astype(band.dtype)

    for s in range(3):
        weight = w_ref[:, s].reshape(x_ref.shape[1], chans)
        acc = jnp.dot(x_ref[...], weight, preferred_element_type=jnp.float32)
        proj[s, 8:, :] = acc.astype(jnp.bfloat16).astype(jnp.float32)

    def short(s, start, size, lanes, allowed):
        total = proj[s, 8 + start : 8 + start + size, lanes] * sw_ref[s, 0:1, lanes]
        for j in range(1, taps):
            window = proj[s, 8 + start - j : 8 + start - j + size, lanes]
            total = total + jnp.where(allowed[j], window * sw_ref[s, j : j + 1, lanes], 0.0)
        return total

    step = 64
    for r in range(rows // step):
        pos = pos_ref[r * step : (r + 1) * step, :]
        allowed = [pos >= j for j in range(taps)]
        for h in range(chans // LANES):
            lanes = slice(h * LANES, (h + 1) * LANES)
            mixed = short(0, r * step, step, lanes, allowed) * short(2, r * step, step, lanes, allowed)
            mix[span + r * step : span + (r + 1) * step, lanes] = mixed.astype(mix.dtype)

    @pl.when(i > 0)
    def _():
        lag = (
            lax.broadcasted_iota(jnp.int32, (span, 2 * span), 0)
            + span
            - lax.broadcasted_iota(jnp.int32, (span, 2 * span), 1)
        )
        lane_group = lax.broadcasted_iota(jnp.int32, (span, LANES), 1) // width
        for b in range(rows // span):
            pos = pos_ref[b * span : (b + 1) * span, :]
            limit = jnp.concatenate([pos] * (2 * span // LANES), axis=1)
            keep = jnp.where(lag <= limit, 1.0, 0.0).astype(band.dtype)
            allowed = [pos >= j for j in range(taps)]
            for h in range(chans // LANES):
                lanes = slice(h * LANES, (h + 1) * LANES)
                some = band[h * per_lanes * span : (h + 1) * per_lanes * span, :]
                some = some.reshape(per_lanes, span, 2 * span) * keep[None]
                full = jnp.dot(
                    some.reshape(per_lanes * span, 2 * span),
                    mix[b * span : (b + 2) * span, lanes],
                    preferred_element_type=jnp.float32,
                )
                medium = full[:span]
                for g in range(1, per_lanes):
                    medium = jnp.where(lane_group == g, full[g * span : (g + 1) * span], medium)
                gate = short(1, b * span, span, lanes, allowed)
                out_ref[b * span : (b + 1) * span, lanes] = (gate * medium).astype(out_ref.dtype)

    proj[:, :8, :] = proj[:, rows : rows + 8, :]
    mix[:span, :] = mix[rows : rows + span, :]


def block(x, w, sw, fr, pos, first_chan, span):
    total, features = x.shape
    pieces, _, depth, chans = w.shape
    taps = sw.shape[1]
    per_tile = CHAN_TILE * fr.shape[0] // sw.shape[2]
    first = first_chan // CHAN_TILE
    grid = (chans // CHAN_TILE, total // ROW_TILE)
    return pl.pallas_call(
        block_kernel,
        grid=grid,
        in_specs=[
            pl.BlockSpec((ROW_TILE, features), lambda j, i: (i, 0)),
            pl.BlockSpec((pieces, 3, depth, CHAN_TILE), lambda j, i: (0, 0, 0, j)),
            pl.BlockSpec((3, taps, CHAN_TILE), lambda j, i: (0, 0, first + j)),
            pl.BlockSpec((per_tile, 2 * span), lambda j, i: (first + j, 0)),
            pl.BlockSpec((ROW_TILE, LANES), lambda j, i: (i, 0)),
        ],
        out_specs=pl.BlockSpec((ROW_TILE, CHAN_TILE), lambda j, i: (jnp.maximum(i - 1, 0), j)),
        out_shape=jax.ShapeDtypeStruct((total - ROW_TILE, chans), jnp.bfloat16),
        scratch_shapes=[
            pltpu.VMEM((3, 8 + ROW_TILE, CHAN_TILE), jnp.float32),
            pltpu.VMEM((span + ROW_TILE, CHAN_TILE), jnp.bfloat16),
            pltpu.VMEM((per_tile * span, 2 * span), jnp.bfloat16),
        ],
        compiler_params=pltpu.CompilerParams(vmem_limit_bytes=40 * 1024 * 1024),
        cost_estimate=pl.CostEstimate(
            flops=2 * total * features * 3 * chans + 2 * total * chans // CHAN_TILE * per_tile * span * 256,
            bytes_accessed=2 * (total * features * grid[0] + 3 * features * chans + total * chans),
            transcendentals=0,
        ),
    )(x, w, sw, fr, pos)


def parameters(short_weight, medium_filter):
    sw = jnp.transpose(short_weight, (1, 0, 2)).astype(jnp.float32)
    span = medium_filter.shape[0]
    fr = jnp.pad(jnp.flip(medium_filter, axis=0).T.astype(jnp.float32), ((0, 0), (1, span - 1)))
    return sw, fr


def chunks_of(chans):
    large = 2 * CHAN_TILE
    widths = [large] * max(0, chans // large - 1)
    rest = chans - sum(widths)
    return widths + [CHAN_TILE] * (rest // CHAN_TILE)


def per_device(tokens, in_weight, short_weight, medium_filter, seq_lengths, stretch_slot):
    row_count = tokens.shape[0]
    chans = in_weight.shape[2]
    span, taps = medium_filter.shape[0], short_weight.shape[0]
    device = lax.axis_index("stretch")
    devices = lax.axis_size("stretch")
    order = jnp.arange(devices, dtype=jnp.int32)
    stretch_id = jnp.sum(jnp.where(stretch_slot == device, order, 0))

    local = jnp.transpose(in_weight, (1, 0, 2))
    gathered, begin = [], 0
    for width in chunks_of(chans):
        part = local[:, :, begin : begin + width]
        gathered.append((begin, lax.all_gather(part, "stretch", axis=0, tiled=False)))
        begin += width

    reach = -(-(span + taps - 1) // 16) * 16
    tail = tokens[row_count - reach :]
    sibling = lax.ppermute(tail, "stretch", [(i, i ^ 1) for i in range(devices)])
    second = stretch_id % 2 == 1
    last = jnp.where(second, tail, sibling)
    before = lax.ppermute(last, "stretch", [(i, i + 2) for i in range(devices - 2)])
    halo = jnp.where(second, sibling, before)
    mine = jnp.concatenate([halo, tokens], axis=0)
    x = lax.all_gather(mine, "chan", axis=1, tiled=True) if lax.axis_size("chan") != 2 else None
    if x is None:
        other = lax.ppermute(mine, "chan", [(0, 1), (1, 0)])
        low = lax.axis_index("chan") == 0
        x = jnp.concatenate([jnp.where(low, mine, other), jnp.where(low, other, mine)], axis=1)
    x = jnp.pad(x, ((ROW_TILE - reach, 0), (0, 0)))

    places = stretch_id * row_count - ROW_TILE + jnp.arange(ROW_TILE + row_count, dtype=jnp.int32)
    pos = jnp.broadcast_to(in_sequence(places, seq_lengths)[:, None], (ROW_TILE + row_count, LANES))
    sw, fr = parameters(short_weight, medium_filter)
    outs = [block(x, w, sw, fr, pos, begin, span) for begin, w in gathered]
    return jnp.concatenate(outs, axis=1)


def solution(mesh):
    return jax.shard_map(
        per_device,
        mesh=mesh,
        in_specs=(
            P("stretch", "chan"),
            P("stretch", None, "chan"),
            P(None, None, "chan"),
            P(None, "chan"),
            P(),
            P(),
        ),
        out_specs=P("stretch", "chan"),
        check_vma=False,
    )
```

time: 504 us -> 486 us (0.964); the launches traced: 497 us -> 486 us
  Pallas kernels: 0 us -> 85.2 us
  matrix products: 63.8 us -> 0 us
  other arithmetic: 45.5 us -> 14.5 us
  waiting for transfers between devices: 304 us -> 333 us
  starting transfers between devices: 22.5 us -> 6.84 us
  local copies, waits for them, and re-layouts: 45.1 us -> 29.9 us
    pallas_call x0 -> x5, Pallas kernels: none -> 85.2 us  [block(): pl.pallas_call(block_kernel, grid=grid, in_specs=[pl.BlockSpec((ROW_TILE,...]
    dot_general x5 -> x0, matrix products: 63.8 us -> none  [the longest x1 32.4 us: per_device(): jnp.einsum('td,dsc->tsc', features, full_weight, preferred_element_type=j...]
    ppermute x8 -> x3, waiting for transfers between devices: 10.2 us -> 72.6 us  [the longest x1 56.4 us: per_device(): other = lax.ppermute(mine, 'chan', [(0, 1), (1, 0)])]
    all_gather x2 -> x5, waiting for transfers between devices: 292 us -> 259 us  [per_device(): lax.all_gather(part, 'stretch', axis=0, tiled=False)]
    add x2 -> x1, other arithmetic: 28.6 us -> 0.01 us  [per_device(): stretch_id * row_count - ROW_TILE]
    convert_element_type x4 -> x0, local copies, waits for them, and re-layouts: 18.4 us -> none  [the longest x1 6.7 us: lag_tables(): lower_band = jnp.einsum('pqj,jg->gpq', lower_hot, medium_filter, preferre...]
    ppermute x8 -> x3, starting transfers between devices: 22.5 us -> 6.68 us  [the longest x1 4.45 us: per_device(): lax.ppermute(last, 'stretch', [(i, i + 2) for i in range(devices - 2)])]
    unnamed x21 -> x31, local copies, waits for them, and re-layouts: 9.7 us -> 23.6 us
  transfers between devices with their start and end apart: 10 -> 8, of which waited for: 3 -> 6; matrix products, arithmetic and copies ran while one was open for 8% -> 4% of each run, Pallas kernels for 0% -> 13%
where the time goes in v1:
time: 486 us
  waiting for transfers between devices  333 us (69%)
  Pallas kernels  85.2 us (18%)
  local copies, waits for them, and re-layouts  29.9 us (6%)
  between operations  15.9 us (3%)
  other arithmetic  14.5 us (3%)
  starting transfers between devices  6.84 us (1%)
    all_gather x5, waiting for transfers between devices, per_device(): lax.all_gather(part, 'stretch', axis=0, tiled=False)  259 us
    pallas_call x5, Pallas kernels, block(): pl.pallas_call(block_kernel, grid=grid, in_specs=[pl.BlockSpec((ROW_TILE,...  85.2 us
    ppermute x1, waiting for transfers between devices, per_device(): other = lax.ppermute(mine, 'chan', [(0, 1), (1, 0)])  56.4 us
    unnamed x31, local copies, waits for them, and re-layouts  23.6 us
    ppermute x1, waiting for transfers between devices, per_device(): lax.ppermute(last, 'stretch', [(i, i + 2) for i in range(devices - 2)])  16.2 us
  transfers between devices with their start and end apart: 8, of which 6 were waited for; matrix products, arithmetic and copies ran while one was open for 4% of the time, Pallas kernels for 13%

profile of v1, /device:TPU:0, one launch (start us, length us, event | category | flops | bytes accessed | tf_op | source)
XLA Modules:
  0.0 485.6 jit_solution(3770980172506880687)
XLA Ops:
  6.5 0.0 all-gather.17.cloned.1.call-start
  6.5 2.1 fusion.4
  8.6 0.0 all-gather.17.cloned.1.call-update
  8.7 0.0 all-gather.19.cloned.1.call-start
  8.7 0.7 all-gather.19.cloned.1.call-update
  9.4 0.0 copy-start.7
  9.4 0.0 all-gather.11.cloned.1.call-start
  9.5 3.2 fusion.5
  12.7 0.0 copy-start.11
  12.7 0.0 all-gather.11.cloned.1.call-update
  12.7 0.0 all-gather.13.cloned.1.call-start
  12.8 0.5 all-gather.13.cloned.1.call-update
  13.3 0.0 all-gather.15.cloned.1.call-start
  13.3 0.5 all-gather.15.cloned.1.call-update
  13.9 0.0 copy-done.7
  13.9 0.5 collective-permute-start
  14.5 0.0 copy-done.11
  14.5 0.7 fusion.3
  17.0 0.0 collective-permute-done
  17.0 0.0 copy-start.8
  17.0 0.1 broadcast_select_fusion.3
  17.1 4.5 collective-permute-start.1
  21.6 0.0 copy-done.8
  21.6 16.2 %collective-permute-done.1 = bf16[144,2048]{1,0:T(8,128)(2,1)S(1)} collective-permute-done((bf16[144,2048]{1,0:T(8,128)(2,1)S(1)}, bf16[144,2048]{1,0:T(8,128)(2,1)S(1)}, u32[]{:S(2)}, u32[]{:S(2)}) %collective-permute-start.1) | collective-permute-done | bytes 589856 | tf_op jit(solution)/shard_map/ppermute | solution.py:162
  37.8 1.1 broadcast_select_fusion.2
  38.9 0.0 copy-start.12
  38.9 0.0 copy-start.10
  38.9 0.0 copy-start.9
  39.0 1.8 pad_maximum_fusion
  40.8 1.7 collective-permute-start.2
  43.1 0.0 copy-done.12
  43.1 0.2 reduce-window.8
  43.3 0.0 copy-done.10
  43.3 0.1 copy.9
  43.4 0.1 rev.4
  43.6 0.1 select_reduce_fusion
  43.6 0.1 pad_convert_fusion.fr_ref
  43.7 0.0 copy-done.9
  43.8 56.4 %collective-permute-done.2 = bf16[656,2048]{1,0:T(8,128)(2,1)} collective-permute-done((bf16[656,2048]{1,0:T(8,128)(2,1)}, bf16[656,2048]{1,0:T(8,128)(2,1)}, u32[]{:S(2)}, u32[]{:S(2)}) %collective-permute-start.2) | collective-permute-done | bytes 2687008 | tf_op jit(solution)/shard_map/ppermute | solution.py:167
  100.1 2.8 broadcast_select_fusion.1
  102.9 7.6 %fusion.2.x_ref = bf16[768,4096]{1,0:T(8,128)(2,1)} fusion(bf16[656,2048]{1,0:T(8,128)(2,1)S(1)} %get-tuple-element.6, bf16[656,2048]{1,0:T(8,128)(2,1)S(1)} %get-tuple-element.5), kind=kLoop, calls=%fused_computation.3 | loop fusion | flops 22020096 | bytes 11665408 | tf_op jit(solution)/shard_map/concatenate | solution.py:169
  110.5 0.0 all-gather.17.cloned.1.call-done
  110.5 0.2 broadcast_in_dim.12.pos_ref
  110.7 2.8 copy-done
  113.5 3.6 copy-done.5
  117.0 9.5 %shard_map.67 = bf16[512,256]{1,0:T(8,128)(2,1)S(1)} custom-call(bf16[768,4096]{1,0:T(8,128)(2,1)S(1)} %copy-done, bf16[16,3,256,256]{3,2,1,0:T(8,128)(2,1)S(1)} %bitcast.12, f32[3,7,2048]{2,1,0:T(8,128)S(1)} %convert_bitcast_fusion.sw_ref, f32[128,256]{1,0:T(8,128)S(1)} %pad_convert_fusion.fr_ref, s32[768,128]{1,0:T(8,128)S(1)} %broadcast_in_dim.12.pos_ref), custom_call_target="tpu_custom_call" | custom-call | flops 5637144576 | bytes 12976128 | tf_op jit(solution)/shard_map/pallas_call | solution.py:101
  126.6 20.7 %all-gather.19.cloned.1.call-done = bf16[48,256,256]{2,1,0:T(8,128)(2,1)} async-done(((bf16[3,256,256]{2,1,0:T(8,128)(2,1)}), bf16[48,256,256]{2,1,0:T(8,128)(2,1)}) %all-gather.19.cloned.1.call-update) | async-done | bytes 6291472 | tf_op jit(solution)/shard_map/all_gather | solution.py:154
  147.2 2.8 copy-done.1
  150.0 2.8 copy-done.6
  152.8 9.5 %shard_map.68 = bf16[512,256]{1,0:T(8,128)(2,1)S(1)} custom-call(bf16[768,4096]{1,0:T(8,128)(2,1)S(1)} %copy-done.1, bf16[16,3,256,256]{3,2,1,0:T(8,128)(2,1)S(1)} %bitcast.13, f32[3,7,2048]{2,1,0:T(8,128)S(1)} %convert_bitcast_fusion.sw_ref, f32[128,256]{1,0:T(8,128)S(1)} %pad_convert_fusion.fr_ref, s32[768,128]{1,0:T(8,128)S(1)} %broadcast_in_dim.12.pos_ref), custom_call_target="tpu_custom_call" | custom-call | flops 5637144576 | bytes 12976128 | tf_op jit(solution)/shard_map/pallas_call | solution.py:101
  162.3 86.6 %all-gather.11.cloned.1.call-done = bf16[48,256,512]{2,1,0:T(8,128)(2,1)} async-done(((bf16[3,256,512]{2,1,0:T(8,128)(2,1)}), bf16[48,256,512]{2,1,0:T(8,128)(2,1)}) %all-gather.11.cloned.1.call-update) | async-done | bytes 12582928 | tf_op jit(solution)/shard_map/all_gather | solution.py:154
  249.0 2.8 copy-done.2
  251.7 22.0 %shard_map.64 = bf16[512,512]{1,0:T(8,128)(2,1)S(1)} custom-call(bf16[768,4096]{1,0:T(8,128)(2,1)S(1)} %copy-done.2, bf16[16,3,256,512]{3,2,1,0:T(8,128)(2,1)} %bitcast.18, f32[3,7,2048]{2,1,0:T(8,128)S(1)} %convert_bitcast_fusion.sw_ref, f32[128,256]{1,0:T(8,128)S(1)} %pad_convert_fusion.fr_ref, s32[768,128]{1,0:T(8,128)S(1)} %broadcast_in_dim.12.pos_ref), custom_call_target="tpu_custom_call" | custom-call | flops 11274289152 | bytes 25952256 | tf_op jit(solution)/shard_map/pallas_call | solution.py:101
  273.8 0.8 constant_dynamic-update-slice_fusion.4
  274.6 75.5 %all-gather.13.cloned.1.call-done = bf16[48,256,512]{2,1,0:T(8,128)(2,1)} async-done(((bf16[3,256,512]{2,1,0:T(8,128)(2,1)}), bf16[48,256,512]{2,1,0:T(8,128)(2,1)}) %all-gather.13.cloned.1.call-update) | async-done | bytes 12582928 | tf_op jit(solution)/shard_map/all_gather | solution.py:154
  350.1 2.8 copy-done.3
  352.9 22.0 %shard_map.65 = bf16[512,512]{1,0:T(8,128)(2,1)S(1)} custom-call(bf16[768,4096]{1,0:T(8,128)(2,1)S(1)} %copy-done.3, bf16[16,3,256,512]{3,2,1,0:T(8,128)(2,1)} %bitcast.19, f32[3,7,2048]{2,1,0:T(8,128)S(1)} %convert_bitcast_fusion.sw_ref, f32[128,256]{1,0:T(8,128)S(1)} %pad_convert_fusion.fr_ref, s32[768,128]{1,0:T(8,128)S(1)} %broadcast_in_dim.12.pos_ref), custom_call_target="tpu_custom_call" | custom-call | flops 11274289152 | bytes 25952256 | tf_op jit(solution)/shard_map/pallas_call | solution.py:101
  374.9 76.3 %all-gather.15.cloned.1.call-done = bf16[48,256,512]{2,1,0:T(8,128)(2,1)} async-done(((bf16[3,256,512]{2,1,0:T(8,128)(2,1)}), bf16[48,256,512]{2,1,0:T(8,128)(2,1)}) %all-gather.15.cloned.1.call-update) | async-done | bytes 12582928 | tf_op jit(solution)/shard_map/all_gather | solution.py:154
  451.2 2.8 copy-done.4
  453.9 22.0 %shard_map.66 = bf16[512,512]{1,0:T(8,128)(2,1)S(1)} custom-call(bf16[768,4096]{1,0:T(8,128)(2,1)S(1)} %copy-done.4, bf16[16,3,256,512]{3,2,1,0:T(8,128)(2,1)} %bitcast.20, f32[3,7,2048]{2,1,0:T(8,128)S(1)} %convert_bitcast_fusion.sw_ref, f32[128,256]{1,0:T(8,128)S(1)} %pad_convert_fusion.fr_ref, s32[768,128]{1,0:T(8,128)S(1)} %broadcast_in_dim.12.pos_ref), custom_call_target="tpu_custom_call" | custom-call | flops 11274289152 | bytes 25952256 | tf_op jit(solution)/shard_map/pallas_call | solution.py:101
  476.0 0.8 constant_dynamic-update-slice_fusion.3
  476.8 0.8 constant_dynamic-update-slice_fusion.2
  477.7 0.7 constant_dynamic-update-slice_fusion.1
  478.4 0.7 constant_dynamic-update-slice_fusion
  (11 shorter events, 0.1 us)
Async XLA Ops:
  6.5 104.0 %all-gather.17.cloned.1.call-start = ((), (), s32[]{:S(2)}) async-start(), calls=%async_computation.3 | async-start | bytes 6684672 | tf_op jit(solution)/shard_map/all_gather | solution.py:154
  8.7 138.6 %all-gather.19.cloned.1.call-start = ((), (), s32[]{:S(2)}) async-start(), calls=%async_computation.4 | async-start | bytes 6684672 | tf_op jit(solution)/shard_map/all_gather | solution.py:154
  9.4 4.5 copy-start.7
  9.4 239.5 %all-gather.11.cloned.1.call-start = ((), (), s32[]{:S(2)}) async-start(), calls=%async_computation | async-start | bytes 13369344 | tf_op jit(solution)/shard_map/all_gather | solution.py:154
  12.7 1.8 copy-start.11
  12.7 337.4 %all-gather.13.cloned.1.call-start = ((), (), s32[]{:S(2)}) async-start(), calls=%async_computation.1 | async-start | bytes 13369344 | tf_op jit(solution)/shard_map/all_gather | solution.py:154
  13.3 437.9 %all-gather.15.cloned.1.call-start = ((), (), s32[]{:S(2)}) async-start(), calls=%async_computation.2 | async-start | bytes 13369344 | tf_op jit(solution)/shard_map/all_gather | solution.py:154
  13.9 3.1 collective-permute-start
  17.0 4.5 copy-start.8
  17.1 20.7 %collective-permute-start.1 = (bf16[144,2048]{1,0:T(8,128)(2,1)S(1)}, bf16[144,2048]{1,0:T(8,128)(2,1)S(1)}, u32[]{:S(2)}, u32[]{:S(2)}) collective-permute-start(bf16[144,2048]{1,0:T(8,128)(2,1)S(1)} %broadcast_select_fusion.3), channel_id=1, source_target_pairs={{0,4},{2,6},{4,8},{6,10},{8,12},{10,14},{12,16},{14,18},{16,20},{1... | collective-permute-start | bytes 1769480 | tf_op jit(solution)/shard_map/ppermute | solution.py:162
  38.9 4.2 copy-start.12
  38.9 4.4 copy-start.10
  38.9 4.8 copy-start.9
  40.8 59.3 %collective-permute-start.2 = (bf16[656,2048]{1,0:T(8,128)(2,1)}, bf16[656,2048]{1,0:T(8,128)(2,1)}, u32[]{:S(2)}, u32[]{:S(2)}) collective-permute-start(bf16[656,2048]{1,0:T(8,128)(2,1)} %pad_maximum_fusion), channel_id=1, source_target_pairs={{0,1},{1,0},{2,3},{3,2},{4,5},{5,4},{6,7},{7,6},{8,9},{9,8},{10,11... | collective-permute-start | bytes 8060936 | tf_op jit(solution)/shard_map/ppermute | solution.py:167
  110.7 2.8 copy-start
  113.5 3.6 copy-start.5
  147.2 2.8 copy-start.1
  150.0 2.8 copy-start.6
  249.0 2.8 copy-start.2
  350.1 2.8 copy-start.3
  451.2 2.8 copy-start.4
Sparse Core Ops, SparseCore 0:
  9.6 74.7 all-gather.16
  86.7 60.4 all-gather.18
  149.5 99.4 all-gather.10
  251.1 98.9 all-gather.12
  352.2 98.9 all-gather.14

commit v2 on v1

v2 whole, which is shorter than its diff:
```python
import jax
import jax.numpy as jnp
from jax import lax
from jax.experimental import pallas as pl
from jax.experimental.pallas import tpu as pltpu
from jax.sharding import PartitionSpec as P

ROW_TILE = 256
CHAN_TILE = 256
LANES = 128


def in_sequence(places, seq_lengths):
    seq_ends = jnp.cumsum(seq_lengths)
    starts = seq_ends - seq_lengths
    inside = (places[:, None] >= starts[None, :]) & (places[:, None] < seq_ends[None, :])
    return jnp.sum(jnp.where(inside, places[:, None] - starts[None, :], 0), axis=1)


def block_kernel(at_ref, x_ref, *refs):
    *w_refs, sw_ref, fr_ref, pos_ref, out_ref, proj, mix, band = refs
    total, rows, chans = x_ref.shape[1], out_ref.shape[1], out_ref.shape[2]
    halo = total - rows
    taps = sw_ref.shape[1]
    groups = fr_ref.shape[0]
    span = band.shape[0] // groups
    per_lanes = groups * LANES // chans
    width = LANES // per_lanes
    depth = w_refs[0].shape[2]

    @pl.when(pl.program_id(1) == 0)
    def _():
        proj[:, :8, :] = jnp.zeros((3, 8, chans), jnp.float32)
        for g in range(groups):
            row = jnp.broadcast_to(fr_ref[g : g + 1, :], (span, 2 * span))
            band[g * span : (g + 1) * span, :] = pltpu.roll(
                row, 0, 1, stride=1, stride_axis=0
            ).astype(band.dtype)

    units = [(w, k) for w in w_refs for k in range(w.shape[0])]
    align = LANES if depth % LANES == 0 else depth
    starts = [pl.multiple_of(at_ref[u], align) for u in range(len(units))]
    edges = [0, halo] + list(range(halo + ROW_TILE, total + 1, ROW_TILE))
    for low, high in zip(edges[:-1], edges[1:]):
        if depth % LANES == 0:
            x = jnp.concatenate([x_ref[0, low:high, pl.ds(at, depth)] for at in starts], axis=1)
        else:
            x = x_ref[0, low:high, :]
        for s in range(3):
            weight = jnp.concatenate([w[k, s] for w, k in units], axis=0)
            acc = jnp.dot(x, weight, preferred_element_type=jnp.float32)
            proj[s, 8 + low : 8 + high, :] = acc.astype(jnp.bfloat16).astype(jnp.float32)

    def short(s, start, size, lanes, allowed):
        running = proj[s, 8 + start : 8 + start + size, lanes] * sw_ref[s, 0:1, lanes]
        for j in range(1, taps):
            window = proj[s, 8 + start - j : 8 + start - j + size, lanes]
            running = running + jnp.where(allowed[j], window * sw_ref[s, j : j + 1, lanes], 0.0)
        return running

    step = 64
    for r in range(halo - span, total, step):
        pos = pos_ref[0, r : r + step, :]
        allowed = [pos >= j for j in range(taps)]
        for h in range(chans // LANES):
            lanes = slice(h * LANES, (h + 1) * LANES)
            mixed = short(0, r, step, lanes, allowed) * short(2, r, step, lanes, allowed)
            mix[r : r + step, lanes] = mixed.astype(mix.dtype)

    lag = (
        lax.broadcasted_iota(jnp.int32, (span, 2 * span), 0)
        + span
        - lax.broadcasted_iota(jnp.int32, (span, 2 * span), 1)
    )
    lane_group = lax.broadcasted_iota(jnp.int32, (span, LANES), 1) // width
    for b in range(rows // span):
        first = halo + b * span
        pos = pos_ref[0, first : first + span, :]
        limit = jnp.concatenate([pos] * (2 * span // LANES), axis=1)
        keep = jnp.where(lag <= limit, 1.0, 0.0).astype(band.dtype)
        allowed = [pos >= j for j in range(taps)]
        for h in range(chans // LANES):
            lanes = slice(h * LANES, (h + 1) * LANES)
            some = band[h * per_lanes * span : (h + 1) * per_lanes * span, :]
            some = some.reshape(per_lanes, span, 2 * span) * keep[None]
            full = jnp.dot(
                some.reshape(per_lanes * span, 2 * span),
                mix[first - span : first + span, lanes],
                preferred_element_type=jnp.float32,
            )
            medium = full[:span]
            for g in range(1, per_lanes):
                medium = jnp.where(lane_group == g, full[g * span : (g + 1) * span], medium)
            gate = short(1, first, span, lanes, allowed)
            out_ref[0, b * span : (b + 1) * span, lanes] = (gate * medium).astype(out_ref.dtype)


def block(at, x, weights, sw, fr, pos, span, rows):
    runs, total, features = x.shape
    depth, chans = weights[0].shape[2:]
    taps = sw.shape[1]
    tile = min(CHAN_TILE, chans)
    per_tile = tile * fr.shape[0] // chans
    grid = (chans // tile, runs)
    return pl.pallas_call(
        block_kernel,
        grid_spec=pltpu.PrefetchScalarGridSpec(
            num_scalar_prefetch=1,
            grid=grid,
            in_specs=[pl.BlockSpec((1, total, features), lambda j, i, at: (i, 0, 0))]
            + [pl.BlockSpec((w.shape[0], 3, depth, tile), lambda j, i, at: (0, 0, 0, j)) for w in weights]
            + [
                pl.BlockSpec((3, taps, tile), lambda j, i, at: (0, 0, j)),
                pl.BlockSpec((per_tile, 2 * span), lambda j, i, at: (j, 0)),
                pl.BlockSpec((1, total, LANES), lambda j, i, at: (i, 0, 0)),
            ],
            out_specs=pl.BlockSpec((1, rows, tile), lambda j, i, at: (i, 0, j)),
            scratch_shapes=[
                pltpu.VMEM((3, 8 + total, tile), jnp.float32),
                pltpu.VMEM((total, tile), jnp.bfloat16),
                pltpu.VMEM((per_tile * span, 2 * span), jnp.bfloat16),
            ],
        ),
        out_shape=jax.ShapeDtypeStruct((runs, rows, chans), jnp.bfloat16),
        compiler_params=pltpu.CompilerParams(vmem_limit_bytes=56 * 1024 * 1024),
        cost_estimate=pl.CostEstimate(
            flops=2 * runs * total * features * 3 * chans + 2 * runs * rows * (chans // tile) * per_tile * span * 256,
            bytes_accessed=2 * (runs * total * features * grid[0] + 3 * features * chans + runs * rows * chans),
            transcendentals=0,
        ),
    )(at, x, *weights, sw, fr, pos)


def parameters(short_weight, medium_filter):
    sw = jnp.transpose(short_weight, (1, 0, 2)).astype(jnp.float32)
    span = medium_filter.shape[0]
    fr = jnp.pad(jnp.flip(medium_filter, axis=0).T.astype(jnp.float32), ((0, 0), (1, span - 1)))
    return sw, fr


def flip(array, bit):
    return lax.ppermute(array, "stretch", [(i, i ^ bit) for i in range(lax.axis_size("stretch"))])


def across(array):
    return lax.ppermute(array, "chan", [(0, 1), (1, 0)])


def rows_before(tokens, stretch_id, reach):
    tail = tokens[tokens.shape[0] - reach :]
    sibling = flip(tail, 1)
    second = stretch_id % 2 == 1
    pairs = [(i, i + 2) for i in range(lax.axis_size("stretch") - 2)]
    before = lax.ppermute(jnp.where(second, tail, sibling), "stretch", pairs)
    return jnp.where(second, sibling, before)


def whole_rows(halo, halo_other, rows, rows_other, low):
    left = jnp.concatenate([jnp.where(low, halo, halo_other), jnp.where(low, rows, rows_other)], axis=0)
    right = jnp.concatenate([jnp.where(low, halo_other, halo), jnp.where(low, rows_other, rows)], axis=0)
    return jnp.concatenate([left, right], axis=1)


def tied(value, other):
    return lax.optimization_barrier((value, other))


def per_device(tokens, in_weight, short_weight, medium_filter, seq_lengths, stretch_slot):
    row_count = tokens.shape[0]
    depth, _, chans = in_weight.shape
    span, taps = medium_filter.shape[0], short_weight.shape[0]
    me = lax.axis_index("stretch")
    devices = lax.axis_size("stretch")
    order = jnp.arange(devices, dtype=jnp.int32)
    reach = -(-(span + taps - 1) // 16) * 16
    sw, fr = parameters(short_weight, medium_filter)
    local = jnp.transpose(in_weight, (1, 0, 2))

    def stretch_at(device):
        return jnp.sum(jnp.where(stretch_slot == device, order, 0))

    def positions(device):
        places = stretch_at(device) * row_count - reach + jnp.arange(reach + row_count, dtype=jnp.int32)
        return jnp.broadcast_to(in_sequence(places, seq_lengths)[:, None], (reach + row_count, LANES))

    if devices != 16 or lax.axis_size("chan") != 2:
        weight = lax.all_gather(local, "stretch", axis=0, tiled=False)
        rows = jnp.concatenate([rows_before(tokens, stretch_at(me), reach), tokens], axis=0)
        x = lax.all_gather(rows, "chan", axis=1, tiled=True)
        out = block(order * depth, x[None], [weight], sw, fr, positions(me)[None], span, row_count)
        return out[0]

    low = lax.axis_index("chan") == 0
    kind = (me >> 2) & 1
    half = chans // 2
    own_begin, other_begin = kind * half, (1 - kind) * half

    peer_rows = flip(tokens, 4)
    rows_other = across(tokens)
    halo = rows_before(tokens, stretch_at(me), reach)
    halo_other = across(halo)
    peer_halo = flip(halo, 4)

    widths = [CHAN_TILE] * (half // CHAN_TILE)
    begins = [sum(widths[:c]) for c in range(len(widths))]
    arrived = []
    for c, (begin, width) in enumerate(zip(begins, widths)):
        here = local
        if c == 1:
            here, peer_rows = tied(here, peer_rows)
        if c >= 2:
            here, arrived[c - 2] = tied(here, arrived[c - 2])
        own = lax.dynamic_slice_in_dim(here, own_begin + begin, width, 2)
        other = lax.dynamic_slice_in_dim(here, other_begin + begin, width, 2)
        arrived.append([own, flip(other, 4), flip(own, 8), flip(other, 12)])

    peer_rows_other = across(peer_rows)
    peer_halo_other = across(peer_halo)
    x = jnp.stack(
        [
            whole_rows(halo, halo_other, tokens, rows_other, low),
            whole_rows(peer_halo, peer_halo_other, peer_rows, peer_rows_other, low),
        ]
    )
    pos = jnp.stack([positions(me), positions(me ^ 4)])
    at = jnp.stack([me ^ (4 * k + q) for q in (0, 2, 1, 3) for k in range(4)]) * depth
    own_sw = lax.dynamic_slice_in_dim(sw, own_begin, half, 2)
    own_fr = lax.dynamic_slice_in_dim(fr, own_begin * fr.shape[0] // chans, fr.shape[0] // 2, 0)

    mine, theirs = [], []
    for c, (begin, width) in enumerate(zip(begins, widths)):
        line = jnp.stack(arrived[c])
        beside = flip(line, 2)
        weights = [line, beside, flip(line, 1), flip(beside, 1)]
        groups = fr.shape[0] * width // chans
        first_group = begin * fr.shape[0] // chans
        out = block(
            at,
            x,
            weights,
            own_sw[:, :, begin : begin + width],
            own_fr[first_group : first_group + groups],
            pos,
            span,
            row_count,
        )
        mine.append(out[0])
        theirs.append(flip(out[1], 4))
    mine, theirs = jnp.concatenate(mine, axis=1), jnp.concatenate(theirs, axis=1)
    even = kind == 0
    return jnp.concatenate([jnp.where(even, mine, theirs), jnp.where(even, theirs, mine)], axis=1)


def solution(mesh):
    return jax.shard_map(
        per_device,
        mesh=mesh,
        in_specs=(
            P("stretch", "chan"),
            P("stretch", None, "chan"),
            P(None, None, "chan"),
            P(None, "chan"),
            P(),
            P(),
        ),
        out_specs=P("stretch", "chan"),
        check_vma=False,
    )
```

time: 486 us -> 361 us (0.74); the launches traced: 486 us -> 356 us
  waiting for transfers between devices: 333 us -> 182 us
  starting transfers between devices: 6.84 us -> 41.3 us
  other arithmetic: 14.5 us -> 35 us
  local copies, waits for them, and re-layouts: 29.9 us -> 14.1 us
  between operations: 15.9 us -> 3.9 us
  Pallas kernels: 85.2 us -> 78.9 us
    all_gather x5 -> x0, waiting for transfers between devices: 259 us -> none  [per_device(): lax.all_gather(part, 'stretch', axis=0, tiled=False)]
    ppermute x3 -> x36, waiting for transfers between devices: 72.6 us -> 182 us  [the longest x31 171 us: flip(): lax.ppermute(array, 'stretch', [(i, i ^ bit) for i in range(lax.axis_size...]
    ppermute x3 -> x36, starting transfers between devices: 6.68 us -> 41.3 us  [the longest x31 32.4 us: flip(): lax.ppermute(array, 'stretch', [(i, i ^ bit) for i in range(lax.axis_size...]
    another operation x1 -> x8, other arithmetic: 0.18 us -> 22.7 us  [the longest x2 17.5 us: per_device(): jnp.stack([whole_rows(halo, halo_other, tokens, rows_other, low), whole_r...]
    unnamed x31 -> x50, local copies, waits for them, and re-layouts: 23.6 us -> 2.15 us
    concatenate x2 -> x1, other arithmetic: 9.38 us -> 1.51 us  [per_device(): jnp.concatenate([jnp.where(even, mine, theirs), jnp.where(even, theirs, m...]
    pallas_call x5 -> x4, Pallas kernels: 85.2 us -> 78.9 us  [block(): pl.pallas_call(block_kernel, grid_spec=pltpu.PrefetchScalarGridSpec(num_s...]
  transfers between devices with their start and end apart: 8 -> 36, of which waited for: 6 -> 14; matrix products, arithmetic and copies ran while one was open for 4% -> 13% of each run, Pallas kernels for 13% -> 22%
where the time goes in v2:
time: 361 us; the launch traced here: 356 us
  waiting for transfers between devices  182 us (50%)
  Pallas kernels  78.9 us (22%)
  starting transfers between devices  41.3 us (11%)
  other arithmetic  35 us (10%)
  local copies, waits for them, and re-layouts  14.1 us (4%)
  between operations  3.9 us (1%)
    ppermute x31, waiting for transfers between devices, flip(): lax.ppermute(array, 'stretch', [(i, i ^ bit) for i in range(lax.axis_size...  171 us
    pallas_call x4, Pallas kernels, block(): pl.pallas_call(block_kernel, grid_spec=pltpu.PrefetchScalarGridSpec(num_s...  78.9 us
    ppermute x31, starting transfers between devices, flip(): lax.ppermute(array, 'stretch', [(i, i ^ bit) for i in range(lax.axis_size...  32.4 us
    another operation x2, other arithmetic, per_device(): jnp.stack([whole_rows(halo, halo_other, tokens, rows_other, low), whole_r...  17.5 us
    ppermute x4, waiting for transfers between devices, across(): return lax.ppermute(array, 'chan', [(0, 1), (1, 0)])  11.8 us
  transfers between devices with their start and end apart: 36, of which 14 were waited for; matrix products, arithmetic and copies ran while one was open for 13% of the time, Pallas kernels for 22%

profile of v2, /device:TPU:0, one launch (start us, length us, event | category | flops | bytes accessed | tf_op | source)
XLA Modules:
  0.0 355.6 jit_solution(6818442423713860046)
XLA Ops:
  0.0 3.0 collective-permute-start.3
  3.1 1.6 collective-permute-start.6
  4.6 1.9 dynamic-slice_bitcast_fusion
  7.0 3.6 %collective-permute-start.10 = (bf16[3,256,256]{2,1,0:T(8,128)(2,1)}, bf16[3,256,256]{2,1,0:T(8,128)(2,1)}, u32[]{:S(2)}, u32[]{:S(2)}) collective-permute-start(bf16[3,256,256]{2,1,0:T(8,128)(2,1)} %get-tuple-element.43), channel_id=1, source_target_pairs={{0,24},{2,26},{4,28},{6,30},{8,16},{10,18},{12,20},{14,22},{16,8},... | collective-permute-start | bytes 1179656 | tf_op jit(solution)/shard_map/ppermute | solution.py:142
  10.6 1.9 slice.51
  12.5 0.7 fusion.2
  15.8 0.6 fusion.4
  16.4 0.9 broadcast_select_fusion.7
  17.3 4.2 %collective-permute-start.1 = (bf16[144,2048]{1,0:T(8,128)(2,1)}, bf16[144,2048]{1,0:T(8,128)(2,1)}, u32[]{:S(2)}, u32[]{:S(2)}) collective-permute-start(bf16[144,2048]{1,0:T(8,128)(2,1)} %broadcast_select_fusion.7), channel_id=1, source_target_pairs={{0,4},{2,6},{4,8},{6,10},{8,12},{10,14},{12,16},{14,18},{16,20},{1... | collective-permute-start | bytes 1769480 | tf_op jit(solution)/shard_map/ppermute | solution.py:154
  21.5 0.6 broadcast_multiply_fusion.at_ref
  23.4 36.1 %collective-permute-done.8 = bf16[3,256,256]{2,1,0:T(8,128)(2,1)S(1)} collective-permute-done((bf16[3,256,256]{2,1,0:T(8,128)(2,1)}, bf16[3,256,256]{2,1,0:T(8,128)(2,1)S(1)}, u32[]{:S(2)}, u32[]{:S(2)}) %collective-permute-start.8) | collective-permute-done | bytes 393248 | tf_op jit(solution)/shard_map/ppermute | solution.py:142
  59.4 3.4 collective-permute-start.9
  62.8 0.8 convert_bitcast_fusion
  63.6 0.7 fusion.3
  64.3 21.2 %collective-permute-done.9 = bf16[3,256,256]{2,1,0:T(8,128)(2,1)} collective-permute-done((bf16[3,256,256]{2,1,0:T(8,128)(2,1)S(1)}, bf16[3,256,256]{2,1,0:T(8,128)(2,1)}, u32[]{:S(2)}, u32[]{:S(2)}) %collective-permute-start.9) | collective-permute-done | bytes 393248 | tf_op jit(solution)/shard_map/ppermute | solution.py:142
  85.5 1.9 constant_dynamic-slice_fusion.3
  87.4 2.1 collective-permute-start.22
  89.5 2.3 collective-permute-start.21
  91.8 1.1 broadcast_select_fusion.6
  93.0 8.6 %collective-permute-done.22 = bf16[3,256,256]{2,1,0:T(8,128)(2,1)S(1)} collective-permute-done((bf16[3,256,256]{2,1,0:T(8,128)(2,1)}, bf16[3,256,256]{2,1,0:T(8,128)(2,1)S(1)}, u32[]{:S(2)}, u32[]{:S(2)}) %collective-permute-start.22) | collective-permute-done | bytes 393248 | tf_op jit(solution)/shard_map/ppermute | solution.py:142
  101.5 0.6 collective-permute-start.2
  102.1 20.4 %collective-permute-done.21 = bf16[3,256,256]{2,1,0:T(8,128)(2,1)S(1)} collective-permute-done((bf16[3,256,256]{2,1,0:T(8,128)(2,1)S(1)}, bf16[3,256,256]{2,1,0:T(8,128)(2,1)S(1)}, u32[]{:S(2)}, u32[]{:S(2)}) %collective-permute-start.21) | collective-permute-done | bytes 393248 | tf_op jit(solution)/shard_map/ppermute | solution.py:142
  122.6 0.7 copy-done.13
  123.7 0.9 pad_add_fusion.refs_6_
  124.7 1.3 pad_maximum_fusion.2.refs_0_
  126.0 5.4 %collective-permute-start.11 = (bf16[4,3,256,256]{3,2,1,0:T(8,128)(2,1)S(1)}, bf16[4,3,256,256]{3,2,1,0:T(8,128)(2,1)S(1)}, u32[]{:S(2)}, u32[]{:S(2)}) collective-permute-start(bf16[4,3,256,256]{3,2,1,0:T(8,128)(2,1)S(1)} %pad_maximum_fusion.2.refs_0_), channel_id=1, source_target_pairs={{0,4},{2,6},{4,0},{6,2},{8,12},{10,14},{12,8},{14,10},{16,20},{18,... | collective-permute-start | bytes 4718600 | tf_op jit(solution)/shard_map/ppermute | solution.py:142
  131.4 1.2 pad_maximum_fusion.4.refs_0_
  132.7 0.7 collective-permute-start.23
  133.5 0.6 collective-permute-start.7
  134.1 3.0 collective-permute-done.4
  137.4 0.9 collective-permute-start.15
  138.2 1.1 broadcast_select_fusion.11
  139.4 13.0 %collective-permute-done.14 = bf16[3,256,256]{2,1,0:T(8,128)(2,1)S(1)} collective-permute-done((bf16[3,256,256]{2,1,0:T(8,128)(2,1)S(1)}, bf16[3,256,256]{2,1,0:T(8,128)(2,1)S(1)}, u32[]{:S(2)}, u32[]{:S(2)}) %collective-permute-start.14) | collective-permute-done | bytes 393248 | tf_op jit(solution)/shard_map/ppermute | solution.py:142
  152.9 8.6 %collective-permute-done.15 = bf16[3,256,256]{2,1,0:T(8,128)(2,1)S(1)} collective-permute-done((bf16[3,256,256]{2,1,0:T(8,128)(2,1)S(1)}, bf16[3,256,256]{2,1,0:T(8,128)(2,1)S(1)}, u32[]{:S(2)}, u32[]{:S(2)}) %collective-permute-start.15) | collective-permute-done | bytes 393248 | tf_op jit(solution)/shard_map/ppermute | solution.py:142
  161.5 1.9 broadcast_select_fusion.3
  163.3 9.7 %collective-permute-done.16 = bf16[3,256,256]{2,1,0:T(8,128)(2,1)S(1)} collective-permute-done((bf16[3,256,256]{2,1,0:T(8,128)(2,1)S(1)}, bf16[3,256,256]{2,1,0:T(8,128)(2,1)S(1)}, u32[]{:S(2)}, u32[]{:S(2)}) %collective-permute-start.16) | collective-permute-done | bytes 393248 | tf_op jit(solution)/shard_map/ppermute | solution.py:142
  173.1 1.4 collective-permute-start.28
  174.5 3.5 collective-permute-start.26
  178.1 11.8 %collective-permute-done.5 = bf16[144,2048]{1,0:T(8,128)(2,1)S(1)} collective-permute-done((bf16[144,2048]{1,0:T(8,128)(2,1)}, bf16[144,2048]{1,0:T(8,128)(2,1)S(1)}, u32[]{:S(2)}, u32[]{:S(2)}) %collective-permute-start.5) | collective-permute-done | bytes 589856 | tf_op jit(solution)/shard_map/ppermute | solution.py:146
  189.8 0.7 collective-permute-start.27
  190.5 1.1 broadcast_select_fusion.9
  191.9 4.1 %collective-permute-done.23.refs_1_ = bf16[4,3,256,256]{3,2,1,0:T(8,128)(2,1)} collective-permute-done((bf16[4,3,256,256]{3,2,1,0:T(8,128)(2,1)S(1)}, bf16[4,3,256,256]{3,2,1,0:T(8,128)(2,1)}, u32[]{:S(2)}, u32[]{:S(2)}) %collective-permute-start.23) | collective-permute-done | bytes 1572896 | tf_op jit(solution)/shard_map/ppermute | solution.py:142
  196.5 10.7 %collective-permute-done.27 = bf16[3,256,256]{2,1,0:T(8,128)(2,1)S(1)} collective-permute-done((bf16[3,256,256]{2,1,0:T(8,128)(2,1)S(1)}, bf16[3,256,256]{2,1,0:T(8,128)(2,1)S(1)}, u32[]{:S(2)}, u32[]{:S(2)}) %collective-permute-start.27) | collective-permute-done | bytes 393248 | tf_op jit(solution)/shard_map/ppermute | solution.py:142
  207.7 1.4 pad_maximum_fusion.5.refs_0_
  209.1 0.8 collective-permute-start.17
  209.9 1.9 broadcast_select_fusion.1
  211.8 12.7 %maximum_bitcast_fusion = (bf16[1,656,4096]{2,1,0:T(8,128)(2,1)S(1)}, bf16[1,656,4096]{2,1,0:T(8,128)(2,1)S(1)}) fusion(bf16[512,2048]{1,0:T(8,128)(2,1)S(1)} %get-tuple-element.34, bf16[144,2048]{1,0:T(8,128)(2,1)S(1)} %get-tuple-element.48, bf16[512,2048]{1,0:T(8,128)(2,1)S(1)} %get-tuple-element.33, bf16[144,2048]{1,0:T(8,128)(2,1)S(1)} %get-tuple-element.47, ...), kind=kLoop, calls=%fused_computation.1 | loop fusion | flops 42991616 | bytes 21495808 | tf_op jit(solution)/shard_map/stack | solution.py:219
  224.5 1.3 collective-permute-start.29
  225.8 4.8 %pad_maximum_fusion.x_ref = bf16[2,656,4096]{2,1,0:T(8,128)(2,1)} fusion(bf16[1,656,4096]{2,1,0:T(8,128)(2,1)S(1)} %get-tuple-element.68, bf16[1,656,4096]{2,1,0:T(8,128)(2,1)S(1)} %get-tuple-element.67), kind=kLoop, calls=%fused_computation | loop fusion | flops 5373952 | bytes 21495808 | tf_op jit(solution)/shard_map/stack | solution.py:219
  230.7 15.8 %collective-permute-done.17.refs_1_ = bf16[4,3,256,256]{3,2,1,0:T(8,128)(2,1)} collective-permute-done((bf16[4,3,256,256]{3,2,1,0:T(8,128)(2,1)S(1)}, bf16[4,3,256,256]{3,2,1,0:T(8,128)(2,1)}, u32[]{:S(2)}, u32[]{:S(2)}) %collective-permute-start.17) | collective-permute-done | bytes 1572896 | tf_op jit(solution)/shard_map/ppermute | solution.py:142
  246.5 19.6 %shard_map.64 = bf16[2,512,256]{2,1,0:T(8,128)(2,1)} custom-call(s32[16]{0:T(128)} %broadcast_multiply_fusion.at_ref, bf16[2,656,4096]{2,1,0:T(8,128)(2,1)} %pad_maximum_fusion.x_ref, bf16[4,3,256,256]{3,2,1,0:T(8,128)(2,1)} %copy-done.3, bf16[4,3,256,256]{3,2,1,0:T(8,128)(2,1)} %copy-done.17, bf16[4,3,256,256]{3,2,1,0:T(8,128)(2,1)} %copy-done.19, ...), custom_call_target="tpu_custom_call" | custom-call | flops 9328132096 | bytes 17563648 | tf_op jit(solution)/shard_map/pallas_call | solution.py:105
  266.0 1.1 slice_bitcast_fusion.7
  267.1 0.6 collective-permute-start.30
  267.7 11.5 %collective-permute-done.29.refs_1_ = bf16[4,3,256,256]{3,2,1,0:T(8,128)(2,1)S(1)} collective-permute-done((bf16[4,3,256,256]{3,2,1,0:T(8,128)(2,1)}, bf16[4,3,256,256]{3,2,1,0:T(8,128)(2,1)S(1)}, u32[]{:S(2)}, u32[]{:S(2)}) %collective-permute-start.29) | collective-permute-done | bytes 1572896 | tf_op jit(solution)/shard_map/ppermute | solution.py:142
  279.2 19.7 %shard_map.66 = bf16[2,512,256]{2,1,0:T(8,128)(2,1)} custom-call(s32[16]{0:T(128)} %broadcast_multiply_fusion.at_ref, bf16[2,656,4096]{2,1,0:T(8,128)(2,1)} %pad_maximum_fusion.x_ref, bf16[4,3,256,256]{3,2,1,0:T(8,128)(2,1)} %copy-done.2, bf16[4,3,256,256]{3,2,1,0:T(8,128)(2,1)} %collective-permute-done.23.refs_1_, ...), custom_call_target="tpu_custom_call" | custom-call | flops 9328132096 | bytes 17563648 | tf_op jit(solution)/shard_map/pallas_call | solution.py:105
  298.9 1.1 slice_bitcast_fusion.5
  300.1 19.8 %shard_map.65 = bf16[2,512,256]{2,1,0:T(8,128)(2,1)} custom-call(s32[16]{0:T(128)} %broadcast_multiply_fusion.at_ref, bf16[2,656,4096]{2,1,0:T(8,128)(2,1)} %pad_maximum_fusion.x_ref, bf16[4,3,256,256]{3,2,1,0:T(8,128)(2,1)} %copy-done.4, bf16[4,3,256,256]{3,2,1,0:T(8,128)(2,1)} %collective-permute-done.17.refs_1_, ...), custom_call_target="tpu_custom_call" | custom-call | flops 9328132096 | bytes 17563648 | tf_op jit(solution)/shard_map/pallas_call | solution.py:105
  319.9 1.1 slice_bitcast_fusion.6
  320.9 2.1 collective-permute-start.33
  323.0 1.1 copy-done.21
  324.2 19.8 %shard_map.67 = bf16[2,512,256]{2,1,0:T(8,128)(2,1)} custom-call(s32[16]{0:T(128)} %broadcast_multiply_fusion.at_ref, bf16[2,656,4096]{2,1,0:T(8,128)(2,1)} %pad_maximum_fusion.x_ref, bf16[4,3,256,256]{3,2,1,0:T(8,128)(2,1)} %pad_maximum_fusion.5.refs_0_, bf16[4,3,256,256]{3,2,1,0:T(8,128)(2,1)} %copy-done.18, bf16[4,3,256,256]{3,2,1,0:T(8,128)(2,1)} %copy-done.21, ...), custom_call_target="tpu_custom_call" | custom-call | flops 9328132096 | bytes 17563648 | tf_op jit(solution)/shard_map/pallas_call | solution.py:105
  344.0 1.1 slice_bitcast_fusion.4
  345.2 8.1 %collective-permute-done.35 = bf16[512,256]{1,0:T(8,128)(2,1)S(1)} collective-permute-done((bf16[512,256]{1,0:T(8,128)(2,1)S(1)}, bf16[512,256]{1,0:T(8,128)(2,1)S(1)}, u32[]{:S(2)}, u32[]{:S(2)}) %collective-permute-start.35) | collective-permute-done | bytes 262176 | tf_op jit(solution)/shard_map/ppermute | solution.py:142
  353.8 1.5 pad_maximum_fusion.1
  (101 shorter events, 4.6 us)
Async XLA Ops:
  0.0 16.4 %copy-start = (bf16[512,2048]{1,0:T(8,128)(2,1)S(1)}, bf16[512,2048]{1,0:T(8,128)(2,1)}, u32[]{:S(2)}) copy-start(bf16[512,2048]{1,0:T(8,128)(2,1)} %param.6) | copy-start | bytes 6291460
  0.0 12.5 %copy-start.16 = (s32[16]{0:T(128)S(1)}, s32[16]{0:T(128)}, u32[]{:S(2)}) copy-start(s32[16]{0:T(128)} %param.11) | copy-start | bytes 196
  0.0 15.2 %copy-start.15 = (bf16[128,128]{1,0:T(8,128)(2,1)S(1)}, bf16[128,128]{1,0:T(8,128)(2,1)}, u32[]{:S(2)}) copy-start(bf16[128,128]{1,0:T(8,128)(2,1)} %param.9) | copy-start | bytes 98308
  0.0 15.4 %copy-start.22 = (s32[8]{0:T(128)S(1)}, s32[8]{0:T(128)}, u32[]{:S(2)}) copy-start(s32[8]{0:T(128)} %param.10) | copy-start | bytes 100
  0.0 137.3 %collective-permute-start.3 = (bf16[512,2048]{1,0:T(8,128)(2,1)}, bf16[512,2048]{1,0:T(8,128)(2,1)}, u32[]{:S(2)}, u32[]{:S(2)}) collective-permute-start(bf16[512,2048]{1,0:T(8,128)(2,1)} %param.6), channel_id=1, source_target_pairs={{0,1},{1,0},{2,3},{3,2},{4,5},{5,4},{6,7},{7,6},{8,9},{9,8},{10,11... | collective-permute-start | bytes 6291464 | tf_op jit(solution)/shard_map/ppermute | solution.py:146
  3.1 129.6 %collective-permute-start.6 = (bf16[512,2048]{1,0:T(8,128)(2,1)}, bf16[512,2048]{1,0:T(8,128)(2,1)}, u32[]{:S(2)}, u32[]{:S(2)}) collective-permute-start(bf16[512,2048]{1,0:T(8,128)(2,1)} %param.6), channel_id=1, source_target_pairs={{0,8},{2,10},{4,12},{6,14},{8,0},{10,2},{12,4},{14,6},{16,24},{18,... | collective-permute-start | bytes 6291464 | tf_op jit(solution)/shard_map/ppermute | solution.py:142
  6.5 80.9 %copy-start.5 = (bf16[3,256,256]{2,1,0:T(8,128)(2,1)}, bf16[3,256,256]{2,1,0:T(8,128)(2,1)S(1)}, u32[]{:S(2)}) copy-start(bf16[3,256,256]{2,1,0:T(8,128)(2,1)S(1)} %get-tuple-element.18) | copy-start | bytes 1179652
  6.6 52.9 %collective-permute-start.8 = (bf16[3,256,256]{2,1,0:T(8,128)(2,1)}, bf16[3,256,256]{2,1,0:T(8,128)(2,1)S(1)}, u32[]{:S(2)}, u32[]{:S(2)}) collective-permute-start(bf16[3,256,256]{2,1,0:T(8,128)(2,1)} %get-tuple-element.43), channel_id=1, source_target_pairs={{0,8},{2,10},{4,12},{6,14},{8,0},{10,2},{12,4},{14,6},{16,24},{18,... | collective-permute-start | bytes 1179656 | tf_op jit(solution)/shard_map/ppermute | solution.py:142
  7.0 78.5 %collective-permute-start.10 = (bf16[3,256,256]{2,1,0:T(8,128)(2,1)}, bf16[3,256,256]{2,1,0:T(8,128)(2,1)}, u32[]{:S(2)}, u32[]{:S(2)}) collective-permute-start(bf16[3,256,256]{2,1,0:T(8,128)(2,1)} %get-tuple-element.43), channel_id=1, source_target_pairs={{0,24},{2,26},{4,28},{6,30},{8,16},{10,18},{12,20},{14,22},{16,8},... | collective-permute-start | bytes 1179656 | tf_op jit(solution)/shard_map/ppermute | solution.py:142
  12.5 3.9 %collective-permute-start = (bf16[144,2048]{1,0:T(8,128)(2,1)}, bf16[144,2048]{1,0:T(8,128)(2,1)S(1)}, u32[]{:S(2)}, u32[]{:S(2)}) collective-permute-start(bf16[144,2048]{1,0:T(8,128)(2,1)} %slice.51), channel_id=1, source_target_pairs={{0,2},{2,0},{4,6},{6,4},{8,10},{10,8},{12,14},{14,12},{16,18},{18,... | collective-permute-start | bytes 1769480 | tf_op jit(solution)/shard_map/ppermute | solution.py:142
  17.3 72.2 %collective-permute-start.1 = (bf16[144,2048]{1,0:T(8,128)(2,1)}, bf16[144,2048]{1,0:T(8,128)(2,1)}, u32[]{:S(2)}, u32[]{:S(2)}) collective-permute-start(bf16[144,2048]{1,0:T(8,128)(2,1)} %broadcast_select_fusion.7), channel_id=1, source_target_pairs={{0,4},{2,6},{4,8},{6,10},{8,12},{10,14},{12,16},{14,18},{16,20},{1... | collective-permute-start | bytes 1769480 | tf_op jit(solution)/shard_map/ppermute | solution.py:154
  59.4 30.1 %copy-start.9 = (bf16[3,256,256]{2,1,0:T(8,128)(2,1)}, bf16[3,256,256]{2,1,0:T(8,128)(2,1)S(1)}, u32[]{:S(2)}) copy-start(bf16[3,256,256]{2,1,0:T(8,128)(2,1)S(1)} %collective-permute-done.8) | copy-start | bytes 1179652
  59.4 26.1 %collective-permute-start.9 = (bf16[3,256,256]{2,1,0:T(8,128)(2,1)S(1)}, bf16[3,256,256]{2,1,0:T(8,128)(2,1)}, u32[]{:S(2)}, u32[]{:S(2)}) collective-permute-start(bf16[3,256,256]{2,1,0:T(8,128)(2,1)S(1)} %get-tuple-element.18), channel_id=1, source_target_pairs={{0,16},{2,18},{4,20},{6,22},{8,24},{10,26},{12,28},{14,30},{16,0},... | collective-permute-start | bytes 1179656 | tf_op jit(solution)/shard_map/ppermute | solution.py:142
  87.4 14.7 %copy-start.7 = (bf16[3,256,256]{2,1,0:T(8,128)(2,1)}, bf16[3,256,256]{2,1,0:T(8,128)(2,1)S(1)}, u32[]{:S(2)}) copy-start(bf16[3,256,256]{2,1,0:T(8,128)(2,1)S(1)} %get-tuple-element.39) | copy-start | bytes 1179652
  87.4 14.1 %collective-permute-start.22 = (bf16[3,256,256]{2,1,0:T(8,128)(2,1)}, bf16[3,256,256]{2,1,0:T(8,128)(2,1)S(1)}, u32[]{:S(2)}, u32[]{:S(2)}) collective-permute-start(bf16[3,256,256]{2,1,0:T(8,128)(2,1)} %get-tuple-element.40), channel_id=1, source_target_pairs={{0,24},{2,26},{4,28},{6,30},{8,16},{10,18},{12,20},{14,22},{16,8},... | collective-permute-start | bytes 1179656 | tf_op jit(solution)/shard_map/ppermute | solution.py:142
  89.5 36.5 %collective-permute-start.20 = (bf16[3,256,256]{2,1,0:T(8,128)(2,1)}, bf16[3,256,256]{2,1,0:T(8,128)(2,1)}, u32[]{:S(2)}, u32[]{:S(2)}) collective-permute-start(bf16[3,256,256]{2,1,0:T(8,128)(2,1)} %get-tuple-element.40), channel_id=1, source_target_pairs={{0,8},{2,10},{4,12},{6,14},{8,0},{10,2},{12,4},{14,6},{16,24},{18,... | collective-permute-start | bytes 1179656 | tf_op jit(solution)/shard_map/ppermute | solution.py:142
  89.5 33.0 %collective-permute-start.21 = (bf16[3,256,256]{2,1,0:T(8,128)(2,1)S(1)}, bf16[3,256,256]{2,1,0:T(8,128)(2,1)S(1)}, u32[]{:S(2)}, u32[]{:S(2)}) collective-permute-start(bf16[3,256,256]{2,1,0:T(8,128)(2,1)S(1)} %get-tuple-element.39), channel_id=1, source_target_pairs={{0,16},{2,18},{4,20},{6,22},{8,24},{10,26},{12,28},{14,30},{16,0},... | collective-permute-start | bytes 1179656 | tf_op jit(solution)/shard_map/ppermute | solution.py:142
  93.0 31.7 %copy-start.6 = (bf16[3,256,256]{2,1,0:T(8,128)(2,1)S(1)}, bf16[3,256,256]{2,1,0:T(8,128)(2,1)}, u32[]{:S(2)}) copy-start(bf16[3,256,256]{2,1,0:T(8,128)(2,1)} %copy-done.5) | copy-start | bytes 1179652
  101.5 21.0 %copy-start.11 = (bf16[3,256,256]{2,1,0:T(8,128)(2,1)}, bf16[3,256,256]{2,1,0:T(8,128)(2,1)S(1)}, u32[]{:S(2)}) copy-start(bf16[3,256,256]{2,1,0:T(8,128)(2,1)S(1)} %collective-permute-done.22) | copy-start | bytes 1179652
  101.5 32.0 %collective-permute-start.2 = (bf16[144,2048]{1,0:T(8,128)(2,1)S(1)}, bf16[144,2048]{1,0:T(8,128)(2,1)}, u32[]{:S(2)}, u32[]{:S(2)}) collective-permute-start(bf16[144,2048]{1,0:T(8,128)(2,1)S(1)} %broadcast_select_fusion.6), channel_id=1, source_target_pairs={{0,1},{1,0},{2,3},{3,2},{4,5},{5,4},{6,7},{7,6},{8,9},{9,8},{10,11... | collective-permute-start | bytes 1769480 | tf_op jit(solution)/shard_map/ppermute | solution.py:146
  122.6 0.7 copy-start.13
  122.6 14.5 %collective-permute-start.4 = (bf16[144,2048]{1,0:T(8,128)(2,1)S(1)}, bf16[144,2048]{1,0:T(8,128)(2,1)}, u32[]{:S(2)}, u32[]{:S(2)}) collective-permute-start(bf16[144,2048]{1,0:T(8,128)(2,1)S(1)} %broadcast_select_fusion.6), channel_id=1, source_target_pairs={{0,8},{2,10},{4,12},{6,14},{8,0},{10,2},{12,4},{14,6},{16,24},{18,... | collective-permute-start | bytes 1769480 | tf_op jit(solution)/shard_map/ppermute | solution.py:142
  123.4 1.3 copy-start.10
  123.7 7.7 %copy-start.8 = (bf16[3,256,256]{2,1,0:T(8,128)(2,1)S(1)}, bf16[3,256,256]{2,1,0:T(8,128)(2,1)}, u32[]{:S(2)}) copy-start(bf16[3,256,256]{2,1,0:T(8,128)(2,1)} %copy-done.7) | copy-start | bytes 1179652
  123.7 7.7 %copy-start.12 = (bf16[3,256,256]{2,1,0:T(8,128)(2,1)S(1)}, bf16[3,256,256]{2,1,0:T(8,128)(2,1)}, u32[]{:S(2)}) copy-start(bf16[3,256,256]{2,1,0:T(8,128)(2,1)} %copy-done.11) | copy-start | bytes 1179652
  123.7 7.7 %copy-start.14 = (bf16[3,256,256]{2,1,0:T(8,128)(2,1)S(1)}, bf16[3,256,256]{2,1,0:T(8,128)(2,1)}, u32[]{:S(2)}) copy-start(bf16[3,256,256]{2,1,0:T(8,128)(2,1)} %copy-done.13) | copy-start | bytes 1179652
  126.0 70.0 %copy-start.3 = (bf16[4,3,256,256]{3,2,1,0:T(8,128)(2,1)}, bf16[4,3,256,256]{3,2,1,0:T(8,128)(2,1)S(1)}, u32[]{:S(2)}) copy-start(bf16[4,3,256,256]{3,2,1,0:T(8,128)(2,1)S(1)} %pad_maximum_fusion.2.refs_0_) | copy-start | bytes 4718596
  126.0 7.4 %copy-start.1 = (bf16[256,3,2048]{2,0,1:T(8,128)(2,1)S(1)}, bf16[256,3,2048]{2,0,1:T(8,128)(2,1)}, u32[]{:S(2)}) copy-start(bf16[256,3,2048]{2,0,1:T(8,128)(2,1)} %param.7) | copy-start | bytes 9437188
  126.0 48.5 %collective-permute-start.11 = (bf16[4,3,256,256]{3,2,1,0:T(8,128)(2,1)S(1)}, bf16[4,3,256,256]{3,2,1,0:T(8,128)(2,1)S(1)}, u32[]{:S(2)}, u32[]{:S(2)}) collective-permute-start(bf16[4,3,256,256]{3,2,1,0:T(8,128)(2,1)S(1)} %pad_maximum_fusion.2.refs_0_), channel_id=1, source_target_pairs={{0,4},{2,6},{4,0},{6,2},{8,12},{10,14},{12,8},{14,10},{16,20},{18,... | collective-permute-start | bytes 4718600 | tf_op jit(solution)/shard_map/ppermute | solution.py:142
  132.6 63.3 %copy-start.2 = (bf16[4,3,256,256]{3,2,1,0:T(8,128)(2,1)}, bf16[4,3,256,256]{3,2,1,0:T(8,128)(2,1)S(1)}, u32[]{:S(2)}) copy-start(bf16[4,3,256,256]{3,2,1,0:T(8,128)(2,1)S(1)} %pad_maximum_fusion.4.refs_0_) | copy-start | bytes 4718596
  132.7 63.3 %collective-permute-start.23 = (bf16[4,3,256,256]{3,2,1,0:T(8,128)(2,1)S(1)}, bf16[4,3,256,256]{3,2,1,0:T(8,128)(2,1)}, u32[]{:S(2)}, u32[]{:S(2)}) collective-permute-start(bf16[4,3,256,256]{3,2,1,0:T(8,128)(2,1)S(1)} %pad_maximum_fusion.4.refs_0_), channel_id=1, source_target_pairs={{0,4},{2,6},{4,0},{6,2},{8,12},{10,14},{12,8},{14,10},{16,20},{18,... | collective-permute-start | bytes 4718600 | tf_op jit(solution)/shard_map/ppermute | solution.py:142
  133.5 75.6 %collective-permute-start.7 = (bf16[512,2048]{1,0:T(8,128)(2,1)}, bf16[512,2048]{1,0:T(8,128)(2,1)S(1)}, u32[]{:S(2)}, u32[]{:S(2)}) collective-permute-start(bf16[512,2048]{1,0:T(8,128)(2,1)} %collective-permute-done.6), channel_id=1, source_target_pairs={{0,1},{1,0},{2,3},{3,2},{4,5},{5,4},{6,7},{7,6},{8,9},{9,8},{10,11... | collective-permute-start | bytes 6291464 | tf_op jit(solution)/shard_map/ppermute | solution.py:146
  137.1 15.3 %collective-permute-start.14 = (bf16[3,256,256]{2,1,0:T(8,128)(2,1)S(1)}, bf16[3,256,256]{2,1,0:T(8,128)(2,1)S(1)}, u32[]{:S(2)}, u32[]{:S(2)}) collective-permute-start(bf16[3,256,256]{2,1,0:T(8,128)(2,1)S(1)} %get-tuple-element.41), channel_id=1, source_target_pairs={{0,8},{2,10},{4,12},{6,14},{8,0},{10,2},{12,4},{14,6},{16,24},{18,... | collective-permute-start | bytes 1179656 | tf_op jit(solution)/shard_map/ppermute | solution.py:142
  137.4 24.1 %collective-permute-start.15 = (bf16[3,256,256]{2,1,0:T(8,128)(2,1)S(1)}, bf16[3,256,256]{2,1,0:T(8,128)(2,1)S(1)}, u32[]{:S(2)}, u32[]{:S(2)}) collective-permute-start(bf16[3,256,256]{2,1,0:T(8,128)(2,1)S(1)} %get-tuple-element.23), channel_id=1, source_target_pairs={{0,16},{2,18},{4,20},{6,22},{8,24},{10,26},{12,28},{14,30},{16,0},... | collective-permute-start | bytes 1179656 | tf_op jit(solution)/shard_map/ppermute | solution.py:142
  152.4 37.4 %collective-permute-start.5 = (bf16[144,2048]{1,0:T(8,128)(2,1)}, bf16[144,2048]{1,0:T(8,128)(2,1)S(1)}, u32[]{:S(2)}, u32[]{:S(2)}) collective-permute-start(bf16[144,2048]{1,0:T(8,128)(2,1)} %collective-permute-done.4), channel_id=1, source_target_pairs={{0,1},{1,0},{2,3},{3,2},{4,5},{5,4},{6,7},{7,6},{8,9},{9,8},{10,11... | collective-permute-start | bytes 1769480 | tf_op jit(solution)/shard_map/ppermute | solution.py:146
  161.5 11.5 %collective-permute-start.16 = (bf16[3,256,256]{2,1,0:T(8,128)(2,1)S(1)}, bf16[3,256,256]{2,1,0:T(8,128)(2,1)S(1)}, u32[]{:S(2)}, u32[]{:S(2)}) collective-permute-start(bf16[3,256,256]{2,1,0:T(8,128)(2,1)S(1)} %get-tuple-element.41), channel_id=1, source_target_pairs={{0,24},{2,26},{4,28},{6,30},{8,16},{10,18},{12,20},{14,22},{16,8},... | collective-permute-start | bytes 1179656 | tf_op jit(solution)/shard_map/ppermute | solution.py:142
  173.1 22.9 %collective-permute-start.28 = (bf16[3,256,256]{2,1,0:T(8,128)(2,1)S(1)}, bf16[3,256,256]{2,1,0:T(8,128)(2,1)S(1)}, u32[]{:S(2)}, u32[]{:S(2)}) collective-permute-start(bf16[3,256,256]{2,1,0:T(8,128)(2,1)S(1)} %get-tuple-element.38), channel_id=1, source_target_pairs={{0,24},{2,26},{4,28},{6,30},{8,16},{10,18},{12,20},{14,22},{16,8},... | collective-permute-start | bytes 1179656 | tf_op jit(solution)/shard_map/ppermute | solution.py:142
  174.5 32.6 %copy-start.17 = (bf16[4,3,256,256]{3,2,1,0:T(8,128)(2,1)}, bf16[4,3,256,256]{3,2,1,0:T(8,128)(2,1)S(1)}, u32[]{:S(2)}) copy-start(bf16[4,3,256,256]{3,2,1,0:T(8,128)(2,1)S(1)} %collective-permute-done.11.refs_1_) | copy-start | bytes 4718596
  174.5 32.6 %collective-permute-start.26 = (bf16[3,256,256]{2,1,0:T(8,128)(2,1)S(1)}, bf16[3,256,256]{2,1,0:T(8,128)(2,1)S(1)}, u32[]{:S(2)}, u32[]{:S(2)}) collective-permute-start(bf16[3,256,256]{2,1,0:T(8,128)(2,1)S(1)} %get-tuple-element.38), channel_id=1, source_target_pairs={{0,8},{2,10},{4,12},{6,14},{8,0},{10,2},{12,4},{14,6},{16,24},{18,... | collective-permute-start | bytes 1179656 | tf_op jit(solution)/shard_map/ppermute | solution.py:142
  189.8 17.3 %collective-permute-start.27 = (bf16[3,256,256]{2,1,0:T(8,128)(2,1)S(1)}, bf16[3,256,256]{2,1,0:T(8,128)(2,1)S(1)}, u32[]{:S(2)}, u32[]{:S(2)}) collective-permute-start(bf16[3,256,256]{2,1,0:T(8,128)(2,1)S(1)} %get-tuple-element.37), channel_id=1, source_target_pairs={{0,16},{2,18},{4,20},{6,22},{8,24},{10,26},{12,28},{14,30},{16,0},... | collective-permute-start | bytes 1179656 | tf_op jit(solution)/shard_map/ppermute | solution.py:142
  191.9 38.7 %copy-start.4 = (bf16[4,3,256,256]{3,2,1,0:T(8,128)(2,1)}, bf16[4,3,256,256]{3,2,1,0:T(8,128)(2,1)S(1)}, u32[]{:S(2)}) copy-start(bf16[4,3,256,256]{3,2,1,0:T(8,128)(2,1)S(1)} %pad_maximum_fusion.3.refs_0_) | copy-start | bytes 4718596
  196.0 28.5 %collective-permute-start.12 = (bf16[4,3,256,256]{3,2,1,0:T(8,128)(2,1)S(1)}, bf16[4,3,256,256]{3,2,1,0:T(8,128)(2,1)S(1)}, u32[]{:S(2)}, u32[]{:S(2)}) collective-permute-start(bf16[4,3,256,256]{3,2,1,0:T(8,128)(2,1)S(1)} %pad_maximum_fusion.2.refs_0_), channel_id=1, source_target_pairs={{0,2},{2,0},{4,6},{6,4},{8,10},{10,8},{12,14},{14,12},{16,18},{18,... | collective-permute-start | bytes 4718600 | tf_op jit(solution)/shard_map/ppermute | solution.py:142
  196.0 71.1 %collective-permute-start.24 = (bf16[4,3,256,256]{3,2,1,0:T(8,128)(2,1)S(1)}, bf16[4,3,256,256]{3,2,1,0:T(8,128)(2,1)}, u32[]{:S(2)}, u32[]{:S(2)}) collective-permute-start(bf16[4,3,256,256]{3,2,1,0:T(8,128)(2,1)S(1)} %pad_maximum_fusion.4.refs_0_), channel_id=1, source_target_pairs={{0,2},{2,0},{4,6},{6,4},{8,10},{10,8},{12,14},{14,12},{16,18},{18,... | collective-permute-start | bytes 4718600 | tf_op jit(solution)/shard_map/ppermute | solution.py:142
  207.1 23.4 %collective-permute-start.13 = (bf16[4,3,256,256]{3,2,1,0:T(8,128)(2,1)S(1)}, bf16[4,3,256,256]{3,2,1,0:T(8,128)(2,1)S(1)}, u32[]{:S(2)}, u32[]{:S(2)}) collective-permute-start(bf16[4,3,256,256]{3,2,1,0:T(8,128)(2,1)S(1)} %collective-permute-done.11.refs_1_), channel_id=1, source_target_pairs={{0,2},{2,0},{4,6},{6,4},{8,10},{10,8},{12,14},{14,12},{16,18},{18,... | collective-permute-start | bytes 4718600 | tf_op jit(solution)/shard_map/ppermute | solution.py:142
  207.2 60.5 %collective-permute-start.25 = (bf16[4,3,256,256]{3,2,1,0:T(8,128)(2,1)}, bf16[4,3,256,256]{3,2,1,0:T(8,128)(2,1)}, u32[]{:S(2)}, u32[]{:S(2)}) collective-permute-start(bf16[4,3,256,256]{3,2,1,0:T(8,128)(2,1)} %collective-permute-done.23.refs_1_), channel_id=1, source_target_pairs={{0,2},{2,0},{4,6},{6,4},{8,10},{10,8},{12,14},{14,12},{16,18},{18,... | collective-permute-start | bytes 4718600 | tf_op jit(solution)/shard_map/ppermute | solution.py:142
  209.1 37.4 %collective-permute-start.17 = (bf16[4,3,256,256]{3,2,1,0:T(8,128)(2,1)S(1)}, bf16[4,3,256,256]{3,2,1,0:T(8,128)(2,1)}, u32[]{:S(2)}, u32[]{:S(2)}) collective-permute-start(bf16[4,3,256,256]{3,2,1,0:T(8,128)(2,1)S(1)} %pad_maximum_fusion.3.refs_0_), channel_id=1, source_target_pairs={{0,4},{2,6},{4,0},{6,2},{8,12},{10,14},{12,8},{14,10},{16,20},{18,... | collective-permute-start | bytes 4718600 | tf_op jit(solution)/shard_map/ppermute | solution.py:142
  224.5 6.1 %copy-start.19 = (bf16[4,3,256,256]{3,2,1,0:T(8,128)(2,1)}, bf16[4,3,256,256]{3,2,1,0:T(8,128)(2,1)S(1)}, u32[]{:S(2)}) copy-start(bf16[4,3,256,256]{3,2,1,0:T(8,128)(2,1)S(1)} %collective-permute-done.12.refs_2_) | copy-start | bytes 4718596
  224.5 54.7 %collective-permute-start.29 = (bf16[4,3,256,256]{3,2,1,0:T(8,128)(2,1)}, bf16[4,3,256,256]{3,2,1,0:T(8,128)(2,1)S(1)}, u32[]{:S(2)}, u32[]{:S(2)}) collective-permute-start(bf16[4,3,256,256]{3,2,1,0:T(8,128)(2,1)} %pad_maximum_fusion.5.refs_0_), channel_id=1, source_target_pairs={{0,4},{2,6},{4,0},{6,2},{8,12},{10,14},{12,8},{14,10},{16,20},{18,... | collective-permute-start | bytes 4718600 | tf_op jit(solution)/shard_map/ppermute | solution.py:142
  230.6 15.9 %copy-start.20 = (bf16[4,3,256,256]{3,2,1,0:T(8,128)(2,1)}, bf16[4,3,256,256]{3,2,1,0:T(8,128)(2,1)S(1)}, u32[]{:S(2)}) copy-start(bf16[4,3,256,256]{3,2,1,0:T(8,128)(2,1)S(1)} %collective-permute-done.13.refs_3_) | copy-start | bytes 4718596
  230.6 69.4 %collective-permute-start.18 = (bf16[4,3,256,256]{3,2,1,0:T(8,128)(2,1)S(1)}, bf16[4,3,256,256]{3,2,1,0:T(8,128)(2,1)}, u32[]{:S(2)}, u32[]{:S(2)}) collective-permute-start(bf16[4,3,256,256]{3,2,1,0:T(8,128)(2,1)S(1)} %pad_maximum_fusion.3.refs_0_), channel_id=1, source_target_pairs={{0,2},{2,0},{4,6},{6,4},{8,10},{10,8},{12,14},{14,12},{16,18},{18,... | collective-permute-start | bytes 4718600 | tf_op jit(solution)/shard_map/ppermute | solution.py:142
  246.5 53.6 %collective-permute-start.19 = (bf16[4,3,256,256]{3,2,1,0:T(8,128)(2,1)}, bf16[4,3,256,256]{3,2,1,0:T(8,128)(2,1)}, u32[]{:S(2)}, u32[]{:S(2)}) collective-permute-start(bf16[4,3,256,256]{3,2,1,0:T(8,128)(2,1)} %collective-permute-done.17.refs_1_), channel_id=1, source_target_pairs={{0,2},{2,0},{4,6},{6,4},{8,10},{10,8},{12,14},{14,12},{16,18},{18,... | collective-permute-start | bytes 4718600 | tf_op jit(solution)/shard_map/ppermute | solution.py:142
  267.1 55.9 %collective-permute-start.30 = (bf16[4,3,256,256]{3,2,1,0:T(8,128)(2,1)}, bf16[4,3,256,256]{3,2,1,0:T(8,128)(2,1)S(1)}, u32[]{:S(2)}, u32[]{:S(2)}) collective-permute-start(bf16[4,3,256,256]{3,2,1,0:T(8,128)(2,1)} %pad_maximum_fusion.5.refs_0_), channel_id=1, source_target_pairs={{0,2},{2,0},{4,6},{6,4},{8,10},{10,8},{12,14},{14,12},{16,18},{18,... | collective-permute-start | bytes 4718600 | tf_op jit(solution)/shard_map/ppermute | solution.py:142
  267.7 77.4 %collective-permute-start.32 = (bf16[512,256]{1,0:T(8,128)(2,1)S(1)}, bf16[512,256]{1,0:T(8,128)(2,1)S(1)}, u32[]{:S(2)}, u32[]{:S(2)}) collective-permute-start(bf16[512,256]{1,0:T(8,128)(2,1)S(1)} %get-tuple-element.52), channel_id=1, source_target_pairs={{0,8},{2,10},{4,12},{6,14},{8,0},{10,2},{12,4},{14,6},{16,24},{18,... | collective-permute-start | bytes 786440 | tf_op jit(solution)/shard_map/ppermute | solution.py:142
  279.2 19.7 %copy-start.18 = (bf16[4,3,256,256]{3,2,1,0:T(8,128)(2,1)}, bf16[4,3,256,256]{3,2,1,0:T(8,128)(2,1)S(1)}, u32[]{:S(2)}) copy-start(bf16[4,3,256,256]{3,2,1,0:T(8,128)(2,1)S(1)} %collective-permute-done.29.refs_1_) | copy-start | bytes 4718596
  279.2 43.8 %collective-permute-start.31 = (bf16[4,3,256,256]{3,2,1,0:T(8,128)(2,1)S(1)}, bf16[4,3,256,256]{3,2,1,0:T(8,128)(2,1)}, u32[]{:S(2)}, u32[]{:S(2)}) collective-permute-start(bf16[4,3,256,256]{3,2,1,0:T(8,128)(2,1)S(1)} %collective-permute-done.29.refs_1_), channel_id=1, source_target_pairs={{0,2},{2,0},{4,6},{6,4},{8,10},{10,8},{12,14},{14,12},{16,18},{18,... | collective-permute-start | bytes 4718600 | tf_op jit(solution)/shard_map/ppermute | solution.py:142
  300.0 45.2 %collective-permute-start.34 = (bf16[512,256]{1,0:T(8,128)(2,1)S(1)}, bf16[512,256]{1,0:T(8,128)(2,1)S(1)}, u32[]{:S(2)}, u32[]{:S(2)}) collective-permute-start(bf16[512,256]{1,0:T(8,128)(2,1)S(1)} %get-tuple-element.56), channel_id=1, source_target_pairs={{0,8},{2,10},{4,12},{6,14},{8,0},{10,2},{12,4},{14,6},{16,24},{18,... | collective-permute-start | bytes 786440 | tf_op jit(solution)/shard_map/ppermute | solution.py:142
  320.9 24.2 %collective-permute-start.33 = (bf16[512,256]{1,0:T(8,128)(2,1)S(1)}, bf16[512,256]{1,0:T(8,128)(2,1)S(1)}, u32[]{:S(2)}, u32[]{:S(2)}) collective-permute-start(bf16[512,256]{1,0:T(8,128)(2,1)S(1)} %get-tuple-element.54), channel_id=1, source_target_pairs={{0,8},{2,10},{4,12},{6,14},{8,0},{10,2},{12,4},{14,6},{16,24},{18,... | collective-permute-start | bytes 786440 | tf_op jit(solution)/shard_map/ppermute | solution.py:142
  323.0 1.2 copy-start.21
  345.0 8.3 %collective-permute-start.35 = (bf16[512,256]{1,0:T(8,128)(2,1)S(1)}, bf16[512,256]{1,0:T(8,128)(2,1)S(1)}, u32[]{:S(2)}, u32[]{:S(2)}) collective-permute-start(bf16[512,256]{1,0:T(8,128)(2,1)S(1)} %get-tuple-element.58), channel_id=1, source_target_pairs={{0,8},{2,10},{4,12},{6,14},{8,0},{10,2},{12,4},{14,6},{16,24},{18,... | collective-permute-start | bytes 786440 | tf_op jit(solution)/shard_map/ppermute | solution.py:142

commit v3 on v2

v3 whole, which is shorter than its diff:
```python
import functools

import jax
import jax.numpy as jnp
from jax import lax
from jax.experimental import pallas as pl
from jax.experimental.pallas import tpu as pltpu
from jax.sharding import PartitionSpec as P

ROW_TILE = 256
CHAN_TILE = 256
LANES = 128
WIDTHS = [256, 256, 256, 256]


def in_sequence(places, seq_lengths):
    seq_ends = jnp.cumsum(seq_lengths)
    starts = seq_ends - seq_lengths
    inside = (places[:, None] >= starts[None, :]) & (places[:, None] < seq_ends[None, :])
    return jnp.sum(jnp.where(inside, places[:, None] - starts[None, :], 0), axis=1)


def block_kernel(runs, halves, at_ref, w_ref, sw_ref, fr_ref, pos_ref, *refs):
    row_refs, halo_refs = refs[: runs * halves], refs[runs * halves : (runs + 1) * halves]
    out_refs = refs[(runs + 1) * halves : (runs + 1) * halves + runs]
    x_ref, sems, proj, mix, band = refs[(runs + 1) * halves + runs :]
    total, features = x_ref.shape[1:]
    rows, chans = out_refs[0].shape
    halo = total - rows
    taps = sw_ref.shape[1]
    groups = fr_ref.shape[0]
    span = band.shape[0] // groups
    per_lanes = groups * LANES // chans
    width = LANES // per_lanes
    outer, inner, _, depth, _ = w_ref.shape
    units = [(q, k) for q in range(outer) for k in range(inner)]
    tile, run = pl.program_id(0), pl.program_id(1)

    def copies(r):
        for h in range(halves):
            piece = features // halves
            where = pl.ds(pl.multiple_of(at_ref[len(units) + h], piece), piece)
            yield pltpu.make_async_copy(
                halo_refs[h].at[r], x_ref.at[r, pl.ds(0, halo), where], sems.at[r, 2 * h]
            )
            yield pltpu.make_async_copy(
                row_refs[r * halves + h], x_ref.at[r, pl.ds(halo, rows), where], sems.at[r, 2 * h + 1]
            )

    @pl.when((tile == 0) & (run == 0))
    def _():
        for r in range(runs):
            for copy in copies(r):
                copy.start()

    @pl.when(run == 0)
    def _():
        proj[:, :, :8, :] = jnp.zeros((3, chans // LANES, 8, LANES), jnp.float32)
        for g in range(groups):
            row = jnp.broadcast_to(fr_ref[g : g + 1, :], (span, 2 * span))
            band[g * span : (g + 1) * span, :] = pltpu.roll(
                row, 0, 1, stride=1, stride_axis=0
            ).astype(band.dtype)

    for r in range(runs):

        @pl.when((tile == 0) & (run == r))
        def _():
            for copy in copies(r):
                copy.wait()

    edges = [0, halo] + list(range(halo + ROW_TILE, total + 1, ROW_TILE))
    for low, high in zip(edges[:-1], edges[1:]):
        if depth % LANES == 0:
            starts = [pl.multiple_of(at_ref[u], LANES) for u in range(len(units))]
            x = jnp.concatenate([x_ref[run, low:high, pl.ds(at, depth)] for at in starts], axis=1)
        else:
            x = x_ref[run, low:high, :]
        for s in range(3):
            weight = jnp.concatenate([w_ref[q, k, s] for q, k in units], axis=0)
            acc = jnp.dot(x, weight, preferred_element_type=jnp.float32)
            acc = acc.astype(jnp.bfloat16).astype(jnp.float32)
            for h in range(chans // LANES):
                proj[s, h, 8 + low : 8 + high, :] = acc[:, h * LANES : (h + 1) * LANES]

    def short(s, start, size, h, allowed):
        lanes = slice(h * LANES, (h + 1) * LANES)
        running = proj[s, h, 8 + start : 8 + start + size, :] * sw_ref[s, 0:1, lanes]
        for j in range(1, taps):
            window = proj[s, h, 8 + start - j : 8 + start - j + size, :]
            running = running + jnp.where(allowed[j], window * sw_ref[s, j : j + 1, lanes], 0.0)
        return running

    step = 64
    for r in range(halo - span, total, step):
        pos = pos_ref[0, r : r + step, :]
        allowed = [pos >= j for j in range(taps)]
        for h in range(chans // LANES):
            mixed = short(0, r, step, h, allowed) * short(2, r, step, h, allowed)
            mix[r : r + step, h * LANES : (h + 1) * LANES] = mixed.astype(mix.dtype)

    lag = (
        lax.broadcasted_iota(jnp.int32, (span, 2 * span), 0)
        + span
        - lax.broadcasted_iota(jnp.int32, (span, 2 * span), 1)
    )
    lane_group = lax.broadcasted_iota(jnp.int32, (span, LANES), 1) // width
    for b in range(rows // span):
        first = halo + b * span
        pos = pos_ref[0, first : first + span, :]
        limit = jnp.concatenate([pos] * (2 * span // LANES), axis=1)
        keep = jnp.where(lag <= limit, 1.0, 0.0).astype(band.dtype)
        allowed = [pos >= j for j in range(taps)]
        for h in range(chans // LANES):
            lanes = slice(h * LANES, (h + 1) * LANES)
            some = band[h * per_lanes * span : (h + 1) * per_lanes * span, :]
            some = some.reshape(per_lanes, span, 2 * span) * keep[None]
            full = jnp.dot(
                some.reshape(per_lanes * span, 2 * span),
                mix[first - span : first + span, lanes],
                preferred_element_type=jnp.float32,
            )
            medium = full[:span]
            for g in range(1, per_lanes):
                medium = jnp.where(lane_group == g, full[g * span : (g + 1) * span], medium)
            gated = (short(1, first, span, h, allowed) * medium).astype(out_refs[0].dtype)
            for r in range(runs):

                @pl.when(run == r)
                def _():
                    out_refs[r][b * span : (b + 1) * span, lanes] = gated


def block(at, rows, halos, weight, sw, fr, pos, span):
    runs, halves = len(rows), len(halos)
    row_count, features = rows[0][0].shape[0], rows[0][0].shape[1] * halves
    total = halos[0].shape[1] + row_count
    outer, inner, _, depth, chans = weight.shape
    taps = sw.shape[1]
    tile = CHAN_TILE if chans % CHAN_TILE == 0 else LANES
    per_tile = tile * fr.shape[0] // chans
    grid = (chans // tile, runs)
    anywhere = pl.BlockSpec(memory_space=pl.ANY)
    return pl.pallas_call(
        functools.partial(block_kernel, runs, halves),
        grid_spec=pltpu.PrefetchScalarGridSpec(
            num_scalar_prefetch=1,
            grid=grid,
            in_specs=[
                pl.BlockSpec((outer, inner, 3, depth, tile), lambda j, i, at: (0, 0, 0, 0, j)),
                pl.BlockSpec((3, taps, tile), lambda j, i, at: (0, 0, j)),
                pl.BlockSpec((per_tile, 2 * span), lambda j, i, at: (j, 0)),
                pl.BlockSpec((1, total, LANES), lambda j, i, at: (i, 0, 0)),
            ]
            + [anywhere] * (runs * halves + halves),
            out_specs=[pl.BlockSpec((row_count, tile), lambda j, i, at: (0, j))] * runs,
            scratch_shapes=[
                pltpu.VMEM((runs, total, features), jnp.bfloat16),
                pltpu.SemaphoreType.DMA((runs, 2 * halves)),
                pltpu.VMEM((3, tile // LANES, 8 + total, LANES), jnp.float32),
                pltpu.VMEM((total, tile), jnp.bfloat16),
                pltpu.VMEM((per_tile * span, 2 * span), jnp.bfloat16),
            ],
        ),
        out_shape=[jax.ShapeDtypeStruct((row_count, chans), jnp.bfloat16)] * runs,
        compiler_params=pltpu.CompilerParams(vmem_limit_bytes=56 * 1024 * 1024),
        cost_estimate=pl.CostEstimate(
            flops=4 * runs * total * features * 3 * chans,
            bytes_accessed=2 * (runs * total * features + 3 * features * chans + runs * row_count * chans),
            transcendentals=0,
        ),
    )(at, weight, sw, fr, pos, *[half for run in rows for half in run], *halos)


def parameters(short_weight, medium_filter):
    sw = jnp.transpose(short_weight, (1, 0, 2)).astype(jnp.float32)
    span = medium_filter.shape[0]
    fr = jnp.pad(jnp.flip(medium_filter, axis=0).T.astype(jnp.float32), ((0, 0), (1, span - 1)))
    return sw, fr


def flip(array, bit):
    return lax.ppermute(array, "stretch", [(i, i ^ bit) for i in range(lax.axis_size("stretch"))])


def across(array):
    return lax.ppermute(array, "chan", [(0, 1), (1, 0)])


def rows_before(tokens, stretch_id, reach):
    tail = tokens[tokens.shape[0] - reach :]
    sibling = flip(tail, 1)
    second = stretch_id % 2 == 1
    pairs = [(i, i + 2) for i in range(lax.axis_size("stretch") - 2)]
    before = lax.ppermute(jnp.where(second, tail, sibling), "stretch", pairs)
    return jnp.where(second, sibling, before)


def nothing(array):
    return (array[(0,) * array.ndim].astype(jnp.float32) * 0.0).astype(jnp.int32)


def per_device(tokens, in_weight, short_weight, medium_filter, seq_lengths, stretch_slot):
    row_count, piece = tokens.shape
    depth, _, chans = in_weight.shape
    span, taps = medium_filter.shape[0], short_weight.shape[0]
    me = lax.axis_index("stretch")
    devices = lax.axis_size("stretch")
    order = jnp.arange(devices, dtype=jnp.int32)
    reach = -(-(span + taps - 1) // 16) * 16
    sw, fr = parameters(short_weight, medium_filter)
    local = jnp.transpose(in_weight, (1, 0, 2))

    def stretch_at(device):
        return jnp.sum(jnp.where(stretch_slot == device, order, 0))

    def positions(device):
        places = stretch_at(device) * row_count - reach + jnp.arange(reach + row_count, dtype=jnp.int32)
        return jnp.broadcast_to(in_sequence(places, seq_lengths)[:, None], (reach + row_count, LANES))

    if devices != 16 or lax.axis_size("chan") != 2:
        weight = lax.all_gather(local, "stretch", axis=0, tiled=False)
        halo = rows_before(tokens, stretch_at(me), reach)
        halo = lax.all_gather(halo, "chan", axis=1, tiled=True)
        rows = lax.all_gather(tokens, "chan", axis=1, tiled=True)
        at = jnp.concatenate([order * depth, jnp.zeros(1, jnp.int32)])
        return block(at, [[rows]], [halo[None]], weight[:, None], sw, fr, positions(me)[None], span)[0]

    side = lax.axis_index("chan")
    kind = (me >> 2) & 1
    half = chans // 2
    own_begin, other_begin = kind * half, (1 - kind) * half
    widths = WIDTHS if sum(WIDTHS) == half else [half]
    begins = [sum(widths[:c]) for c in range(len(widths))]

    halo = rows_before(tokens, stretch_at(me), reach)
    peer_rows = flip(tokens, 4)
    rows_other = across(tokens)
    peer_rows_other = across(peer_rows)
    peer_halo = flip(halo, 4)
    halos = jnp.stack([halo, peer_halo])
    halos_other = across(halos)
    after = {1: [peer_rows], 2: [rows_other, peer_halo], 3: [peer_rows_other]}

    planes = [[4 * z + q for q in range(4)] for z in range(devices // 4)]
    arrived, gathered = [], []
    for c, (begin, width) in enumerate(zip(begins, widths)):
        units = [lax.dynamic_slice_in_dim(local, own_begin + begin, width, 2)]
        for k in (1, 2, 3):
            start = (own_begin if k == 2 else other_begin) + begin
            if c > 0:
                start = start + sum(nothing(first) for first in [arrived[c - 1][k]] + after.get(c, []))
            units.append(flip(lax.dynamic_slice_in_dim(local, start, width, 2), 4 * k))
        arrived.append(units)
        whole = lax.all_gather(jnp.stack(units), "stretch", axis=0, tiled=False, axis_index_groups=planes)
        gathered.append(whole)
        after.setdefault(c + 2, []).append(whole)

    pos = jnp.stack([positions(me), positions(me ^ 4)])
    at = jnp.concatenate(
        [
            jnp.stack([((me ^ (4 * k)) // 4 * 4 + q) * depth for q in range(4) for k in range(4)]),
            jnp.stack([side * piece, (1 - side) * piece]),
        ]
    )
    own_sw = lax.dynamic_slice_in_dim(sw, own_begin, half, 2)
    own_fr = lax.dynamic_slice_in_dim(fr, own_begin * fr.shape[0] // chans, fr.shape[0] // 2, 0)

    mine, theirs = [], []
    for c, (begin, width) in enumerate(zip(begins, widths)):
        groups = fr.shape[0] * width // chans
        first_group = begin * fr.shape[0] // chans
        out, peer_out = block(
            at,
            [[tokens, rows_other], [peer_rows, peer_rows_other]],
            [halos, halos_other],
            gathered[c],
            own_sw[:, :, begin : begin + width],
            own_fr[first_group : first_group + groups],
            pos,
            span,
        )
        mine.append(out)
        theirs.append(flip(peer_out, 4))
    mine, theirs = jnp.concatenate(mine, axis=1), jnp.concatenate(theirs, axis=1)
    even = kind == 0
    return jnp.concatenate([jnp.where(even, mine, theirs), jnp.where(even, theirs, mine)], axis=1)


def solution(mesh):
    return jax.shard_map(
        per_device,
        mesh=mesh,
        in_specs=(
            P("stretch", "chan"),
            P("stretch", None, "chan"),
            P(None, None, "chan"),
            P(None, "chan"),
            P(),
            P(),
        ),
        out_specs=P("stretch", "chan"),
        check_vma=False,
    )
```

time: 361 us -> 464 us (1.29)
  waiting for transfers between devices: 182 us -> 252 us
  between operations: 3.9 us -> 26.3 us
  other arithmetic: 35 us -> 15.5 us
  local copies, waits for them, and re-layouts: 14.1 us -> 31.8 us
  Pallas kernels: 78.9 us -> 96.5 us
    ppermute x4 -> x3, waiting for transfers between devices: 11.8 us -> 60.2 us  [across(): return lax.ppermute(array, 'chan', [(0, 1), (1, 0)])]
    pallas_call x4, Pallas kernels: 78.9 us -> 96.5 us  [block(): pl.pallas_call(functools.partial(block_kernel, runs, halves), grid_spec=p...]
    ppermute x1, waiting for transfers between devices: 0.01 us -> 17.1 us  [rows_before(): before = lax.ppermute(jnp.where(second, tail, sibling), 'stretch', pairs)]
    slice x0 -> x15, local copies, waits for them, and re-layouts: none -> 15.5 us  [nothing(): array[(0,) * array.ndim].astype(jnp.float32) * 0.0]
    another operation x7 -> x6, other arithmetic: 21.8 us -> 8.89 us  [the longest x4 7.35 us: per_device(): jnp.stack(units)]
    select_n x4 -> x0, other arithmetic: 6.02 us -> none  [the longest x2 3.73 us: whole_rows(): jnp.where(low, rows, rows_other)]
    ppermute x31 -> x19, waiting for transfers between devices: 171 us -> 175 us  [flip(): lax.ppermute(array, 'stretch', [(i, i ^ bit) for i in range(lax.axis_size...]
    ppermute x31 -> x19, starting transfers between devices: 32.4 us -> 29.5 us  [flip(): lax.ppermute(array, 'stretch', [(i, i ^ bit) for i in range(lax.axis_size...]
  transfers between devices with their start and end apart: 36 -> 27, of which waited for: 14 -> 16; matrix products, arithmetic and copies ran while one was open for 13% -> 7% of each run, Pallas kernels for 22% -> 21%
where the time goes in v3:
time: 464 us; the launch traced here: 460 us
  waiting for transfers between devices  252 us (54%)
  Pallas kernels  96.5 us (21%)
  starting transfers between devices  37.5 us (8%)
  local copies, waits for them, and re-layouts  31.8 us (7%)
  between operations  26.3 us (6%)
  other arithmetic  15.5 us (3%)
    ppermute x19, waiting for transfers between devices, flip(): lax.ppermute(array, 'stretch', [(i, i ^ bit) for i in range(lax.axis_size...  175 us
    pallas_call x4, Pallas kernels, block(): pl.pallas_call(functools.partial(block_kernel, runs, halves), grid_spec=p...  96.5 us
    ppermute x3, waiting for transfers between devices, across(): return lax.ppermute(array, 'chan', [(0, 1), (1, 0)])  60.2 us
    ppermute x19, starting transfers between devices, flip(): lax.ppermute(array, 'stretch', [(i, i ^ bit) for i in range(lax.axis_size...  29.5 us
    ppermute x1, waiting for transfers between devices, rows_before(): before = lax.ppermute(jnp.where(second, tail, sibling), 'stretch', pairs)  17.1 us
    slice x15, local copies, waits for them, and re-layouts, nothing(): array[(0,) * array.ndim].astype(jnp.float32) * 0.0  15.5 us
  transfers between devices with their start and end apart: 27, of which 16 were waited for; matrix products, arithmetic and copies ran while one was open for 7% of the time, Pallas kernels for 21%

profile of v3, /device:TPU:0, one launch (start us, length us, event | category | flops | bytes accessed | tf_op | source)
XLA Modules:
  0.0 459.6 jit_solution(5695986352173354083)
XLA Ops:
  6.5 3.0 collective-permute-start.4
  9.6 1.2 dynamic-slice_bitcast_fusion.14
  10.7 2.7 collective-permute-start.1
  13.4 0.9 collective-permute-start
  14.3 49.9 %collective-permute-done.1 = bf16[3,256,256]{2,1,0:T(8,128)(2,1)S(1)} collective-permute-done((bf16[3,256,256]{2,1,0:T(8,128)(2,1)S(1)}, bf16[3,256,256]{2,1,0:T(8,128)(2,1)S(1)}, u32[]{:S(2)}, u32[]{:S(2)}) %collective-permute-start.1) | collective-permute-done | bytes 393248 | tf_op jit(solution)/shard_map/ppermute | solution.py:183
  65.4 10.2 %collective-permute-done.2 = bf16[3,256,256]{2,1,0:T(8,128)(2,1)S(1)} collective-permute-done((bf16[3,256,256]{2,1,0:T(8,128)(2,1)S(1)}, bf16[3,256,256]{2,1,0:T(8,128)(2,1)S(1)}, u32[]{:S(2)}, u32[]{:S(2)}) %collective-permute-start.2) | collective-permute-done | bytes 393248 | tf_op jit(solution)/shard_map/ppermute | solution.py:183
  76.8 3.9 collective-permute-done
  81.9 1.1 slice.111
  83.7 3.5 dynamic-slice_bitcast_fusion.3
  87.2 1.3 pad_maximum_fusion.1
  88.7 3.7 collective-permute-start.12
  92.3 0.8 collective-permute-start.10
  93.1 9.6 %collective-permute-done.12 = bf16[3,256,256]{2,1,0:T(8,128)(2,1)S(1)} collective-permute-done((bf16[3,256,256]{2,1,0:T(8,128)(2,1)S(1)}, bf16[3,256,256]{2,1,0:T(8,128)(2,1)S(1)}, u32[]{:S(2)}, u32[]{:S(2)}) %collective-permute-start.12) | collective-permute-done | bytes 393248 | tf_op jit(solution)/shard_map/ppermute | solution.py:183
  102.7 22.3 %collective-permute-done.11 = bf16[3,256,256]{2,1,0:T(8,128)(2,1)S(1)} collective-permute-done((bf16[3,256,256]{2,1,0:T(8,128)(2,1)S(1)}, bf16[3,256,256]{2,1,0:T(8,128)(2,1)S(1)}, u32[]{:S(2)}, u32[]{:S(2)}) %collective-permute-start.11) | collective-permute-done | bytes 393248 | tf_op jit(solution)/shard_map/ppermute | solution.py:183
  125.0 0.7 copy-done.3
  125.8 1.3 pad_maximum_fusion.2
  127.2 1.9 slice.86
  129.1 1.5 collective-permute-start.3
  133.3 1.3 broadcast_select_fusion.3
  134.6 3.6 collective-permute-start.7
  138.7 17.1 %collective-permute-done.7 = bf16[144,2048]{1,0:T(8,128)(2,1)S(1)} collective-permute-done((bf16[144,2048]{1,0:T(8,128)(2,1)S(1)}, bf16[144,2048]{1,0:T(8,128)(2,1)S(1)}, u32[]{:S(2)}, u32[]{:S(2)}) %collective-permute-start.7) | collective-permute-done | bytes 589856 | tf_op jit(solution)/shard_map/ppermute | solution.py:195
  155.8 1.9 broadcast_select_fusion.2
  157.8 11.9 %collective-permute-done.8 = bf16[144,2048]{1,0:T(8,128)(2,1)} collective-permute-done((bf16[144,2048]{1,0:T(8,128)(2,1)}, bf16[144,2048]{1,0:T(8,128)(2,1)}, u32[]{:S(2)}, u32[]{:S(2)}) %collective-permute-start.8) | collective-permute-done | bytes 589856 | tf_op jit(solution)/shard_map/ppermute | solution.py:183
  169.6 1.1 slice.118
  171.3 6.6 %collective-permute-done.3.refs_1_ = bf16[512,2048]{1,0:T(8,128)(2,1)} collective-permute-done((bf16[512,2048]{1,0:T(8,128)(2,1)}, bf16[512,2048]{1,0:T(8,128)(2,1)}, u32[]{:S(2)}, u32[]{:S(2)}) %collective-permute-start.3) | collective-permute-done | bytes 2097184 | tf_op jit(solution)/shard_map/ppermute | solution.py:187
  177.9 1.1 slice.117
  179.6 1.2 slice.116
  181.4 1.2 slice.119
  183.2 1.0 dynamic-slice_bitcast_fusion.6
  184.2 1.2 slice.121
  186.0 1.2 slice.120
  187.9 34.6 %collective-permute-done.5.refs_3_ = bf16[512,2048]{1,0:T(8,128)(2,1)} collective-permute-done((bf16[512,2048]{1,0:T(8,128)(2,1)}, bf16[512,2048]{1,0:T(8,128)(2,1)}, u32[]{:S(2)}, u32[]{:S(2)}) %collective-permute-start.5) | collective-permute-done | bytes 2097184 | tf_op jit(solution)/shard_map/ppermute | solution.py:187
  222.4 1.1 slice.125
  224.2 1.2 slice.126
  226.0 1.2 slice.124
  227.9 1.3 dynamic-slice_bitcast_fusion.2
  229.2 2.6 collective-permute-start.15
  231.8 11.2 %collective-permute-done.15 = bf16[3,256,256]{2,1,0:T(8,128)(2,1)S(1)} collective-permute-done((bf16[3,256,256]{2,1,0:T(8,128)(2,1)S(1)}, bf16[3,256,256]{2,1,0:T(8,128)(2,1)S(1)}, u32[]{:S(2)}, u32[]{:S(2)}) %collective-permute-start.15) | collective-permute-done | bytes 393248 | tf_op jit(solution)/shard_map/ppermute | solution.py:183
  243.0 21.4 %collective-permute-done.14 = bf16[3,256,256]{2,1,0:T(8,128)(2,1)S(1)} collective-permute-done((bf16[3,256,256]{2,1,0:T(8,128)(2,1)S(1)}, bf16[3,256,256]{2,1,0:T(8,128)(2,1)S(1)}, u32[]{:S(2)}, u32[]{:S(2)}) %collective-permute-start.14) | collective-permute-done | bytes 393248 | tf_op jit(solution)/shard_map/ppermute | solution.py:183
  264.5 0.7 copy-done.6
  265.2 2.3 pad_maximum_fusion.3
  268.2 1.1 slice.128
  269.9 1.1 slice.127
  272.0 1.8 collective-permute-start.17
  273.8 2.6 collective-permute-start.18
  276.4 5.4 %collective-permute-done.16 = bf16[3,256,256]{2,1,0:T(8,128)(2,1)} collective-permute-done((bf16[3,256,256]{2,1,0:T(8,128)(2,1)}, bf16[3,256,256]{2,1,0:T(8,128)(2,1)}, u32[]{:S(2)}, u32[]{:S(2)}) %collective-permute-start.16) | collective-permute-done | bytes 393248 | tf_op jit(solution)/shard_map/ppermute | solution.py:183
  281.8 19.7 %collective-permute-done.17 = bf16[3,256,256]{2,1,0:T(8,128)(2,1)S(1)} collective-permute-done((bf16[3,256,256]{2,1,0:T(8,128)(2,1)S(1)}, bf16[3,256,256]{2,1,0:T(8,128)(2,1)S(1)}, u32[]{:S(2)}, u32[]{:S(2)}) %collective-permute-start.17) | collective-permute-done | bytes 393248 | tf_op jit(solution)/shard_map/ppermute | solution.py:183
  301.5 2.3 pad_maximum_fusion.4
  305.1 1.4 pad_maximum_fusion.5.refs_4_
  306.5 1.6 collective-permute-start.9
  309.7 0.9 pad_add_fusion.pos_ref
  311.9 19.1 %collective-permute-done.9.refs_5_ = bf16[2,144,2048]{2,1,0:T(8,128)(2,1)S(1)} collective-permute-done((bf16[2,144,2048]{2,1,0:T(8,128)(2,1)S(1)}, bf16[2,144,2048]{2,1,0:T(8,128)(2,1)S(1)}, u32[]{:S(2)}, u32[]{:S(2)}) %collective-permute-start.9) | collective-permute-done | bytes 1179680 | tf_op jit(solution)/shard_map/ppermute | solution.py:187
  331.0 1.0 copy-done.13
  332.0 24.0 %shard_map.64 = (bf16[512,256]{1,0:T(8,128)(2,1)}, bf16[512,256]{1,0:T(8,128)(2,1)}) custom-call(s32[18]{0:T(128)} %concatenate.12.at_ref, bf16[4,4,3,256,256]{4,3,2,1,0:T(8,128)(2,1)} %bitcast.107, f32[3,7,256]{2,1,0:T(8,128)} %get-tuple-element.44.sw_ref, f32[16,256]{1,0:T(8,128)} %get-tuple-element.48.fr_ref, s32[2,656,128]{2,1,0:T(8,128)} %pad_add_fusion.pos_ref, ...), custom_call_target="tpu_custom_call" | custom-call | flops 16508780544 | bytes 17563648 | tf_op jit(solution)/shard_map/pallas_call | solution.py:144
  355.9 9.1 %collective-permute-start.19 = (bf16[512,256]{1,0:T(8,128)(2,1)}, bf16[512,256]{1,0:T(8,128)(2,1)S(1)}, u32[]{:S(2)}, u32[]{:S(2)}) collective-permute-start(bf16[512,256]{1,0:T(8,128)(2,1)} %get-tuple-element.17), channel_id=1, source_target_pairs={{0,8},{2,10},{4,12},{6,14},{8,0},{10,2},{12,4},{14,6},{16,24},{18,... | collective-permute-start | bytes 786440 | tf_op jit(solution)/shard_map/ppermute | solution.py:183
  365.0 24.2 %shard_map.65 = (bf16[512,256]{1,0:T(8,128)(2,1)}, bf16[512,256]{1,0:T(8,128)(2,1)}) custom-call(s32[18]{0:T(128)} %concatenate.12.at_ref, bf16[4,4,3,256,256]{4,3,2,1,0:T(8,128)(2,1)} %bitcast.109, f32[3,7,256]{2,1,0:T(8,128)} %get-tuple-element.43.sw_ref, f32[16,256]{1,0:T(8,128)} %get-tuple-element.47.fr_ref, s32[2,656,128]{2,1,0:T(8,128)} %pad_add_fusion.pos_ref, ...), custom_call_target="tpu_custom_call" | custom-call | flops 16508780544 | bytes 17563648 | tf_op jit(solution)/shard_map/pallas_call | solution.py:144
  389.4 1.0 constant_dynamic-update-slice_fusion.2
  390.4 5.5 %collective-permute-done.20 = bf16[512,256]{1,0:T(8,128)(2,1)S(1)} collective-permute-done((bf16[512,256]{1,0:T(8,128)(2,1)}, bf16[512,256]{1,0:T(8,128)(2,1)S(1)}, u32[]{:S(2)}, u32[]{:S(2)}) %collective-permute-start.20) | collective-permute-done | bytes 262176 | tf_op jit(solution)/shard_map/ppermute | solution.py:183
  395.9 24.1 %shard_map.66 = (bf16[512,256]{1,0:T(8,128)(2,1)}, bf16[512,256]{1,0:T(8,128)(2,1)}) custom-call(s32[18]{0:T(128)} %concatenate.12.at_ref, bf16[4,4,3,256,256]{4,3,2,1,0:T(8,128)(2,1)} %bitcast.110, f32[3,7,256]{2,1,0:T(8,128)} %get-tuple-element.42.sw_ref, f32[16,256]{1,0:T(8,128)} %get-tuple-element.46.fr_ref, s32[2,656,128]{2,1,0:T(8,128)} %pad_add_fusion.pos_ref, ...), custom_call_target="tpu_custom_call" | custom-call | flops 16508780544 | bytes 17563648 | tf_op jit(solution)/shard_map/pallas_call | solution.py:144
  420.2 24.3 %shard_map.67 = (bf16[512,256]{1,0:T(8,128)(2,1)}, bf16[512,256]{1,0:T(8,128)(2,1)}) custom-call(s32[18]{0:T(128)} %concatenate.12.at_ref, bf16[4,4,3,256,256]{4,3,2,1,0:T(8,128)(2,1)} %bitcast.111, f32[3,7,256]{2,1,0:T(8,128)} %get-tuple-element.41.sw_ref, f32[16,256]{1,0:T(8,128)} %get-tuple-element.45.fr_ref, s32[2,656,128]{2,1,0:T(8,128)} %pad_add_fusion.pos_ref, ...), custom_call_target="tpu_custom_call" | custom-call | flops 16508780544 | bytes 17563648 | tf_op jit(solution)/shard_map/pallas_call | solution.py:144
  444.5 2.0 collective-permute-start.22
  446.6 1.0 constant_dynamic-update-slice_fusion
  447.5 3.6 collective-permute-done.22
  451.3 1.5 pad_maximum_fusion
  (81 shorter events, 7.5 us)
Async XLA Ops:
  6.5 174.9 %all-gather.9.cloned.1.call-start = ((), (), s32[]{:S(2)}) async-start(), calls=%async_computation | async-start | bytes 7864320 | tf_op jit(solution)/shard_map/all_gather | solution.py:255
  6.5 75.4 %collective-permute-start.4 = (bf16[512,2048]{1,0:T(8,128)(2,1)}, bf16[512,2048]{1,0:T(8,128)(2,1)}, u32[]{:S(2)}, u32[]{:S(2)}) collective-permute-start(bf16[512,2048]{1,0:T(8,128)(2,1)} %refs_0_.7), channel_id=1, source_target_pairs={{0,8},{2,10},{4,12},{6,14},{8,0},{10,2},{12,4},{14,6},{16,24},{18,... | collective-permute-start | bytes 6291464 | tf_op jit(solution)/shard_map/ppermute | solution.py:183
  10.7 53.5 %collective-permute-start.1 = (bf16[3,256,256]{2,1,0:T(8,128)(2,1)S(1)}, bf16[3,256,256]{2,1,0:T(8,128)(2,1)S(1)}, u32[]{:S(2)}, u32[]{:S(2)}) collective-permute-start(bf16[3,256,256]{2,1,0:T(8,128)(2,1)S(1)} %get-tuple-element.37), channel_id=1, source_target_pairs={{0,16},{2,18},{4,20},{6,22},{8,24},{10,26},{12,28},{14,30},{16,0},... | collective-permute-start | bytes 1179656 | tf_op jit(solution)/shard_map/ppermute | solution.py:183
  13.4 62.2 %collective-permute-start.2 = (bf16[3,256,256]{2,1,0:T(8,128)(2,1)S(1)}, bf16[3,256,256]{2,1,0:T(8,128)(2,1)S(1)}, u32[]{:S(2)}, u32[]{:S(2)}) collective-permute-start(bf16[3,256,256]{2,1,0:T(8,128)(2,1)S(1)} %get-tuple-element.38), channel_id=1, source_target_pairs={{0,24},{2,26},{4,28},{6,30},{8,16},{10,18},{12,20},{14,22},{16,8},... | collective-permute-start | bytes 1179656 | tf_op jit(solution)/shard_map/ppermute | solution.py:183
  13.4 67.3 %collective-permute-start = (bf16[3,256,256]{2,1,0:T(8,128)(2,1)S(1)}, bf16[3,256,256]{2,1,0:T(8,128)(2,1)S(1)}, u32[]{:S(2)}, u32[]{:S(2)}) collective-permute-start(bf16[3,256,256]{2,1,0:T(8,128)(2,1)S(1)} %get-tuple-element.38), channel_id=1, source_target_pairs={{0,8},{2,10},{4,12},{6,14},{8,0},{10,2},{12,4},{14,6},{16,24},{18,... | collective-permute-start | bytes 1179656 | tf_op jit(solution)/shard_map/ppermute | solution.py:183
  88.6 135.6 %all-gather.11.cloned.1.call-start = ((), (), s32[]{:S(2)}) async-start(), calls=%async_computation.1 | async-start | bytes 7864320 | tf_op jit(solution)/shard_map/all_gather | solution.py:255
  88.7 14.0 %collective-permute-start.12 = (bf16[3,256,256]{2,1,0:T(8,128)(2,1)S(1)}, bf16[3,256,256]{2,1,0:T(8,128)(2,1)S(1)}, u32[]{:S(2)}, u32[]{:S(2)}) collective-permute-start(bf16[3,256,256]{2,1,0:T(8,128)(2,1)S(1)} %get-tuple-element.28), channel_id=1, source_target_pairs={{0,24},{2,26},{4,28},{6,30},{8,16},{10,18},{12,20},{14,22},{16,8},... | collective-permute-start | bytes 1179656 | tf_op jit(solution)/shard_map/ppermute | solution.py:183
  92.3 32.7 %collective-permute-start.11 = (bf16[3,256,256]{2,1,0:T(8,128)(2,1)S(1)}, bf16[3,256,256]{2,1,0:T(8,128)(2,1)S(1)}, u32[]{:S(2)}, u32[]{:S(2)}) collective-permute-start(bf16[3,256,256]{2,1,0:T(8,128)(2,1)S(1)} %get-tuple-element.29), channel_id=1, source_target_pairs={{0,16},{2,18},{4,20},{6,22},{8,24},{10,26},{12,28},{14,30},{16,0},... | collective-permute-start | bytes 1179656 | tf_op jit(solution)/shard_map/ppermute | solution.py:183
  92.3 32.7 %collective-permute-start.10 = (bf16[3,256,256]{2,1,0:T(8,128)(2,1)S(1)}, bf16[3,256,256]{2,1,0:T(8,128)(2,1)S(1)}, u32[]{:S(2)}, u32[]{:S(2)}) collective-permute-start(bf16[3,256,256]{2,1,0:T(8,128)(2,1)S(1)} %get-tuple-element.30), channel_id=1, source_target_pairs={{0,8},{2,10},{4,12},{6,14},{8,0},{10,2},{12,4},{14,6},{16,24},{18,... | collective-permute-start | bytes 1179656 | tf_op jit(solution)/shard_map/ppermute | solution.py:183
  102.7 22.3 %copy-start.4 = (bf16[3,256,256]{2,1,0:T(8,128)(2,1)}, bf16[3,256,256]{2,1,0:T(8,128)(2,1)S(1)}, u32[]{:S(2)}) copy-start(bf16[3,256,256]{2,1,0:T(8,128)(2,1)S(1)} %collective-permute-done.12) | copy-start | bytes 1179652
  125.0 0.7 copy-start.3
  125.0 8.2 %copy-start.5 = (bf16[3,256,256]{2,1,0:T(8,128)(2,1)}, bf16[3,256,256]{2,1,0:T(8,128)(2,1)S(1)}, u32[]{:S(2)}) copy-start(bf16[3,256,256]{2,1,0:T(8,128)(2,1)S(1)} %collective-permute-done.10) | copy-start | bytes 1179652
  127.1 3.5 copy-start.12
  127.1 268.8 %all-gather.13.cloned.1.call-start = ((), (), s32[]{:S(2)}) async-start(), calls=%async_computation.2 | async-start | bytes 7864320 | tf_op jit(solution)/shard_map/all_gather | solution.py:255
  129.1 4.1 collective-permute-start.6
  129.1 48.7 %collective-permute-start.3 = (bf16[512,2048]{1,0:T(8,128)(2,1)}, bf16[512,2048]{1,0:T(8,128)(2,1)}, u32[]{:S(2)}, u32[]{:S(2)}) collective-permute-start(bf16[512,2048]{1,0:T(8,128)(2,1)} %refs_0_.7), channel_id=1, source_target_pairs={{0,1},{1,0},{2,3},{3,2},{4,5},{5,4},{6,7},{7,6},{8,9},{9,8},{10,11... | collective-permute-start | bytes 6291464 | tf_op jit(solution)/shard_map/ppermute | solution.py:187
  133.2 50.0 %copy-start = (bf16[256,3,2048]{2,0,1:T(8,128)(2,1)S(1)}, bf16[256,3,2048]{2,0,1:T(8,128)(2,1)}, u32[]{:S(2)}) copy-start(bf16[256,3,2048]{2,0,1:T(8,128)(2,1)} %param.7) | copy-start | bytes 9437188
  134.6 21.3 %collective-permute-start.7 = (bf16[144,2048]{1,0:T(8,128)(2,1)S(1)}, bf16[144,2048]{1,0:T(8,128)(2,1)S(1)}, u32[]{:S(2)}, u32[]{:S(2)}) collective-permute-start(bf16[144,2048]{1,0:T(8,128)(2,1)S(1)} %broadcast_select_fusion.3), channel_id=1, source_target_pairs={{0,4},{2,6},{4,8},{6,10},{8,12},{10,14},{12,16},{14,18},{16,20},{1... | collective-permute-start | bytes 1769480 | tf_op jit(solution)/shard_map/ppermute | solution.py:195
  138.2 84.2 %collective-permute-start.5 = (bf16[512,2048]{1,0:T(8,128)(2,1)}, bf16[512,2048]{1,0:T(8,128)(2,1)}, u32[]{:S(2)}, u32[]{:S(2)}) collective-permute-start(bf16[512,2048]{1,0:T(8,128)(2,1)} %collective-permute-done.4.refs_2_), channel_id=1, source_target_pairs={{0,1},{1,0},{2,3},{3,2},{4,5},{5,4},{6,7},{7,6},{8,9},{9,8},{10,11... | collective-permute-start | bytes 6291464 | tf_op jit(solution)/shard_map/ppermute | solution.py:187
  157.8 11.9 %collective-permute-start.8 = (bf16[144,2048]{1,0:T(8,128)(2,1)}, bf16[144,2048]{1,0:T(8,128)(2,1)}, u32[]{:S(2)}, u32[]{:S(2)}) collective-permute-start(bf16[144,2048]{1,0:T(8,128)(2,1)} %broadcast_select_fusion.2), channel_id=1, source_target_pairs={{0,8},{2,10},{4,12},{6,14},{8,0},{10,2},{12,4},{14,6},{16,24},{18,... | collective-permute-start | bytes 1769480 | tf_op jit(solution)/shard_map/ppermute | solution.py:183
  184.2 41.8 %collective-permute-start.13 = (bf16[3,256,256]{2,1,0:T(8,128)(2,1)}, bf16[3,256,256]{2,1,0:T(8,128)(2,1)}, u32[]{:S(2)}, u32[]{:S(2)}) collective-permute-start(bf16[3,256,256]{2,1,0:T(8,128)(2,1)} %dynamic-slice_bitcast_fusion.6), channel_id=1, source_target_pairs={{0,8},{2,10},{4,12},{6,14},{8,0},{10,2},{12,4},{14,6},{16,24},{18,... | collective-permute-start | bytes 1179656 | tf_op jit(solution)/shard_map/ppermute | solution.py:183
  227.9 37.3 %copy-start.1 = (bf16[1,3,256,256]{3,2,1,0:T(8,128)(2,1)S(1)}, bf16[1,3,256,256]{3,2,1,0:T(8,128)(2,1)}, u32[]{:S(2)}) copy-start(bf16[1,3,256,256]{3,2,1,0:T(8,128)(2,1)} %get-tuple-element.27) | copy-start | bytes 1179652
  229.2 13.9 %collective-permute-start.15 = (bf16[3,256,256]{2,1,0:T(8,128)(2,1)S(1)}, bf16[3,256,256]{2,1,0:T(8,128)(2,1)S(1)}, u32[]{:S(2)}, u32[]{:S(2)}) collective-permute-start(bf16[3,256,256]{2,1,0:T(8,128)(2,1)S(1)} %get-tuple-element.33), channel_id=1, source_target_pairs={{0,24},{2,26},{4,28},{6,30},{8,16},{10,18},{12,20},{14,22},{16,8},... | collective-permute-start | bytes 1179656 | tf_op jit(solution)/shard_map/ppermute | solution.py:183
  231.8 32.6 %collective-permute-start.14 = (bf16[3,256,256]{2,1,0:T(8,128)(2,1)S(1)}, bf16[3,256,256]{2,1,0:T(8,128)(2,1)S(1)}, u32[]{:S(2)}, u32[]{:S(2)}) collective-permute-start(bf16[3,256,256]{2,1,0:T(8,128)(2,1)S(1)} %get-tuple-element.34), channel_id=1, source_target_pairs={{0,16},{2,18},{4,20},{6,22},{8,24},{10,26},{12,28},{14,30},{16,0},... | collective-permute-start | bytes 1179656 | tf_op jit(solution)/shard_map/ppermute | solution.py:183
  243.0 21.4 %copy-start.7 = (bf16[3,256,256]{2,1,0:T(8,128)(2,1)}, bf16[3,256,256]{2,1,0:T(8,128)(2,1)S(1)}, u32[]{:S(2)}) copy-start(bf16[3,256,256]{2,1,0:T(8,128)(2,1)S(1)} %collective-permute-done.15) | copy-start | bytes 1179652
  264.5 0.7 copy-start.6
  267.6 152.6 %all-gather.15.cloned.1.call-start = ((), (), s32[]{:S(2)}) async-start(), calls=%async_computation.3 | async-start | bytes 7864320 | tf_op jit(solution)/shard_map/all_gather | solution.py:255
  268.1 13.6 %collective-permute-start.16 = (bf16[3,256,256]{2,1,0:T(8,128)(2,1)}, bf16[3,256,256]{2,1,0:T(8,128)(2,1)}, u32[]{:S(2)}, u32[]{:S(2)}) collective-permute-start(bf16[3,256,256]{2,1,0:T(8,128)(2,1)} %get-tuple-element.32), channel_id=1, source_target_pairs={{0,8},{2,10},{4,12},{6,14},{8,0},{10,2},{12,4},{14,6},{16,24},{18,... | collective-permute-start | bytes 1179656 | tf_op jit(solution)/shard_map/ppermute | solution.py:183
  272.0 29.5 %collective-permute-start.17 = (bf16[3,256,256]{2,1,0:T(8,128)(2,1)S(1)}, bf16[3,256,256]{2,1,0:T(8,128)(2,1)S(1)}, u32[]{:S(2)}, u32[]{:S(2)}) collective-permute-start(bf16[3,256,256]{2,1,0:T(8,128)(2,1)S(1)} %get-tuple-element.35), channel_id=1, source_target_pairs={{0,16},{2,18},{4,20},{6,22},{8,24},{10,26},{12,28},{14,30},{16,0},... | collective-permute-start | bytes 1179656 | tf_op jit(solution)/shard_map/ppermute | solution.py:183
  273.8 27.7 %collective-permute-start.18 = (bf16[3,256,256]{2,1,0:T(8,128)(2,1)S(1)}, bf16[3,256,256]{2,1,0:T(8,128)(2,1)S(1)}, u32[]{:S(2)}, u32[]{:S(2)}) collective-permute-start(bf16[3,256,256]{2,1,0:T(8,128)(2,1)S(1)} %get-tuple-element.36), channel_id=1, source_target_pairs={{0,24},{2,26},{4,28},{6,30},{8,16},{10,18},{12,20},{14,22},{16,8},... | collective-permute-start | bytes 1179656 | tf_op jit(solution)/shard_map/ppermute | solution.py:183
  303.9 4.2 copy-start.14
  303.9 4.4 copy-start.10
  303.9 5.4 %copy-start.11 = (bf16[7,3,2048]{2,0,1:T(8,128)(2,1)S(1)}, bf16[7,3,2048]{2,0,1:T(8,128)(2,1)}, u32[]{:S(2)}) copy-start(bf16[7,3,2048]{2,0,1:T(8,128)(2,1)} %param.8) | copy-start | bytes 258052
  306.5 24.5 %copy-start.2 = (bf16[2,144,2048]{2,1,0:T(8,128)(2,1)}, bf16[2,144,2048]{2,1,0:T(8,128)(2,1)S(1)}, u32[]{:S(2)}) copy-start(bf16[2,144,2048]{2,1,0:T(8,128)(2,1)S(1)} %pad_maximum_fusion.5.refs_4_) | copy-start | bytes 3538948
  306.5 24.5 %collective-permute-start.9 = (bf16[2,144,2048]{2,1,0:T(8,128)(2,1)S(1)}, bf16[2,144,2048]{2,1,0:T(8,128)(2,1)S(1)}, u32[]{:S(2)}, u32[]{:S(2)}) collective-permute-start(bf16[2,144,2048]{2,1,0:T(8,128)(2,1)S(1)} %pad_maximum_fusion.5.refs_4_), channel_id=1, source_target_pairs={{0,1},{1,0},{2,3},{3,2},{4,5},{5,4},{6,7},{7,6},{8,9},{9,8},{10,11... | collective-permute-start | bytes 3538952 | tf_op jit(solution)/shard_map/ppermute | solution.py:187
  331.0 1.0 copy-start.13
  355.9 33.4 %collective-permute-start.19 = (bf16[512,256]{1,0:T(8,128)(2,1)}, bf16[512,256]{1,0:T(8,128)(2,1)S(1)}, u32[]{:S(2)}, u32[]{:S(2)}) collective-permute-start(bf16[512,256]{1,0:T(8,128)(2,1)} %get-tuple-element.17), channel_id=1, source_target_pairs={{0,8},{2,10},{4,12},{6,14},{8,0},{10,2},{12,4},{14,6},{16,24},{18,... | collective-permute-start | bytes 786440 | tf_op jit(solution)/shard_map/ppermute | solution.py:183
  365.0 24.3 %copy-start.9 = (bf16[512,256]{1,0:T(8,128)(2,1)S(1)}, bf16[512,256]{1,0:T(8,128)(2,1)}, u32[]{:S(2)}) copy-start(bf16[512,256]{1,0:T(8,128)(2,1)} %get-tuple-element.13) | copy-start | bytes 786436
  389.2 6.6 %collective-permute-start.20 = (bf16[512,256]{1,0:T(8,128)(2,1)}, bf16[512,256]{1,0:T(8,128)(2,1)S(1)}, u32[]{:S(2)}, u32[]{:S(2)}) collective-permute-start(bf16[512,256]{1,0:T(8,128)(2,1)} %get-tuple-element.18), channel_id=1, source_target_pairs={{0,8},{2,10},{4,12},{6,14},{8,0},{10,2},{12,4},{14,6},{16,24},{18,... | collective-permute-start | bytes 786440 | tf_op jit(solution)/shard_map/ppermute | solution.py:183
  420.0 26.5 %collective-permute-start.21 = (bf16[512,256]{1,0:T(8,128)(2,1)}, bf16[512,256]{1,0:T(8,128)(2,1)S(1)}, u32[]{:S(2)}, u32[]{:S(2)}) collective-permute-start(bf16[512,256]{1,0:T(8,128)(2,1)} %get-tuple-element.19), channel_id=1, source_target_pairs={{0,8},{2,10},{4,12},{6,14},{8,0},{10,2},{12,4},{14,6},{16,24},{18,... | collective-permute-start | bytes 786440 | tf_op jit(solution)/shard_map/ppermute | solution.py:183
  420.1 26.4 %copy-start.8 = (bf16[512,256]{1,0:T(8,128)(2,1)S(1)}, bf16[512,256]{1,0:T(8,128)(2,1)}, u32[]{:S(2)}) copy-start(bf16[512,256]{1,0:T(8,128)(2,1)} %get-tuple-element.15) | copy-start | bytes 786436
  444.5 6.6 %collective-permute-start.22 = (bf16[512,256]{1,0:T(8,128)(2,1)}, bf16[512,256]{1,0:T(8,128)(2,1)S(1)}, u32[]{:S(2)}, u32[]{:S(2)}) collective-permute-start(bf16[512,256]{1,0:T(8,128)(2,1)} %get-tuple-element.20), channel_id=1, source_target_pairs={{0,8},{2,10},{4,12},{6,14},{8,0},{10,2},{12,4},{14,6},{16,24},{18,... | collective-permute-start | bytes 786440 | tf_op jit(solution)/shard_map/ppermute | solution.py:183
Sparse Core Ops, SparseCore 0:
  88.7 47.6 all-gather.8
  137.9 46.7 all-gather.10
  267.7 45.1 all-gather.12
  314.3 46.3 all-gather.14

commit v4 on v3

--- a/solution.py
+++ b/solution.py
@@ -20,10 +20,11 @@
     return jnp.sum(jnp.where(inside, places[:, None] - starts[None, :], 0), axis=1)
 
 
-def block_kernel(runs, halves, at_ref, w_ref, sw_ref, fr_ref, pos_ref, *refs):
+def block_kernel(runs, halves, parts, at_ref, *refs):
+    w_refs, (sw_ref, fr_ref, pos_ref), refs = refs[:parts], refs[parts : parts + 3], refs[parts + 3 :]
     row_refs, halo_refs = refs[: runs * halves], refs[runs * halves : (runs + 1) * halves]
     out_refs = refs[(runs + 1) * halves : (runs + 1) * halves + runs]
-    x_ref, sems, proj, mix, band = refs[(runs + 1) * halves + runs :]
+    x_ref, sems, proj, mix, band, done = refs[(runs + 1) * halves + runs :]
     total, features = x_ref.shape[1:]
     rows, chans = out_refs[0].shape
     halo = total - rows
@@ -32,8 +33,8 @@
     span = band.shape[0] // groups
     per_lanes = groups * LANES // chans
     width = LANES // per_lanes
-    outer, inner, _, depth, _ = w_ref.shape
-    units = [(q, k) for q in range(outer) for k in range(inner)]
+    depth = w_refs[0].shape[3]
+    units = [(w, q, k) for w in w_refs for q in range(w.shape[0]) for k in range(w.shape[1])]
     tile, run = pl.program_id(0), pl.program_id(1)
 
     def copies(r):
@@ -76,12 +77,16 @@
             x = jnp.concatenate([x_ref[run, low:high, pl.ds(at, depth)] for at in starts], axis=1)
         else:
             x = x_ref[run, low:high, :]
-        for s in range(3):
-            weight = jnp.concatenate([w_ref[q, k, s] for q, k in units], axis=0)
+        for streams in [(0, 1, 2)] if chans == LANES else [(0,), (1,), (2,)]:
+            weight = jnp.concatenate(
+                [jnp.concatenate([w[q, k, s] for w, q, k in units], axis=0) for s in streams], axis=1
+            )
             acc = jnp.dot(x, weight, preferred_element_type=jnp.float32)
             acc = acc.astype(jnp.bfloat16).astype(jnp.float32)
-            for h in range(chans // LANES):
-                proj[s, h, 8 + low : 8 + high, :] = acc[:, h * LANES : (h + 1) * LANES]
+            for n, s in enumerate(streams):
+                for h in range(chans // LANES):
+                    lane = n * chans + h * LANES
+                    proj[s, h, 8 + low : 8 + high, :] = acc[:, lane : lane + LANES]
 
     def short(s, start, size, h, allowed):
         lanes = slice(h * LANES, (h + 1) * LANES)
@@ -123,31 +128,36 @@
             medium = full[:span]
             for g in range(1, per_lanes):
                 medium = jnp.where(lane_group == g, full[g * span : (g + 1) * span], medium)
-            gated = (short(1, first, span, h, allowed) * medium).astype(out_refs[0].dtype)
-            for r in range(runs):
-
-                @pl.when(run == r)
-                def _():
-                    out_refs[r][b * span : (b + 1) * span, lanes] = gated
-
-
-def block(at, rows, halos, weight, sw, fr, pos, span):
+            gated = short(1, first, span, h, allowed) * medium
+            done[b * span : (b + 1) * span, lanes] = gated.astype(done.dtype)
+
+    for r in range(runs):
+
+        @pl.when(run == r)
+        def _():
+            out_refs[r][...] = done[...]
+
+
+def block(at, rows, halos, weights, sw, fr, pos, span, chans):
     runs, halves = len(rows), len(halos)
     row_count, features = rows[0][0].shape[0], rows[0][0].shape[1] * halves
     total = halos[0].shape[1] + row_count
-    outer, inner, _, depth, chans = weight.shape
     taps = sw.shape[1]
-    tile = CHAN_TILE if chans % CHAN_TILE == 0 else LANES
+    tile = CHAN_TILE if all(n % CHAN_TILE == 0 for n in [chans] + [first for first, _ in weights]) else LANES
     per_tile = tile * fr.shape[0] // chans
     grid = (chans // tile, runs)
     anywhere = pl.BlockSpec(memory_space=pl.ANY)
+
+    def weight_spec(first, w):
+        return pl.BlockSpec(w.shape[:4] + (tile,), lambda j, i, at: (0, 0, 0, 0, first // tile + j))
+
     return pl.pallas_call(
-        functools.partial(block_kernel, runs, halves),
+        functools.partial(block_kernel, runs, halves, len(weights)),
         grid_spec=pltpu.PrefetchScalarGridSpec(
             num_scalar_prefetch=1,
             grid=grid,
-            in_specs=[
-                pl.BlockSpec((outer, inner, 3, depth, tile), lambda j, i, at: (0, 0, 0, 0, j)),
+            in_specs=[weight_spec(first, w) for first, w in weights]
+            + [
                 pl.BlockSpec((3, taps, tile), lambda j, i, at: (0, 0, j)),
                 pl.BlockSpec((per_tile, 2 * span), lambda j, i, at: (j, 0)),
                 pl.BlockSpec((1, total, LANES), lambda j, i, at: (i, 0, 0)),
@@ -160,6 +170,7 @@
                 pltpu.VMEM((3, tile // LANES, 8 + total, LANES), jnp.float32),
                 pltpu.VMEM((total, tile), jnp.bfloat16),
                 pltpu.VMEM((per_tile * span, 2 * span), jnp.bfloat16),
+                pltpu.VMEM((row_count, tile), jnp.bfloat16),
             ],
         ),
         out_shape=[jax.ShapeDtypeStruct((row_count, chans), jnp.bfloat16)] * runs,
@@ -169,7 +180,7 @@
             bytes_accessed=2 * (runs * total * features + 3 * features * chans + runs * row_count * chans),
             transcendentals=0,
         ),
-    )(at, weight, sw, fr, pos, *[half for run in rows for half in run], *halos)
+    )(at, *[w for _, w in weights], sw, fr, pos, *[half for run in rows for half in run], *halos)
 
 
 def parameters(short_weight, medium_filter):
@@ -224,7 +235,7 @@
         halo = lax.all_gather(halo, "chan", axis=1, tiled=True)
         rows = lax.all_gather(tokens, "chan", axis=1, tiled=True)
         at = jnp.concatenate([order * depth, jnp.zeros(1, jnp.int32)])
-        return block(at, [[rows]], [halo[None]], weight[:, None], sw, fr, positions(me)[None], span)[0]
+        return block(at, [[rows]], [halo[None]], [(0, weight[:, None])], sw, fr, positions(me)[None], span, chans)[0]
 
     side = lax.axis_index("chan")
     kind = (me >> 2) & 1
@@ -240,26 +251,36 @@
     peer_halo = flip(halo, 4)
     halos = jnp.stack([halo, peer_halo])
     halos_other = across(halos)
-    after = {1: [peer_rows], 2: [rows_other, peer_halo], 3: [peer_rows_other]}
+    after = {0: [peer_rows, rows_other, halo], 1: [peer_halo, peer_rows_other], 2: [halos_other]}
 
     planes = [[4 * z + q for q in range(4)] for z in range(devices // 4)]
-    arrived, gathered = [], []
+
+    def spread(array):
+        return lax.all_gather(array, "stretch", axis=0, tiled=False, axis_index_groups=planes)
+
+    own = lax.dynamic_slice_in_dim(local, own_begin, half, 2)
+    peers = [
+        flip(lax.dynamic_slice_in_dim(local, other_begin + begin, width, 2), 4) for begin, width in zip(begins, widths)
+    ]
+    for c, peer in enumerate(peers[1:]):
+        after[c] = after.get(c, []) + [peer]
+    gathered, stack = [spread(own[None])], None
     for c, (begin, width) in enumerate(zip(begins, widths)):
-        units = [lax.dynamic_slice_in_dim(local, own_begin + begin, width, 2)]
-        for k in (1, 2, 3):
-            start = (own_begin if k == 2 else other_begin) + begin
-            if c > 0:
-                start = start + sum(nothing(first) for first in [arrived[c - 1][k]] + after.get(c, []))
-            units.append(flip(lax.dynamic_slice_in_dim(local, start, width, 2), 4 * k))
-        arrived.append(units)
-        whole = lax.all_gather(jnp.stack(units), "stretch", axis=0, tiled=False, axis_index_groups=planes)
-        gathered.append(whole)
-        after.setdefault(c + 2, []).append(whole)
+        mine = own[:, :, begin : begin + width]
+        peer = peers[c]
+        pair = jnp.stack([mine, peer])
+        if c > 0:
+            pair = pair + nothing(stack).astype(jnp.bfloat16)
+        stack = jnp.concatenate([peer[None], flip(pair, 8)])
+        waits = sum(nothing(array) for array in after.get(c, []) + [gathered[-1]])
+        stack = stack + waits.astype(jnp.bfloat16)
+        gathered.append(spread(stack))
 
     pos = jnp.stack([positions(me), positions(me ^ 4)])
     at = jnp.concatenate(
         [
-            jnp.stack([((me ^ (4 * k)) // 4 * 4 + q) * depth for q in range(4) for k in range(4)]),
+            jnp.stack([(me // 4 * 4 + q) * depth for q in range(4)]),
+            jnp.stack([((me ^ (4 * k)) // 4 * 4 + q) * depth for q in range(4) for k in (1, 2, 3)]),
             jnp.stack([side * piece, (1 - side) * piece]),
         ]
     )
@@ -274,11 +295,12 @@
             at,
             [[tokens, rows_other], [peer_rows, peer_rows_other]],
             [halos, halos_other],
-            gathered[c],
+            [(begin, gathered[0]), (0, gathered[c + 1])],
             own_sw[:, :, begin : begin + width],
             own_fr[first_group : first_group + groups],
             pos,
             span,
+            width,
         )
         mine.append(out)
         theirs.append(flip(peer_out, 4))

time: 464 us -> 364 us (0.78)
  waiting for transfers between devices: 252 us -> 189 us
  Pallas kernels: 96.5 us -> 80.3 us
  local copies, waits for them, and re-layouts: 31.8 us -> 23.9 us
  starting transfers between devices: 37.5 us -> 30.4 us
    ppermute x3, waiting for transfers between devices: 60.2 us -> 0.96 us  [across(): return lax.ppermute(array, 'chan', [(0, 1), (1, 0)])]
    all_gather x4 -> x5, waiting for transfers between devices: 0.07 us -> 39.6 us  [spread(): lax.all_gather(array, 'stretch', axis=0, tiled=False, axis_index_groups=p...]
    ppermute x19 -> x15, waiting for transfers between devices: 175 us -> 149 us  [flip(): lax.ppermute(array, 'stretch', [(i, i ^ bit) for i in range(lax.axis_size...]
    ppermute x1, waiting for transfers between devices: 17.1 us -> 0.01 us  [rows_before(): before = lax.ppermute(jnp.where(second, tail, sibling), 'stretch', pairs)]
    pallas_call x4, Pallas kernels: 96.5 us -> 80.3 us  [block(): pl.pallas_call(functools.partial(block_kernel, runs, halves, len(weights)...]
    ppermute x19 -> x15, starting transfers between devices: 29.5 us -> 22.2 us  [flip(): lax.ppermute(array, 'stretch', [(i, i ^ bit) for i in range(lax.axis_size...]
    another operation x5 -> x2, other arithmetic: 7.54 us -> 1.13 us  [the longest x1 0.94 us: per_device(): pair = jnp.stack([mine, peer])]
    add x0 -> x7, other arithmetic: none -> 5.75 us  [the longest x4 4.59 us: per_device(): stack = stack + waits.astype(jnp.bfloat16)]
  transfers between devices with their start and end apart: 27 -> 24, of which waited for: 16 -> 9; matrix products, arithmetic and copies ran while one was open for 7% -> 7% of each run, Pallas kernels for 21% -> 22%
where the time goes in v4:
time: 364 us
  waiting for transfers between devices  189 us (52%)
  Pallas kernels  80.3 us (22%)
  starting transfers between devices  30.4 us (8%)
  between operations  27 us (7%)
  local copies, waits for them, and re-layouts  23.9 us (7%)
  other arithmetic  12.8 us (4%)
    ppermute x15, waiting for transfers between devices, flip(): lax.ppermute(array, 'stretch', [(i, i ^ bit) for i in range(lax.axis_size...  149 us
    pallas_call x4, Pallas kernels, block(): pl.pallas_call(functools.partial(block_kernel, runs, halves, len(weights)...  80.3 us
    all_gather x5, waiting for transfers between devices, spread(): lax.all_gather(array, 'stretch', axis=0, tiled=False, axis_index_groups=p...  39.6 us
    ppermute x15, starting transfers between devices, flip(): lax.ppermute(array, 'stretch', [(i, i ^ bit) for i in range(lax.axis_size...  22.2 us
    slice x16, local copies, waits for them, and re-layouts, nothing(): array[(0,) * array.ndim].astype(jnp.float32) * 0.0  12.6 us
  transfers between devices with their start and end apart: 24, of which 9 were waited for; matrix products, arithmetic and copies ran while one was open for 7% of the time, Pallas kernels for 22%

profile of v4, /device:TPU:0, one launch (start us, length us, event | category | flops | bytes accessed | tf_op | source)
XLA Modules:
  0.0 363.8 jit_solution(12578581628642658052)
XLA Ops:
  6.5 2.8 dynamic-slice_bitcast_fusion
  9.4 1.9 slice.90
  11.4 0.5 collective-permute-start.4
  11.8 2.5 collective-permute-start.3
  14.3 1.6 collective-permute-start.2
  15.9 1.2 dynamic-slice_bitcast_fusion.1
  17.6 1.6 collective-permute-start
  19.2 0.6 fusion.2
  21.7 1.3 broadcast_select_fusion.3
  23.0 3.8 %collective-permute-start.5 = (bf16[144,2048]{1,0:T(8,128)(2,1)S(1)}, bf16[144,2048]{1,0:T(8,128)(2,1)S(1)}, u32[]{:S(2)}, u32[]{:S(2)}) collective-permute-start(bf16[144,2048]{1,0:T(8,128)(2,1)S(1)} %broadcast_select_fusion.3), channel_id=1, source_target_pairs={{0,4},{2,6},{4,8},{6,10},{8,12},{10,14},{12,16},{14,18},{16,20},{1... | collective-permute-start | bytes 1769480 | tf_op jit(solution)/shard_map/ppermute | solution.py:206
  26.9 52.2 %collective-permute-done = bf16[3,256,256]{2,1,0:T(8,128)(2,1)S(1)} collective-permute-done((bf16[3,256,256]{2,1,0:T(8,128)(2,1)}, bf16[3,256,256]{2,1,0:T(8,128)(2,1)S(1)}, u32[]{:S(2)}, u32[]{:S(2)}) %collective-permute-start) | collective-permute-done | bytes 393248 | tf_op jit(solution)/shard_map/ppermute | solution.py:194
  79.2 0.9 pad_maximum_fusion.2
  80.1 2.6 collective-permute-start.1
  82.7 0.6 slice.120
  84.0 1.1 broadcast_select_fusion.2
  85.1 0.5 slice.119
  86.2 1.2 slice.118
  87.9 1.1 slice.117
  89.6 1.2 slice.121
  91.4 25.5 %collective-permute-done.1 = bf16[2,3,256,256]{3,2,1,0:T(8,128)(2,1)S(1)} collective-permute-done((bf16[2,3,256,256]{3,2,1,0:T(8,128)(2,1)}, bf16[2,3,256,256]{3,2,1,0:T(8,128)(2,1)S(1)}, u32[]{:S(2)}, u32[]{:S(2)}) %collective-permute-start.1) | collective-permute-done | bytes 786464 | tf_op jit(solution)/shard_map/ppermute | solution.py:194
  116.9 1.2 maximum_add_fusion
  118.2 0.8 collective-permute-start.7
  118.9 0.5 slice.146
  120.1 1.0 maximum_add_fusion.4
  121.1 3.9 %collective-permute-start.8 = (bf16[144,2048]{1,0:T(8,128)(2,1)S(1)}, bf16[144,2048]{1,0:T(8,128)(2,1)S(1)}, u32[]{:S(2)}, u32[]{:S(2)}) collective-permute-start(bf16[144,2048]{1,0:T(8,128)(2,1)S(1)} %broadcast_select_fusion.2), channel_id=1, source_target_pairs={{0,8},{2,10},{4,12},{6,14},{8,0},{10,2},{12,4},{14,6},{16,24},{18,... | collective-permute-start | bytes 1769480 | tf_op jit(solution)/shard_map/ppermute | solution.py:194
  125.0 36.6 %collective-permute-done.11 = bf16[3,256,256]{2,1,0:T(8,128)(2,1)S(1)} collective-permute-done((bf16[3,256,256]{2,1,0:T(8,128)(2,1)}, bf16[3,256,256]{2,1,0:T(8,128)(2,1)S(1)}, u32[]{:S(2)}, u32[]{:S(2)}) %collective-permute-start.11) | collective-permute-done | bytes 393248 | tf_op jit(solution)/shard_map/ppermute | solution.py:194
  161.6 0.5 slice.127
  162.8 0.5 slice.125
  163.9 1.0 collective-permute-done.7.refs_8_
  164.9 1.3 copy-done.11
  166.2 0.6 slice.126
  167.5 1.2 slice.128
  169.4 1.1 maximum_add_fusion.1
  170.7 1.0 collective-permute-start.9
  171.7 0.6 slice.148
  173.0 1.9 collective-permute-start.12
  174.9 2.9 collective-permute-start.13
  177.8 21.4 %collective-permute-done.13 = bf16[3,256,256]{2,1,0:T(8,128)(2,1)S(1)} collective-permute-done((bf16[3,256,256]{2,1,0:T(8,128)(2,1)S(1)}, bf16[3,256,256]{2,1,0:T(8,128)(2,1)S(1)}, u32[]{:S(2)}, u32[]{:S(2)}) %collective-permute-start.13) | collective-permute-done | bytes 393248 | tf_op jit(solution)/shard_map/ppermute | solution.py:194
  199.2 0.6 slice.133
  200.5 1.0 copy-done.12
  201.5 0.5 slice.132
  202.7 5.8 %all-gather.9.cloned.1.call-done.refs_1_ = bf16[4,3,3,256,256]{4,3,2,1,0:T(8,128)(2,1)} async-done(((bf16[1,3,3,256,256]{4,3,2,1,0:T(8,128)(2,1)}), bf16[4,3,3,256,256]{4,3,2,1,0:T(8,128)(2,1)}) %all-gather.9.cloned.1.call-update) | async-done | bytes 4718608 | tf_op jit(solution)/shard_map/all_gather | solution.py:259
  208.5 1.2 slice.134
  210.4 1.1 maximum_add_fusion.2
  211.6 0.6 slice.150
  213.0 2.5 collective-permute-start.14
  215.5 33.7 %all-gather.11.cloned.1.call-done.refs_1_ = bf16[4,3,3,256,256]{4,3,2,1,0:T(8,128)(2,1)} async-done(((bf16[1,3,3,256,256]{4,3,2,1,0:T(8,128)(2,1)}), bf16[4,3,3,256,256]{4,3,2,1,0:T(8,128)(2,1)}) %all-gather.11.cloned.1.call-update) | async-done | bytes 4718608 | tf_op jit(solution)/shard_map/all_gather | solution.py:259
  249.2 1.2 slice.138
  251.1 1.1 maximum_add_fusion.3
  254.0 0.6 concatenate.74.at_ref
  255.1 0.9 pad_add_fusion.refs_4_
  256.0 0.6 fusion.4
  256.6 0.7 fusion.3
  257.3 20.5 %shard_map.64 = (bf16[512,256]{1,0:T(8,128)(2,1)}, bf16[512,256]{1,0:T(8,128)(2,1)}) custom-call(s32[18]{0:T(128)} %concatenate.74.at_ref, bf16[4,1,3,256,1024]{4,3,2,1,0:T(8,128)(2,1)} %bitcast.92, bf16[4,3,3,256,256]{4,3,2,1,0:T(8,128)(2,1)} %all-gather.7.cloned.1.call-done.refs_1_, f32[3,7,256]{2,1,0:T(8,128)} %get-tuple-element.38.refs_2_, ...), custom_call_target="tpu_custom_call" | custom-call | flops 16508780544 | bytes 17563648 | tf_op jit(solution)/shard_map/pallas_call | solution.py:154
  277.8 1.7 collective-permute-start.15
  279.5 19.9 %shard_map.65 = (bf16[512,256]{1,0:T(8,128)(2,1)}, bf16[512,256]{1,0:T(8,128)(2,1)}) custom-call(s32[18]{0:T(128)} %concatenate.74.at_ref, bf16[4,1,3,256,1024]{4,3,2,1,0:T(8,128)(2,1)} %bitcast.93, bf16[4,3,3,256,256]{4,3,2,1,0:T(8,128)(2,1)} %all-gather.9.cloned.1.call-done.refs_1_, f32[3,7,256]{2,1,0:T(8,128)} %get-tuple-element.37.refs_2_, ...), custom_call_target="tpu_custom_call" | custom-call | flops 16508780544 | bytes 17563648 | tf_op jit(solution)/shard_map/pallas_call | solution.py:154
  299.4 0.6 collective-permute-start.16
  300.4 7.5 %collective-permute-done.16 = bf16[512,256]{1,0:T(8,128)(2,1)S(1)} collective-permute-done((bf16[512,256]{1,0:T(8,128)(2,1)}, bf16[512,256]{1,0:T(8,128)(2,1)S(1)}, u32[]{:S(2)}, u32[]{:S(2)}) %collective-permute-start.16) | collective-permute-done | bytes 262176 | tf_op jit(solution)/shard_map/ppermute | solution.py:194
  307.9 19.9 %shard_map.66 = (bf16[512,256]{1,0:T(8,128)(2,1)}, bf16[512,256]{1,0:T(8,128)(2,1)}) custom-call(s32[18]{0:T(128)} %concatenate.74.at_ref, bf16[4,1,3,256,1024]{4,3,2,1,0:T(8,128)(2,1)} %bitcast.94, bf16[4,3,3,256,256]{4,3,2,1,0:T(8,128)(2,1)} %all-gather.11.cloned.1.call-done.refs_1_, f32[3,7,256]{2,1,0:T(8,128)} %get-tuple-element.36.refs_2_, ...), custom_call_target="tpu_custom_call" | custom-call | flops 16508780544 | bytes 17563648 | tf_op jit(solution)/shard_map/pallas_call | solution.py:154
  327.8 0.5 collective-permute-start.17
  328.3 20.0 %shard_map.67 = (bf16[512,256]{1,0:T(8,128)(2,1)}, bf16[512,256]{1,0:T(8,128)(2,1)}) custom-call(s32[18]{0:T(128)} %concatenate.74.at_ref, bf16[4,1,3,256,1024]{4,3,2,1,0:T(8,128)(2,1)} %bitcast.95, bf16[4,3,3,256,256]{4,3,2,1,0:T(8,128)(2,1)} %all-gather.13.cloned.1.call-done.refs_1_, f32[3,7,256]{2,1,0:T(8,128)} %get-tuple-element.35.refs_2_, ...), custom_call_target="tpu_custom_call" | custom-call | flops 16508780544 | bytes 17563648 | tf_op jit(solution)/shard_map/pallas_call | solution.py:154
  348.4 1.7 collective-permute-start.18
  350.1 5.5 %collective-permute-done.18 = bf16[512,256]{1,0:T(8,128)(2,1)S(1)} collective-permute-done((bf16[512,256]{1,0:T(8,128)(2,1)}, bf16[512,256]{1,0:T(8,128)(2,1)S(1)}, u32[]{:S(2)}, u32[]{:S(2)}) %collective-permute-start.18) | collective-permute-done | bytes 262176 | tf_op jit(solution)/shard_map/ppermute | solution.py:194
  355.8 1.5 pad_maximum_fusion
  (77 shorter events, 2.7 us)
Async XLA Ops:
  6.5 83.1 %all-gather.15.cloned.1.call-start = ((), (), s32[]{:S(2)}) async-start(), calls=%async_computation.4 | async-start | bytes 7864320 | tf_op jit(solution)/shard_map/all_gather | solution.py:259
  6.5 9.4 %copy-start.1 = (bf16[256,3,2048]{2,0,1:T(8,128)(2,1)S(1)}, bf16[256,3,2048]{2,0,1:T(8,128)(2,1)}, u32[]{:S(2)}) copy-start(bf16[256,3,2048]{2,0,1:T(8,128)(2,1)} %param.7) | copy-start | bytes 9437188
  9.4 158.1 %all-gather.7.cloned.1.call-start = ((), (), s32[]{:S(2)}) async-start(), calls=%async_computation | async-start | bytes 5898240 | tf_op jit(solution)/shard_map/all_gather | solution.py:259
  11.4 10.3 %collective-permute-start.4 = (bf16[144,2048]{1,0:T(8,128)(2,1)}, bf16[144,2048]{1,0:T(8,128)(2,1)}, u32[]{:S(2)}, u32[]{:S(2)}) collective-permute-start(bf16[144,2048]{1,0:T(8,128)(2,1)} %slice.90), channel_id=1, source_target_pairs={{0,2},{2,0},{4,6},{6,4},{8,10},{10,8},{12,14},{14,12},{16,18},{18,... | collective-permute-start | bytes 1769480 | tf_op jit(solution)/shard_map/ppermute | solution.py:194
  11.8 74.3 %collective-permute-start.3 = (bf16[512,2048]{1,0:T(8,128)(2,1)}, bf16[512,2048]{1,0:T(8,128)(2,1)}, u32[]{:S(2)}, u32[]{:S(2)}) collective-permute-start(bf16[512,2048]{1,0:T(8,128)(2,1)} %refs_5_.7), channel_id=1, source_target_pairs={{0,1},{1,0},{2,3},{3,2},{4,5},{5,4},{6,7},{7,6},{8,9},{9,8},{10,11... | collective-permute-start | bytes 6291464 | tf_op jit(solution)/shard_map/ppermute | solution.py:198
  14.3 73.6 %collective-permute-start.2 = (bf16[512,2048]{1,0:T(8,128)(2,1)}, bf16[512,2048]{1,0:T(8,128)(2,1)}, u32[]{:S(2)}, u32[]{:S(2)}) collective-permute-start(bf16[512,2048]{1,0:T(8,128)(2,1)} %refs_5_.7), channel_id=1, source_target_pairs={{0,8},{2,10},{4,12},{6,14},{8,0},{10,2},{12,4},{14,6},{16,24},{18,... | collective-permute-start | bytes 6291464 | tf_op jit(solution)/shard_map/ppermute | solution.py:194
  15.9 3.3 copy-start.10
  17.1 9.7 %copy-start = (bf16[3,256,1024]{2,1,0:T(8,128)(2,1)S(1)}, bf16[3,256,1024]{2,1,0:T(8,128)(2,1)}, u32[]{:S(2)}) copy-start(bf16[3,256,1024]{2,1,0:T(8,128)(2,1)} %dynamic-slice_bitcast_fusion) | copy-start | bytes 4718596
  17.1 65.5 %collective-permute-start.6 = (bf16[3,256,256]{2,1,0:T(8,128)(2,1)}, bf16[3,256,256]{2,1,0:T(8,128)(2,1)S(1)}, u32[]{:S(2)}, u32[]{:S(2)}) collective-permute-start(bf16[3,256,256]{2,1,0:T(8,128)(2,1)} %get-tuple-element.26), channel_id=1, source_target_pairs={{0,8},{2,10},{4,12},{6,14},{8,0},{10,2},{12,4},{14,6},{16,24},{18,... | collective-permute-start | bytes 1179656 | tf_op jit(solution)/shard_map/ppermute | solution.py:194
  17.6 61.6 %collective-permute-start = (bf16[3,256,256]{2,1,0:T(8,128)(2,1)}, bf16[3,256,256]{2,1,0:T(8,128)(2,1)S(1)}, u32[]{:S(2)}, u32[]{:S(2)}) collective-permute-start(bf16[3,256,256]{2,1,0:T(8,128)(2,1)} %get-tuple-element.27), channel_id=1, source_target_pairs={{0,8},{2,10},{4,12},{6,14},{8,0},{10,2},{12,4},{14,6},{16,24},{18,... | collective-permute-start | bytes 1179656 | tf_op jit(solution)/shard_map/ppermute | solution.py:194
  23.0 60.9 %collective-permute-start.5 = (bf16[144,2048]{1,0:T(8,128)(2,1)S(1)}, bf16[144,2048]{1,0:T(8,128)(2,1)S(1)}, u32[]{:S(2)}, u32[]{:S(2)}) collective-permute-start(bf16[144,2048]{1,0:T(8,128)(2,1)S(1)} %broadcast_select_fusion.3), channel_id=1, source_target_pairs={{0,4},{2,6},{4,8},{6,10},{8,12},{10,14},{12,16},{14,18},{16,20},{1... | collective-permute-start | bytes 1769480 | tf_op jit(solution)/shard_map/ppermute | solution.py:206
  80.1 36.8 %collective-permute-start.1 = (bf16[2,3,256,256]{3,2,1,0:T(8,128)(2,1)}, bf16[2,3,256,256]{3,2,1,0:T(8,128)(2,1)S(1)}, u32[]{:S(2)}, u32[]{:S(2)}) collective-permute-start(bf16[2,3,256,256]{3,2,1,0:T(8,128)(2,1)} %pad_maximum_fusion.2), channel_id=1, source_target_pairs={{0,16},{2,18},{4,20},{6,22},{8,24},{10,26},{12,28},{14,30},{16,0},... | collective-permute-start | bytes 2359304 | tf_op jit(solution)/shard_map/ppermute | solution.py:194
  118.1 90.4 %all-gather.9.cloned.1.call-start = ((), (), s32[]{:S(2)}) async-start(), calls=%async_computation.1 | async-start | bytes 5898240 | tf_op jit(solution)/shard_map/all_gather | solution.py:259
  118.2 46.7 %collective-permute-start.7 = (bf16[512,2048]{1,0:T(8,128)(2,1)}, bf16[512,2048]{1,0:T(8,128)(2,1)S(1)}, u32[]{:S(2)}, u32[]{:S(2)}) collective-permute-start(bf16[512,2048]{1,0:T(8,128)(2,1)} %collective-permute-done.2.refs_7_), channel_id=1, source_target_pairs={{0,1},{1,0},{2,3},{3,2},{4,5},{5,4},{6,7},{7,6},{8,9},{9,8},{10,11... | collective-permute-start | bytes 6291464 | tf_op jit(solution)/shard_map/ppermute | solution.py:198
  121.1 48.3 %collective-permute-start.10 = (bf16[2,3,256,256]{3,2,1,0:T(8,128)(2,1)}, bf16[2,3,256,256]{3,2,1,0:T(8,128)(2,1)S(1)}, u32[]{:S(2)}, u32[]{:S(2)}) collective-permute-start(bf16[2,3,256,256]{3,2,1,0:T(8,128)(2,1)} %maximum_add_fusion.4), channel_id=1, source_target_pairs={{0,16},{2,18},{4,20},{6,22},{8,24},{10,26},{12,28},{14,30},{16,0},... | collective-permute-start | bytes 2359304 | tf_op jit(solution)/shard_map/ppermute | solution.py:194
  121.1 41.7 %collective-permute-start.8 = (bf16[144,2048]{1,0:T(8,128)(2,1)S(1)}, bf16[144,2048]{1,0:T(8,128)(2,1)S(1)}, u32[]{:S(2)}, u32[]{:S(2)}) collective-permute-start(bf16[144,2048]{1,0:T(8,128)(2,1)S(1)} %broadcast_select_fusion.2), channel_id=1, source_target_pairs={{0,8},{2,10},{4,12},{6,14},{8,0},{10,2},{12,4},{14,6},{16,24},{18,... | collective-permute-start | bytes 1769480 | tf_op jit(solution)/shard_map/ppermute | solution.py:194
  125.0 36.6 %collective-permute-start.11 = (bf16[3,256,256]{2,1,0:T(8,128)(2,1)}, bf16[3,256,256]{2,1,0:T(8,128)(2,1)S(1)}, u32[]{:S(2)}, u32[]{:S(2)}) collective-permute-start(bf16[3,256,256]{2,1,0:T(8,128)(2,1)} %get-tuple-element.28), channel_id=1, source_target_pairs={{0,8},{2,10},{4,12},{6,14},{8,0},{10,2},{12,4},{14,6},{16,24},{18,... | collective-permute-start | bytes 1179656 | tf_op jit(solution)/shard_map/ppermute | solution.py:194
  164.9 1.3 copy-start.11
  170.5 78.7 %all-gather.11.cloned.1.call-start = ((), (), s32[]{:S(2)}) async-start(), calls=%async_computation.2 | async-start | bytes 5898240 | tf_op jit(solution)/shard_map/all_gather | solution.py:259
  170.7 28.5 %copy-start.2 = (bf16[2,144,2048]{2,1,0:T(8,128)(2,1)}, bf16[2,144,2048]{2,1,0:T(8,128)(2,1)S(1)}, u32[]{:S(2)}) copy-start(bf16[2,144,2048]{2,1,0:T(8,128)(2,1)S(1)} %pad_maximum_fusion.1.refs_9_) | copy-start | bytes 3538948
  170.7 4.2 %copy-start.3 = (bf16[3,256,256]{2,1,0:T(8,128)(2,1)S(1)}, bf16[3,256,256]{2,1,0:T(8,128)(2,1)}, u32[]{:S(2)}) copy-start(bf16[3,256,256]{2,1,0:T(8,128)(2,1)} %get-tuple-element.25) | copy-start | bytes 1179652
  170.7 29.8 %collective-permute-start.9 = (bf16[2,144,2048]{2,1,0:T(8,128)(2,1)S(1)}, bf16[2,144,2048]{2,1,0:T(8,128)(2,1)S(1)}, u32[]{:S(2)}, u32[]{:S(2)}) collective-permute-start(bf16[2,144,2048]{2,1,0:T(8,128)(2,1)S(1)} %pad_maximum_fusion.1.refs_9_), channel_id=1, source_target_pairs={{0,1},{1,0},{2,3},{3,2},{4,5},{5,4},{6,7},{7,6},{8,9},{9,8},{10,11... | collective-permute-start | bytes 3538952 | tf_op jit(solution)/shard_map/ppermute | solution.py:198
  173.0 37.4 %collective-permute-start.12 = (bf16[2,3,256,256]{3,2,1,0:T(8,128)(2,1)S(1)}, bf16[2,3,256,256]{3,2,1,0:T(8,128)(2,1)S(1)}, u32[]{:S(2)}, u32[]{:S(2)}) collective-permute-start(bf16[2,3,256,256]{3,2,1,0:T(8,128)(2,1)S(1)} %maximum_add_fusion.5), channel_id=1, source_target_pairs={{0,16},{2,18},{4,20},{6,22},{8,24},{10,26},{12,28},{14,30},{16,0},... | collective-permute-start | bytes 2359304 | tf_op jit(solution)/shard_map/ppermute | solution.py:194
  174.9 24.3 %collective-permute-start.13 = (bf16[3,256,256]{2,1,0:T(8,128)(2,1)S(1)}, bf16[3,256,256]{2,1,0:T(8,128)(2,1)S(1)}, u32[]{:S(2)}, u32[]{:S(2)}) collective-permute-start(bf16[3,256,256]{2,1,0:T(8,128)(2,1)S(1)} %copy-done.3), channel_id=1, source_target_pairs={{0,8},{2,10},{4,12},{6,14},{8,0},{10,2},{12,4},{14,6},{16,24},{18,... | collective-permute-start | bytes 1179656 | tf_op jit(solution)/shard_map/ppermute | solution.py:194
  200.5 1.0 copy-start.12
  211.6 116.7 %all-gather.13.cloned.1.call-start = ((), (), s32[]{:S(2)}) async-start(), calls=%async_computation.3 | async-start | bytes 5898240 | tf_op jit(solution)/shard_map/all_gather | solution.py:259
  213.0 38.1 %collective-permute-start.14 = (bf16[2,3,256,256]{3,2,1,0:T(8,128)(2,1)S(1)}, bf16[2,3,256,256]{3,2,1,0:T(8,128)(2,1)S(1)}, u32[]{:S(2)}, u32[]{:S(2)}) collective-permute-start(bf16[2,3,256,256]{3,2,1,0:T(8,128)(2,1)S(1)} %maximum_add_fusion.6), channel_id=1, source_target_pairs={{0,16},{2,18},{4,20},{6,22},{8,24},{10,26},{12,28},{14,30},{16,0},... | collective-permute-start | bytes 2359304 | tf_op jit(solution)/shard_map/ppermute | solution.py:194
  252.2 1.3 copy-start.13
  252.2 1.5 copy-start.8
  252.2 2.5 copy-start.9
  277.8 22.2 %collective-permute-start.15 = (bf16[512,256]{1,0:T(8,128)(2,1)}, bf16[512,256]{1,0:T(8,128)(2,1)S(1)}, u32[]{:S(2)}, u32[]{:S(2)}) collective-permute-start(bf16[512,256]{1,0:T(8,128)(2,1)} %get-tuple-element.17), channel_id=1, source_target_pairs={{0,8},{2,10},{4,12},{6,14},{8,0},{10,2},{12,4},{14,6},{16,24},{18,... | collective-permute-start | bytes 786440 | tf_op jit(solution)/shard_map/ppermute | solution.py:194
  279.5 20.5 %copy-start.6 = (bf16[512,256]{1,0:T(8,128)(2,1)S(1)}, bf16[512,256]{1,0:T(8,128)(2,1)}, u32[]{:S(2)}) copy-start(bf16[512,256]{1,0:T(8,128)(2,1)} %get-tuple-element.13) | copy-start | bytes 786436
  299.4 1.0 copy-start.7
  299.4 8.5 %collective-permute-start.16 = (bf16[512,256]{1,0:T(8,128)(2,1)}, bf16[512,256]{1,0:T(8,128)(2,1)S(1)}, u32[]{:S(2)}, u32[]{:S(2)}) collective-permute-start(bf16[512,256]{1,0:T(8,128)(2,1)} %get-tuple-element.18), channel_id=1, source_target_pairs={{0,8},{2,10},{4,12},{6,14},{8,0},{10,2},{12,4},{14,6},{16,24},{18,... | collective-permute-start | bytes 786440 | tf_op jit(solution)/shard_map/ppermute | solution.py:194
  327.8 22.2 %collective-permute-start.17 = (bf16[512,256]{1,0:T(8,128)(2,1)}, bf16[512,256]{1,0:T(8,128)(2,1)S(1)}, u32[]{:S(2)}, u32[]{:S(2)}) collective-permute-start(bf16[512,256]{1,0:T(8,128)(2,1)} %get-tuple-element.19), channel_id=1, source_target_pairs={{0,8},{2,10},{4,12},{6,14},{8,0},{10,2},{12,4},{14,6},{16,24},{18,... | collective-permute-start | bytes 786440 | tf_op jit(solution)/shard_map/ppermute | solution.py:194
  328.3 21.7 %copy-start.4 = (bf16[512,256]{1,0:T(8,128)(2,1)S(1)}, bf16[512,256]{1,0:T(8,128)(2,1)}, u32[]{:S(2)}) copy-start(bf16[512,256]{1,0:T(8,128)(2,1)} %get-tuple-element.15) | copy-start | bytes 786436
  348.3 1.7 copy-start.5
  348.4 7.3 %collective-permute-start.18 = (bf16[512,256]{1,0:T(8,128)(2,1)}, bf16[512,256]{1,0:T(8,128)(2,1)S(1)}, u32[]{:S(2)}, u32[]{:S(2)}) collective-permute-start(bf16[512,256]{1,0:T(8,128)(2,1)} %get-tuple-element.20), channel_id=1, source_target_pairs={{0,8},{2,10},{4,12},{6,14},{8,0},{10,2},{12,4},{14,6},{16,24},{18,... | collective-permute-start | bytes 786440 | tf_op jit(solution)/shard_map/ppermute | solution.py:194
Sparse Core Ops, SparseCore 0:
  9.5 57.9 all-gather.14
  118.2 37.7 all-gather.6
  170.7 37.7 all-gather.8
  211.7 37.4 all-gather.10
  252.4 37.4 all-gather.12

commit v5 on v4

--- a/solution.py
+++ b/solution.py
@@ -264,18 +264,6 @@
     ]
     for c, peer in enumerate(peers[1:]):
         after[c] = after.get(c, []) + [peer]
-    gathered, stack = [spread(own[None])], None
-    for c, (begin, width) in enumerate(zip(begins, widths)):
-        mine = own[:, :, begin : begin + width]
-        peer = peers[c]
-        pair = jnp.stack([mine, peer])
-        if c > 0:
-            pair = pair + nothing(stack).astype(jnp.bfloat16)
-        stack = jnp.concatenate([peer[None], flip(pair, 8)])
-        waits = sum(nothing(array) for array in after.get(c, []) + [gathered[-1]])
-        stack = stack + waits.astype(jnp.bfloat16)
-        gathered.append(spread(stack))
-
     pos = jnp.stack([positions(me), positions(me ^ 4)])
     at = jnp.concatenate(
         [
@@ -287,8 +275,19 @@
     own_sw = lax.dynamic_slice_in_dim(sw, own_begin, half, 2)
     own_fr = lax.dynamic_slice_in_dim(fr, own_begin * fr.shape[0] // chans, fr.shape[0] // 2, 0)
 
+    gathered, stack = [spread(own[None])], None
     mine, theirs = [], []
     for c, (begin, width) in enumerate(zip(begins, widths)):
+        same, peer = own[:, :, begin : begin + width], peers[c]
+        if c == 0:
+            other = lax.dynamic_slice_in_dim(local, other_begin, width, 2)
+            stack = jnp.stack([peer, flip(same, 8), flip(other, 12)])
+        else:
+            pair = jnp.stack([same, peer]) + nothing(stack).astype(jnp.bfloat16)
+            stack = jnp.concatenate([peer[None], flip(pair, 8)])
+        waits = sum(nothing(array) for array in after.get(c, []) + [gathered[-1]])
+        stack = stack + waits.astype(jnp.bfloat16)
+        gathered.append(spread(stack))
         groups = fr.shape[0] * width // chans
         first_group = begin * fr.shape[0] // chans
         out, peer_out = block(
@@ -304,6 +303,7 @@
         )
         mine.append(out)
         theirs.append(flip(peer_out, 4))
+        after[c + 3] = [out]
     mine, theirs = jnp.concatenate(mine, axis=1), jnp.concatenate(theirs, axis=1)
     even = kind == 0
     return jnp.concatenate([jnp.where(even, mine, theirs), jnp.where(even, theirs, mine)], axis=1)

time: 364 us -> 342 us (0.940)
  waiting for transfers between devices: 189 us -> 152 us
  starting transfers between devices: 30.4 us -> 38.1 us
    ppermute x15 -> x16, waiting for transfers between devices: 149 us -> 126 us  [flip(): lax.ppermute(array, 'stretch', [(i, i ^ bit) for i in range(lax.axis_size...]
    all_gather x5, waiting for transfers between devices: 39.6 us -> 24.6 us  [spread(): lax.all_gather(array, 'stretch', axis=0, tiled=False, axis_index_groups=p...]
    ppermute x15 -> x16, starting transfers between devices: 22.2 us -> 28.8 us  [flip(): lax.ppermute(array, 'stretch', [(i, i ^ bit) for i in range(lax.axis_size...]
    slice x16 -> x17, local copies, waits for them, and re-layouts: 12.6 us -> 13.6 us  [nothing(): array[(0,) * array.ndim].astype(jnp.float32) * 0.0]
  transfers between devices with their start and end apart: 24 -> 25, of which waited for: 9 -> 13; matrix products, arithmetic and copies ran while one was open for 7% -> 8% of each run, Pallas kernels for 22% -> 24%
where the time goes in v5:
time: 342 us; the launch traced here: 341 us
  waiting for transfers between devices  152 us (44%)
  Pallas kernels  81.1 us (24%)
  starting transfers between devices  38.1 us (11%)
  between operations  27.6 us (8%)
  local copies, waits for them, and re-layouts  26.3 us (8%)
  other arithmetic  15.7 us (5%)
    ppermute x16, waiting for transfers between devices, flip(): lax.ppermute(array, 'stretch', [(i, i ^ bit) for i in range(lax.axis_size...  126 us
    pallas_call x4, Pallas kernels, block(): pl.pallas_call(functools.partial(block_kernel, runs, halves, len(weights)...  81.1 us
    ppermute x16, starting transfers between devices, flip(): lax.ppermute(array, 'stretch', [(i, i ^ bit) for i in range(lax.axis_size...  28.8 us
    all_gather x5, waiting for transfers between devices, spread(): lax.all_gather(array, 'stretch', axis=0, tiled=False, axis_index_groups=p...  24.6 us
    slice x17, local copies, waits for them, and re-layouts, nothing(): array[(0,) * array.ndim].astype(jnp.float32) * 0.0  13.6 us
  transfers between devices with their start and end apart: 25, of which 13 were waited for; matrix products, arithmetic and copies ran while one was open for 8% of the time, Pallas kernels for 24%

profile of v5, /device:TPU:0, one launch (start us, length us, event | category | flops | bytes accessed | tf_op | source)
XLA Modules:
  0.0 341.2 jit_solution(871202036204586144)
XLA Ops:
  6.5 2.7 dynamic-slice_bitcast_fusion
  9.3 2.1 slice.93
  11.8 2.5 collective-permute-start.4
  14.3 1.6 collective-permute-start.3
  15.9 0.7 fusion.2
  18.7 2.1 broadcast_select_fusion.3
  20.8 4.5 %collective-permute-start.6 = (bf16[144,2048]{1,0:T(8,128)(2,1)}, bf16[144,2048]{1,0:T(8,128)(2,1)}, u32[]{:S(2)}, u32[]{:S(2)}) collective-permute-start(bf16[144,2048]{1,0:T(8,128)(2,1)} %broadcast_select_fusion.3), channel_id=1, source_target_pairs={{0,4},{2,6},{4,8},{6,10},{8,12},{10,14},{12,16},{14,18},{16,20},{1... | collective-permute-start | bytes 1769480 | tf_op jit(solution)/shard_map/ppermute | solution.py:206
  25.3 1.1 dynamic-slice_bitcast_fusion.1
  26.4 3.0 collective-permute-start.2
  29.6 41.2 %collective-permute-done.7 = bf16[3,256,256]{2,1,0:T(8,128)(2,1)S(1)} collective-permute-done((bf16[3,256,256]{2,1,0:T(8,128)(2,1)S(1)}, bf16[3,256,256]{2,1,0:T(8,128)(2,1)S(1)}, u32[]{:S(2)}, u32[]{:S(2)}) %collective-permute-start.7) | collective-permute-done | bytes 393248 | tf_op jit(solution)/shard_map/ppermute | solution.py:194
  70.7 2.3 collective-permute-start
  73.0 0.6 slice.124
  74.3 10.0 %collective-permute-start.1 = (bf16[3,256,256]{2,1,0:T(8,128)(2,1)S(1)}, bf16[3,256,256]{2,1,0:T(8,128)(2,1)}, u32[]{:S(2)}, u32[]{:S(2)}) collective-permute-start(bf16[3,256,256]{2,1,0:T(8,128)(2,1)S(1)} %get-tuple-element.34), channel_id=1, source_target_pairs={{0,16},{2,18},{4,20},{6,22},{8,24},{10,26},{12,28},{14,30},{16,0},... | collective-permute-start | bytes 1179656 | tf_op jit(solution)/shard_map/ppermute | solution.py:194
  84.3 1.1 broadcast_select_fusion.2
  85.4 0.5 slice.123
  86.5 1.2 slice.122
  88.3 1.2 slice.121
  90.1 1.2 slice.125
  91.9 5.6 %collective-permute-done = bf16[3,256,256]{2,1,0:T(8,128)(2,1)S(1)} collective-permute-done((bf16[3,256,256]{2,1,0:T(8,128)(2,1)}, bf16[3,256,256]{2,1,0:T(8,128)(2,1)S(1)}, u32[]{:S(2)}, u32[]{:S(2)}) %collective-permute-start) | collective-permute-done | bytes 393248 | tf_op jit(solution)/shard_map/ppermute | solution.py:194
  97.5 1.1 collective-permute-done.1
  98.6 2.2 maximum_add_fusion
  100.9 0.6 collective-permute-start.8
  101.4 0.6 slice.149
  102.6 1.0 maximum_add_fusion.4
  103.8 2.9 collective-permute-start.9
  106.7 36.4 %collective-permute-done.12 = bf16[3,256,256]{2,1,0:T(8,128)(2,1)S(1)} collective-permute-done((bf16[3,256,256]{2,1,0:T(8,128)(2,1)}, bf16[3,256,256]{2,1,0:T(8,128)(2,1)S(1)}, u32[]{:S(2)}, u32[]{:S(2)}) %collective-permute-start.12) | collective-permute-done | bytes 393248 | tf_op jit(solution)/shard_map/ppermute | solution.py:194
  143.1 0.5 slice.131
  144.3 0.6 slice.129
  145.5 1.9 collective-permute-done.8.refs_8_
  147.4 1.3 copy-done.12
  149.8 15.2 %all-gather.7.cloned.1.call-done.refs_1_ = bf16[4,3,3,256,256]{4,3,2,1,0:T(8,128)(2,1)} async-done(((bf16[1,3,3,256,256]{4,3,2,1,0:T(8,128)(2,1)}), bf16[4,3,3,256,256]{4,3,2,1,0:T(8,128)(2,1)}) %all-gather.7.cloned.1.call-update) | async-done | bytes 4718608 | tf_op jit(solution)/shard_map/all_gather | solution.py:259
  165.0 1.3 slice.132
  167.0 1.1 maximum_add_fusion.1
  168.2 1.2 pad_maximum_fusion.1.refs_9_
  169.4 1.5 collective-permute-start.10
  172.0 1.0 maximum_add_fusion.5
  173.0 2.4 collective-permute-start.13
  175.4 1.5 collective-permute-start.14
  176.9 24.1 %collective-permute-done.14 = bf16[3,256,256]{2,1,0:T(8,128)(2,1)S(1)} collective-permute-done((bf16[3,256,256]{2,1,0:T(8,128)(2,1)S(1)}, bf16[3,256,256]{2,1,0:T(8,128)(2,1)S(1)}, u32[]{:S(2)}, u32[]{:S(2)}) %collective-permute-start.14) | collective-permute-done | bytes 393248 | tf_op jit(solution)/shard_map/ppermute | solution.py:194
  202.1 1.0 copy-done.13
  204.2 1.6 all-gather.9.cloned.1.call-done.refs_1_
  205.7 1.2 slice.138
  207.6 2.8 collective-permute-done.13
  210.4 1.1 maximum_add_fusion.2
  213.5 0.7 concatenate.65.at_ref
  214.7 0.9 pad_add_fusion.refs_4_
  215.6 0.6 fusion.4
  216.2 0.6 fusion.3
  218.1 20.4 %shard_map.64 = (bf16[512,256]{1,0:T(8,128)(2,1)}, bf16[512,256]{1,0:T(8,128)(2,1)}) custom-call(s32[18]{0:T(128)} %concatenate.65.at_ref, bf16[4,1,3,256,1024]{4,3,2,1,0:T(8,128)(2,1)} %bitcast.93, bf16[4,3,3,256,256]{4,3,2,1,0:T(8,128)(2,1)} %all-gather.7.cloned.1.call-done.refs_1_, f32[3,7,256]{2,1,0:T(8,128)} %get-tuple-element.38.refs_2_, ...), custom_call_target="tpu_custom_call" | custom-call | flops 16508780544 | bytes 17563648 | tf_op jit(solution)/shard_map/pallas_call | solution.py:154
  238.5 1.2 slice.116
  240.4 7.8 %all-gather.11.cloned.1.call-done.refs_1_ = bf16[4,3,3,256,256]{4,3,2,1,0:T(8,128)(2,1)} async-done(((bf16[1,3,3,256,256]{4,3,2,1,0:T(8,128)(2,1)}), bf16[4,3,3,256,256]{4,3,2,1,0:T(8,128)(2,1)}) %all-gather.11.cloned.1.call-update) | async-done | bytes 4718608 | tf_op jit(solution)/shard_map/all_gather | solution.py:259
  248.2 1.2 slice.142
  250.1 4.4 %collective-permute-done.15 = bf16[2,3,256,256]{3,2,1,0:T(8,128)(2,1)S(1)} collective-permute-done((bf16[2,3,256,256]{3,2,1,0:T(8,128)(2,1)S(1)}, bf16[2,3,256,256]{3,2,1,0:T(8,128)(2,1)S(1)}, u32[]{:S(2)}, u32[]{:S(2)}) %collective-permute-start.15) | collective-permute-done | bytes 786464 | tf_op jit(solution)/shard_map/ppermute | solution.py:194
  254.4 1.1 maximum_add_fusion.3
  255.6 0.9 copy-done.14
  256.5 20.8 %shard_map.65 = (bf16[512,256]{1,0:T(8,128)(2,1)}, bf16[512,256]{1,0:T(8,128)(2,1)}) custom-call(s32[18]{0:T(128)} %concatenate.65.at_ref, bf16[4,1,3,256,1024]{4,3,2,1,0:T(8,128)(2,1)} %bitcast.94, bf16[4,3,3,256,256]{4,3,2,1,0:T(8,128)(2,1)} %all-gather.9.cloned.1.call-done.refs_1_, f32[3,7,256]{2,1,0:T(8,128)} %get-tuple-element.37.refs_2_, ...), custom_call_target="tpu_custom_call" | custom-call | flops 16508780544 | bytes 17563648 | tf_op jit(solution)/shard_map/pallas_call | solution.py:154
  277.4 2.2 collective-permute-start.17
  279.7 4.4 %collective-permute-done.17 = bf16[512,256]{1,0:T(8,128)(2,1)S(1)} collective-permute-done((bf16[512,256]{1,0:T(8,128)(2,1)}, bf16[512,256]{1,0:T(8,128)(2,1)S(1)}, u32[]{:S(2)}, u32[]{:S(2)}) %collective-permute-start.17) | collective-permute-done | bytes 262176 | tf_op jit(solution)/shard_map/ppermute | solution.py:194
  284.2 19.9 %shard_map.66 = (bf16[512,256]{1,0:T(8,128)(2,1)}, bf16[512,256]{1,0:T(8,128)(2,1)}) custom-call(s32[18]{0:T(128)} %concatenate.65.at_ref, bf16[4,1,3,256,1024]{4,3,2,1,0:T(8,128)(2,1)} %bitcast.95, bf16[4,3,3,256,256]{4,3,2,1,0:T(8,128)(2,1)} %all-gather.11.cloned.1.call-done.refs_1_, f32[3,7,256]{2,1,0:T(8,128)} %get-tuple-element.36.refs_2_, ...), custom_call_target="tpu_custom_call" | custom-call | flops 16508780544 | bytes 17563648 | tf_op jit(solution)/shard_map/pallas_call | solution.py:154
  304.1 2.1 collective-permute-start.18
  306.2 20.0 %shard_map.67 = (bf16[512,256]{1,0:T(8,128)(2,1)}, bf16[512,256]{1,0:T(8,128)(2,1)}) custom-call(s32[18]{0:T(128)} %concatenate.65.at_ref, bf16[4,1,3,256,1024]{4,3,2,1,0:T(8,128)(2,1)} %bitcast.96, bf16[4,3,3,256,256]{4,3,2,1,0:T(8,128)(2,1)} %all-gather.13.cloned.1.call-done.refs_1_, f32[3,7,256]{2,1,0:T(8,128)} %get-tuple-element.35.refs_2_, ...), custom_call_target="tpu_custom_call" | custom-call | flops 16508780544 | bytes 17563648 | tf_op jit(solution)/shard_map/pallas_call | solution.py:154
  326.5 0.8 copy-done.7
  327.3 5.7 %collective-permute-done.19 = bf16[512,256]{1,0:T(8,128)(2,1)S(1)} collective-permute-done((bf16[512,256]{1,0:T(8,128)(2,1)}, bf16[512,256]{1,0:T(8,128)(2,1)S(1)}, u32[]{:S(2)}, u32[]{:S(2)}) %collective-permute-start.19) | collective-permute-done | bytes 262176 | tf_op jit(solution)/shard_map/ppermute | solution.py:194
  333.1 1.5 pad_maximum_fusion
  (83 shorter events, 5.0 us)
Async XLA Ops:
  6.5 83.5 %all-gather.15.cloned.1.call-start = ((), (), s32[]{:S(2)}) async-start(), calls=%async_computation.4 | async-start | bytes 7864320 | tf_op jit(solution)/shard_map/all_gather | solution.py:259
  9.2 6.7 %copy-start.11 = (s32[16]{0:T(128)S(1)}, s32[16]{0:T(128)}, u32[]{:S(2)}) copy-start(s32[16]{0:T(128)} %param.11) | copy-start | bytes 196
  9.2 16.1 %copy-start.1 = (bf16[256,3,2048]{2,0,1:T(8,128)(2,1)S(1)}, bf16[256,3,2048]{2,0,1:T(8,128)(2,1)}, u32[]{:S(2)}) copy-start(bf16[256,3,2048]{2,0,1:T(8,128)(2,1)} %param.7) | copy-start | bytes 9437188
  9.2 155.8 %all-gather.7.cloned.1.call-start = ((), (), s32[]{:S(2)}) async-start(), calls=%async_computation | async-start | bytes 5898240 | tf_op jit(solution)/shard_map/all_gather | solution.py:259
  11.4 7.4 %collective-permute-start.5 = (bf16[144,2048]{1,0:T(8,128)(2,1)}, bf16[144,2048]{1,0:T(8,128)(2,1)}, u32[]{:S(2)}, u32[]{:S(2)}) collective-permute-start(bf16[144,2048]{1,0:T(8,128)(2,1)} %slice.93), channel_id=1, source_target_pairs={{0,2},{2,0},{4,6},{6,4},{8,10},{10,8},{12,14},{14,12},{16,18},{18,... | collective-permute-start | bytes 1769480 | tf_op jit(solution)/shard_map/ppermute | solution.py:194
  11.8 74.7 %collective-permute-start.4 = (bf16[512,2048]{1,0:T(8,128)(2,1)}, bf16[512,2048]{1,0:T(8,128)(2,1)}, u32[]{:S(2)}, u32[]{:S(2)}) collective-permute-start(bf16[512,2048]{1,0:T(8,128)(2,1)} %refs_5_.7), channel_id=1, source_target_pairs={{0,1},{1,0},{2,3},{3,2},{4,5},{5,4},{6,7},{7,6},{8,9},{9,8},{10,11... | collective-permute-start | bytes 6291464 | tf_op jit(solution)/shard_map/ppermute | solution.py:198
  14.3 73.9 %collective-permute-start.3 = (bf16[512,2048]{1,0:T(8,128)(2,1)}, bf16[512,2048]{1,0:T(8,128)(2,1)}, u32[]{:S(2)}, u32[]{:S(2)}) collective-permute-start(bf16[512,2048]{1,0:T(8,128)(2,1)} %refs_5_.7), channel_id=1, source_target_pairs={{0,8},{2,10},{4,12},{6,14},{8,0},{10,2},{12,4},{14,6},{16,24},{18,... | collective-permute-start | bytes 6291464 | tf_op jit(solution)/shard_map/ppermute | solution.py:194
  20.8 53.4 %collective-permute-start.6 = (bf16[144,2048]{1,0:T(8,128)(2,1)}, bf16[144,2048]{1,0:T(8,128)(2,1)}, u32[]{:S(2)}, u32[]{:S(2)}) collective-permute-start(bf16[144,2048]{1,0:T(8,128)(2,1)} %broadcast_select_fusion.3), channel_id=1, source_target_pairs={{0,4},{2,6},{4,8},{6,10},{8,12},{10,14},{12,16},{14,18},{16,20},{1... | collective-permute-start | bytes 1769480 | tf_op jit(solution)/shard_map/ppermute | solution.py:206
  25.3 4.1 %copy-start = (bf16[3,256,1024]{2,1,0:T(8,128)(2,1)S(1)}, bf16[3,256,1024]{2,1,0:T(8,128)(2,1)}, u32[]{:S(2)}) copy-start(bf16[3,256,1024]{2,1,0:T(8,128)(2,1)} %dynamic-slice_bitcast_fusion) | copy-start | bytes 4718596
  26.4 44.4 %collective-permute-start.7 = (bf16[3,256,256]{2,1,0:T(8,128)(2,1)S(1)}, bf16[3,256,256]{2,1,0:T(8,128)(2,1)S(1)}, u32[]{:S(2)}, u32[]{:S(2)}) collective-permute-start(bf16[3,256,256]{2,1,0:T(8,128)(2,1)S(1)} %get-tuple-element.26), channel_id=1, source_target_pairs={{0,8},{2,10},{4,12},{6,14},{8,0},{10,2},{12,4},{14,6},{16,24},{18,... | collective-permute-start | bytes 1179656 | tf_op jit(solution)/shard_map/ppermute | solution.py:194
  26.4 65.6 %collective-permute-start.2 = (bf16[3,256,256]{2,1,0:T(8,128)(2,1)}, bf16[3,256,256]{2,1,0:T(8,128)(2,1)S(1)}, u32[]{:S(2)}, u32[]{:S(2)}) collective-permute-start(bf16[3,256,256]{2,1,0:T(8,128)(2,1)} %get-tuple-element.27), channel_id=1, source_target_pairs={{0,24},{2,26},{4,28},{6,30},{8,16},{10,18},{12,20},{14,22},{16,8},... | collective-permute-start | bytes 1179656 | tf_op jit(solution)/shard_map/ppermute | solution.py:194
  70.7 26.8 %collective-permute-start = (bf16[3,256,256]{2,1,0:T(8,128)(2,1)}, bf16[3,256,256]{2,1,0:T(8,128)(2,1)S(1)}, u32[]{:S(2)}, u32[]{:S(2)}) collective-permute-start(bf16[3,256,256]{2,1,0:T(8,128)(2,1)} %get-tuple-element.27), channel_id=1, source_target_pairs={{0,8},{2,10},{4,12},{6,14},{8,0},{10,2},{12,4},{14,6},{16,24},{18,... | collective-permute-start | bytes 1179656 | tf_op jit(solution)/shard_map/ppermute | solution.py:194
  74.3 24.3 %collective-permute-start.1 = (bf16[3,256,256]{2,1,0:T(8,128)(2,1)S(1)}, bf16[3,256,256]{2,1,0:T(8,128)(2,1)}, u32[]{:S(2)}, u32[]{:S(2)}) collective-permute-start(bf16[3,256,256]{2,1,0:T(8,128)(2,1)S(1)} %get-tuple-element.34), channel_id=1, source_target_pairs={{0,16},{2,18},{4,20},{6,22},{8,24},{10,26},{12,28},{14,30},{16,0},... | collective-permute-start | bytes 1179656 | tf_op jit(solution)/shard_map/ppermute | solution.py:194
  100.8 104.9 %all-gather.9.cloned.1.call-start = ((), (), s32[]{:S(2)}) async-start(), calls=%async_computation.1 | async-start | bytes 5898240 | tf_op jit(solution)/shard_map/all_gather | solution.py:259
  100.9 46.6 %collective-permute-start.8 = (bf16[512,2048]{1,0:T(8,128)(2,1)}, bf16[512,2048]{1,0:T(8,128)(2,1)S(1)}, u32[]{:S(2)}, u32[]{:S(2)}) collective-permute-start(bf16[512,2048]{1,0:T(8,128)(2,1)} %collective-permute-done.3.refs_7_), channel_id=1, source_target_pairs={{0,1},{1,0},{2,3},{3,2},{4,5},{5,4},{6,7},{7,6},{8,9},{9,8},{10,11... | collective-permute-start | bytes 6291464 | tf_op jit(solution)/shard_map/ppermute | solution.py:198
  103.7 63.3 %collective-permute-start.11 = (bf16[2,3,256,256]{3,2,1,0:T(8,128)(2,1)}, bf16[2,3,256,256]{3,2,1,0:T(8,128)(2,1)S(1)}, u32[]{:S(2)}, u32[]{:S(2)}) collective-permute-start(bf16[2,3,256,256]{3,2,1,0:T(8,128)(2,1)} %maximum_add_fusion.4), channel_id=1, source_target_pairs={{0,16},{2,18},{4,20},{6,22},{8,24},{10,26},{12,28},{14,30},{16,0},... | collective-permute-start | bytes 2359304 | tf_op jit(solution)/shard_map/ppermute | solution.py:194
  103.8 40.5 %collective-permute-start.9 = (bf16[144,2048]{1,0:T(8,128)(2,1)S(1)}, bf16[144,2048]{1,0:T(8,128)(2,1)S(1)}, u32[]{:S(2)}, u32[]{:S(2)}) collective-permute-start(bf16[144,2048]{1,0:T(8,128)(2,1)S(1)} %broadcast_select_fusion.2), channel_id=1, source_target_pairs={{0,8},{2,10},{4,12},{6,14},{8,0},{10,2},{12,4},{14,6},{16,24},{18,... | collective-permute-start | bytes 1769480 | tf_op jit(solution)/shard_map/ppermute | solution.py:194
  106.6 36.4 %collective-permute-start.12 = (bf16[3,256,256]{2,1,0:T(8,128)(2,1)}, bf16[3,256,256]{2,1,0:T(8,128)(2,1)S(1)}, u32[]{:S(2)}, u32[]{:S(2)}) collective-permute-start(bf16[3,256,256]{2,1,0:T(8,128)(2,1)} %get-tuple-element.28), channel_id=1, source_target_pairs={{0,8},{2,10},{4,12},{6,14},{8,0},{10,2},{12,4},{14,6},{16,24},{18,... | collective-permute-start | bytes 1179656 | tf_op jit(solution)/shard_map/ppermute | solution.py:194
  144.3 23.9 %copy-start.3 = (bf16[144,2048]{1,0:T(8,128)(2,1)}, bf16[144,2048]{1,0:T(8,128)(2,1)S(1)}, u32[]{:S(2)}) copy-start(bf16[144,2048]{1,0:T(8,128)(2,1)S(1)} %collective-permute-done.9) | copy-start | bytes 1769476
  147.4 1.3 copy-start.12
  168.1 80.1 %all-gather.11.cloned.1.call-start = ((), (), s32[]{:S(2)}) async-start(), calls=%async_computation.2 | async-start | bytes 5898240 | tf_op jit(solution)/shard_map/all_gather | solution.py:259
  169.4 42.1 %copy-start.2 = (bf16[2,144,2048]{2,1,0:T(8,128)(2,1)}, bf16[2,144,2048]{2,1,0:T(8,128)(2,1)S(1)}, u32[]{:S(2)}) copy-start(bf16[2,144,2048]{2,1,0:T(8,128)(2,1)S(1)} %pad_maximum_fusion.1.refs_9_) | copy-start | bytes 3538948
  169.4 6.0 %copy-start.4 = (bf16[3,256,256]{2,1,0:T(8,128)(2,1)S(1)}, bf16[3,256,256]{2,1,0:T(8,128)(2,1)}, u32[]{:S(2)}) copy-start(bf16[3,256,256]{2,1,0:T(8,128)(2,1)} %get-tuple-element.25) | copy-start | bytes 1179652
  169.4 32.7 %collective-permute-start.10 = (bf16[2,144,2048]{2,1,0:T(8,128)(2,1)S(1)}, bf16[2,144,2048]{2,1,0:T(8,128)(2,1)S(1)}, u32[]{:S(2)}, u32[]{:S(2)}) collective-permute-start(bf16[2,144,2048]{2,1,0:T(8,128)(2,1)S(1)} %pad_maximum_fusion.1.refs_9_), channel_id=1, source_target_pairs={{0,1},{1,0},{2,3},{3,2},{4,5},{5,4},{6,7},{7,6},{8,9},{9,8},{10,11... | collective-permute-start | bytes 3538952 | tf_op jit(solution)/shard_map/ppermute | solution.py:198
  173.0 37.4 %collective-permute-start.13 = (bf16[2,3,256,256]{3,2,1,0:T(8,128)(2,1)}, bf16[2,3,256,256]{3,2,1,0:T(8,128)(2,1)S(1)}, u32[]{:S(2)}, u32[]{:S(2)}) collective-permute-start(bf16[2,3,256,256]{3,2,1,0:T(8,128)(2,1)} %maximum_add_fusion.5), channel_id=1, source_target_pairs={{0,16},{2,18},{4,20},{6,22},{8,24},{10,26},{12,28},{14,30},{16,0},... | collective-permute-start | bytes 2359304 | tf_op jit(solution)/shard_map/ppermute | solution.py:194
  175.4 25.6 %collective-permute-start.14 = (bf16[3,256,256]{2,1,0:T(8,128)(2,1)S(1)}, bf16[3,256,256]{2,1,0:T(8,128)(2,1)S(1)}, u32[]{:S(2)}, u32[]{:S(2)}) collective-permute-start(bf16[3,256,256]{2,1,0:T(8,128)(2,1)S(1)} %copy-done.4), channel_id=1, source_target_pairs={{0,8},{2,10},{4,12},{6,14},{8,0},{10,2},{12,4},{14,6},{16,24},{18,... | collective-permute-start | bytes 1179656 | tf_op jit(solution)/shard_map/ppermute | solution.py:194
  202.1 1.0 copy-start.13
  211.5 1.5 copy-start.15
  211.5 1.7 copy-start.9
  211.5 2.8 copy-start.10
  211.5 94.7 %all-gather.13.cloned.1.call-start = ((), (), s32[]{:S(2)}) async-start(), calls=%async_computation.3 | async-start | bytes 5898240 | tf_op jit(solution)/shard_map/all_gather | solution.py:259
  218.0 36.4 %collective-permute-start.15 = (bf16[2,3,256,256]{3,2,1,0:T(8,128)(2,1)S(1)}, bf16[2,3,256,256]{3,2,1,0:T(8,128)(2,1)S(1)}, u32[]{:S(2)}, u32[]{:S(2)}) collective-permute-start(bf16[2,3,256,256]{3,2,1,0:T(8,128)(2,1)S(1)} %maximum_add_fusion.6), channel_id=1, source_target_pairs={{0,16},{2,18},{4,20},{6,22},{8,24},{10,26},{12,28},{14,30},{16,0},... | collective-permute-start | bytes 2359304 | tf_op jit(solution)/shard_map/ppermute | solution.py:194
  255.6 0.9 copy-start.14
  256.5 23.1 %collective-permute-start.16 = (bf16[512,256]{1,0:T(8,128)(2,1)S(1)}, bf16[512,256]{1,0:T(8,128)(2,1)S(1)}, u32[]{:S(2)}, u32[]{:S(2)}) collective-permute-start(bf16[512,256]{1,0:T(8,128)(2,1)S(1)} %copy-done.14), channel_id=1, source_target_pairs={{0,8},{2,10},{4,12},{6,14},{8,0},{10,2},{12,4},{14,6},{16,24},{18,... | collective-permute-start | bytes 786440 | tf_op jit(solution)/shard_map/ppermute | solution.py:194
  256.5 23.1 %copy-start.5 = (bf16[512,256]{1,0:T(8,128)(2,1)S(1)}, bf16[512,256]{1,0:T(8,128)(2,1)}, u32[]{:S(2)}) copy-start(bf16[512,256]{1,0:T(8,128)(2,1)} %get-tuple-element.13) | copy-start | bytes 786436
  277.4 2.3 copy-start.8
  277.4 6.8 %collective-permute-start.17 = (bf16[512,256]{1,0:T(8,128)(2,1)}, bf16[512,256]{1,0:T(8,128)(2,1)S(1)}, u32[]{:S(2)}, u32[]{:S(2)}) collective-permute-start(bf16[512,256]{1,0:T(8,128)(2,1)} %get-tuple-element.18), channel_id=1, source_target_pairs={{0,8},{2,10},{4,12},{6,14},{8,0},{10,2},{12,4},{14,6},{16,24},{18,... | collective-permute-start | bytes 786440 | tf_op jit(solution)/shard_map/ppermute | solution.py:194
  304.1 22.4 %collective-permute-start.18 = (bf16[512,256]{1,0:T(8,128)(2,1)}, bf16[512,256]{1,0:T(8,128)(2,1)S(1)}, u32[]{:S(2)}, u32[]{:S(2)}) collective-permute-start(bf16[512,256]{1,0:T(8,128)(2,1)} %get-tuple-element.19), channel_id=1, source_target_pairs={{0,8},{2,10},{4,12},{6,14},{8,0},{10,2},{12,4},{14,6},{16,24},{18,... | collective-permute-start | bytes 786440 | tf_op jit(solution)/shard_map/ppermute | solution.py:194
  306.2 20.2 %copy-start.6 = (bf16[512,256]{1,0:T(8,128)(2,1)S(1)}, bf16[512,256]{1,0:T(8,128)(2,1)}, u32[]{:S(2)}) copy-start(bf16[512,256]{1,0:T(8,128)(2,1)} %get-tuple-element.15) | copy-start | bytes 786436
  326.3 1.0 copy-start.7
  326.3 6.6 %collective-permute-start.19 = (bf16[512,256]{1,0:T(8,128)(2,1)}, bf16[512,256]{1,0:T(8,128)(2,1)S(1)}, u32[]{:S(2)}, u32[]{:S(2)}) collective-permute-start(bf16[512,256]{1,0:T(8,128)(2,1)} %get-tuple-element.20), channel_id=1, source_target_pairs={{0,8},{2,10},{4,12},{6,14},{8,0},{10,2},{12,4},{14,6},{16,24},{18,... | collective-permute-start | bytes 786440 | tf_op jit(solution)/shard_map/ppermute | solution.py:194
Sparse Core Ops, SparseCore 0:
  9.4 57.9 all-gather.14
  100.9 64.0 all-gather.6
  168.3 37.4 all-gather.8
  211.7 36.5 all-gather.10
  255.7 35.8 all-gather.12

commit v6 on v5

--- a/solution.py
+++ b/solution.py
@@ -22,9 +22,9 @@
 
 def block_kernel(runs, halves, parts, at_ref, *refs):
     w_refs, (sw_ref, fr_ref, pos_ref), refs = refs[:parts], refs[parts : parts + 3], refs[parts + 3 :]
-    row_refs, halo_refs = refs[: runs * halves], refs[runs * halves : (runs + 1) * halves]
-    out_refs = refs[(runs + 1) * halves : (runs + 1) * halves + runs]
-    x_ref, sems, proj, mix, band, done = refs[(runs + 1) * halves + runs :]
+    row_refs, halo_refs = refs[: runs * halves], refs[runs * halves : 2 * runs * halves]
+    out_refs = refs[2 * runs * halves : 2 * runs * halves + runs]
+    x_ref, sems, proj, mix, band, done = refs[2 * runs * halves + runs :]
     total, features = x_ref.shape[1:]
     rows, chans = out_refs[0].shape
     halo = total - rows
@@ -42,7 +42,7 @@
             piece = features // halves
             where = pl.ds(pl.multiple_of(at_ref[len(units) + h], piece), piece)
             yield pltpu.make_async_copy(
-                halo_refs[h].at[r], x_ref.at[r, pl.ds(0, halo), where], sems.at[r, 2 * h]
+                halo_refs[r * halves + h], x_ref.at[r, pl.ds(0, halo), where], sems.at[r, 2 * h]
             )
             yield pltpu.make_async_copy(
                 row_refs[r * halves + h], x_ref.at[r, pl.ds(halo, rows), where], sems.at[r, 2 * h + 1]
@@ -139,9 +139,9 @@
 
 
 def block(at, rows, halos, weights, sw, fr, pos, span, chans):
-    runs, halves = len(rows), len(halos)
+    runs, halves = len(rows), len(rows[0])
     row_count, features = rows[0][0].shape[0], rows[0][0].shape[1] * halves
-    total = halos[0].shape[1] + row_count
+    total = halos[0][0].shape[0] + row_count
     taps = sw.shape[1]
     tile = CHAN_TILE if all(n % CHAN_TILE == 0 for n in [chans] + [first for first, _ in weights]) else LANES
     per_tile = tile * fr.shape[0] // chans
@@ -162,7 +162,7 @@
                 pl.BlockSpec((per_tile, 2 * span), lambda j, i, at: (j, 0)),
                 pl.BlockSpec((1, total, LANES), lambda j, i, at: (i, 0, 0)),
             ]
-            + [anywhere] * (runs * halves + halves),
+            + [anywhere] * (2 * runs * halves),
             out_specs=[pl.BlockSpec((row_count, tile), lambda j, i, at: (0, j))] * runs,
             scratch_shapes=[
                 pltpu.VMEM((runs, total, features), jnp.bfloat16),
@@ -180,7 +180,7 @@
             bytes_accessed=2 * (runs * total * features + 3 * features * chans + runs * row_count * chans),
             transcendentals=0,
         ),
-    )(at, *[w for _, w in weights], sw, fr, pos, *[half for run in rows for half in run], *halos)
+    )(at, *[w for _, w in weights], sw, fr, pos, *[half for run in rows + halos for half in run])
 
 
 def parameters(short_weight, medium_filter):
@@ -235,7 +235,7 @@
         halo = lax.all_gather(halo, "chan", axis=1, tiled=True)
         rows = lax.all_gather(tokens, "chan", axis=1, tiled=True)
         at = jnp.concatenate([order * depth, jnp.zeros(1, jnp.int32)])
-        return block(at, [[rows]], [halo[None]], [(0, weight[:, None])], sw, fr, positions(me)[None], span, chans)[0]
+        return block(at, [[rows]], [[halo]], [(0, weight[:, None])], sw, fr, positions(me)[None], span, chans)[0]
 
     side = lax.axis_index("chan")
     kind = (me >> 2) & 1
@@ -244,26 +244,29 @@
     widths = WIDTHS if sum(WIDTHS) == half else [half]
     begins = [sum(widths[:c]) for c in range(len(widths))]
 
-    halo = rows_before(tokens, stretch_at(me), reach)
-    peer_rows = flip(tokens, 4)
-    rows_other = across(tokens)
-    peer_rows_other = across(peer_rows)
-    peer_halo = flip(halo, 4)
-    halos = jnp.stack([halo, peer_halo])
-    halos_other = across(halos)
-    after = {0: [peer_rows, rows_other, halo], 1: [peer_halo, peer_rows_other], 2: [halos_other]}
-
     planes = [[4 * z + q for q in range(4)] for z in range(devices // 4)]
 
     def spread(array):
         return lax.all_gather(array, "stretch", axis=0, tiled=False, axis_index_groups=planes)
 
     own = lax.dynamic_slice_in_dim(local, own_begin, half, 2)
-    peers = [
-        flip(lax.dynamic_slice_in_dim(local, other_begin + begin, width, 2), 4) for begin, width in zip(begins, widths)
-    ]
-    for c, peer in enumerate(peers[1:]):
-        after[c] = after.get(c, []) + [peer]
+    other = lax.dynamic_slice_in_dim(local, other_begin, half, 2)
+    peers = flip(other, 4)
+    firsts = [peers[:, :, : widths[0]], flip(own[:, :, : widths[0]], 8), flip(other[:, :, : widths[0]], 12)]
+
+    rows_other = across(tokens)
+    peer_rows = flip(tokens, 4)
+    peer_rows_other = across(peer_rows)
+    halo = rows_before(tokens, stretch_at(me), reach)
+    halo_other = across(halo)
+    peer_halo = flip(halo, 4)
+    peer_halo_other = across(peer_halo)
+    after = {
+        0: [rows_other, halo],
+        1: [peer_rows, halo_other],
+        2: [peer_rows_other, peer_halo_other],
+    }
+
     pos = jnp.stack([positions(me), positions(me ^ 4)])
     at = jnp.concatenate(
         [
@@ -278,11 +281,11 @@
     gathered, stack = [spread(own[None])], None
     mine, theirs = [], []
     for c, (begin, width) in enumerate(zip(begins, widths)):
-        same, peer = own[:, :, begin : begin + width], peers[c]
         if c == 0:
-            other = lax.dynamic_slice_in_dim(local, other_begin, width, 2)
-            stack = jnp.stack([peer, flip(same, 8), flip(other, 12)])
+            stack = jnp.stack(firsts)
         else:
+            same = own[:, :, begin : begin + width]
+            peer = peers[:, :, begin : begin + width]
             pair = jnp.stack([same, peer]) + nothing(stack).astype(jnp.bfloat16)
             stack = jnp.concatenate([peer[None], flip(pair, 8)])
         waits = sum(nothing(array) for array in after.get(c, []) + [gathered[-1]])
@@ -293,7 +296,7 @@
         out, peer_out = block(
             at,
             [[tokens, rows_other], [peer_rows, peer_rows_other]],
-            [halos, halos_other],
+            [[halo, halo_other], [peer_halo, peer_halo_other]],
             [(begin, gathered[0]), (0, gathered[c + 1])],
             own_sw[:, :, begin : begin + width],
             own_fr[first_group : first_group + groups],
@@ -303,7 +306,7 @@
         )
         mine.append(out)
         theirs.append(flip(peer_out, 4))
-        after[c + 3] = [out]
+        after[c + 3] = after.get(c + 3, []) + [out]
     mine, theirs = jnp.concatenate(mine, axis=1), jnp.concatenate(theirs, axis=1)
     even = kind == 0
     return jnp.concatenate([jnp.where(even, mine, theirs), jnp.where(even, theirs, mine)], axis=1)

time: 342 us -> 358 us (1.047)
  starting transfers between devices: 38.1 us -> 75.1 us
  waiting for transfers between devices: 152 us -> 130 us
  local copies, waits for them, and re-layouts: 26.3 us -> 30.2 us
    ppermute x16 -> x13, waiting for transfers between devices: 126 us -> 67.8 us  [flip(): lax.ppermute(array, 'stretch', [(i, i ^ bit) for i in range(lax.axis_size...]
    ppermute x16 -> x13, starting transfers between devices: 28.8 us -> 66.5 us  [flip(): lax.ppermute(array, 'stretch', [(i, i ^ bit) for i in range(lax.axis_size...]
    ppermute x3 -> x4, waiting for transfers between devices: 1.94 us -> 33.9 us  [across(): return lax.ppermute(array, 'chan', [(0, 1), (1, 0)])]
    ppermute x1, waiting for transfers between devices: 0.01 us -> 21.4 us  [rows_before(): before = lax.ppermute(jnp.where(second, tail, sibling), 'stretch', pairs)]
    all_gather x5, waiting for transfers between devices: 24.6 us -> 7.12 us  [spread(): lax.all_gather(array, 'stretch', axis=0, tiled=False, axis_index_groups=p...]
    slice x17 -> x14, local copies, waits for them, and re-layouts: 13.6 us -> 13.1 us  [nothing(): array[(0,) * array.ndim].astype(jnp.float32) * 0.0]
  transfers between devices with their start and end apart: 25 -> 23, of which waited for: 13 -> 10; matrix products, arithmetic and copies ran while one was open for 8% -> 8% of each run, Pallas kernels for 24% -> 23%
where the time goes in v6:
time: 358 us; the launch traced here: 356 us
  waiting for transfers between devices  130 us (36%)
  Pallas kernels  80.2 us (22%)
  starting transfers between devices  75.1 us (21%)
  local copies, waits for them, and re-layouts  30.2 us (8%)
  between operations  26 us (7%)
  other arithmetic  14.2 us (4%)
    pallas_call x4, Pallas kernels, block(): pl.pallas_call(functools.partial(block_kernel, runs, halves, len(weights)...  80.2 us
    ppermute x13, waiting for transfers between devices, flip(): lax.ppermute(array, 'stretch', [(i, i ^ bit) for i in range(lax.axis_size...  67.8 us
    ppermute x13, starting transfers between devices, flip(): lax.ppermute(array, 'stretch', [(i, i ^ bit) for i in range(lax.axis_size...  66.5 us
    ppermute x4, waiting for transfers between devices, across(): return lax.ppermute(array, 'chan', [(0, 1), (1, 0)])  33.9 us
    ppermute x1, waiting for transfers between devices, rows_before(): before = lax.ppermute(jnp.where(second, tail, sibling), 'stretch', pairs)  21.4 us
    slice x14, local copies, waits for them, and re-layouts, nothing(): array[(0,) * array.ndim].astype(jnp.float32) * 0.0  13.1 us
  transfers between devices with their start and end apart: 23, of which 10 were waited for; matrix products, arithmetic and copies ran while one was open for 8% of the time, Pallas kernels for 23%

profile of v6, /device:TPU:0, one launch (start us, length us, event | category | flops | bytes accessed | tf_op | source)
XLA Modules:
  0.0 356.0 jit_solution(17793515305767864493)
XLA Ops:
  6.5 3.5 dynamic-slice_bitcast_fusion
  10.1 2.0 slice.100
  12.5 2.5 collective-permute-start.3
  15.1 1.6 collective-permute-start
  16.6 0.7 fusion.2
  19.2 1.5 broadcast_select_fusion.3
  20.7 3.2 collective-permute-start.5
  23.9 0.8 slice.130
  24.7 2.7 collective-permute-start.2
  27.4 1.1 slice_bitcast_fusion
  28.5 21.4 %collective-permute-done.5 = bf16[144,2048]{1,0:T(8,128)(2,1)S(1)} collective-permute-done((bf16[144,2048]{1,0:T(8,128)(2,1)S(1)}, bf16[144,2048]{1,0:T(8,128)(2,1)S(1)}, u32[]{:S(2)}, u32[]{:S(2)}) %collective-permute-start.5) | collective-permute-done | bytes 589856 | tf_op jit(solution)/shard_map/ppermute | solution.py:206
  49.9 0.9 broadcast_select_fusion.2.refs_9_
  50.8 1.2 slice.132
  52.6 15.9 %collective-permute-done = bf16[3,256,1024]{2,1,0:T(8,128)(2,1)} collective-permute-done((bf16[3,256,1024]{2,1,0:T(8,128)(2,1)S(1)}, bf16[3,256,1024]{2,1,0:T(8,128)(2,1)}, u32[]{:S(2)}, u32[]{:S(2)}) %collective-permute-start) | collective-permute-done | bytes 1572896 | tf_op jit(solution)/shard_map/ppermute | solution.py:194
  68.5 2.5 slice_bitcast_fusion.4
  71.0 1.2 slice.131
  73.0 1.2 slice.133
  74.9 2.3 maximum_add_fusion
  77.3 1.8 collective-permute-start.6
  79.0 1.2 slice.167
  81.0 1.0 maximum_add_fusion.4
  82.0 19.8 %collective-permute-start.11 = (bf16[2,3,256,256]{3,2,1,0:T(8,128)(2,1)}, bf16[2,3,256,256]{3,2,1,0:T(8,128)(2,1)}, u32[]{:S(2)}, u32[]{:S(2)}) collective-permute-start(bf16[2,3,256,256]{3,2,1,0:T(8,128)(2,1)} %maximum_add_fusion.4), channel_id=1, source_target_pairs={{0,16},{2,18},{4,20},{6,22},{8,24},{10,26},{12,28},{14,30},{16,0},... | collective-permute-start | bytes 2359304 | tf_op jit(solution)/shard_map/ppermute | solution.py:194
  101.7 0.5 collective-permute-start.8
  102.2 12.7 %collective-permute-done.8.refs_10_ = bf16[144,2048]{1,0:T(8,128)(2,1)S(1)} collective-permute-done((bf16[144,2048]{1,0:T(8,128)(2,1)}, bf16[144,2048]{1,0:T(8,128)(2,1)S(1)}, u32[]{:S(2)}, u32[]{:S(2)}) %collective-permute-start.8) | collective-permute-done | bytes 589856 | tf_op jit(solution)/shard_map/ppermute | solution.py:198
  115.0 0.5 slice.139
  116.2 25.6 %collective-permute-done.6.refs_7_ = bf16[512,2048]{1,0:T(8,128)(2,1)S(1)} collective-permute-done((bf16[512,2048]{1,0:T(8,128)(2,1)}, bf16[512,2048]{1,0:T(8,128)(2,1)S(1)}, u32[]{:S(2)}, u32[]{:S(2)}) %collective-permute-start.6) | collective-permute-done | bytes 2097184 | tf_op jit(solution)/shard_map/ppermute | solution.py:194
  141.8 1.3 copy-done.8
  143.1 0.6 slice.138
  144.4 1.3 slice.140
  146.3 2.3 maximum_add_fusion.1
  148.7 0.7 collective-permute-start.7
  149.4 13.7 %collective-permute-start.9 = (bf16[144,2048]{1,0:T(8,128)(2,1)}, bf16[144,2048]{1,0:T(8,128)(2,1)S(1)}, u32[]{:S(2)}, u32[]{:S(2)}) collective-permute-start(bf16[144,2048]{1,0:T(8,128)(2,1)} %broadcast_select_fusion.2.refs_9_), channel_id=1, source_target_pairs={{0,8},{2,10},{4,12},{6,14},{8,0},{10,2},{12,4},{14,6},{16,24},{18,... | collective-permute-start | bytes 1769480 | tf_op jit(solution)/shard_map/ppermute | solution.py:194
  163.1 0.6 slice.170
  164.4 6.2 %collective-permute-start.12 = (bf16[2,3,256,256]{3,2,1,0:T(8,128)(2,1)S(1)}, bf16[2,3,256,256]{3,2,1,0:T(8,128)(2,1)S(1)}, u32[]{:S(2)}, u32[]{:S(2)}) collective-permute-start(bf16[2,3,256,256]{3,2,1,0:T(8,128)(2,1)S(1)} %maximum_add_fusion.5), channel_id=1, source_target_pairs={{0,16},{2,18},{4,20},{6,22},{8,24},{10,26},{12,28},{14,30},{16,0},... | collective-permute-start | bytes 2359304 | tf_op jit(solution)/shard_map/ppermute | solution.py:194
  170.6 14.8 %collective-permute-done.9.refs_11_ = bf16[144,2048]{1,0:T(8,128)(2,1)S(1)} collective-permute-done((bf16[144,2048]{1,0:T(8,128)(2,1)}, bf16[144,2048]{1,0:T(8,128)(2,1)S(1)}, u32[]{:S(2)}, u32[]{:S(2)}) %collective-permute-start.9) | collective-permute-done | bytes 589856 | tf_op jit(solution)/shard_map/ppermute | solution.py:194
  185.5 1.5 collective-permute-start.10
  187.0 21.2 %collective-permute-done.10.refs_12_ = bf16[144,2048]{1,0:T(8,128)(2,1)S(1)} collective-permute-done((bf16[144,2048]{1,0:T(8,128)(2,1)S(1)}, bf16[144,2048]{1,0:T(8,128)(2,1)S(1)}, u32[]{:S(2)}, u32[]{:S(2)}) %collective-permute-start.10) | collective-permute-done | bytes 589856 | tf_op jit(solution)/shard_map/ppermute | solution.py:198
  208.1 0.5 slice.146
  209.3 1.3 copy-done.9
  211.7 1.3 slice.147
  213.7 1.2 maximum_add_fusion.2
  216.8 0.7 concatenate.65.at_ref
  218.0 0.9 pad_add_fusion.refs_4_
  218.9 0.6 fusion.4
  219.5 0.6 fusion.3
  220.2 0.6 slice.172
  221.5 16.1 %collective-permute-start.13 = (bf16[2,3,256,256]{3,2,1,0:T(8,128)(2,1)S(1)}, bf16[2,3,256,256]{3,2,1,0:T(8,128)(2,1)S(1)}, u32[]{:S(2)}, u32[]{:S(2)}) collective-permute-start(bf16[2,3,256,256]{3,2,1,0:T(8,128)(2,1)S(1)} %maximum_add_fusion.6), channel_id=1, source_target_pairs={{0,16},{2,18},{4,20},{6,22},{8,24},{10,26},{12,28},{14,30},{16,0},... | collective-permute-start | bytes 2359304 | tf_op jit(solution)/shard_map/ppermute | solution.py:194
  237.7 19.7 %shard_map.64 = (bf16[512,256]{1,0:T(8,128)(2,1)}, bf16[512,256]{1,0:T(8,128)(2,1)}) custom-call(s32[18]{0:T(128)} %concatenate.65.at_ref, bf16[4,1,3,256,1024]{4,3,2,1,0:T(8,128)(2,1)} %bitcast.77, bf16[4,3,3,256,256]{4,3,2,1,0:T(8,128)(2,1)} %all-gather.7.cloned.1.call-done.refs_1_, f32[3,7,256]{2,1,0:T(8,128)} %get-tuple-element.44.refs_2_, ...), custom_call_target="tpu_custom_call" | custom-call | flops 16508780544 | bytes 17563648 | tf_op jit(solution)/shard_map/pallas_call | solution.py:154
  257.4 1.2 slice.124
  259.2 7.1 %all-gather.11.cloned.1.call-done.refs_1_ = bf16[4,3,3,256,256]{4,3,2,1,0:T(8,128)(2,1)} async-done(((bf16[1,3,3,256,256]{4,3,2,1,0:T(8,128)(2,1)}), bf16[4,3,3,256,256]{4,3,2,1,0:T(8,128)(2,1)}) %all-gather.11.cloned.1.call-update) | async-done | bytes 4718608 | tf_op jit(solution)/shard_map/all_gather | solution.py:250
  266.2 1.3 slice.152
  268.2 0.5 collective-permute-done.13
  268.7 1.2 maximum_add_fusion.3
  270.0 1.0 collective-permute-start.14
  271.0 20.6 %shard_map.65 = (bf16[512,256]{1,0:T(8,128)(2,1)}, bf16[512,256]{1,0:T(8,128)(2,1)}) custom-call(s32[18]{0:T(128)} %concatenate.65.at_ref, bf16[4,1,3,256,1024]{4,3,2,1,0:T(8,128)(2,1)} %bitcast.78, bf16[4,3,3,256,256]{4,3,2,1,0:T(8,128)(2,1)} %all-gather.9.cloned.1.call-done.refs_1_, f32[3,7,256]{2,1,0:T(8,128)} %get-tuple-element.43.refs_2_, ...), custom_call_target="tpu_custom_call" | custom-call | flops 16508780544 | bytes 17563648 | tf_op jit(solution)/shard_map/pallas_call | solution.py:154
  291.6 1.0 collective-permute-start.15
  292.7 1.0 constant_dynamic-update-slice_fusion.2
  293.7 6.3 %collective-permute-done.15 = bf16[512,256]{1,0:T(8,128)(2,1)S(1)} collective-permute-done((bf16[512,256]{1,0:T(8,128)(2,1)}, bf16[512,256]{1,0:T(8,128)(2,1)S(1)}, u32[]{:S(2)}, u32[]{:S(2)}) %collective-permute-start.15) | collective-permute-done | bytes 262176 | tf_op jit(solution)/shard_map/ppermute | solution.py:194
  300.1 19.9 %shard_map.66 = (bf16[512,256]{1,0:T(8,128)(2,1)}, bf16[512,256]{1,0:T(8,128)(2,1)}) custom-call(s32[18]{0:T(128)} %concatenate.65.at_ref, bf16[4,1,3,256,1024]{4,3,2,1,0:T(8,128)(2,1)} %bitcast.79, bf16[4,3,3,256,256]{4,3,2,1,0:T(8,128)(2,1)} %all-gather.11.cloned.1.call-done.refs_1_, f32[3,7,256]{2,1,0:T(8,128)} %get-tuple-element.42.refs_2_, ...), custom_call_target="tpu_custom_call" | custom-call | flops 16508780544 | bytes 17563648 | tf_op jit(solution)/shard_map/pallas_call | solution.py:154
  320.4 20.1 %shard_map.67 = (bf16[512,256]{1,0:T(8,128)(2,1)}, bf16[512,256]{1,0:T(8,128)(2,1)}) custom-call(s32[18]{0:T(128)} %concatenate.65.at_ref, bf16[4,1,3,256,1024]{4,3,2,1,0:T(8,128)(2,1)} %bitcast.80, bf16[4,3,3,256,256]{4,3,2,1,0:T(8,128)(2,1)} %all-gather.13.cloned.1.call-done.refs_1_, f32[3,7,256]{2,1,0:T(8,128)} %get-tuple-element.41.refs_2_, ...), custom_call_target="tpu_custom_call" | custom-call | flops 16508780544 | bytes 17563648 | tf_op jit(solution)/shard_map/pallas_call | solution.py:154
  340.4 1.7 collective-permute-start.17
  342.2 1.0 constant_dynamic-update-slice_fusion
  343.2 4.6 %collective-permute-done.17 = bf16[512,256]{1,0:T(8,128)(2,1)S(1)} collective-permute-done((bf16[512,256]{1,0:T(8,128)(2,1)}, bf16[512,256]{1,0:T(8,128)(2,1)S(1)}, u32[]{:S(2)}, u32[]{:S(2)}) %collective-permute-start.17) | collective-permute-done | bytes 262176 | tf_op jit(solution)/shard_map/ppermute | solution.py:194
  348.0 1.5 pad_maximum_fusion
  (74 shorter events, 3.1 us)
Async XLA Ops:
  6.5 66.5 %all-gather.15.cloned.1.call-start = ((), (), s32[]{:S(2)}) async-start(), calls=%async_computation.4 | async-start | bytes 7864320 | tf_op jit(solution)/shard_map/all_gather | solution.py:250
  10.0 6.6 %copy-start.7 = (s32[16]{0:T(128)S(1)}, s32[16]{0:T(128)}, u32[]{:S(2)}) copy-start(s32[16]{0:T(128)} %param.11) | copy-start | bytes 196
  10.1 134.3 %all-gather.7.cloned.1.call-start = ((), (), s32[]{:S(2)}) async-start(), calls=%async_computation | async-start | bytes 5898240 | tf_op jit(solution)/shard_map/all_gather | solution.py:250
  12.1 15.3 %copy-start = (bf16[3,256,1024]{2,1,0:T(8,128)(2,1)S(1)}, bf16[3,256,1024]{2,1,0:T(8,128)(2,1)}, u32[]{:S(2)}) copy-start(bf16[3,256,1024]{2,1,0:T(8,128)(2,1)} %get-tuple-element.26) | copy-start | bytes 4718596
  12.1 7.1 %collective-permute-start.4 = (bf16[144,2048]{1,0:T(8,128)(2,1)}, bf16[144,2048]{1,0:T(8,128)(2,1)}, u32[]{:S(2)}, u32[]{:S(2)}) collective-permute-start(bf16[144,2048]{1,0:T(8,128)(2,1)} %slice.100), channel_id=1, source_target_pairs={{0,2},{2,0},{4,6},{6,4},{8,10},{10,8},{12,14},{14,12},{16,18},{18,... | collective-permute-start | bytes 1769480 | tf_op jit(solution)/shard_map/ppermute | solution.py:194
  12.5 58.5 %collective-permute-start.3 = (bf16[512,2048]{1,0:T(8,128)(2,1)}, bf16[512,2048]{1,0:T(8,128)(2,1)}, u32[]{:S(2)}, u32[]{:S(2)}) collective-permute-start(bf16[512,2048]{1,0:T(8,128)(2,1)} %refs_5_.7), channel_id=1, source_target_pairs={{0,1},{1,0},{2,3},{3,2},{4,5},{5,4},{6,7},{7,6},{8,9},{9,8},{10,11... | collective-permute-start | bytes 6291464 | tf_op jit(solution)/shard_map/ppermute | solution.py:198
  15.1 53.5 %collective-permute-start = (bf16[3,256,1024]{2,1,0:T(8,128)(2,1)S(1)}, bf16[3,256,1024]{2,1,0:T(8,128)(2,1)}, u32[]{:S(2)}, u32[]{:S(2)}) collective-permute-start(bf16[3,256,1024]{2,1,0:T(8,128)(2,1)S(1)} %get-tuple-element.25), channel_id=1, source_target_pairs={{0,8},{2,10},{4,12},{6,14},{8,0},{10,2},{12,4},{14,6},{16,24},{18,... | collective-permute-start | bytes 4718600 | tf_op jit(solution)/shard_map/ppermute | solution.py:194
  20.7 29.2 %collective-permute-start.5 = (bf16[144,2048]{1,0:T(8,128)(2,1)S(1)}, bf16[144,2048]{1,0:T(8,128)(2,1)S(1)}, u32[]{:S(2)}, u32[]{:S(2)}) collective-permute-start(bf16[144,2048]{1,0:T(8,128)(2,1)S(1)} %broadcast_select_fusion.3), channel_id=1, source_target_pairs={{0,4},{2,6},{4,8},{6,10},{8,12},{10,14},{12,16},{14,18},{16,20},{1... | collective-permute-start | bytes 1769480 | tf_op jit(solution)/shard_map/ppermute | solution.py:206
  24.7 50.1 %collective-permute-start.2 = (bf16[3,256,256]{2,1,0:T(8,128)(2,1)}, bf16[3,256,256]{2,1,0:T(8,128)(2,1)}, u32[]{:S(2)}, u32[]{:S(2)}) collective-permute-start(bf16[3,256,256]{2,1,0:T(8,128)(2,1)} %slice.130), channel_id=1, source_target_pairs={{0,24},{2,26},{4,28},{6,30},{8,16},{10,18},{12,20},{14,22},{16,8},... | collective-permute-start | bytes 1179656 | tf_op jit(solution)/shard_map/ppermute | solution.py:194
  28.5 46.4 %collective-permute-start.1 = (bf16[3,256,256]{2,1,0:T(8,128)(2,1)}, bf16[3,256,256]{2,1,0:T(8,128)(2,1)}, u32[]{:S(2)}, u32[]{:S(2)}) collective-permute-start(bf16[3,256,256]{2,1,0:T(8,128)(2,1)} %get-tuple-element.40), channel_id=1, source_target_pairs={{0,16},{2,18},{4,20},{6,22},{8,24},{10,26},{12,28},{14,30},{16,0},... | collective-permute-start | bytes 1179656 | tf_op jit(solution)/shard_map/ppermute | solution.py:194
  74.9 6.1 %copy-start.2 = (bf16[1,3,256,256]{3,2,1,0:T(8,128)(2,1)S(1)}, bf16[1,3,256,256]{3,2,1,0:T(8,128)(2,1)}, u32[]{:S(2)}) copy-start(bf16[1,3,256,256]{3,2,1,0:T(8,128)(2,1)} %get-tuple-element.39) | copy-start | bytes 1179652
  77.2 134.5 %all-gather.9.cloned.1.call-start = ((), (), s32[]{:S(2)}) async-start(), calls=%async_computation.1 | async-start | bytes 5898240 | tf_op jit(solution)/shard_map/all_gather | solution.py:250
  77.3 64.5 %collective-permute-start.6 = (bf16[512,2048]{1,0:T(8,128)(2,1)}, bf16[512,2048]{1,0:T(8,128)(2,1)S(1)}, u32[]{:S(2)}, u32[]{:S(2)}) collective-permute-start(bf16[512,2048]{1,0:T(8,128)(2,1)} %refs_5_.7), channel_id=1, source_target_pairs={{0,8},{2,10},{4,12},{6,14},{8,0},{10,2},{12,4},{14,6},{16,24},{18,... | collective-permute-start | bytes 6291464 | tf_op jit(solution)/shard_map/ppermute | solution.py:194
  82.0 64.3 %collective-permute-start.11 = (bf16[2,3,256,256]{3,2,1,0:T(8,128)(2,1)}, bf16[2,3,256,256]{3,2,1,0:T(8,128)(2,1)}, u32[]{:S(2)}, u32[]{:S(2)}) collective-permute-start(bf16[2,3,256,256]{3,2,1,0:T(8,128)(2,1)} %maximum_add_fusion.4), channel_id=1, source_target_pairs={{0,16},{2,18},{4,20},{6,22},{8,24},{10,26},{12,28},{14,30},{16,0},... | collective-permute-start | bytes 2359304 | tf_op jit(solution)/shard_map/ppermute | solution.py:194
  101.7 13.2 %collective-permute-start.8 = (bf16[144,2048]{1,0:T(8,128)(2,1)}, bf16[144,2048]{1,0:T(8,128)(2,1)S(1)}, u32[]{:S(2)}, u32[]{:S(2)}) collective-permute-start(bf16[144,2048]{1,0:T(8,128)(2,1)} %broadcast_select_fusion.2.refs_9_), channel_id=1, source_target_pairs={{0,1},{1,0},{2,3},{3,2},{4,5},{5,4},{6,7},{7,6},{8,9},{9,8},{10,11... | collective-permute-start | bytes 1769480 | tf_op jit(solution)/shard_map/ppermute | solution.py:198
  115.0 28.7 %copy-start.10 = (bf16[144,2048]{1,0:T(8,128)(2,1)}, bf16[144,2048]{1,0:T(8,128)(2,1)S(1)}, u32[]{:S(2)}) copy-start(bf16[144,2048]{1,0:T(8,128)(2,1)S(1)} %collective-permute-done.8.refs_10_) | copy-start | bytes 1769476
  141.8 1.3 copy-start.8
  146.3 18.0 %copy-start.1 = (bf16[1,3,256,256]{3,2,1,0:T(8,128)(2,1)S(1)}, bf16[1,3,256,256]{3,2,1,0:T(8,128)(2,1)}, u32[]{:S(2)}) copy-start(bf16[1,3,256,256]{3,2,1,0:T(8,128)(2,1)} %get-tuple-element.38) | copy-start | bytes 1179652
  148.7 117.6 %all-gather.11.cloned.1.call-start = ((), (), s32[]{:S(2)}) async-start(), calls=%async_computation.2 | async-start | bytes 5898240 | tf_op jit(solution)/shard_map/all_gather | solution.py:250
  148.7 60.5 %collective-permute-start.7 = (bf16[512,2048]{1,0:T(8,128)(2,1)}, bf16[512,2048]{1,0:T(8,128)(2,1)S(1)}, u32[]{:S(2)}, u32[]{:S(2)}) collective-permute-start(bf16[512,2048]{1,0:T(8,128)(2,1)} %copy-done.8), channel_id=1, source_target_pairs={{0,1},{1,0},{2,3},{3,2},{4,5},{5,4},{6,7},{7,6},{8,9},{9,8},{10,11... | collective-permute-start | bytes 6291464 | tf_op jit(solution)/shard_map/ppermute | solution.py:198
  149.4 36.1 %collective-permute-start.9 = (bf16[144,2048]{1,0:T(8,128)(2,1)}, bf16[144,2048]{1,0:T(8,128)(2,1)S(1)}, u32[]{:S(2)}, u32[]{:S(2)}) collective-permute-start(bf16[144,2048]{1,0:T(8,128)(2,1)} %broadcast_select_fusion.2.refs_9_), channel_id=1, source_target_pairs={{0,8},{2,10},{4,12},{6,14},{8,0},{10,2},{12,4},{14,6},{16,24},{18,... | collective-permute-start | bytes 1769480 | tf_op jit(solution)/shard_map/ppermute | solution.py:194
  164.4 49.3 %collective-permute-start.12 = (bf16[2,3,256,256]{3,2,1,0:T(8,128)(2,1)S(1)}, bf16[2,3,256,256]{3,2,1,0:T(8,128)(2,1)S(1)}, u32[]{:S(2)}, u32[]{:S(2)}) collective-permute-start(bf16[2,3,256,256]{3,2,1,0:T(8,128)(2,1)S(1)} %maximum_add_fusion.5), channel_id=1, source_target_pairs={{0,16},{2,18},{4,20},{6,22},{8,24},{10,26},{12,28},{14,30},{16,0},... | collective-permute-start | bytes 2359304 | tf_op jit(solution)/shard_map/ppermute | solution.py:194
  185.5 25.6 %copy-start.11 = (bf16[144,2048]{1,0:T(8,128)(2,1)}, bf16[144,2048]{1,0:T(8,128)(2,1)S(1)}, u32[]{:S(2)}) copy-start(bf16[144,2048]{1,0:T(8,128)(2,1)S(1)} %collective-permute-done.9.refs_11_) | copy-start | bytes 1769476
  185.5 22.7 %collective-permute-start.10 = (bf16[144,2048]{1,0:T(8,128)(2,1)S(1)}, bf16[144,2048]{1,0:T(8,128)(2,1)S(1)}, u32[]{:S(2)}, u32[]{:S(2)}) collective-permute-start(bf16[144,2048]{1,0:T(8,128)(2,1)S(1)} %collective-permute-done.9.refs_11_), channel_id=1, source_target_pairs={{0,1},{1,0},{2,3},{3,2},{4,5},{5,4},{6,7},{7,6},{8,9},{9,8},{10,11... | collective-permute-start | bytes 1769480 | tf_op jit(solution)/shard_map/ppermute | solution.py:198
  208.1 3.5 copy-start.12
  209.2 1.3 copy-start.9
  213.7 2.7 copy-start.14
  213.7 2.9 copy-start.5
  213.7 3.8 %copy-start.6 = (bf16[7,3,2048]{2,0,1:T(8,128)(2,1)S(1)}, bf16[7,3,2048]{2,0,1:T(8,128)(2,1)}, u32[]{:S(2)}) copy-start(bf16[7,3,2048]{2,0,1:T(8,128)(2,1)} %param.8) | copy-start | bytes 258052
  215.0 105.4 %all-gather.13.cloned.1.call-start = ((), (), s32[]{:S(2)}) async-start(), calls=%async_computation.3 | async-start | bytes 5898240 | tf_op jit(solution)/shard_map/all_gather | solution.py:250
  221.5 47.2 %collective-permute-start.13 = (bf16[2,3,256,256]{3,2,1,0:T(8,128)(2,1)S(1)}, bf16[2,3,256,256]{3,2,1,0:T(8,128)(2,1)S(1)}, u32[]{:S(2)}, u32[]{:S(2)}) collective-permute-start(bf16[2,3,256,256]{3,2,1,0:T(8,128)(2,1)S(1)} %maximum_add_fusion.6), channel_id=1, source_target_pairs={{0,16},{2,18},{4,20},{6,22},{8,24},{10,26},{12,28},{14,30},{16,0},... | collective-permute-start | bytes 2359304 | tf_op jit(solution)/shard_map/ppermute | solution.py:194
  268.7 1.3 copy-start.13
  270.0 22.7 %collective-permute-start.14 = (bf16[512,256]{1,0:T(8,128)(2,1)S(1)}, bf16[512,256]{1,0:T(8,128)(2,1)S(1)}, u32[]{:S(2)}, u32[]{:S(2)}) collective-permute-start(bf16[512,256]{1,0:T(8,128)(2,1)S(1)} %copy-done.13), channel_id=1, source_target_pairs={{0,8},{2,10},{4,12},{6,14},{8,0},{10,2},{12,4},{14,6},{16,24},{18,... | collective-permute-start | bytes 786440 | tf_op jit(solution)/shard_map/ppermute | solution.py:194
  271.0 21.6 %copy-start.3 = (bf16[512,256]{1,0:T(8,128)(2,1)S(1)}, bf16[512,256]{1,0:T(8,128)(2,1)}, u32[]{:S(2)}) copy-start(bf16[512,256]{1,0:T(8,128)(2,1)} %get-tuple-element.13) | copy-start | bytes 786436
  291.6 8.4 %collective-permute-start.15 = (bf16[512,256]{1,0:T(8,128)(2,1)}, bf16[512,256]{1,0:T(8,128)(2,1)S(1)}, u32[]{:S(2)}, u32[]{:S(2)}) collective-permute-start(bf16[512,256]{1,0:T(8,128)(2,1)} %get-tuple-element.18), channel_id=1, source_target_pairs={{0,8},{2,10},{4,12},{6,14},{8,0},{10,2},{12,4},{14,6},{16,24},{18,... | collective-permute-start | bytes 786440 | tf_op jit(solution)/shard_map/ppermute | solution.py:194
  320.0 22.3 %collective-permute-start.16 = (bf16[512,256]{1,0:T(8,128)(2,1)}, bf16[512,256]{1,0:T(8,128)(2,1)S(1)}, u32[]{:S(2)}, u32[]{:S(2)}) collective-permute-start(bf16[512,256]{1,0:T(8,128)(2,1)} %get-tuple-element.19), channel_id=1, source_target_pairs={{0,8},{2,10},{4,12},{6,14},{8,0},{10,2},{12,4},{14,6},{16,24},{18,... | collective-permute-start | bytes 786440 | tf_op jit(solution)/shard_map/ppermute | solution.py:194
  320.4 21.8 %copy-start.4 = (bf16[512,256]{1,0:T(8,128)(2,1)S(1)}, bf16[512,256]{1,0:T(8,128)(2,1)}, u32[]{:S(2)}) copy-start(bf16[512,256]{1,0:T(8,128)(2,1)} %get-tuple-element.15) | copy-start | bytes 786436
  340.4 7.4 %collective-permute-start.17 = (bf16[512,256]{1,0:T(8,128)(2,1)}, bf16[512,256]{1,0:T(8,128)(2,1)S(1)}, u32[]{:S(2)}, u32[]{:S(2)}) collective-permute-start(bf16[512,256]{1,0:T(8,128)(2,1)} %get-tuple-element.20), channel_id=1, source_target_pairs={{0,8},{2,10},{4,12},{6,14},{8,0},{10,2},{12,4},{14,6},{16,24},{18,... | collective-permute-start | bytes 786440 | tf_op jit(solution)/shard_map/ppermute | solution.py:194
Sparse Core Ops, SparseCore 0:
  10.2 57.9 all-gather.14
  77.4 54.0 all-gather.6
  148.8 52.6 all-gather.8
  215.1 51.0 all-gather.10
  270.1 36.9 all-gather.12

commit v7 on v6

--- a/solution.py
+++ b/solution.py
@@ -7,7 +7,6 @@
 from jax.experimental.pallas import tpu as pltpu
 from jax.sharding import PartitionSpec as P
 
-ROW_TILE = 256
 CHAN_TILE = 256
 LANES = 128
 WIDTHS = [256, 256, 256, 256]
@@ -33,20 +32,25 @@
     span = band.shape[0] // groups
     per_lanes = groups * LANES // chans
     width = LANES // per_lanes
-    depth = w_refs[0].shape[3]
-    units = [(w, q, k) for w in w_refs for q in range(w.shape[0]) for k in range(w.shape[1])]
+    units = [(w, q, k) for w in w_refs for k in range(w.shape[1]) for q in range(w.shape[0])]
     tile, run = pl.program_id(0), pl.program_id(1)
+
+    blocks = at_ref.shape[0] // halves
+    piece = features // (halves * blocks)
 
     def copies(r):
         for h in range(halves):
-            piece = features // halves
-            where = pl.ds(pl.multiple_of(at_ref[len(units) + h], piece), piece)
-            yield pltpu.make_async_copy(
-                halo_refs[r * halves + h], x_ref.at[r, pl.ds(0, halo), where], sems.at[r, 2 * h]
-            )
-            yield pltpu.make_async_copy(
-                row_refs[r * halves + h], x_ref.at[r, pl.ds(halo, rows), where], sems.at[r, 2 * h + 1]
-            )
+            for b in range(blocks):
+                n = h * blocks + b
+                source = pl.ds(b * piece, piece)
+                target = pl.ds(pl.multiple_of(at_ref[n], piece), piece)
+                halo_from, rows_from = halo_refs[r * halves + h], row_refs[r * halves + h]
+                yield pltpu.make_async_copy(
+                    halo_from.at[:, source], x_ref.at[r, pl.ds(0, halo), target], sems.at[r, 2 * n]
+                )
+                yield pltpu.make_async_copy(
+                    rows_from.at[:, source], x_ref.at[r, pl.ds(halo, rows), target], sems.at[r, 2 * n + 1]
+                )
 
     @pl.when((tile == 0) & (run == 0))
     def _():
@@ -70,23 +74,16 @@
             for copy in copies(r):
                 copy.wait()
 
-    edges = [0, halo] + list(range(halo + ROW_TILE, total + 1, ROW_TILE))
-    for low, high in zip(edges[:-1], edges[1:]):
-        if depth % LANES == 0:
-            starts = [pl.multiple_of(at_ref[u], LANES) for u in range(len(units))]
-            x = jnp.concatenate([x_ref[run, low:high, pl.ds(at, depth)] for at in starts], axis=1)
-        else:
-            x = x_ref[run, low:high, :]
-        for streams in [(0, 1, 2)] if chans == LANES else [(0,), (1,), (2,)]:
-            weight = jnp.concatenate(
-                [jnp.concatenate([w[q, k, s] for w, q, k in units], axis=0) for s in streams], axis=1
-            )
-            acc = jnp.dot(x, weight, preferred_element_type=jnp.float32)
-            acc = acc.astype(jnp.bfloat16).astype(jnp.float32)
-            for n, s in enumerate(streams):
-                for h in range(chans // LANES):
-                    lane = n * chans + h * LANES
-                    proj[s, h, 8 + low : 8 + high, :] = acc[:, lane : lane + LANES]
+    for streams in [(0, 1, 2)] if chans == LANES else [(0,), (1,), (2,)]:
+        weight = jnp.concatenate(
+            [jnp.concatenate([w[q, k, s] for w, q, k in units], axis=0) for s in streams], axis=1
+        )
+        acc = jnp.dot(x_ref[run], weight, preferred_element_type=jnp.float32)
+        acc = acc.astype(jnp.bfloat16).astype(jnp.float32)
+        for n, s in enumerate(streams):
+            for h in range(chans // LANES):
+                lane = n * chans + h * LANES
+                proj[s, h, 8:, :] = acc[:, lane : lane + LANES]
 
     def short(s, start, size, h, allowed):
         lanes = slice(h * LANES, (h + 1) * LANES)
@@ -166,7 +163,7 @@
             out_specs=[pl.BlockSpec((row_count, tile), lambda j, i, at: (0, j))] * runs,
             scratch_shapes=[
                 pltpu.VMEM((runs, total, features), jnp.bfloat16),
-                pltpu.SemaphoreType.DMA((runs, 2 * halves)),
+                pltpu.SemaphoreType.DMA((runs, 2 * at.shape[0])),
                 pltpu.VMEM((3, tile // LANES, 8 + total, LANES), jnp.float32),
                 pltpu.VMEM((total, tile), jnp.bfloat16),
                 pltpu.VMEM((per_tile * span, 2 * span), jnp.bfloat16),
@@ -234,8 +231,7 @@
         halo = rows_before(tokens, stretch_at(me), reach)
         halo = lax.all_gather(halo, "chan", axis=1, tiled=True)
         rows = lax.all_gather(tokens, "chan", axis=1, tiled=True)
-        at = jnp.concatenate([order * depth, jnp.zeros(1, jnp.int32)])
-        return block(at, [[rows]], [[halo]], [(0, weight[:, None])], sw, fr, positions(me)[None], span, chans)[0]
+        return block(jnp.zeros(1, jnp.int32), [[rows]], [[halo]], [(0, weight[:, None])], sw, fr, positions(me)[None], span, chans)[0]
 
     side = lax.axis_index("chan")
     kind = (me >> 2) & 1
@@ -251,8 +247,9 @@
 
     own = lax.dynamic_slice_in_dim(local, own_begin, half, 2)
     other = lax.dynamic_slice_in_dim(local, other_begin, half, 2)
-    peers = flip(other, 4)
-    firsts = [peers[:, :, : widths[0]], flip(own[:, :, : widths[0]], 8), flip(other[:, :, : widths[0]], 12)]
+    early = widths[0] + widths[1]
+    peers = [flip(other[:, :, :early], 4), flip(other[:, :, early:], 4)]
+    firsts = [peers[0][:, :, : widths[0]], flip(own[:, :, : widths[0]], 8), flip(other[:, :, : widths[0]], 12)]
 
     rows_other = across(tokens)
     peer_rows = flip(tokens, 4)
@@ -262,19 +259,13 @@
     peer_halo = flip(halo, 4)
     peer_halo_other = across(peer_halo)
     after = {
-        0: [rows_other, halo],
-        1: [peer_rows, halo_other],
-        2: [peer_rows_other, peer_halo_other],
+        0: [rows_other, peer_rows],
+        1: [peer_rows_other, halo, peers[1]],
+        2: [halo_other, peer_halo_other],
     }
 
     pos = jnp.stack([positions(me), positions(me ^ 4)])
-    at = jnp.concatenate(
-        [
-            jnp.stack([(me // 4 * 4 + q) * depth for q in range(4)]),
-            jnp.stack([((me ^ (4 * k)) // 4 * 4 + q) * depth for q in range(4) for k in (1, 2, 3)]),
-            jnp.stack([side * piece, (1 - side) * piece]),
-        ]
-    )
+    at = jnp.stack([((me >> 2) ^ (2 * part + b)) * 4 * depth for part in (side, 1 - side) for b in range(2)])
     own_sw = lax.dynamic_slice_in_dim(sw, own_begin, half, 2)
     own_fr = lax.dynamic_slice_in_dim(fr, own_begin * fr.shape[0] // chans, fr.shape[0] // 2, 0)
 
@@ -285,7 +276,8 @@
             stack = jnp.stack(firsts)
         else:
             same = own[:, :, begin : begin + width]
-            peer = peers[:, :, begin : begin + width]
+            late = begin >= early
+            peer = peers[late][:, :, begin - late * early : begin - late * early + width]
             pair = jnp.stack([same, peer]) + nothing(stack).astype(jnp.bfloat16)
             stack = jnp.concatenate([peer[None], flip(pair, 8)])
         waits = sum(nothing(array) for array in after.get(c, []) + [gathered[-1]])

time: 358 us -> 348 us (0.972)
  starting transfers between devices: 75.1 us -> 32.5 us
  waiting for transfers between devices: 130 us -> 149 us
  Pallas kernels: 80.2 us -> 96.6 us
    ppermute x13 -> x14, waiting for transfers between devices: 67.8 us -> 116 us  [flip(): lax.ppermute(array, 'stretch', [(i, i ^ bit) for i in range(lax.axis_size...]
    ppermute x13 -> x14, starting transfers between devices: 66.5 us -> 22.6 us  [flip(): lax.ppermute(array, 'stretch', [(i, i ^ bit) for i in range(lax.axis_size...]
    ppermute x1, waiting for transfers between devices: 21.4 us -> 4.88 us  [rows_before(): before = lax.ppermute(jnp.where(second, tail, sibling), 'stretch', pairs)]
    pallas_call x4, Pallas kernels: 80.2 us -> 96.6 us  [block(): pl.pallas_call(functools.partial(block_kernel, runs, halves, len(weights)...]
    ppermute x4, waiting for transfers between devices: 33.9 us -> 22.8 us  [across(): return lax.ppermute(array, 'chan', [(0, 1), (1, 0)])]
    slice x14 -> x15, local copies, waits for them, and re-layouts: 13.1 us -> 14.1 us  [nothing(): array[(0,) * array.ndim].astype(jnp.float32) * 0.0]
  transfers between devices with their start and end apart: 23 -> 24, of which waited for: 10 -> 11; matrix products, arithmetic and copies ran while one was open for 8% -> 8% of each run, Pallas kernels for 23% -> 28%
where the time goes in v7:
time: 348 us; the launch traced here: 347 us
  waiting for transfers between devices  149 us (43%)
  Pallas kernels  96.6 us (28%)
  starting transfers between devices  32.5 us (9%)
  local copies, waits for them, and re-layouts  29.4 us (8%)
  between operations  26.6 us (8%)
  other arithmetic  13.3 us (4%)
    ppermute x14, waiting for transfers between devices, flip(): lax.ppermute(array, 'stretch', [(i, i ^ bit) for i in range(lax.axis_size...  116 us
    pallas_call x4, Pallas kernels, block(): pl.pallas_call(functools.partial(block_kernel, runs, halves, len(weights)...  96.6 us
    ppermute x4, waiting for transfers between devices, across(): return lax.ppermute(array, 'chan', [(0, 1), (1, 0)])  22.8 us
    ppermute x14, starting transfers between devices, flip(): lax.ppermute(array, 'stretch', [(i, i ^ bit) for i in range(lax.axis_size...  22.6 us
    slice x15, local copies, waits for them, and re-layouts, nothing(): array[(0,) * array.ndim].astype(jnp.float32) * 0.0  14.1 us
  transfers between devices with their start and end apart: 24, of which 11 were waited for; matrix products, arithmetic and copies ran while one was open for 8% of the time, Pallas kernels for 28%

profile of v7, /device:TPU:0, one launch (start us, length us, event | category | flops | bytes accessed | tf_op | source)
XLA Modules:
  0.0 347.2 jit_solution(8209590565826132292)
XLA Ops:
  6.5 3.5 %dynamic-slice_bitcast_fusion = (bf16[3,256,1024]{2,1,0:T(8,128)(2,1)S(1)}, bf16[3,256,1024]{2,1,0:T(8,128)(2,1)}) fusion(bf16[256,3,2048]{2,0,1:T(8,128)(2,1)} %param.7, s32[]{:T(128)S(6)} %select_n.62, s32[]{:T(128)S(6)} %select_n.61), kind=kLoop, calls=%fused_computation.1 | loop fusion | bytes 6291464 | tf_op jit(solution)/shard_map/dynamic_slice | solution.py:249
  10.2 3.1 collective-permute-start.4
  13.2 1.5 collective-permute-start.3
  14.8 1.0 fusion.3
  16.2 0.8 slice.143
  17.0 3.6 %collective-permute-start.2 = (bf16[3,256,256]{2,1,0:T(8,128)(2,1)}, bf16[3,256,256]{2,1,0:T(8,128)(2,1)S(1)}, u32[]{:S(2)}, u32[]{:S(2)}) collective-permute-start(bf16[3,256,256]{2,1,0:T(8,128)(2,1)} %slice.143), channel_id=1, source_target_pairs={{0,24},{2,26},{4,28},{6,30},{8,16},{10,18},{12,20},{14,22},{16,8},... | collective-permute-start | bytes 1179656 | tf_op jit(solution)/shard_map/ppermute | solution.py:191
  20.8 72.0 %collective-permute-done = bf16[3,256,512]{2,1,0:T(8,128)(2,1)S(1)} collective-permute-done((bf16[3,256,512]{2,1,0:T(8,128)(2,1)S(1)}, bf16[3,256,512]{2,1,0:T(8,128)(2,1)S(1)}, u32[]{:S(2)}, u32[]{:S(2)}) %collective-permute-start) | collective-permute-done | bytes 786464 | tf_op jit(solution)/shard_map/ppermute | solution.py:191
  92.8 0.9 slice_bitcast_fusion.8
  93.7 1.3 copy-done.8
  96.2 1.3 copy-done.9
  98.7 1.2 slice.146
  100.6 2.2 maximum_add_fusion
  102.9 1.1 slice.114
  104.1 1.7 collective-permute-start.5
  105.9 0.7 fusion.1
  108.7 1.1 broadcast_select_fusion.3
  109.8 3.4 collective-permute-start.7
  113.2 1.2 slice.182
  115.1 1.0 maximum_add_fusion.4
  116.1 4.2 %collective-permute-start.11 = (bf16[2,3,256,256]{3,2,1,0:T(8,128)(2,1)}, bf16[2,3,256,256]{3,2,1,0:T(8,128)(2,1)S(1)}, u32[]{:S(2)}, u32[]{:S(2)}) collective-permute-start(bf16[2,3,256,256]{3,2,1,0:T(8,128)(2,1)} %maximum_add_fusion.4), channel_id=1, source_target_pairs={{0,16},{2,18},{4,20},{6,22},{8,24},{10,26},{12,28},{14,30},{16,0},... | collective-permute-start | bytes 2359304 | tf_op jit(solution)/shard_map/ppermute | solution.py:191
  120.3 12.2 %collective-permute-done.12 = bf16[3,256,512]{2,1,0:T(8,128)(2,1)} collective-permute-done((bf16[3,256,512]{2,1,0:T(8,128)(2,1)}, bf16[3,256,512]{2,1,0:T(8,128)(2,1)}, u32[]{:S(2)}, u32[]{:S(2)}) %collective-permute-start.12) | collective-permute-done | bytes 786464 | tf_op jit(solution)/shard_map/ppermute | solution.py:191
  132.4 1.1 slice.154
  134.1 4.9 %collective-permute-done.7 = bf16[144,2048]{1,0:T(8,128)(2,1)S(1)} collective-permute-done((bf16[144,2048]{1,0:T(8,128)(2,1)S(1)}, bf16[144,2048]{1,0:T(8,128)(2,1)S(1)}, u32[]{:S(2)}, u32[]{:S(2)}) %collective-permute-start.7) | collective-permute-done | bytes 589856 | tf_op jit(solution)/shard_map/ppermute | solution.py:203
  139.0 0.9 broadcast_select_fusion.2.refs_9_
  139.9 1.2 slice.152
  141.7 10.8 %collective-permute-done.5.refs_8_ = bf16[512,2048]{1,0:T(8,128)(2,1)} collective-permute-done((bf16[512,2048]{1,0:T(8,128)(2,1)}, bf16[512,2048]{1,0:T(8,128)(2,1)}, u32[]{:S(2)}, u32[]{:S(2)}) %collective-permute-start.5) | collective-permute-done | bytes 2097184 | tf_op jit(solution)/shard_map/ppermute | solution.py:195
  152.5 1.1 slice.151
  154.2 1.3 slice.155
  156.2 1.1 maximum_add_fusion.1
  157.4 1.9 collective-permute-start.9
  159.8 1.2 slice_bitcast_fusion.4
  161.7 2.6 collective-permute-start.13
  164.3 1.5 collective-permute-start.8
  165.8 17.6 %collective-permute-done.9.refs_11_ = bf16[144,2048]{1,0:T(8,128)(2,1)S(1)} collective-permute-done((bf16[144,2048]{1,0:T(8,128)(2,1)}, bf16[144,2048]{1,0:T(8,128)(2,1)S(1)}, u32[]{:S(2)}, u32[]{:S(2)}) %collective-permute-start.9) | collective-permute-done | bytes 589856 | tf_op jit(solution)/shard_map/ppermute | solution.py:191
  183.4 0.8 copy-done.10
  184.2 1.5 collective-permute-start.10
  185.7 0.6 slice.160
  187.0 12.0 %collective-permute-done.10.refs_12_ = bf16[144,2048]{1,0:T(8,128)(2,1)S(1)} collective-permute-done((bf16[144,2048]{1,0:T(8,128)(2,1)S(1)}, bf16[144,2048]{1,0:T(8,128)(2,1)S(1)}, u32[]{:S(2)}, u32[]{:S(2)}) %collective-permute-start.10) | collective-permute-done | bytes 589856 | tf_op jit(solution)/shard_map/ppermute | solution.py:195
  199.1 0.6 slice.161
  200.6 0.6 all-gather.9.cloned.1.call-done.refs_1_
  201.2 1.1 slice.162
  202.9 1.2 maximum_add_fusion.2
  206.0 0.7 pad_add_fusion.1.at_ref
  207.2 0.9 pad_add_fusion.refs_4_
  208.1 0.6 fusion.5
  208.8 0.7 fusion.4
  209.4 0.5 slice.187
  210.7 2.5 collective-permute-start.14
  213.2 24.3 %shard_map.64 = (bf16[512,256]{1,0:T(8,128)(2,1)}, bf16[512,256]{1,0:T(8,128)(2,1)}) custom-call(s32[4]{0:T(128)} %pad_add_fusion.1.at_ref, bf16[4,1,3,256,1024]{4,3,2,1,0:T(8,128)(2,1)} %bitcast.66, bf16[4,3,3,256,256]{4,3,2,1,0:T(8,128)(2,1)} %all-gather.7.cloned.1.call-done.refs_1_, f32[3,7,256]{2,1,0:T(8,128)} %get-tuple-element.46.refs_2_, ...), custom_call_target="tpu_custom_call" | custom-call | flops 16508780544 | bytes 17563648 | tf_op jit(solution)/shard_map/pallas_call | solution.py:151
  237.5 1.2 slice.136
  239.4 3.9 %all-gather.11.cloned.1.call-done.refs_1_ = bf16[4,3,3,256,256]{4,3,2,1,0:T(8,128)(2,1)} async-done(((bf16[1,3,3,256,256]{4,3,2,1,0:T(8,128)(2,1)}), bf16[4,3,3,256,256]{4,3,2,1,0:T(8,128)(2,1)}) %all-gather.11.cloned.1.call-update) | async-done | bytes 4718608 | tf_op jit(solution)/shard_map/all_gather | solution.py:246
  243.3 1.2 slice.167
  245.2 3.0 collective-permute-done.14
  248.2 1.2 maximum_add_fusion.3
  249.5 0.9 copy-done.13
  250.9 24.5 %shard_map.65 = (bf16[512,256]{1,0:T(8,128)(2,1)}, bf16[512,256]{1,0:T(8,128)(2,1)}) custom-call(s32[4]{0:T(128)} %pad_add_fusion.1.at_ref, bf16[4,1,3,256,1024]{4,3,2,1,0:T(8,128)(2,1)} %bitcast.67, bf16[4,3,3,256,256]{4,3,2,1,0:T(8,128)(2,1)} %all-gather.9.cloned.1.call-done.refs_1_, f32[3,7,256]{2,1,0:T(8,128)} %get-tuple-element.45.refs_2_, ...), custom_call_target="tpu_custom_call" | custom-call | flops 16508780544 | bytes 17563648 | tf_op jit(solution)/shard_map/pallas_call | solution.py:151
  275.4 1.6 collective-permute-start.16
  277.1 6.5 %collective-permute-done.16 = bf16[512,256]{1,0:T(8,128)(2,1)S(1)} collective-permute-done((bf16[512,256]{1,0:T(8,128)(2,1)}, bf16[512,256]{1,0:T(8,128)(2,1)S(1)}, u32[]{:S(2)}, u32[]{:S(2)}) %collective-permute-start.16) | collective-permute-done | bytes 262176 | tf_op jit(solution)/shard_map/ppermute | solution.py:191
  283.6 23.8 %shard_map.66 = (bf16[512,256]{1,0:T(8,128)(2,1)}, bf16[512,256]{1,0:T(8,128)(2,1)}) custom-call(s32[4]{0:T(128)} %pad_add_fusion.1.at_ref, bf16[4,1,3,256,1024]{4,3,2,1,0:T(8,128)(2,1)} %bitcast.68, bf16[4,3,3,256,256]{4,3,2,1,0:T(8,128)(2,1)} %all-gather.11.cloned.1.call-done.refs_1_, f32[3,7,256]{2,1,0:T(8,128)} %get-tuple-element.44.refs_2_, ...), custom_call_target="tpu_custom_call" | custom-call | flops 16508780544 | bytes 17563648 | tf_op jit(solution)/shard_map/pallas_call | solution.py:151
  307.5 0.6 collective-permute-start.17
  308.1 24.0 %shard_map.67 = (bf16[512,256]{1,0:T(8,128)(2,1)}, bf16[512,256]{1,0:T(8,128)(2,1)}) custom-call(s32[4]{0:T(128)} %pad_add_fusion.1.at_ref, bf16[4,1,3,256,1024]{4,3,2,1,0:T(8,128)(2,1)} %bitcast.69, bf16[4,3,3,256,256]{4,3,2,1,0:T(8,128)(2,1)} %all-gather.13.cloned.1.call-done.refs_1_, f32[3,7,256]{2,1,0:T(8,128)} %get-tuple-element.43.refs_2_, ...), custom_call_target="tpu_custom_call" | custom-call | flops 16508780544 | bytes 17563648 | tf_op jit(solution)/shard_map/pallas_call | solution.py:151
  332.1 1.5 collective-permute-start.18
  333.7 5.2 %collective-permute-done.18 = bf16[512,256]{1,0:T(8,128)(2,1)S(1)} collective-permute-done((bf16[512,256]{1,0:T(8,128)(2,1)}, bf16[512,256]{1,0:T(8,128)(2,1)S(1)}, u32[]{:S(2)}, u32[]{:S(2)}) %collective-permute-start.18) | collective-permute-done | bytes 262176 | tf_op jit(solution)/shard_map/ppermute | solution.py:191
  339.1 1.5 pad_maximum_fusion
  (79 shorter events, 4.7 us)
Async XLA Ops:
  6.5 92.2 %all-gather.15.cloned.1.call-start = ((), (), s32[]{:S(2)}) async-start(), calls=%async_computation.4 | async-start | bytes 7864320 | tf_op jit(solution)/shard_map/all_gather | solution.py:246
  10.1 144.1 %all-gather.7.cloned.1.call-start = ((), (), s32[]{:S(2)}) async-start(), calls=%async_computation | async-start | bytes 5898240 | tf_op jit(solution)/shard_map/all_gather | solution.py:246
  10.2 83.5 %collective-permute-start.4 = (bf16[512,2048]{1,0:T(8,128)(2,1)}, bf16[512,2048]{1,0:T(8,128)(2,1)S(1)}, u32[]{:S(2)}, u32[]{:S(2)}) collective-permute-start(bf16[512,2048]{1,0:T(8,128)(2,1)} %refs_5_.7), channel_id=1, source_target_pairs={{0,8},{2,10},{4,12},{6,14},{8,0},{10,2},{12,4},{14,6},{16,24},{18,... | collective-permute-start | bytes 6291464 | tf_op jit(solution)/shard_map/ppermute | solution.py:191
  13.2 83.0 %collective-permute-start.3 = (bf16[512,2048]{1,0:T(8,128)(2,1)}, bf16[512,2048]{1,0:T(8,128)(2,1)S(1)}, u32[]{:S(2)}, u32[]{:S(2)}) collective-permute-start(bf16[512,2048]{1,0:T(8,128)(2,1)} %refs_5_.7), channel_id=1, source_target_pairs={{0,1},{1,0},{2,3},{3,2},{4,5},{5,4},{6,7},{7,6},{8,9},{9,8},{10,11... | collective-permute-start | bytes 6291464 | tf_op jit(solution)/shard_map/ppermute | solution.py:195
  14.8 5.8 %copy-start = (bf16[3,256,1024]{2,1,0:T(8,128)(2,1)S(1)}, bf16[3,256,1024]{2,1,0:T(8,128)(2,1)}, u32[]{:S(2)}) copy-start(bf16[3,256,1024]{2,1,0:T(8,128)(2,1)} %get-tuple-element.26) | copy-start | bytes 4718596
  15.7 77.1 %collective-permute-start = (bf16[3,256,512]{2,1,0:T(8,128)(2,1)S(1)}, bf16[3,256,512]{2,1,0:T(8,128)(2,1)S(1)}, u32[]{:S(2)}, u32[]{:S(2)}) collective-permute-start(bf16[3,256,512]{2,1,0:T(8,128)(2,1)S(1)} %get-tuple-element.34), channel_id=1, source_target_pairs={{0,8},{2,10},{4,12},{6,14},{8,0},{10,2},{12,4},{14,6},{16,24},{18,... | collective-permute-start | bytes 2359304 | tf_op jit(solution)/shard_map/ppermute | solution.py:191
  17.0 83.6 %collective-permute-start.2 = (bf16[3,256,256]{2,1,0:T(8,128)(2,1)}, bf16[3,256,256]{2,1,0:T(8,128)(2,1)S(1)}, u32[]{:S(2)}, u32[]{:S(2)}) collective-permute-start(bf16[3,256,256]{2,1,0:T(8,128)(2,1)} %slice.143), channel_id=1, source_target_pairs={{0,24},{2,26},{4,28},{6,30},{8,16},{10,18},{12,20},{14,22},{16,8},... | collective-permute-start | bytes 1179656 | tf_op jit(solution)/shard_map/ppermute | solution.py:191
  20.7 79.9 %collective-permute-start.1 = (bf16[3,256,256]{2,1,0:T(8,128)(2,1)S(1)}, bf16[3,256,256]{2,1,0:T(8,128)(2,1)}, u32[]{:S(2)}, u32[]{:S(2)}) collective-permute-start(bf16[3,256,256]{2,1,0:T(8,128)(2,1)S(1)} %get-tuple-element.32), channel_id=1, source_target_pairs={{0,16},{2,18},{4,20},{6,22},{8,24},{10,26},{12,28},{14,30},{16,0},... | collective-permute-start | bytes 1179656 | tf_op jit(solution)/shard_map/ppermute | solution.py:191
  93.7 1.4 copy-start.8
  96.2 1.3 copy-start.9
  102.8 3.0 copy-start.7
  102.9 98.3 %all-gather.9.cloned.1.call-start = ((), (), s32[]{:S(2)}) async-start(), calls=%async_computation.1 | async-start | bytes 5898240 | tf_op jit(solution)/shard_map/all_gather | solution.py:246
  104.0 4.6 %collective-permute-start.6 = (bf16[144,2048]{1,0:T(8,128)(2,1)S(1)}, bf16[144,2048]{1,0:T(8,128)(2,1)S(1)}, u32[]{:S(2)}, u32[]{:S(2)}) collective-permute-start(bf16[144,2048]{1,0:T(8,128)(2,1)S(1)} %slice.114), channel_id=1, source_target_pairs={{0,2},{2,0},{4,6},{6,4},{8,10},{10,8},{12,14},{14,12},{16,18},{18,... | collective-permute-start | bytes 1769480 | tf_op jit(solution)/shard_map/ppermute | solution.py:191
  104.1 48.4 %collective-permute-start.5 = (bf16[512,2048]{1,0:T(8,128)(2,1)}, bf16[512,2048]{1,0:T(8,128)(2,1)}, u32[]{:S(2)}, u32[]{:S(2)}) collective-permute-start(bf16[512,2048]{1,0:T(8,128)(2,1)} %copy-done.8), channel_id=1, source_target_pairs={{0,1},{1,0},{2,3},{3,2},{4,5},{5,4},{6,7},{7,6},{8,9},{9,8},{10,11... | collective-permute-start | bytes 6291464 | tf_op jit(solution)/shard_map/ppermute | solution.py:195
  105.8 26.6 %collective-permute-start.12 = (bf16[3,256,512]{2,1,0:T(8,128)(2,1)}, bf16[3,256,512]{2,1,0:T(8,128)(2,1)}, u32[]{:S(2)}, u32[]{:S(2)}) collective-permute-start(bf16[3,256,512]{2,1,0:T(8,128)(2,1)} %get-tuple-element.33), channel_id=1, source_target_pairs={{0,8},{2,10},{4,12},{6,14},{8,0},{10,2},{12,4},{14,6},{16,24},{18,... | collective-permute-start | bytes 2359304 | tf_op jit(solution)/shard_map/ppermute | solution.py:191
  109.8 29.2 %collective-permute-start.7 = (bf16[144,2048]{1,0:T(8,128)(2,1)S(1)}, bf16[144,2048]{1,0:T(8,128)(2,1)S(1)}, u32[]{:S(2)}, u32[]{:S(2)}) collective-permute-start(bf16[144,2048]{1,0:T(8,128)(2,1)S(1)} %broadcast_select_fusion.3), channel_id=1, source_target_pairs={{0,4},{2,6},{4,8},{6,10},{8,12},{10,14},{12,16},{14,18},{16,20},{1... | collective-permute-start | bytes 1769480 | tf_op jit(solution)/shard_map/ppermute | solution.py:203
  116.1 40.1 %collective-permute-start.11 = (bf16[2,3,256,256]{3,2,1,0:T(8,128)(2,1)}, bf16[2,3,256,256]{3,2,1,0:T(8,128)(2,1)S(1)}, u32[]{:S(2)}, u32[]{:S(2)}) collective-permute-start(bf16[2,3,256,256]{3,2,1,0:T(8,128)(2,1)} %maximum_add_fusion.4), channel_id=1, source_target_pairs={{0,16},{2,18},{4,20},{6,22},{8,24},{10,26},{12,28},{14,30},{16,0},... | collective-permute-start | bytes 2359304 | tf_op jit(solution)/shard_map/ppermute | solution.py:191
  157.4 85.9 %all-gather.11.cloned.1.call-start = ((), (), s32[]{:S(2)}) async-start(), calls=%async_computation.2 | async-start | bytes 5898240 | tf_op jit(solution)/shard_map/all_gather | solution.py:246
  157.4 26.0 %collective-permute-start.9 = (bf16[144,2048]{1,0:T(8,128)(2,1)}, bf16[144,2048]{1,0:T(8,128)(2,1)S(1)}, u32[]{:S(2)}, u32[]{:S(2)}) collective-permute-start(bf16[144,2048]{1,0:T(8,128)(2,1)} %broadcast_select_fusion.2.refs_9_), channel_id=1, source_target_pairs={{0,8},{2,10},{4,12},{6,14},{8,0},{10,2},{12,4},{14,6},{16,24},{18,... | collective-permute-start | bytes 1769480 | tf_op jit(solution)/shard_map/ppermute | solution.py:191
  161.7 41.2 %collective-permute-start.13 = (bf16[2,3,256,256]{3,2,1,0:T(8,128)(2,1)S(1)}, bf16[2,3,256,256]{3,2,1,0:T(8,128)(2,1)S(1)}, u32[]{:S(2)}, u32[]{:S(2)}) collective-permute-start(bf16[2,3,256,256]{3,2,1,0:T(8,128)(2,1)S(1)} %maximum_add_fusion.5), channel_id=1, source_target_pairs={{0,16},{2,18},{4,20},{6,22},{8,24},{10,26},{12,28},{14,30},{16,0},... | collective-permute-start | bytes 2359304 | tf_op jit(solution)/shard_map/ppermute | solution.py:191
  164.3 21.4 %collective-permute-start.8 = (bf16[144,2048]{1,0:T(8,128)(2,1)}, bf16[144,2048]{1,0:T(8,128)(2,1)S(1)}, u32[]{:S(2)}, u32[]{:S(2)}) collective-permute-start(bf16[144,2048]{1,0:T(8,128)(2,1)} %broadcast_select_fusion.2.refs_9_), channel_id=1, source_target_pairs={{0,1},{1,0},{2,3},{3,2},{4,5},{5,4},{6,7},{7,6},{8,9},{9,8},{10,11... | collective-permute-start | bytes 1769480 | tf_op jit(solution)/shard_map/ppermute | solution.py:195
  183.4 0.8 copy-start.10
  184.2 14.8 %collective-permute-start.10 = (bf16[144,2048]{1,0:T(8,128)(2,1)S(1)}, bf16[144,2048]{1,0:T(8,128)(2,1)S(1)}, u32[]{:S(2)}, u32[]{:S(2)}) collective-permute-start(bf16[144,2048]{1,0:T(8,128)(2,1)S(1)} %collective-permute-done.9.refs_11_), channel_id=1, source_target_pairs={{0,1},{1,0},{2,3},{3,2},{4,5},{5,4},{6,7},{7,6},{8,9},{9,8},{10,11... | collective-permute-start | bytes 1769480 | tf_op jit(solution)/shard_map/ppermute | solution.py:195
  185.7 13.4 %copy-start.11 = (bf16[144,2048]{1,0:T(8,128)(2,1)}, bf16[144,2048]{1,0:T(8,128)(2,1)S(1)}, u32[]{:S(2)}) copy-start(bf16[144,2048]{1,0:T(8,128)(2,1)S(1)} %collective-permute-done.8.refs_10_) | copy-start | bytes 1769476
  199.1 0.8 copy-start.12
  204.1 1.4 copy-start.14
  204.1 1.6 copy-start.5
  204.2 2.6 copy-start.6
  204.2 103.9 %all-gather.13.cloned.1.call-start = ((), (), s32[]{:S(2)}) async-start(), calls=%async_computation.3 | async-start | bytes 5898240 | tf_op jit(solution)/shard_map/all_gather | solution.py:246
  210.7 37.5 %collective-permute-start.14 = (bf16[2,3,256,256]{3,2,1,0:T(8,128)(2,1)S(1)}, bf16[2,3,256,256]{3,2,1,0:T(8,128)(2,1)S(1)}, u32[]{:S(2)}, u32[]{:S(2)}) collective-permute-start(bf16[2,3,256,256]{3,2,1,0:T(8,128)(2,1)S(1)} %maximum_add_fusion.6), channel_id=1, source_target_pairs={{0,16},{2,18},{4,20},{6,22},{8,24},{10,26},{12,28},{14,30},{16,0},... | collective-permute-start | bytes 2359304 | tf_op jit(solution)/shard_map/ppermute | solution.py:191
  249.5 0.9 copy-start.13
  250.4 26.6 %collective-permute-start.15 = (bf16[512,256]{1,0:T(8,128)(2,1)S(1)}, bf16[512,256]{1,0:T(8,128)(2,1)S(1)}, u32[]{:S(2)}, u32[]{:S(2)}) collective-permute-start(bf16[512,256]{1,0:T(8,128)(2,1)S(1)} %copy-done.13), channel_id=1, source_target_pairs={{0,8},{2,10},{4,12},{6,14},{8,0},{10,2},{12,4},{14,6},{16,24},{18,... | collective-permute-start | bytes 786440 | tf_op jit(solution)/shard_map/ppermute | solution.py:191
  250.9 26.1 %copy-start.1 = (bf16[512,256]{1,0:T(8,128)(2,1)S(1)}, bf16[512,256]{1,0:T(8,128)(2,1)}, u32[]{:S(2)}) copy-start(bf16[512,256]{1,0:T(8,128)(2,1)} %get-tuple-element.13) | copy-start | bytes 786436
  275.4 1.6 copy-start.4
  275.4 8.2 %collective-permute-start.16 = (bf16[512,256]{1,0:T(8,128)(2,1)}, bf16[512,256]{1,0:T(8,128)(2,1)S(1)}, u32[]{:S(2)}, u32[]{:S(2)}) collective-permute-start(bf16[512,256]{1,0:T(8,128)(2,1)} %get-tuple-element.18), channel_id=1, source_target_pairs={{0,8},{2,10},{4,12},{6,14},{8,0},{10,2},{12,4},{14,6},{16,24},{18,... | collective-permute-start | bytes 786440 | tf_op jit(solution)/shard_map/ppermute | solution.py:191
  307.5 26.2 %collective-permute-start.17 = (bf16[512,256]{1,0:T(8,128)(2,1)}, bf16[512,256]{1,0:T(8,128)(2,1)S(1)}, u32[]{:S(2)}, u32[]{:S(2)}) collective-permute-start(bf16[512,256]{1,0:T(8,128)(2,1)} %get-tuple-element.19), channel_id=1, source_target_pairs={{0,8},{2,10},{4,12},{6,14},{8,0},{10,2},{12,4},{14,6},{16,24},{18,... | collective-permute-start | bytes 786440 | tf_op jit(solution)/shard_map/ppermute | solution.py:191
  308.1 25.5 %copy-start.2 = (bf16[512,256]{1,0:T(8,128)(2,1)S(1)}, bf16[512,256]{1,0:T(8,128)(2,1)}, u32[]{:S(2)}) copy-start(bf16[512,256]{1,0:T(8,128)(2,1)} %get-tuple-element.15) | copy-start | bytes 786436
  332.1 1.6 copy-start.3
  332.1 6.8 %collective-permute-start.18 = (bf16[512,256]{1,0:T(8,128)(2,1)}, bf16[512,256]{1,0:T(8,128)(2,1)S(1)}, u32[]{:S(2)}, u32[]{:S(2)}) collective-permute-start(bf16[512,256]{1,0:T(8,128)(2,1)} %get-tuple-element.20), channel_id=1, source_target_pairs={{0,8},{2,10},{4,12},{6,14},{8,0},{10,2},{12,4},{14,6},{16,24},{18,... | collective-permute-start | bytes 786440 | tf_op jit(solution)/shard_map/ppermute | solution.py:191
Sparse Core Ops, SparseCore 0:
  10.2 49.0 all-gather.14
  103.0 47.8 all-gather.6
  157.5 43.6 all-gather.8
  204.3 38.9 all-gather.10
  249.6 37.4 all-gather.12

commit v8 on v7

--- a/solution.py
+++ b/solution.py
@@ -7,6 +7,7 @@
 from jax.experimental.pallas import tpu as pltpu
 from jax.sharding import PartitionSpec as P
 
+ROW_TILE = 256
 CHAN_TILE = 256
 LANES = 128
 WIDTHS = [256, 256, 256, 256]
@@ -74,16 +75,18 @@
             for copy in copies(r):
                 copy.wait()
 
+    edges = [0, halo] + list(range(halo + ROW_TILE, total + 1, ROW_TILE))
     for streams in [(0, 1, 2)] if chans == LANES else [(0,), (1,), (2,)]:
-        weight = jnp.concatenate(
-            [jnp.concatenate([w[q, k, s] for w, q, k in units], axis=0) for s in streams], axis=1
-        )
-        acc = jnp.dot(x_ref[run], weight, preferred_element_type=jnp.float32)
-        acc = acc.astype(jnp.bfloat16).astype(jnp.float32)
-        for n, s in enumerate(streams):
-            for h in range(chans // LANES):
-                lane = n * chans + h * LANES
-                proj[s, h, 8:, :] = acc[:, lane : lane + LANES]
+        for low, high in zip(edges[:-1], edges[1:]):
+            weight = jnp.concatenate(
+                [jnp.concatenate([w[q, k, s] for w, q, k in units], axis=0) for s in streams], axis=1
+            )
+            acc = jnp.dot(x_ref[run, low:high, :], weight, preferred_element_type=jnp.float32)
+            acc = acc.astype(jnp.bfloat16).astype(jnp.float32)
+            for n, s in enumerate(streams):
+                for h in range(chans // LANES):
+                    lane = n * chans + h * LANES
+                    proj[s, h, 8 + low : 8 + high, :] = acc[:, lane : lane + LANES]
 
     def short(s, start, size, h, allowed):
         lanes = slice(h * LANES, (h + 1) * LANES)
@@ -204,8 +207,20 @@
     return jnp.where(second, sibling, before)
 
 
-def nothing(array):
-    return (array[(0,) * array.ndim].astype(jnp.float32) * 0.0).astype(jnp.int32)
+def nothing_kernel(*refs):
+    pass
+
+
+def tied(value, *others):
+    return pl.pallas_call(
+        nothing_kernel,
+        in_specs=[pl.BlockSpec(memory_space=pl.ANY)] * (1 + len(others)),
+        out_specs=pl.BlockSpec(memory_space=pl.ANY),
+        out_shape=jax.ShapeDtypeStruct(value.shape, value.dtype),
+        input_output_aliases={0: 0},
+        compiler_params=pltpu.CompilerParams(vmem_limit_bytes=56 * 1024 * 1024),
+        cost_estimate=pl.CostEstimate(flops=0, bytes_accessed=0, transcendentals=0),
+    )(value, *others)
 
 
 def per_device(tokens, in_weight, short_weight, medium_filter, seq_lengths, stretch_slot):
@@ -269,6 +284,7 @@
     own_sw = lax.dynamic_slice_in_dim(sw, own_begin, half, 2)
     own_fr = lax.dynamic_slice_in_dim(fr, own_begin * fr.shape[0] // chans, fr.shape[0] // 2, 0)
 
+    after[0] += [pos, own_sw, own_fr]
     gathered, stack = [spread(own[None])], None
     mine, theirs = [], []
     for c, (begin, width) in enumerate(zip(begins, widths)):
@@ -278,10 +294,9 @@
             same = own[:, :, begin : begin + width]
             late = begin >= early
             peer = peers[late][:, :, begin - late * early : begin - late * early + width]
-            pair = jnp.stack([same, peer]) + nothing(stack).astype(jnp.bfloat16)
+            pair = tied(jnp.stack([same, peer]), stack)
             stack = jnp.concatenate([peer[None], flip(pair, 8)])
-        waits = sum(nothing(array) for array in after.get(c, []) + [gathered[-1]])
-        stack = stack + waits.astype(jnp.bfloat16)
+        stack = tied(stack, gathered[-1], *after.get(c, []))
         gathered.append(spread(stack))
         groups = fr.shape[0] * width // chans
         first_group = begin * fr.shape[0] // chans

time: 348 us -> 323 us (0.928)
  local copies, waits for them, and re-layouts: 29.4 us -> 13.7 us
  Pallas kernels: 96.6 us -> 81.5 us
  waiting for transfers between devices: 149 us -> 163 us
  between operations: 26.6 us -> 16.6 us
    ppermute x4, waiting for transfers between devices: 22.8 us -> 2.36 us  [across(): return lax.ppermute(array, 'chan', [(0, 1), (1, 0)])]
    ppermute x14, waiting for transfers between devices: 116 us -> 136 us  [flip(): lax.ppermute(array, 'stretch', [(i, i ^ bit) for i in range(lax.axis_size...]
    ppermute x1, waiting for transfers between devices: 4.88 us -> 20.4 us  [rows_before(): before = lax.ppermute(jnp.where(second, tail, sibling), 'stretch', pairs)]
    pallas_call x4, Pallas kernels: 96.6 us -> 81.5 us  [block(): pl.pallas_call(functools.partial(block_kernel, runs, halves, len(weights)...]
    slice x15 -> x0, local copies, waits for them, and re-layouts: 14.1 us -> none  [nothing(): array[(0,) * array.ndim].astype(jnp.float32) * 0.0]
    add x7 -> x0, other arithmetic: 6.93 us -> none  [the longest x4 5.82 us: per_device(): stack = stack + waits.astype(jnp.bfloat16)]
    another operation x1 -> x5, other arithmetic: 0.18 us -> 5.19 us  [the longest x3 2.86 us: per_device(): pair = tied(jnp.stack([same, peer]), stack)]
  transfers between devices with their start and end apart: 24 -> 24, of which waited for: 11 -> 11; matrix products, arithmetic and copies ran while one was open for 8% -> 7% of each run, Pallas kernels for 28% -> 25%
where the time goes in v8:
time: 323 us; the launch traced here: 322 us
  waiting for transfers between devices  163 us (50%)
  Pallas kernels  81.5 us (25%)
  starting transfers between devices  31.5 us (10%)
  between operations  16.6 us (5%)
  other arithmetic  15.9 us (5%)
  local copies, waits for them, and re-layouts  13.7 us (4%)
    ppermute x14, waiting for transfers between devices, flip(): lax.ppermute(array, 'stretch', [(i, i ^ bit) for i in range(lax.axis_size...  136 us
    pallas_call x4, Pallas kernels, block(): pl.pallas_call(functools.partial(block_kernel, runs, halves, len(weights)...  81.5 us
    ppermute x14, starting transfers between devices, flip(): lax.ppermute(array, 'stretch', [(i, i ^ bit) for i in range(lax.axis_size...  21.2 us
    ppermute x1, waiting for transfers between devices, rows_before(): before = lax.ppermute(jnp.where(second, tail, sibling), 'stretch', pairs)  20.4 us
    ppermute x4, starting transfers between devices, across(): return lax.ppermute(array, 'chan', [(0, 1), (1, 0)])  6.51 us
  transfers between devices with their start and end apart: 24, of which 11 were waited for; matrix products, arithmetic and copies ran while one was open for 7% of the time, Pallas kernels for 25%

profile of v8, /device:TPU:0, one launch (start us, length us, event | category | flops | bytes accessed | tf_op | source)
XLA Modules:
  0.0 322.2 jit_solution(18254336438938807022)
XLA Ops:
  6.5 3.5 %dynamic-slice_bitcast_fusion = (bf16[3,256,1024]{2,1,0:T(8,128)(2,1)S(1)}, bf16[3,256,1024]{2,1,0:T(8,128)(2,1)}) fusion(bf16[256,3,2048]{2,0,1:T(8,128)(2,1)} %param.7, s32[]{:T(128)S(6)} %select_n.62, s32[]{:T(128)S(6)} %select_n.61), kind=kLoop, calls=%fused_computation.1 | loop fusion | bytes 6291464 | tf_op jit(solution)/shard_map/dynamic_slice | solution.py:264
  10.1 3.0 collective-permute-start.3
  13.1 1.6 collective-permute-start.4
  14.7 0.8 slice.83
  15.5 2.5 collective-permute-start.2
  18.0 1.1 slice_bitcast_fusion
  19.2 0.2 collective-permute-start.1
  19.3 1.0 fusion.3
  20.4 1.8 collective-permute-start
  22.2 0.7 fusion.1
  24.2 0.2 reduce-window.8
  24.6 0.7 convert_bitcast_fusion.refs_5_
  25.4 0.7 fusion.refs_6_
  26.1 0.1 stack_broadcast_in_dim.5
  26.2 0.1 stack_broadcast_in_dim.4
  26.4 0.9 pad_add_fusion.refs_4_
  27.3 66.9 %collective-permute-done = bf16[3,256,512]{2,1,0:T(8,128)(2,1)S(1)} collective-permute-done((bf16[3,256,512]{2,1,0:T(8,128)(2,1)}, bf16[3,256,512]{2,1,0:T(8,128)(2,1)S(1)}, u32[]{:S(2)}, u32[]{:S(2)}) %collective-permute-start) | collective-permute-done | bytes 786464 | tf_op jit(solution)/shard_map/ppermute | solution.py:194
  94.2 2.1 pad_maximum_fusion.1.refs_0_
  96.5 1.1 slice.66
  97.7 0.4 collective-permute-start.5
  100.0 1.1 broadcast_select_fusion.3
  101.2 3.6 %collective-permute-start.7 = (bf16[144,2048]{1,0:T(8,128)(2,1)S(1)}, bf16[144,2048]{1,0:T(8,128)(2,1)S(1)}, u32[]{:S(2)}, u32[]{:S(2)}) collective-permute-start(bf16[144,2048]{1,0:T(8,128)(2,1)S(1)} %broadcast_select_fusion.3), channel_id=1, source_target_pairs={{0,4},{2,6},{4,8},{6,10},{8,12},{10,14},{12,16},{14,18},{16,20},{1... | collective-permute-start | bytes 1769480 | tf_op jit(solution)/shard_map/ppermute | solution.py:206
  104.8 0.9 pad_maximum_fusion.5.refs_0_
  105.7 2.6 collective-permute-start.11
  108.3 1.6 collective-permute-start.12
  109.8 20.4 %collective-permute-done.7 = bf16[144,2048]{1,0:T(8,128)(2,1)S(1)} collective-permute-done((bf16[144,2048]{1,0:T(8,128)(2,1)S(1)}, bf16[144,2048]{1,0:T(8,128)(2,1)S(1)}, u32[]{:S(2)}, u32[]{:S(2)}) %collective-permute-start.7) | collective-permute-done | bytes 589856 | tf_op jit(solution)/shard_map/ppermute | solution.py:206
  130.3 0.9 broadcast_select_fusion.2.refs_9_.refs_3_
  131.2 11.9 %collective-permute-done.11 = bf16[2,3,256,256]{3,2,1,0:T(8,128)(2,1)S(1)} collective-permute-done((bf16[2,3,256,256]{3,2,1,0:T(8,128)(2,1)}, bf16[2,3,256,256]{3,2,1,0:T(8,128)(2,1)S(1)}, u32[]{:S(2)}, u32[]{:S(2)}) %collective-permute-start.11) | collective-permute-done | bytes 786464 | tf_op jit(solution)/shard_map/ppermute | solution.py:194
  143.1 1.1 pad_maximum_fusion.2.refs_0_
  144.2 1.9 collective-permute-done.5.refs_8_.refs_2_
  146.2 1.0 copy-done.3
  147.2 1.9 collective-permute-start.9
  149.1 1.0 pad_maximum_fusion.6.refs_0_
  150.1 2.6 collective-permute-start.13
  152.7 1.5 collective-permute-start.8
  154.2 19.9 %collective-permute-done.9.refs_11_ = bf16[144,2048]{1,0:T(8,128)(2,1)S(1)} collective-permute-done((bf16[144,2048]{1,0:T(8,128)(2,1)S(1)}, bf16[144,2048]{1,0:T(8,128)(2,1)S(1)}, u32[]{:S(2)}, u32[]{:S(2)}) %collective-permute-start.9) | collective-permute-done | bytes 589856 | tf_op jit(solution)/shard_map/ppermute | solution.py:194
  174.1 1.5 collective-permute-start.10
  175.6 11.9 %collective-permute-done.13 = bf16[2,3,256,256]{3,2,1,0:T(8,128)(2,1)S(1)} collective-permute-done((bf16[2,3,256,256]{3,2,1,0:T(8,128)(2,1)}, bf16[2,3,256,256]{3,2,1,0:T(8,128)(2,1)S(1)}, u32[]{:S(2)}, u32[]{:S(2)}) %collective-permute-start.13) | collective-permute-done | bytes 786464 | tf_op jit(solution)/shard_map/ppermute | solution.py:194
  187.5 1.1 pad_maximum_fusion.3.refs_0_
  188.7 0.5 collective-permute-done.10.refs_12_.refs_3_
  189.1 4.1 %all-gather.15.cloned.1.call-done = bf16[12,3,256,256]{3,2,1,0:T(8,128)(2,1)} async-done(((bf16[3,3,256,256]{3,2,1,0:T(8,128)(2,1)}), bf16[12,3,256,256]{3,2,1,0:T(8,128)(2,1)}) %all-gather.15.cloned.1.call-update) | async-done | bytes 4718608 | tf_op jit(solution)/shard_map/all_gather | solution.py:261
  193.3 0.6 pad_add_fusion.1.at_ref
  193.9 0.1 copy-done.8
  194.1 0.6 fusion.5
  194.7 0.7 fusion.4
  195.4 0.9 pad_maximum_fusion.7.refs_0_
  196.3 2.4 collective-permute-start.14
  198.7 20.4 %shard_map.65 = (bf16[512,256]{1,0:T(8,128)(2,1)}, bf16[512,256]{1,0:T(8,128)(2,1)}) custom-call(s32[4]{0:T(128)} %pad_add_fusion.1.at_ref, bf16[4,1,3,256,1024]{4,3,2,1,0:T(8,128)(2,1)} %bitcast.36, bf16[4,3,3,256,256]{4,3,2,1,0:T(8,128)(2,1)} %bitcast.41, f32[3,7,256]{2,1,0:T(8,128)} %get-tuple-element.42.refs_2_, f32[16,256]{1,0:T(8,128)} %get-tuple-element.46.refs_3_, ...), custom_call_target="tpu_custom_call" | custom-call | flops 16508780544 | bytes 17563648 | tf_op jit(solution)/shard_map/pallas_call | solution.py:154
  219.2 14.8 %collective-permute-done.14 = bf16[2,3,256,256]{3,2,1,0:T(8,128)(2,1)S(1)} collective-permute-done((bf16[2,3,256,256]{3,2,1,0:T(8,128)(2,1)}, bf16[2,3,256,256]{3,2,1,0:T(8,128)(2,1)S(1)}, u32[]{:S(2)}, u32[]{:S(2)}) %collective-permute-start.14) | collective-permute-done | bytes 786464 | tf_op jit(solution)/shard_map/ppermute | solution.py:194
  234.0 1.1 pad_maximum_fusion.4.refs_0_
  235.1 0.9 copy-done.15
  236.1 0.7 collective-permute-start.15
  236.7 20.7 %shard_map.68 = (bf16[512,256]{1,0:T(8,128)(2,1)}, bf16[512,256]{1,0:T(8,128)(2,1)}) custom-call(s32[4]{0:T(128)} %pad_add_fusion.1.at_ref, bf16[4,1,3,256,1024]{4,3,2,1,0:T(8,128)(2,1)} %bitcast.37, bf16[4,3,3,256,256]{4,3,2,1,0:T(8,128)(2,1)} %bitcast.45, f32[3,7,256]{2,1,0:T(8,128)} %get-tuple-element.41.refs_2_, f32[16,256]{1,0:T(8,128)} %get-tuple-element.45.refs_3_, ...), custom_call_target="tpu_custom_call" | custom-call | flops 16508780544 | bytes 17563648 | tf_op jit(solution)/shard_map/pallas_call | solution.py:154
  257.4 1.3 collective-permute-start.16
  258.8 1.0 constant_dynamic-update-slice_fusion.2
  259.8 6.1 %collective-permute-done.16 = bf16[512,256]{1,0:T(8,128)(2,1)S(1)} collective-permute-done((bf16[512,256]{1,0:T(8,128)(2,1)}, bf16[512,256]{1,0:T(8,128)(2,1)S(1)}, u32[]{:S(2)}, u32[]{:S(2)}) %collective-permute-start.16) | collective-permute-done | bytes 262176 | tf_op jit(solution)/shard_map/ppermute | solution.py:194
  265.9 20.1 %shard_map.71 = (bf16[512,256]{1,0:T(8,128)(2,1)}, bf16[512,256]{1,0:T(8,128)(2,1)}) custom-call(s32[4]{0:T(128)} %pad_add_fusion.1.at_ref, bf16[4,1,3,256,1024]{4,3,2,1,0:T(8,128)(2,1)} %bitcast.38, bf16[4,3,3,256,256]{4,3,2,1,0:T(8,128)(2,1)} %bitcast.43, f32[3,7,256]{2,1,0:T(8,128)} %get-tuple-element.40.refs_2_, f32[16,256]{1,0:T(8,128)} %get-tuple-element.44.refs_3_, ...), custom_call_target="tpu_custom_call" | custom-call | flops 16508780544 | bytes 17563648 | tf_op jit(solution)/shard_map/pallas_call | solution.py:154
  286.0 0.5 collective-permute-start.17
  286.4 20.2 %shard_map.74 = (bf16[512,256]{1,0:T(8,128)(2,1)}, bf16[512,256]{1,0:T(8,128)(2,1)}) custom-call(s32[4]{0:T(128)} %pad_add_fusion.1.at_ref, bf16[4,1,3,256,1024]{4,3,2,1,0:T(8,128)(2,1)} %bitcast.39, bf16[4,3,3,256,256]{4,3,2,1,0:T(8,128)(2,1)} %bitcast.49, f32[3,7,256]{2,1,0:T(8,128)} %get-tuple-element.39.refs_2_, f32[16,256]{1,0:T(8,128)} %get-tuple-element.43.refs_3_, ...), custom_call_target="tpu_custom_call" | custom-call | flops 16508780544 | bytes 17563648 | tf_op jit(solution)/shard_map/pallas_call | solution.py:154
  306.7 1.7 collective-permute-start.18
  308.5 1.0 constant_dynamic-update-slice_fusion
  309.4 4.5 %collective-permute-done.18 = bf16[512,256]{1,0:T(8,128)(2,1)S(1)} collective-permute-done((bf16[512,256]{1,0:T(8,128)(2,1)}, bf16[512,256]{1,0:T(8,128)(2,1)S(1)}, u32[]{:S(2)}, u32[]{:S(2)}) %collective-permute-start.18) | collective-permute-done | bytes 262176 | tf_op jit(solution)/shard_map/ppermute | solution.py:194
  314.0 0.1 broadcast_select_fusion.1
  314.2 1.5 pad_maximum_fusion
  (75 shorter events, 1.0 us)
Async XLA Ops:
  6.5 89.9 %all-gather.11.cloned.1.call-start = ((), (), s32[]{:S(2)}) async-start(), calls=%async_computation | async-start | bytes 7864320 | tf_op jit(solution)/shard_map/all_gather | solution.py:261
  10.0 8.0 %copy-start = (bf16[3,256,1024]{2,1,0:T(8,128)(2,1)S(1)}, bf16[3,256,1024]{2,1,0:T(8,128)(2,1)}, u32[]{:S(2)}) copy-start(bf16[3,256,1024]{2,1,0:T(8,128)(2,1)} %get-tuple-element.26) | copy-start | bytes 4718596
  10.1 136.0 %all-gather.13.cloned.1.call-start = ((), (), s32[]{:S(2)}) async-start(), calls=%async_computation.1 | async-start | bytes 5898240 | tf_op jit(solution)/shard_map/all_gather | solution.py:261
  10.1 86.3 %collective-permute-start.3 = (bf16[512,2048]{1,0:T(8,128)(2,1)}, bf16[512,2048]{1,0:T(8,128)(2,1)}, u32[]{:S(2)}, u32[]{:S(2)}) collective-permute-start(bf16[512,2048]{1,0:T(8,128)(2,1)} %refs_5_.7), channel_id=1, source_target_pairs={{0,1},{1,0},{2,3},{3,2},{4,5},{5,4},{6,7},{7,6},{8,9},{9,8},{10,11... | collective-permute-start | bytes 6291464 | tf_op jit(solution)/shard_map/ppermute | solution.py:198
  13.1 83.2 %collective-permute-start.4 = (bf16[512,2048]{1,0:T(8,128)(2,1)}, bf16[512,2048]{1,0:T(8,128)(2,1)}, u32[]{:S(2)}, u32[]{:S(2)}) collective-permute-start(bf16[512,2048]{1,0:T(8,128)(2,1)} %refs_5_.7), channel_id=1, source_target_pairs={{0,8},{2,10},{4,12},{6,14},{8,0},{10,2},{12,4},{14,6},{16,24},{18,... | collective-permute-start | bytes 6291464 | tf_op jit(solution)/shard_map/ppermute | solution.py:194
  15.5 78.7 %collective-permute-start.2 = (bf16[3,256,256]{2,1,0:T(8,128)(2,1)}, bf16[3,256,256]{2,1,0:T(8,128)(2,1)}, u32[]{:S(2)}, u32[]{:S(2)}) collective-permute-start(bf16[3,256,256]{2,1,0:T(8,128)(2,1)} %slice.83), channel_id=1, source_target_pairs={{0,24},{2,26},{4,28},{6,30},{8,16},{10,18},{12,20},{14,22},{16,8},... | collective-permute-start | bytes 1179656 | tf_op jit(solution)/shard_map/ppermute | solution.py:194
  19.2 3.0 copy-start.13
  19.2 5.0 %copy-start.16 = (s32[8]{0:T(128)S(1)}, s32[8]{0:T(128)}, u32[]{:S(2)}) copy-start(s32[8]{0:T(128)} %param.10) | copy-start | bytes 100
  19.2 5.2 %copy-start.11 = (bf16[128,128]{1,0:T(8,128)(2,1)S(1)}, bf16[128,128]{1,0:T(8,128)(2,1)}, u32[]{:S(2)}) copy-start(bf16[128,128]{1,0:T(8,128)(2,1)} %param.9) | copy-start | bytes 98308
  19.2 5.4 %copy-start.12 = (bf16[7,3,2048]{2,0,1:T(8,128)(2,1)S(1)}, bf16[7,3,2048]{2,0,1:T(8,128)(2,1)}, u32[]{:S(2)}) copy-start(bf16[7,3,2048]{2,0,1:T(8,128)(2,1)} %param.8) | copy-start | bytes 258052
  19.2 75.1 %collective-permute-start.1 = (bf16[3,256,256]{2,1,0:T(8,128)(2,1)}, bf16[3,256,256]{2,1,0:T(8,128)(2,1)S(1)}, u32[]{:S(2)}, u32[]{:S(2)}) collective-permute-start(bf16[3,256,256]{2,1,0:T(8,128)(2,1)} %get-tuple-element.32), channel_id=1, source_target_pairs={{0,16},{2,18},{4,20},{6,22},{8,24},{10,26},{12,28},{14,30},{16,0},... | collective-permute-start | bytes 1179656 | tf_op jit(solution)/shard_map/ppermute | solution.py:194
  20.4 73.8 %collective-permute-start = (bf16[3,256,512]{2,1,0:T(8,128)(2,1)}, bf16[3,256,512]{2,1,0:T(8,128)(2,1)S(1)}, u32[]{:S(2)}, u32[]{:S(2)}) collective-permute-start(bf16[3,256,512]{2,1,0:T(8,128)(2,1)} %get-tuple-element.34), channel_id=1, source_target_pairs={{0,8},{2,10},{4,12},{6,14},{8,0},{10,2},{12,4},{14,6},{16,24},{18,... | collective-permute-start | bytes 2359304 | tf_op jit(solution)/shard_map/ppermute | solution.py:194
  96.4 8.3 %copy-start.5 = (bf16[1,3,256,256]{3,2,1,0:T(8,128)(2,1)S(1)}, bf16[1,3,256,256]{3,2,1,0:T(8,128)(2,1)}, u32[]{:S(2)}) copy-start(bf16[1,3,256,256]{3,2,1,0:T(8,128)(2,1)} %get-tuple-element.31) | copy-start | bytes 1179652
  96.4 96.8 %all-gather.15.cloned.1.call-start = ((), (), s32[]{:S(2)}) async-start(), calls=%async_computation.2 | async-start | bytes 5898240 | tf_op jit(solution)/shard_map/all_gather | solution.py:261
  97.6 2.4 collective-permute-start.6
  97.7 48.4 %collective-permute-start.5 = (bf16[512,2048]{1,0:T(8,128)(2,1)}, bf16[512,2048]{1,0:T(8,128)(2,1)}, u32[]{:S(2)}, u32[]{:S(2)}) collective-permute-start(bf16[512,2048]{1,0:T(8,128)(2,1)} %collective-permute-done.4.refs_3_.refs_7_), channel_id=1, source_target_pairs={{0,1},{1,0},{2,3},{3,2},{4,5},{5,4},{6,7},{7,6},{8,9},{9,8},{10,11... | collective-permute-start | bytes 6291464 | tf_op jit(solution)/shard_map/ppermute | solution.py:198
  101.2 29.1 %collective-permute-start.7 = (bf16[144,2048]{1,0:T(8,128)(2,1)S(1)}, bf16[144,2048]{1,0:T(8,128)(2,1)S(1)}, u32[]{:S(2)}, u32[]{:S(2)}) collective-permute-start(bf16[144,2048]{1,0:T(8,128)(2,1)S(1)} %broadcast_select_fusion.3), channel_id=1, source_target_pairs={{0,4},{2,6},{4,8},{6,10},{8,12},{10,14},{12,16},{14,18},{16,20},{1... | collective-permute-start | bytes 1769480 | tf_op jit(solution)/shard_map/ppermute | solution.py:206
  105.7 37.4 %collective-permute-start.11 = (bf16[2,3,256,256]{3,2,1,0:T(8,128)(2,1)}, bf16[2,3,256,256]{3,2,1,0:T(8,128)(2,1)S(1)}, u32[]{:S(2)}, u32[]{:S(2)}) collective-permute-start(bf16[2,3,256,256]{3,2,1,0:T(8,128)(2,1)} %shard_map.66), channel_id=1, source_target_pairs={{0,16},{2,18},{4,20},{6,22},{8,24},{10,26},{12,28},{14,30},{16,0},... | collective-permute-start | bytes 2359304 | tf_op jit(solution)/shard_map/ppermute | solution.py:194
  108.3 35.9 %collective-permute-start.12 = (bf16[3,256,512]{2,1,0:T(8,128)(2,1)S(1)}, bf16[3,256,512]{2,1,0:T(8,128)(2,1)S(1)}, u32[]{:S(2)}, u32[]{:S(2)}) collective-permute-start(bf16[3,256,512]{2,1,0:T(8,128)(2,1)S(1)} %get-tuple-element.33), channel_id=1, source_target_pairs={{0,8},{2,10},{4,12},{6,14},{8,0},{10,2},{12,4},{14,6},{16,24},{18,... | collective-permute-start | bytes 2359304 | tf_op jit(solution)/shard_map/ppermute | solution.py:194
  144.2 1.9 copy-start.1
  146.1 1.1 copy-start.3
  146.1 3.0 copy-start.2
  146.1 3.0 copy-start.4
  146.1 89.0 %all-gather.17.cloned.1.call-start = ((), (), s32[]{:S(2)}) async-start(), calls=%async_computation.3 | async-start | bytes 5898240 | tf_op jit(solution)/shard_map/all_gather | solution.py:261
  147.2 26.9 %collective-permute-start.9 = (bf16[144,2048]{1,0:T(8,128)(2,1)S(1)}, bf16[144,2048]{1,0:T(8,128)(2,1)S(1)}, u32[]{:S(2)}, u32[]{:S(2)}) collective-permute-start(bf16[144,2048]{1,0:T(8,128)(2,1)S(1)} %copy-done.3), channel_id=1, source_target_pairs={{0,8},{2,10},{4,12},{6,14},{8,0},{10,2},{12,4},{14,6},{16,24},{18,... | collective-permute-start | bytes 1769480 | tf_op jit(solution)/shard_map/ppermute | solution.py:194
  150.1 37.4 %collective-permute-start.13 = (bf16[2,3,256,256]{3,2,1,0:T(8,128)(2,1)}, bf16[2,3,256,256]{3,2,1,0:T(8,128)(2,1)S(1)}, u32[]{:S(2)}, u32[]{:S(2)}) collective-permute-start(bf16[2,3,256,256]{3,2,1,0:T(8,128)(2,1)} %shard_map.69), channel_id=1, source_target_pairs={{0,16},{2,18},{4,20},{6,22},{8,24},{10,26},{12,28},{14,30},{16,0},... | collective-permute-start | bytes 2359304 | tf_op jit(solution)/shard_map/ppermute | solution.py:194
  152.7 36.0 %collective-permute-start.8 = (bf16[144,2048]{1,0:T(8,128)(2,1)S(1)}, bf16[144,2048]{1,0:T(8,128)(2,1)S(1)}, u32[]{:S(2)}, u32[]{:S(2)}) collective-permute-start(bf16[144,2048]{1,0:T(8,128)(2,1)S(1)} %copy-done.3), channel_id=1, source_target_pairs={{0,1},{1,0},{2,3},{3,2},{4,5},{5,4},{6,7},{7,6},{8,9},{9,8},{10,11... | collective-permute-start | bytes 1769480 | tf_op jit(solution)/shard_map/ppermute | solution.py:198
  174.1 14.6 %copy-start.14 = (bf16[144,2048]{1,0:T(8,128)(2,1)}, bf16[144,2048]{1,0:T(8,128)(2,1)S(1)}, u32[]{:S(2)}) copy-start(bf16[144,2048]{1,0:T(8,128)(2,1)S(1)} %collective-permute-done.9.refs_11_) | copy-start | bytes 1769476
  174.1 15.1 %collective-permute-start.10 = (bf16[144,2048]{1,0:T(8,128)(2,1)S(1)}, bf16[144,2048]{1,0:T(8,128)(2,1)}, u32[]{:S(2)}, u32[]{:S(2)}) collective-permute-start(bf16[144,2048]{1,0:T(8,128)(2,1)S(1)} %collective-permute-done.9.refs_11_), channel_id=1, source_target_pairs={{0,1},{1,0},{2,3},{3,2},{4,5},{5,4},{6,7},{7,6},{8,9},{9,8},{10,11... | collective-permute-start | bytes 1769480 | tf_op jit(solution)/shard_map/ppermute | solution.py:198
  188.7 4.6 %copy-start.9 = (bf16[144,2048]{1,0:T(8,128)(2,1)}, bf16[144,2048]{1,0:T(8,128)(2,1)S(1)}, u32[]{:S(2)}) copy-start(bf16[144,2048]{1,0:T(8,128)(2,1)S(1)} %collective-permute-done.8.refs_10_.refs_2_) | copy-start | bytes 1769476
  193.2 0.8 copy-start.8
  193.2 1.5 copy-start.7
  193.3 93.2 %all-gather.19.cloned.1.call-start = ((), (), s32[]{:S(2)}) async-start(), calls=%async_computation.4 | async-start | bytes 5898240 | tf_op jit(solution)/shard_map/all_gather | solution.py:261
  196.3 37.7 %collective-permute-start.14 = (bf16[2,3,256,256]{3,2,1,0:T(8,128)(2,1)}, bf16[2,3,256,256]{3,2,1,0:T(8,128)(2,1)S(1)}, u32[]{:S(2)}, u32[]{:S(2)}) collective-permute-start(bf16[2,3,256,256]{3,2,1,0:T(8,128)(2,1)} %shard_map.72), channel_id=1, source_target_pairs={{0,16},{2,18},{4,20},{6,22},{8,24},{10,26},{12,28},{14,30},{16,0},... | collective-permute-start | bytes 2359304 | tf_op jit(solution)/shard_map/ppermute | solution.py:194
  235.1 1.0 copy-start.15
  236.1 22.7 %collective-permute-start.15 = (bf16[512,256]{1,0:T(8,128)(2,1)S(1)}, bf16[512,256]{1,0:T(8,128)(2,1)S(1)}, u32[]{:S(2)}, u32[]{:S(2)}) collective-permute-start(bf16[512,256]{1,0:T(8,128)(2,1)S(1)} %copy-done.15), channel_id=1, source_target_pairs={{0,8},{2,10},{4,12},{6,14},{8,0},{10,2},{12,4},{14,6},{16,24},{18,... | collective-permute-start | bytes 786440 | tf_op jit(solution)/shard_map/ppermute | solution.py:194
  236.7 22.0 %copy-start.6 = (bf16[512,256]{1,0:T(8,128)(2,1)S(1)}, bf16[512,256]{1,0:T(8,128)(2,1)}, u32[]{:S(2)}) copy-start(bf16[512,256]{1,0:T(8,128)(2,1)} %get-tuple-element.13.refs_2_) | copy-start | bytes 786436
  257.4 8.4 %collective-permute-start.16 = (bf16[512,256]{1,0:T(8,128)(2,1)}, bf16[512,256]{1,0:T(8,128)(2,1)S(1)}, u32[]{:S(2)}, u32[]{:S(2)}) collective-permute-start(bf16[512,256]{1,0:T(8,128)(2,1)} %get-tuple-element.18), channel_id=1, source_target_pairs={{0,8},{2,10},{4,12},{6,14},{8,0},{10,2},{12,4},{14,6},{16,24},{18,... | collective-permute-start | bytes 786440 | tf_op jit(solution)/shard_map/ppermute | solution.py:194
  286.0 22.4 %collective-permute-start.17 = (bf16[512,256]{1,0:T(8,128)(2,1)}, bf16[512,256]{1,0:T(8,128)(2,1)S(1)}, u32[]{:S(2)}, u32[]{:S(2)}) collective-permute-start(bf16[512,256]{1,0:T(8,128)(2,1)} %get-tuple-element.19), channel_id=1, source_target_pairs={{0,8},{2,10},{4,12},{6,14},{8,0},{10,2},{12,4},{14,6},{16,24},{18,... | collective-permute-start | bytes 786440 | tf_op jit(solution)/shard_map/ppermute | solution.py:194
  286.4 21.9 %copy-start.10 = (bf16[512,256]{1,0:T(8,128)(2,1)S(1)}, bf16[512,256]{1,0:T(8,128)(2,1)}, u32[]{:S(2)}) copy-start(bf16[512,256]{1,0:T(8,128)(2,1)} %get-tuple-element.15) | copy-start | bytes 786436
  306.7 7.3 %collective-permute-start.18 = (bf16[512,256]{1,0:T(8,128)(2,1)}, bf16[512,256]{1,0:T(8,128)(2,1)S(1)}, u32[]{:S(2)}, u32[]{:S(2)}) collective-permute-start(bf16[512,256]{1,0:T(8,128)(2,1)} %get-tuple-element.20), channel_id=1, source_target_pairs={{0,8},{2,10},{4,12},{6,14},{8,0},{10,2},{12,4},{14,6},{16,24},{18,... | collective-permute-start | bytes 786440 | tf_op jit(solution)/shard_map/ppermute | solution.py:194
Sparse Core Ops, SparseCore 0:
  10.2 49.0 all-gather.10
  96.6 46.4 all-gather.12
  146.3 46.9 all-gather.14
  194.6 39.6 all-gather.16
  235.7 37.4 all-gather.18

commit v9 on v8

--- a/solution.py
+++ b/solution.py
@@ -10,7 +10,7 @@
 ROW_TILE = 256
 CHAN_TILE = 256
 LANES = 128
-WIDTHS = [256, 256, 256, 256]
+WIDTHS = [256, 256, 384, 128]
 
 
 def in_sequence(places, seq_lengths):
@@ -241,7 +241,7 @@
         places = stretch_at(device) * row_count - reach + jnp.arange(reach + row_count, dtype=jnp.int32)
         return jnp.broadcast_to(in_sequence(places, seq_lengths)[:, None], (reach + row_count, LANES))
 
-    if devices != 16 or lax.axis_size("chan") != 2:
+    if devices != 16 or lax.axis_size("chan") != 2 or chans != 2 * sum(WIDTHS):
         weight = lax.all_gather(local, "stretch", axis=0, tiled=False)
         halo = rows_before(tokens, stretch_at(me), reach)
         halo = lax.all_gather(halo, "chan", axis=1, tiled=True)
@@ -252,7 +252,7 @@
     kind = (me >> 2) & 1
     half = chans // 2
     own_begin, other_begin = kind * half, (1 - kind) * half
-    widths = WIDTHS if sum(WIDTHS) == half else [half]
+    widths = WIDTHS
     begins = [sum(widths[:c]) for c in range(len(widths))]
 
     planes = [[4 * z + q for q in range(4)] for z in range(devices // 4)]
@@ -287,6 +287,27 @@
     after[0] += [pos, own_sw, own_fr]
     gathered, stack = [spread(own[None])], None
     mine, theirs = [], []
+
+    def convolve(c, scale):
+        for start in range(0, widths[c], CHAN_TILE):
+            width = min(CHAN_TILE, widths[c] - start)
+            first = begins[c] + start
+            groups, first_group = (n * fr.shape[0] // chans for n in (width, first))
+            out, peer_out = block(
+                at,
+                [[tokens, rows_other], [peer_rows, peer_rows_other]],
+                [[halo, halo_other], [peer_halo, peer_halo_other]],
+                [(first, gathered[0]), (start, gathered[c + 1])],
+                scale[:, :, first : first + width],
+                own_fr[first_group : first_group + groups],
+                pos,
+                span,
+                width,
+            )
+            mine.append(out)
+            theirs.append(flip(peer_out, 4))
+
+    last = len(widths) - 1
     for c, (begin, width) in enumerate(zip(begins, widths)):
         if c == 0:
             stack = jnp.stack(firsts)
@@ -296,24 +317,14 @@
             peer = peers[late][:, :, begin - late * early : begin - late * early + width]
             pair = tied(jnp.stack([same, peer]), stack)
             stack = jnp.concatenate([peer[None], flip(pair, 8)])
+        if c == last:
+            convolve(0, own_sw)
+            convolve(1, tied(own_sw, stack))
+            after[c] = after.get(c, []) + mine
         stack = tied(stack, gathered[-1], *after.get(c, []))
         gathered.append(spread(stack))
-        groups = fr.shape[0] * width // chans
-        first_group = begin * fr.shape[0] // chans
-        out, peer_out = block(
-            at,
-            [[tokens, rows_other], [peer_rows, peer_rows_other]],
-            [[halo, halo_other], [peer_halo, peer_halo_other]],
-            [(begin, gathered[0]), (0, gathered[c + 1])],
-            own_sw[:, :, begin : begin + width],
-            own_fr[first_group : first_group + groups],
-            pos,
-            span,
-            width,
-        )
-        mine.append(out)
-        theirs.append(flip(peer_out, 4))
-        after[c + 3] = after.get(c + 3, []) + [out]
+    for c in range(2, len(widths)):
+        convolve(c, own_sw)
     mine, theirs = jnp.concatenate(mine, axis=1), jnp.concatenate(theirs, axis=1)
     even = kind == 0
     return jnp.concatenate([jnp.where(even, mine, theirs), jnp.where(even, theirs, mine)], axis=1)

time: 323 us -> 343 us (1.062)
  Pallas kernels: 81.5 us -> 88.8 us
  waiting for transfers between devices: 163 us -> 170 us
  local copies, waits for them, and re-layouts: 13.7 us -> 17.8 us
    pallas_call x4 -> x5, Pallas kernels: 81.5 us -> 88.8 us  [block(): pl.pallas_call(functools.partial(block_kernel, runs, halves, len(weights)...]
    all_gather x5, waiting for transfers between devices: 4.09 us -> 8.87 us  [spread(): lax.all_gather(array, 'stretch', axis=0, tiled=False, axis_index_groups=p...]
    ppermute x14 -> x15, waiting for transfers between devices: 136 us -> 139 us  [flip(): lax.ppermute(array, 'stretch', [(i, i ^ bit) for i in range(lax.axis_size...]
    ppermute x14 -> x15, starting transfers between devices: 21.2 us -> 22.1 us  [flip(): lax.ppermute(array, 'stretch', [(i, i ^ bit) for i in range(lax.axis_size...]
  transfers between devices with their start and end apart: 24 -> 25, of which waited for: 11 -> 10; matrix products, arithmetic and copies ran while one was open for 7% -> 8% of each run, Pallas kernels for 25% -> 26%
where the time goes in v9:
time: 343 us
  waiting for transfers between devices  170 us (50%)
  Pallas kernels  88.8 us (26%)
  starting transfers between devices  32.3 us (9%)
  local copies, waits for them, and re-layouts  17.8 us (5%)
  other arithmetic  17 us (5%)
  between operations  16.6 us (5%)
    ppermute x15, waiting for transfers between devices, flip(): lax.ppermute(array, 'stretch', [(i, i ^ bit) for i in range(lax.axis_size...  139 us
    pallas_call x5, Pallas kernels, block(): pl.pallas_call(functools.partial(block_kernel, runs, halves, len(weights)...  88.8 us
    ppermute x15, starting transfers between devices, flip(): lax.ppermute(array, 'stretch', [(i, i ^ bit) for i in range(lax.axis_size...  22.1 us
    ppermute x1, waiting for transfers between devices, rows_before(): before = lax.ppermute(jnp.where(second, tail, sibling), 'stretch', pairs)  20.4 us
    all_gather x5, waiting for transfers between devices, spread(): lax.all_gather(array, 'stretch', axis=0, tiled=False, axis_index_groups=p...  8.87 us
  transfers between devices with their start and end apart: 25, of which 10 were waited for; matrix products, arithmetic and copies ran while one was open for 8% of the time, Pallas kernels for 26%

profile of v9, /device:TPU:0, one launch (start us, length us, event | category | flops | bytes accessed | tf_op | source)
XLA Modules:
  0.0 342.5 jit_solution(10679042879257649061)
XLA Ops:
  6.5 3.5 %dynamic-slice_bitcast_fusion = (bf16[3,256,1024]{2,1,0:T(8,128)(2,1)S(1)}, bf16[3,256,1024]{2,1,0:T(8,128)(2,1)}) fusion(bf16[256,3,2048]{2,0,1:T(8,128)(2,1)} %param.7, s32[]{:T(128)S(6)} %select_n.62, s32[]{:T(128)S(6)} %select_n.61), kind=kLoop, calls=%fused_computation.2 | loop fusion | bytes 6291464 | tf_op jit(solution)/shard_map/dynamic_slice | solution.py:264
  10.1 3.0 collective-permute-start.3
  13.1 1.6 collective-permute-start.4
  14.7 0.8 slice.91
  15.5 2.5 collective-permute-start.2
  18.0 0.8 slice_bitcast_fusion.2
  18.9 1.3 fusion.3
  20.3 1.8 collective-permute-start
  22.0 0.7 fusion.1
  24.1 0.9 copy.17
  25.1 1.5 convert_bitcast_fusion.refs_5_.refs_0_
  26.7 0.7 fusion.refs_6_
  27.7 0.9 pad_add_fusion.refs_4_
  28.6 65.5 %collective-permute-done = bf16[3,256,512]{2,1,0:T(8,128)(2,1)S(1)} collective-permute-done((bf16[3,256,512]{2,1,0:T(8,128)(2,1)}, bf16[3,256,512]{2,1,0:T(8,128)(2,1)S(1)}, u32[]{:S(2)}, u32[]{:S(2)}) %collective-permute-start) | collective-permute-done | bytes 786464 | tf_op jit(solution)/shard_map/ppermute | solution.py:194
  94.2 2.3 pad_maximum_fusion.2.refs_0_
  96.6 1.1 slice.72
  97.8 0.4 collective-permute-start.5
  100.1 1.1 broadcast_select_fusion.3
  101.2 3.6 %collective-permute-start.7 = (bf16[144,2048]{1,0:T(8,128)(2,1)S(1)}, bf16[144,2048]{1,0:T(8,128)(2,1)S(1)}, u32[]{:S(2)}, u32[]{:S(2)}) collective-permute-start(bf16[144,2048]{1,0:T(8,128)(2,1)S(1)} %broadcast_select_fusion.3), channel_id=1, source_target_pairs={{0,4},{2,6},{4,8},{6,10},{8,12},{10,14},{12,16},{14,18},{16,20},{1... | collective-permute-start | bytes 1769480 | tf_op jit(solution)/shard_map/ppermute | solution.py:206
  104.8 0.9 pad_maximum_fusion.5.refs_0_
  105.8 2.6 collective-permute-start.11
  108.3 1.6 collective-permute-start.12
  109.9 20.4 %collective-permute-done.7 = bf16[144,2048]{1,0:T(8,128)(2,1)S(1)} collective-permute-done((bf16[144,2048]{1,0:T(8,128)(2,1)S(1)}, bf16[144,2048]{1,0:T(8,128)(2,1)S(1)}, u32[]{:S(2)}, u32[]{:S(2)}) %collective-permute-start.7) | collective-permute-done | bytes 589856 | tf_op jit(solution)/shard_map/ppermute | solution.py:206
  130.3 0.9 broadcast_select_fusion.2.refs_9_.refs_3_
  131.2 11.9 %collective-permute-done.11 = bf16[2,3,256,256]{3,2,1,0:T(8,128)(2,1)S(1)} collective-permute-done((bf16[2,3,256,256]{3,2,1,0:T(8,128)(2,1)}, bf16[2,3,256,256]{3,2,1,0:T(8,128)(2,1)S(1)}, u32[]{:S(2)}, u32[]{:S(2)}) %collective-permute-start.11) | collective-permute-done | bytes 786464 | tf_op jit(solution)/shard_map/ppermute | solution.py:194
  143.1 1.2 pad_maximum_fusion.3.refs_0_
  144.3 1.8 collective-permute-done.5.refs_8_.refs_2_
  146.3 1.0 copy-done.2
  147.4 1.1 pad_maximum_fusion.4.refs_0_
  148.5 2.9 collective-permute-start.13
  151.4 1.6 collective-permute-start.9
  153.0 1.5 collective-permute-start.8
  154.5 35.4 %collective-permute-done.9.refs_11_ = bf16[144,2048]{1,0:T(8,128)(2,1)S(1)} collective-permute-done((bf16[144,2048]{1,0:T(8,128)(2,1)S(1)}, bf16[144,2048]{1,0:T(8,128)(2,1)S(1)}, u32[]{:S(2)}, u32[]{:S(2)}) %collective-permute-start.9) | collective-permute-done | bytes 589856 | tf_op jit(solution)/shard_map/ppermute | solution.py:194
  190.0 1.5 collective-permute-start.10
  191.5 11.8 %collective-permute-done.13 = bf16[2,3,256,384]{3,2,1,0:T(8,128)(2,1)S(1)} collective-permute-done((bf16[2,3,256,384]{3,2,1,0:T(8,128)(2,1)}, bf16[2,3,256,384]{3,2,1,0:T(8,128)(2,1)S(1)}, u32[]{:S(2)}, u32[]{:S(2)}) %collective-permute-start.13) | collective-permute-done | bytes 1179680 | tf_op jit(solution)/shard_map/ppermute | solution.py:194
  203.3 1.4 pad_maximum_fusion.1.refs_0_
  204.7 0.8 copy-done.9
  205.6 0.7 pad_add_fusion.1.at_ref
  206.4 0.6 fusion.4
  207.0 0.6 fusion.7
  207.7 0.6 fusion.5
  208.4 0.8 pad_maximum_fusion.7.refs_0_
  209.1 1.7 collective-permute-start.14
  210.8 19.9 %shard_map.65 = (bf16[512,256]{1,0:T(8,128)(2,1)}, bf16[512,256]{1,0:T(8,128)(2,1)}) custom-call(s32[4]{0:T(128)} %pad_add_fusion.1.at_ref, bf16[4,1,3,256,1024]{4,3,2,1,0:T(8,128)(2,1)} %bitcast.39, bf16[4,3,3,256,256]{4,3,2,1,0:T(8,128)(2,1)} %bitcast.45, f32[3,7,256]{2,1,0:T(8,128)} %get-tuple-element.42.refs_2_, f32[16,256]{1,0:T(8,128)} %get-tuple-element.47.refs_3_, ...), custom_call_target="tpu_custom_call" | custom-call | flops 16508780544 | bytes 17563648 | tf_op jit(solution)/shard_map/pallas_call | solution.py:154
  230.8 0.9 pad_maximum_fusion.6.refs_1_.refs_0_
  231.6 1.3 slice.101.refs_2_
  233.0 20.1 %shard_map.72 = (bf16[512,256]{1,0:T(8,128)(2,1)}, bf16[512,256]{1,0:T(8,128)(2,1)}) custom-call(s32[4]{0:T(128)} %pad_add_fusion.1.at_ref, bf16[4,1,3,256,1024]{4,3,2,1,0:T(8,128)(2,1)} %bitcast.40, bf16[4,3,3,256,256]{4,3,2,1,0:T(8,128)(2,1)} %bitcast.47, f32[3,7,256]{2,1,0:T(8,128)} %slice.101.refs_2_, f32[16,256]{1,0:T(8,128)} %get-tuple-element.46.refs_3_, ...), custom_call_target="tpu_custom_call" | custom-call | flops 16508780544 | bytes 17563648 | tf_op jit(solution)/shard_map/pallas_call | solution.py:154
  253.1 8.8 %all-gather.17.cloned.1.call-done = bf16[12,3,256,384]{3,2,1,0:T(8,128)(2,1)} async-done(((bf16[3,3,256,384]{3,2,1,0:T(8,128)(2,1)}), bf16[12,3,256,384]{3,2,1,0:T(8,128)(2,1)}) %all-gather.17.cloned.1.call-update) | async-done | bytes 7077904 | tf_op jit(solution)/shard_map/all_gather | solution.py:261
  262.0 0.9 copy-done.13
  262.9 1.5 collective-permute-start.15
  264.4 0.6 fusion.6
  265.0 0.5 collective-permute-start.16
  265.6 6.5 %collective-permute-done.15 = bf16[512,256]{1,0:T(8,128)(2,1)S(1)} collective-permute-done((bf16[512,256]{1,0:T(8,128)(2,1)S(1)}, bf16[512,256]{1,0:T(8,128)(2,1)S(1)}, u32[]{:S(2)}, u32[]{:S(2)}) %collective-permute-start.15) | collective-permute-done | bytes 262176 | tf_op jit(solution)/shard_map/ppermute | solution.py:194
  272.1 4.9 %collective-permute-done.16 = bf16[512,256]{1,0:T(8,128)(2,1)S(1)} collective-permute-done((bf16[512,256]{1,0:T(8,128)(2,1)S(1)}, bf16[512,256]{1,0:T(8,128)(2,1)S(1)}, u32[]{:S(2)}, u32[]{:S(2)}) %collective-permute-start.16) | collective-permute-done | bytes 262176 | tf_op jit(solution)/shard_map/ppermute | solution.py:194
  277.0 20.1 %shard_map.73 = (bf16[512,256]{1,0:T(8,128)(2,1)}, bf16[512,256]{1,0:T(8,128)(2,1)}) custom-call(s32[4]{0:T(128)} %pad_add_fusion.1.at_ref, bf16[4,1,3,256,1024]{4,3,2,1,0:T(8,128)(2,1)} %bitcast.41, bf16[4,3,3,256,384]{4,3,2,1,0:T(8,128)(2,1)} %bitcast.36, f32[3,7,256]{2,1,0:T(8,128)} %get-tuple-element.41.refs_2_, f32[16,256]{1,0:T(8,128)} %get-tuple-element.45.refs_3_, ...), custom_call_target="tpu_custom_call" | custom-call | flops 16508780544 | bytes 17563648 | tf_op jit(solution)/shard_map/pallas_call | solution.py:154
  297.2 1.6 collective-permute-start.17
  298.8 14.2 %shard_map.74 = (bf16[512,128]{1,0:T(8,128)(2,1)}, bf16[512,128]{1,0:T(8,128)(2,1)}) custom-call(s32[4]{0:T(128)} %pad_add_fusion.1.at_ref, bf16[4,1,3,256,1024]{4,3,2,1,0:T(8,128)(2,1)} %bitcast.42, bf16[4,3,3,256,384]{4,3,2,1,0:T(8,128)(2,1)} %bitcast.37, f32[3,7,128]{2,1,0:T(8,128)} %get-tuple-element.40.refs_2_, f32[8,256]{1,0:T(8,128)} %get-tuple-element.44.refs_3_, ...), custom_call_target="tpu_custom_call" | custom-call | flops 8254390272 | bytes 14155776 | tf_op jit(solution)/shard_map/pallas_call | solution.py:154
  313.0 0.6 collective-permute-start.18
  313.6 0.9 constant_dynamic-update-slice_fusion.1
  314.6 14.4 %shard_map.76 = (bf16[512,128]{1,0:T(8,128)(2,1)}, bf16[512,128]{1,0:T(8,128)(2,1)}) custom-call(s32[4]{0:T(128)} %pad_add_fusion.1.at_ref, bf16[4,1,3,256,1024]{4,3,2,1,0:T(8,128)(2,1)} %bitcast.43, bf16[4,3,3,256,128]{4,3,2,1,0:T(8,128)(2,1)} %bitcast.50, f32[3,7,128]{2,1,0:T(8,128)} %get-tuple-element.39.refs_2_, f32[8,256]{1,0:T(8,128)} %get-tuple-element.43.refs_3_, ...), custom_call_target="tpu_custom_call" | custom-call | flops 8254390272 | bytes 14155776 | tf_op jit(solution)/shard_map/pallas_call | solution.py:154
  329.1 1.6 collective-permute-start.19
  330.7 0.9 constant_dynamic-update-slice_fusion
  331.6 2.7 collective-permute-done.19
  334.5 1.5 pad_maximum_fusion
  (85 shorter events, 2.0 us)
Async XLA Ops:
  6.5 90.0 %all-gather.11.cloned.1.call-start = ((), (), s32[]{:S(2)}) async-start(), calls=%async_computation | async-start | bytes 7864320 | tf_op jit(solution)/shard_map/all_gather | solution.py:261
  10.0 8.0 %copy-start = (bf16[3,256,1024]{2,1,0:T(8,128)(2,1)S(1)}, bf16[3,256,1024]{2,1,0:T(8,128)(2,1)}, u32[]{:S(2)}) copy-start(bf16[3,256,1024]{2,1,0:T(8,128)(2,1)} %get-tuple-element.30) | copy-start | bytes 4718596
  10.1 136.1 %all-gather.13.cloned.1.call-start = ((), (), s32[]{:S(2)}) async-start(), calls=%async_computation.1 | async-start | bytes 5898240 | tf_op jit(solution)/shard_map/all_gather | solution.py:261
  10.1 86.4 %collective-permute-start.3 = (bf16[512,2048]{1,0:T(8,128)(2,1)}, bf16[512,2048]{1,0:T(8,128)(2,1)}, u32[]{:S(2)}, u32[]{:S(2)}) collective-permute-start(bf16[512,2048]{1,0:T(8,128)(2,1)} %refs_5_.9), channel_id=1, source_target_pairs={{0,1},{1,0},{2,3},{3,2},{4,5},{5,4},{6,7},{7,6},{8,9},{9,8},{10,11... | collective-permute-start | bytes 6291464 | tf_op jit(solution)/shard_map/ppermute | solution.py:198
  13.1 83.3 %collective-permute-start.4 = (bf16[512,2048]{1,0:T(8,128)(2,1)}, bf16[512,2048]{1,0:T(8,128)(2,1)}, u32[]{:S(2)}, u32[]{:S(2)}) collective-permute-start(bf16[512,2048]{1,0:T(8,128)(2,1)} %refs_5_.9), channel_id=1, source_target_pairs={{0,8},{2,10},{4,12},{6,14},{8,0},{10,2},{12,4},{14,6},{16,24},{18,... | collective-permute-start | bytes 6291464 | tf_op jit(solution)/shard_map/ppermute | solution.py:194
  15.5 78.7 %collective-permute-start.2 = (bf16[3,256,256]{2,1,0:T(8,128)(2,1)}, bf16[3,256,256]{2,1,0:T(8,128)(2,1)}, u32[]{:S(2)}, u32[]{:S(2)}) collective-permute-start(bf16[3,256,256]{2,1,0:T(8,128)(2,1)} %slice.91), channel_id=1, source_target_pairs={{0,24},{2,26},{4,28},{6,30},{8,16},{10,18},{12,20},{14,22},{16,8},... | collective-permute-start | bytes 1179656 | tf_op jit(solution)/shard_map/ppermute | solution.py:194
  18.8 3.2 copy-start.11
  18.8 5.1 %copy-start.15 = (s32[8]{0:T(128)S(1)}, s32[8]{0:T(128)}, u32[]{:S(2)}) copy-start(s32[8]{0:T(128)} %param.10) | copy-start | bytes 100
  18.8 75.4 %collective-permute-start.1 = (bf16[3,256,256]{2,1,0:T(8,128)(2,1)}, bf16[3,256,256]{2,1,0:T(8,128)(2,1)}, u32[]{:S(2)}, u32[]{:S(2)}) collective-permute-start(bf16[3,256,256]{2,1,0:T(8,128)(2,1)} %get-tuple-element.36), channel_id=1, source_target_pairs={{0,16},{2,18},{4,20},{6,22},{8,24},{10,26},{12,28},{14,30},{16,0},... | collective-permute-start | bytes 1179656 | tf_op jit(solution)/shard_map/ppermute | solution.py:194
  20.3 73.9 %collective-permute-start = (bf16[3,256,512]{2,1,0:T(8,128)(2,1)}, bf16[3,256,512]{2,1,0:T(8,128)(2,1)S(1)}, u32[]{:S(2)}, u32[]{:S(2)}) collective-permute-start(bf16[3,256,512]{2,1,0:T(8,128)(2,1)} %get-tuple-element.34), channel_id=1, source_target_pairs={{0,8},{2,10},{4,12},{6,14},{8,0},{10,2},{12,4},{14,6},{16,24},{18,... | collective-permute-start | bytes 2359304 | tf_op jit(solution)/shard_map/ppermute | solution.py:194
  96.5 108.2 %all-gather.15.cloned.1.call-start = ((), (), s32[]{:S(2)}) async-start(), calls=%async_computation.2 | async-start | bytes 5898240 | tf_op jit(solution)/shard_map/all_gather | solution.py:261
  97.7 2.4 collective-permute-start.6
  97.8 48.4 %collective-permute-start.5 = (bf16[512,2048]{1,0:T(8,128)(2,1)}, bf16[512,2048]{1,0:T(8,128)(2,1)}, u32[]{:S(2)}, u32[]{:S(2)}) collective-permute-start(bf16[512,2048]{1,0:T(8,128)(2,1)} %collective-permute-done.4.refs_3_.refs_7_), channel_id=1, source_target_pairs={{0,1},{1,0},{2,3},{3,2},{4,5},{5,4},{6,7},{7,6},{8,9},{9,8},{10,11... | collective-permute-start | bytes 6291464 | tf_op jit(solution)/shard_map/ppermute | solution.py:198
  101.2 29.1 %collective-permute-start.7 = (bf16[144,2048]{1,0:T(8,128)(2,1)S(1)}, bf16[144,2048]{1,0:T(8,128)(2,1)S(1)}, u32[]{:S(2)}, u32[]{:S(2)}) collective-permute-start(bf16[144,2048]{1,0:T(8,128)(2,1)S(1)} %broadcast_select_fusion.3), channel_id=1, source_target_pairs={{0,4},{2,6},{4,8},{6,10},{8,12},{10,14},{12,16},{14,18},{16,20},{1... | collective-permute-start | bytes 1769480 | tf_op jit(solution)/shard_map/ppermute | solution.py:206
  105.8 2.6 copy-start.7
  105.8 37.4 %collective-permute-start.11 = (bf16[2,3,256,256]{3,2,1,0:T(8,128)(2,1)}, bf16[2,3,256,256]{3,2,1,0:T(8,128)(2,1)S(1)}, u32[]{:S(2)}, u32[]{:S(2)}) collective-permute-start(bf16[2,3,256,256]{3,2,1,0:T(8,128)(2,1)} %shard_map.66), channel_id=1, source_target_pairs={{0,16},{2,18},{4,20},{6,22},{8,24},{10,26},{12,28},{14,30},{16,0},... | collective-permute-start | bytes 2359304 | tf_op jit(solution)/shard_map/ppermute | solution.py:194
  108.3 36.0 %collective-permute-start.12 = (bf16[3,256,512]{2,1,0:T(8,128)(2,1)S(1)}, bf16[3,256,512]{2,1,0:T(8,128)(2,1)S(1)}, u32[]{:S(2)}, u32[]{:S(2)}) collective-permute-start(bf16[3,256,512]{2,1,0:T(8,128)(2,1)S(1)} %copy-done.7), channel_id=1, source_target_pairs={{0,8},{2,10},{4,12},{6,14},{8,0},{10,2},{12,4},{14,6},{16,24},{18,... | collective-permute-start | bytes 2359304 | tf_op jit(solution)/shard_map/ppermute | solution.py:194
  144.3 1.8 copy-start.1
  146.2 1.1 copy-start.2
  146.2 115.8 %all-gather.17.cloned.1.call-start = ((), (), s32[]{:S(2)}) async-start(), calls=%async_computation.3 | async-start | bytes 8847360 | tf_op jit(solution)/shard_map/all_gather | solution.py:261
  148.5 2.9 copy-start.3
  148.5 54.8 %collective-permute-start.13 = (bf16[2,3,256,384]{3,2,1,0:T(8,128)(2,1)}, bf16[2,3,256,384]{3,2,1,0:T(8,128)(2,1)S(1)}, u32[]{:S(2)}, u32[]{:S(2)}) collective-permute-start(bf16[2,3,256,384]{3,2,1,0:T(8,128)(2,1)} %shard_map.68), channel_id=1, source_target_pairs={{0,16},{2,18},{4,20},{6,22},{8,24},{10,26},{12,28},{14,30},{16,0},... | collective-permute-start | bytes 3538952 | tf_op jit(solution)/shard_map/ppermute | solution.py:194
  151.4 38.5 %collective-permute-start.9 = (bf16[144,2048]{1,0:T(8,128)(2,1)S(1)}, bf16[144,2048]{1,0:T(8,128)(2,1)S(1)}, u32[]{:S(2)}, u32[]{:S(2)}) collective-permute-start(bf16[144,2048]{1,0:T(8,128)(2,1)S(1)} %copy-done.3), channel_id=1, source_target_pairs={{0,8},{2,10},{4,12},{6,14},{8,0},{10,2},{12,4},{14,6},{16,24},{18,... | collective-permute-start | bytes 1769480 | tf_op jit(solution)/shard_map/ppermute | solution.py:194
  153.0 51.7 %collective-permute-start.8 = (bf16[144,2048]{1,0:T(8,128)(2,1)S(1)}, bf16[144,2048]{1,0:T(8,128)(2,1)S(1)}, u32[]{:S(2)}, u32[]{:S(2)}) collective-permute-start(bf16[144,2048]{1,0:T(8,128)(2,1)S(1)} %copy-done.3), channel_id=1, source_target_pairs={{0,1},{1,0},{2,3},{3,2},{4,5},{5,4},{6,7},{7,6},{8,9},{9,8},{10,11... | collective-permute-start | bytes 1769480 | tf_op jit(solution)/shard_map/ppermute | solution.py:198
  190.0 14.7 %copy-start.12 = (bf16[144,2048]{1,0:T(8,128)(2,1)}, bf16[144,2048]{1,0:T(8,128)(2,1)S(1)}, u32[]{:S(2)}) copy-start(bf16[144,2048]{1,0:T(8,128)(2,1)S(1)} %collective-permute-done.9.refs_11_) | copy-start | bytes 1769476
  190.0 14.8 %collective-permute-start.10 = (bf16[144,2048]{1,0:T(8,128)(2,1)S(1)}, bf16[144,2048]{1,0:T(8,128)(2,1)}, u32[]{:S(2)}, u32[]{:S(2)}) collective-permute-start(bf16[144,2048]{1,0:T(8,128)(2,1)S(1)} %collective-permute-done.9.refs_11_), channel_id=1, source_target_pairs={{0,1},{1,0},{2,3},{3,2},{4,5},{5,4},{6,7},{7,6},{8,9},{9,8},{10,11... | collective-permute-start | bytes 1769480 | tf_op jit(solution)/shard_map/ppermute | solution.py:198
  204.7 0.8 copy-start.9
  205.5 0.9 copy-start.4
  205.5 1.5 copy-start.8
  205.6 109.1 %all-gather.19.cloned.1.call-start = ((), (), s32[]{:S(2)}) async-start(), calls=%async_computation.4 | async-start | bytes 2949120 | tf_op jit(solution)/shard_map/all_gather | solution.py:261
  209.1 21.6 %collective-permute-start.14 = (bf16[2,3,256,128]{3,2,1,0:T(8,128)(2,1)}, bf16[2,3,256,128]{3,2,1,0:T(8,128)(2,1)S(1)}, u32[]{:S(2)}, u32[]{:S(2)}) collective-permute-start(bf16[2,3,256,128]{3,2,1,0:T(8,128)(2,1)} %shard_map.70), channel_id=1, source_target_pairs={{0,16},{2,18},{4,20},{6,22},{8,24},{10,26},{12,28},{14,30},{16,0},... | collective-permute-start | bytes 1179656 | tf_op jit(solution)/shard_map/ppermute | solution.py:194
  262.0 0.9 copy-start.13
  262.0 3.0 copy-start.14
  262.0 3.6 %copy-start.5 = (bf16[512,256]{1,0:T(8,128)(2,1)S(1)}, bf16[512,256]{1,0:T(8,128)(2,1)}, u32[]{:S(2)}) copy-start(bf16[512,256]{1,0:T(8,128)(2,1)} %get-tuple-element.15.refs_2_) | copy-start | bytes 786436
  262.0 10.1 %copy-start.6 = (bf16[512,256]{1,0:T(8,128)(2,1)S(1)}, bf16[512,256]{1,0:T(8,128)(2,1)}, u32[]{:S(2)}) copy-start(bf16[512,256]{1,0:T(8,128)(2,1)} %get-tuple-element.16.refs_3_) | copy-start | bytes 786436
  262.9 9.1 %collective-permute-start.15 = (bf16[512,256]{1,0:T(8,128)(2,1)S(1)}, bf16[512,256]{1,0:T(8,128)(2,1)S(1)}, u32[]{:S(2)}, u32[]{:S(2)}) collective-permute-start(bf16[512,256]{1,0:T(8,128)(2,1)S(1)} %copy-done.13), channel_id=1, source_target_pairs={{0,8},{2,10},{4,12},{6,14},{8,0},{10,2},{12,4},{14,6},{16,24},{18,... | collective-permute-start | bytes 786440 | tf_op jit(solution)/shard_map/ppermute | solution.py:194
  265.0 12.0 %collective-permute-start.16 = (bf16[512,256]{1,0:T(8,128)(2,1)S(1)}, bf16[512,256]{1,0:T(8,128)(2,1)S(1)}, u32[]{:S(2)}, u32[]{:S(2)}) collective-permute-start(bf16[512,256]{1,0:T(8,128)(2,1)S(1)} %copy-done.14), channel_id=1, source_target_pairs={{0,8},{2,10},{4,12},{6,14},{8,0},{10,2},{12,4},{14,6},{16,24},{18,... | collective-permute-start | bytes 786440 | tf_op jit(solution)/shard_map/ppermute | solution.py:194
  297.2 17.4 %collective-permute-start.17 = (bf16[512,256]{1,0:T(8,128)(2,1)}, bf16[512,256]{1,0:T(8,128)(2,1)S(1)}, u32[]{:S(2)}, u32[]{:S(2)}) collective-permute-start(bf16[512,256]{1,0:T(8,128)(2,1)} %get-tuple-element.22), channel_id=1, source_target_pairs={{0,8},{2,10},{4,12},{6,14},{8,0},{10,2},{12,4},{14,6},{16,24},{18,... | collective-permute-start | bytes 786440 | tf_op jit(solution)/shard_map/ppermute | solution.py:194
  298.8 14.8 %copy-start.10 = (bf16[512,256]{1,0:T(8,128)(2,1)S(1)}, bf16[512,256]{1,0:T(8,128)(2,1)}, u32[]{:S(2)}) copy-start(bf16[512,256]{1,0:T(8,128)(2,1)} %get-tuple-element.17) | copy-start | bytes 786436
  313.0 17.7 %collective-permute-start.18 = (bf16[512,128]{1,0:T(8,128)(2,1)}, bf16[512,128]{1,0:T(8,128)(2,1)S(1)}, u32[]{:S(2)}, u32[]{:S(2)}) collective-permute-start(bf16[512,128]{1,0:T(8,128)(2,1)} %get-tuple-element.23), channel_id=1, source_target_pairs={{0,8},{2,10},{4,12},{6,14},{8,0},{10,2},{12,4},{14,6},{16,24},{18,... | collective-permute-start | bytes 393224 | tf_op jit(solution)/shard_map/ppermute | solution.py:194
  329.1 5.2 %collective-permute-start.19 = (bf16[512,128]{1,0:T(8,128)(2,1)}, bf16[512,128]{1,0:T(8,128)(2,1)S(1)}, u32[]{:S(2)}, u32[]{:S(2)}) collective-permute-start(bf16[512,128]{1,0:T(8,128)(2,1)} %get-tuple-element.24), channel_id=1, source_target_pairs={{0,8},{2,10},{4,12},{6,14},{8,0},{10,2},{12,4},{14,6},{16,24},{18,... | collective-permute-start | bytes 393224 | tf_op jit(solution)/shard_map/ppermute | solution.py:194
Sparse Core Ops, SparseCore 0:
  10.2 49.0 all-gather.10
  96.7 46.3 all-gather.12
  146.3 46.9 all-gather.14
  205.7 56.2 all-gather.16
  263.4 24.0 all-gather.18

commit v10 on v9

--- a/solution.py
+++ b/solution.py
@@ -10,7 +10,7 @@
 ROW_TILE = 256
 CHAN_TILE = 256
 LANES = 128
-WIDTHS = [256, 256, 384, 128]
+WIDTHS = [256, 256, 256, 256]
 
 
 def in_sequence(places, seq_lengths):
@@ -75,9 +75,8 @@
             for copy in copies(r):
                 copy.wait()
 
-    edges = [0, halo] + list(range(halo + ROW_TILE, total + 1, ROW_TILE))
-    for streams in [(0, 1, 2)] if chans == LANES else [(0,), (1,), (2,)]:
-        for low, high in zip(edges[:-1], edges[1:]):
+    def project(low, high):
+        for streams in [(0, 1, 2)] if chans == LANES else [(0,), (1,), (2,)]:
             weight = jnp.concatenate(
                 [jnp.concatenate([w[q, k, s] for w, q, k in units], axis=0) for s in streams], axis=1
             )
@@ -97,39 +96,47 @@
         return running
 
     step = 64
-    for r in range(halo - span, total, step):
-        pos = pos_ref[0, r : r + step, :]
-        allowed = [pos >= j for j in range(taps)]
-        for h in range(chans // LANES):
-            mixed = short(0, r, step, h, allowed) * short(2, r, step, h, allowed)
-            mix[r : r + step, h * LANES : (h + 1) * LANES] = mixed.astype(mix.dtype)
-
     lag = (
         lax.broadcasted_iota(jnp.int32, (span, 2 * span), 0)
         + span
         - lax.broadcasted_iota(jnp.int32, (span, 2 * span), 1)
     )
     lane_group = lax.broadcasted_iota(jnp.int32, (span, LANES), 1) // width
-    for b in range(rows // span):
-        first = halo + b * span
-        pos = pos_ref[0, first : first + span, :]
-        limit = jnp.concatenate([pos] * (2 * span // LANES), axis=1)
-        keep = jnp.where(lag <= limit, 1.0, 0.0).astype(band.dtype)
-        allowed = [pos >= j for j in range(taps)]
-        for h in range(chans // LANES):
-            lanes = slice(h * LANES, (h + 1) * LANES)
-            some = band[h * per_lanes * span : (h + 1) * per_lanes * span, :]
-            some = some.reshape(per_lanes, span, 2 * span) * keep[None]
-            full = jnp.dot(
-                some.reshape(per_lanes * span, 2 * span),
-                mix[first - span : first + span, lanes],
-                preferred_element_type=jnp.float32,
-            )
-            medium = full[:span]
-            for g in range(1, per_lanes):
-                medium = jnp.where(lane_group == g, full[g * span : (g + 1) * span], medium)
-            gated = short(1, first, span, h, allowed) * medium
-            done[b * span : (b + 1) * span, lanes] = gated.astype(done.dtype)
+
+    def convolve(low, high):
+        for r in range(max(low, halo - span), high, step):
+            pos = pos_ref[0, r : r + step, :]
+            allowed = [pos >= j for j in range(taps)]
+            for h in range(chans // LANES):
+                mixed = short(0, r, step, h, allowed) * short(2, r, step, h, allowed)
+                mix[r : r + step, h * LANES : (h + 1) * LANES] = mixed.astype(mix.dtype)
+        for first in range(max(low, halo), high, span):
+            pos = pos_ref[0, first : first + span, :]
+            limit = jnp.concatenate([pos] * (2 * span // LANES), axis=1)
+            keep = jnp.where(lag <= limit, 1.0, 0.0).astype(band.dtype)
+            allowed = [pos >= j for j in range(taps)]
+            for h in range(chans // LANES):
+                lanes = slice(h * LANES, (h + 1) * LANES)
+                some = band[h * per_lanes * span : (h + 1) * per_lanes * span, :]
+                some = some.reshape(per_lanes, span, 2 * span) * keep[None]
+                full = jnp.dot(
+                    some.reshape(per_lanes * span, 2 * span),
+                    mix[first - span : first + span, lanes],
+                    preferred_element_type=jnp.float32,
+                )
+                medium = full[:span]
+                for g in range(1, per_lanes):
+                    medium = jnp.where(lane_group == g, full[g * span : (g + 1) * span], medium)
+                gated = short(1, first, span, h, allowed) * medium
+                done[first - halo : first - halo + span, lanes] = gated.astype(done.dtype)
+
+    edges = [0, halo] + list(range(halo + ROW_TILE, total + 1, ROW_TILE))
+    tiles = list(zip(edges[:-1], edges[1:]))
+    project(*tiles[0])
+    for before, now in zip(tiles[:-1], tiles[1:]):
+        project(*now)
+        convolve(*before)
+    convolve(*tiles[-1])
 
     for r in range(runs):
 
@@ -176,8 +183,8 @@
         out_shape=[jax.ShapeDtypeStruct((row_count, chans), jnp.bfloat16)] * runs,
         compiler_params=pltpu.CompilerParams(vmem_limit_bytes=56 * 1024 * 1024),
         cost_estimate=pl.CostEstimate(
-            flops=4 * runs * total * features * 3 * chans,
-            bytes_accessed=2 * (runs * total * features + 3 * features * chans + runs * row_count * chans),
+            flops=runs * total * features * chans,
+            bytes_accessed=runs * row_count * chans,
             transcendentals=0,
         ),
     )(at, *[w for _, w in weights], sw, fr, pos, *[half for run in rows + halos for half in run])
@@ -319,7 +326,7 @@
             stack = jnp.concatenate([peer[None], flip(pair, 8)])
         if c == last:
             convolve(0, own_sw)
-            convolve(1, tied(own_sw, stack))
+            convolve(1, own_sw)
             after[c] = after.get(c, []) + mine
         stack = tied(stack, gathered[-1], *after.get(c, []))
         gathered.append(spread(stack))

time: 343 us -> 323 us (0.942)
  waiting for transfers between devices: 170 us -> 157 us
  Pallas kernels: 88.8 us -> 80.1 us
  local copies, waits for them, and re-layouts: 17.8 us -> 21.5 us
    ppermute x15 -> x14, waiting for transfers between devices: 139 us -> 121 us  [flip(): lax.ppermute(array, 'stretch', [(i, i ^ bit) for i in range(lax.axis_size...]
    pallas_call x5 -> x4, Pallas kernels: 88.8 us -> 80.1 us  [block(): pl.pallas_call(functools.partial(block_kernel, runs, halves, len(weights)...]
    all_gather x5, waiting for transfers between devices: 8.87 us -> 13.1 us  [spread(): lax.all_gather(array, 'stretch', axis=0, tiled=False, axis_index_groups=p...]
    ppermute x15 -> x14, starting transfers between devices: 22.1 us -> 21.8 us  [flip(): lax.ppermute(array, 'stretch', [(i, i ^ bit) for i in range(lax.axis_size...]
  transfers between devices with their start and end apart: 25 -> 24, of which waited for: 10 -> 10; matrix products, arithmetic and copies ran while one was open for 8% -> 9% of each run, Pallas kernels for 26% -> 25%
where the time goes in v10:
time: 323 us
  waiting for transfers between devices  157 us (49%)
  Pallas kernels  80.1 us (25%)
  starting transfers between devices  30 us (9%)
  local copies, waits for them, and re-layouts  21.5 us (7%)
  other arithmetic  17.5 us (5%)
  between operations  16.9 us (5%)
    ppermute x14, waiting for transfers between devices, flip(): lax.ppermute(array, 'stretch', [(i, i ^ bit) for i in range(lax.axis_size...  121 us
    pallas_call x4, Pallas kernels, block(): pl.pallas_call(functools.partial(block_kernel, runs, halves, len(weights)...  80.1 us
    ppermute x14, starting transfers between devices, flip(): lax.ppermute(array, 'stretch', [(i, i ^ bit) for i in range(lax.axis_size...  21.8 us
    ppermute x1, waiting for transfers between devices, rows_before(): before = lax.ppermute(jnp.where(second, tail, sibling), 'stretch', pairs)  20.7 us
    all_gather x5, waiting for transfers between devices, spread(): lax.all_gather(array, 'stretch', axis=0, tiled=False, axis_index_groups=p...  13.1 us
  transfers between devices with their start and end apart: 24, of which 10 were waited for; matrix products, arithmetic and copies ran while one was open for 9% of the time, Pallas kernels for 25%

profile of v10, /device:TPU:0, one launch (start us, length us, event | category | flops | bytes accessed | tf_op | source)
XLA Modules:
  0.0 322.8 jit_solution(13555720329682369745)
XLA Ops:
  6.5 4.2 %dynamic-slice_bitcast_fusion = (bf16[3,256,1024]{2,1,0:T(8,128)(2,1)}, bf16[3,256,1024]{2,1,0:T(8,128)(2,1)}) fusion(bf16[256,3,2048]{2,0,1:T(8,128)(2,1)} %param.7, s32[]{:T(128)S(6)} %select_n.62, s32[]{:T(128)S(6)} %select_n.61), kind=kLoop, calls=%fused_computation.1 | loop fusion | bytes 6291464 | tf_op jit(solution)/shard_map/dynamic_slice | solution.py:271
  10.8 3.0 collective-permute-start.3
  13.9 1.6 collective-permute-start.4
  15.4 1.8 slice.83
  17.2 2.5 collective-permute-start.2
  19.7 2.7 slice_bitcast_fusion
  22.5 1.3 fusion.3
  23.8 1.7 collective-permute-start
  25.4 0.7 fusion.1
  27.5 0.2 reduce-window.8
  27.9 0.7 convert_bitcast_fusion.refs_5_
  28.7 0.7 fusion.refs_6_
  29.4 0.1 stack_broadcast_in_dim.5
  29.5 0.1 stack_broadcast_in_dim.4
  29.7 0.9 pad_add_fusion.refs_4_
  30.6 64.4 %collective-permute-done = bf16[3,256,512]{2,1,0:T(8,128)(2,1)} collective-permute-done((bf16[3,256,512]{2,1,0:T(8,128)(2,1)}, bf16[3,256,512]{2,1,0:T(8,128)(2,1)}, u32[]{:S(2)}, u32[]{:S(2)}) %collective-permute-start) | collective-permute-done | bytes 786464 | tf_op jit(solution)/shard_map/ppermute | solution.py:201
  95.0 1.2 slice_bitcast_fusion.5
  96.2 2.3 pad_maximum_fusion.1.refs_0_
  98.5 1.3 copy-done.1
  99.9 1.9 slice.66
  101.8 0.4 collective-permute-start.5
  104.3 1.3 broadcast_select_fusion.3
  105.6 3.6 %collective-permute-start.7 = (bf16[144,2048]{1,0:T(8,128)(2,1)S(1)}, bf16[144,2048]{1,0:T(8,128)(2,1)S(1)}, u32[]{:S(2)}, u32[]{:S(2)}) collective-permute-start(bf16[144,2048]{1,0:T(8,128)(2,1)S(1)} %broadcast_select_fusion.3), channel_id=1, source_target_pairs={{0,4},{2,6},{4,8},{6,10},{8,12},{10,14},{12,16},{14,18},{16,20},{1... | collective-permute-start | bytes 1769480 | tf_op jit(solution)/shard_map/ppermute | solution.py:213
  109.2 1.0 pad_maximum_fusion.5.refs_0_
  110.2 2.6 collective-permute-start.11
  112.7 1.6 collective-permute-start.12
  114.3 20.7 %collective-permute-done.7 = bf16[144,2048]{1,0:T(8,128)(2,1)S(1)} collective-permute-done((bf16[144,2048]{1,0:T(8,128)(2,1)S(1)}, bf16[144,2048]{1,0:T(8,128)(2,1)S(1)}, u32[]{:S(2)}, u32[]{:S(2)}) %collective-permute-start.7) | collective-permute-done | bytes 589856 | tf_op jit(solution)/shard_map/ppermute | solution.py:213
  135.1 1.9 broadcast_select_fusion.2.refs_9_.refs_3_
  137.0 10.6 %collective-permute-done.11 = bf16[2,3,256,256]{3,2,1,0:T(8,128)(2,1)S(1)} collective-permute-done((bf16[2,3,256,256]{3,2,1,0:T(8,128)(2,1)}, bf16[2,3,256,256]{3,2,1,0:T(8,128)(2,1)S(1)}, u32[]{:S(2)}, u32[]{:S(2)}) %collective-permute-start.11) | collective-permute-done | bytes 786464 | tf_op jit(solution)/shard_map/ppermute | solution.py:201
  147.6 1.1 pad_maximum_fusion.2.refs_0_
  148.8 1.3 collective-permute-done.5.refs_8_.refs_2_
  150.1 1.4 copy-done
  151.5 1.0 copy-done.2
  152.5 1.6 collective-permute-start.9
  154.2 1.0 pad_maximum_fusion.6.refs_0_
  155.2 2.6 collective-permute-start.13
  157.7 0.5 collective-permute-start.8
  158.2 20.5 %collective-permute-done.9.refs_11_ = bf16[144,2048]{1,0:T(8,128)(2,1)S(1)} collective-permute-done((bf16[144,2048]{1,0:T(8,128)(2,1)S(1)}, bf16[144,2048]{1,0:T(8,128)(2,1)S(1)}, u32[]{:S(2)}, u32[]{:S(2)}) %collective-permute-start.9) | collective-permute-done | bytes 589856 | tf_op jit(solution)/shard_map/ppermute | solution.py:201
  178.8 0.6 collective-permute-start.10
  179.3 12.7 %collective-permute-done.13 = bf16[2,3,256,256]{3,2,1,0:T(8,128)(2,1)S(1)} collective-permute-done((bf16[2,3,256,256]{3,2,1,0:T(8,128)(2,1)}, bf16[2,3,256,256]{3,2,1,0:T(8,128)(2,1)S(1)}, u32[]{:S(2)}, u32[]{:S(2)}) %collective-permute-start.13) | collective-permute-done | bytes 786464 | tf_op jit(solution)/shard_map/ppermute | solution.py:201
  192.1 1.2 pad_maximum_fusion.3.refs_0_
  193.3 5.2 %all-gather.15.cloned.1.call-done = bf16[12,3,256,256]{3,2,1,0:T(8,128)(2,1)} async-done(((bf16[3,3,256,256]{3,2,1,0:T(8,128)(2,1)}), bf16[12,3,256,256]{3,2,1,0:T(8,128)(2,1)}) %all-gather.15.cloned.1.call-update) | async-done | bytes 4718608 | tf_op jit(solution)/shard_map/all_gather | solution.py:268
  198.6 0.9 copy-done.10
  199.5 1.0 pad_maximum_fusion.7.refs_0_
  200.5 2.4 collective-permute-start.14
  202.9 0.6 pad_add_fusion.1.at_ref
  203.5 0.6 fusion.5
  204.2 0.6 fusion.4
  204.8 20.1 %shard_map.65 = (bf16[512,256]{1,0:T(8,128)(2,1)}, bf16[512,256]{1,0:T(8,128)(2,1)}) custom-call(s32[4]{0:T(128)} %pad_add_fusion.1.at_ref, bf16[4,1,3,256,1024]{4,3,2,1,0:T(8,128)(2,1)} %bitcast.36, bf16[4,3,3,256,256]{4,3,2,1,0:T(8,128)(2,1)} %bitcast.41, f32[3,7,256]{2,1,0:T(8,128)} %get-tuple-element.42.refs_2_, f32[16,256]{1,0:T(8,128)} %get-tuple-element.46.refs_3_, ...), custom_call_target="tpu_custom_call" | custom-call | flops 1375731712 | bytes 262144 | tf_op jit(solution)/shard_map/pallas_call | solution.py:161
  224.9 19.8 %shard_map.68 = (bf16[512,256]{1,0:T(8,128)(2,1)}, bf16[512,256]{1,0:T(8,128)(2,1)}) custom-call(s32[4]{0:T(128)} %pad_add_fusion.1.at_ref, bf16[4,1,3,256,1024]{4,3,2,1,0:T(8,128)(2,1)} %bitcast.37, bf16[4,3,3,256,256]{4,3,2,1,0:T(8,128)(2,1)} %bitcast.43, f32[3,7,256]{2,1,0:T(8,128)} %get-tuple-element.41.refs_2_, f32[16,256]{1,0:T(8,128)} %get-tuple-element.45.refs_3_, ...), custom_call_target="tpu_custom_call" | custom-call | flops 1375731712 | bytes 262144 | tf_op jit(solution)/shard_map/pallas_call | solution.py:161
  244.7 1.1 pad_maximum_fusion.4.refs_0_
  245.9 0.9 copy-done.22
  246.8 1.4 collective-permute-start.15
  248.3 0.7 collective-permute-start.16
  248.9 7.1 %collective-permute-done.15 = bf16[512,256]{1,0:T(8,128)(2,1)S(1)} collective-permute-done((bf16[512,256]{1,0:T(8,128)(2,1)S(1)}, bf16[512,256]{1,0:T(8,128)(2,1)S(1)}, u32[]{:S(2)}, u32[]{:S(2)}) %collective-permute-start.15) | collective-permute-done | bytes 262176 | tf_op jit(solution)/shard_map/ppermute | solution.py:201
  256.1 20.3 %shard_map.71 = (bf16[512,256]{1,0:T(8,128)(2,1)}, bf16[512,256]{1,0:T(8,128)(2,1)}) custom-call(s32[4]{0:T(128)} %pad_add_fusion.1.at_ref, bf16[4,1,3,256,1024]{4,3,2,1,0:T(8,128)(2,1)} %bitcast.38, bf16[4,3,3,256,256]{4,3,2,1,0:T(8,128)(2,1)} %bitcast.45, f32[3,7,256]{2,1,0:T(8,128)} %get-tuple-element.40.refs_2_, f32[16,256]{1,0:T(8,128)} %get-tuple-element.44.refs_3_, ...), custom_call_target="tpu_custom_call" | custom-call | flops 1375731712 | bytes 262144 | tf_op jit(solution)/shard_map/pallas_call | solution.py:161
  276.4 1.6 collective-permute-start.17
  278.1 7.9 %all-gather.19.cloned.1.call-done = bf16[12,3,256,256]{3,2,1,0:T(8,128)(2,1)} async-done(((bf16[3,3,256,256]{3,2,1,0:T(8,128)(2,1)}), bf16[12,3,256,256]{3,2,1,0:T(8,128)(2,1)}) %all-gather.19.cloned.1.call-update) | async-done | bytes 4718608 | tf_op jit(solution)/shard_map/all_gather | solution.py:268
  285.9 19.9 %shard_map.74 = (bf16[512,256]{1,0:T(8,128)(2,1)}, bf16[512,256]{1,0:T(8,128)(2,1)}) custom-call(s32[4]{0:T(128)} %pad_add_fusion.1.at_ref, bf16[4,1,3,256,1024]{4,3,2,1,0:T(8,128)(2,1)} %bitcast.39, bf16[4,3,3,256,256]{4,3,2,1,0:T(8,128)(2,1)} %bitcast.46, f32[3,7,256]{2,1,0:T(8,128)} %get-tuple-element.39.refs_2_, f32[16,256]{1,0:T(8,128)} %get-tuple-element.43.refs_3_, ...), custom_call_target="tpu_custom_call" | custom-call | flops 1375731712 | bytes 262144 | tf_op jit(solution)/shard_map/pallas_call | solution.py:161
  305.8 1.6 collective-permute-start.18
  307.4 1.0 constant_dynamic-update-slice_fusion
  308.4 6.1 %collective-permute-done.18 = bf16[512,256]{1,0:T(8,128)(2,1)S(1)} collective-permute-done((bf16[512,256]{1,0:T(8,128)(2,1)}, bf16[512,256]{1,0:T(8,128)(2,1)S(1)}, u32[]{:S(2)}, u32[]{:S(2)}) %collective-permute-start.18) | collective-permute-done | bytes 262176 | tf_op jit(solution)/shard_map/ppermute | solution.py:201
  314.6 0.1 broadcast_select_fusion.1
  314.7 1.5 pad_maximum_fusion
  (89 shorter events, 1.0 us)
Async XLA Ops:
  6.5 92.0 %all-gather.11.cloned.1.call-start = ((), (), s32[]{:S(2)}) async-start(), calls=%async_computation | async-start | bytes 7864320 | tf_op jit(solution)/shard_map/all_gather | solution.py:268
  10.8 139.3 %all-gather.13.cloned.1.call-start = ((), (), s32[]{:S(2)}) async-start(), calls=%async_computation.1 | async-start | bytes 5898240 | tf_op jit(solution)/shard_map/all_gather | solution.py:268
  10.8 87.6 %collective-permute-start.3 = (bf16[512,2048]{1,0:T(8,128)(2,1)}, bf16[512,2048]{1,0:T(8,128)(2,1)S(1)}, u32[]{:S(2)}, u32[]{:S(2)}) collective-permute-start(bf16[512,2048]{1,0:T(8,128)(2,1)} %refs_5_.7), channel_id=1, source_target_pairs={{0,1},{1,0},{2,3},{3,2},{4,5},{5,4},{6,7},{7,6},{8,9},{9,8},{10,11... | collective-permute-start | bytes 6291464 | tf_op jit(solution)/shard_map/ppermute | solution.py:205
  13.9 84.6 %collective-permute-start.4 = (bf16[512,2048]{1,0:T(8,128)(2,1)}, bf16[512,2048]{1,0:T(8,128)(2,1)}, u32[]{:S(2)}, u32[]{:S(2)}) collective-permute-start(bf16[512,2048]{1,0:T(8,128)(2,1)} %refs_5_.7), channel_id=1, source_target_pairs={{0,8},{2,10},{4,12},{6,14},{8,0},{10,2},{12,4},{14,6},{16,24},{18,... | collective-permute-start | bytes 6291464 | tf_op jit(solution)/shard_map/ppermute | solution.py:201
  17.2 5.3 %copy-start.6 = (bf16[3,256,1024]{2,1,0:T(8,128)(2,1)S(1)}, bf16[3,256,1024]{2,1,0:T(8,128)(2,1)}, u32[]{:S(2)}) copy-start(bf16[3,256,1024]{2,1,0:T(8,128)(2,1)} %get-tuple-element.25) | copy-start | bytes 4718596
  17.2 78.9 %collective-permute-start.2 = (bf16[3,256,256]{2,1,0:T(8,128)(2,1)}, bf16[3,256,256]{2,1,0:T(8,128)(2,1)}, u32[]{:S(2)}, u32[]{:S(2)}) collective-permute-start(bf16[3,256,256]{2,1,0:T(8,128)(2,1)} %slice.83), channel_id=1, source_target_pairs={{0,24},{2,26},{4,28},{6,30},{8,16},{10,18},{12,20},{14,22},{16,8},... | collective-permute-start | bytes 1179656 | tf_op jit(solution)/shard_map/ppermute | solution.py:201
  22.4 3.1 copy-start.20
  22.4 5.1 %copy-start.23 = (s32[8]{0:T(128)S(1)}, s32[8]{0:T(128)}, u32[]{:S(2)}) copy-start(s32[8]{0:T(128)} %param.10) | copy-start | bytes 100
  22.4 5.3 %copy-start.18 = (bf16[128,128]{1,0:T(8,128)(2,1)S(1)}, bf16[128,128]{1,0:T(8,128)(2,1)}, u32[]{:S(2)}) copy-start(bf16[128,128]{1,0:T(8,128)(2,1)} %param.9) | copy-start | bytes 98308
  22.4 5.5 %copy-start.19 = (bf16[7,3,2048]{2,0,1:T(8,128)(2,1)S(1)}, bf16[7,3,2048]{2,0,1:T(8,128)(2,1)}, u32[]{:S(2)}) copy-start(bf16[7,3,2048]{2,0,1:T(8,128)(2,1)} %param.8) | copy-start | bytes 258052
  22.4 73.8 %collective-permute-start.1 = (bf16[3,256,256]{2,1,0:T(8,128)(2,1)}, bf16[3,256,256]{2,1,0:T(8,128)(2,1)}, u32[]{:S(2)}, u32[]{:S(2)}) collective-permute-start(bf16[3,256,256]{2,1,0:T(8,128)(2,1)} %get-tuple-element.32), channel_id=1, source_target_pairs={{0,16},{2,18},{4,20},{6,22},{8,24},{10,26},{12,28},{14,30},{16,0},... | collective-permute-start | bytes 1179656 | tf_op jit(solution)/shard_map/ppermute | solution.py:201
  23.8 71.2 %collective-permute-start = (bf16[3,256,512]{2,1,0:T(8,128)(2,1)}, bf16[3,256,512]{2,1,0:T(8,128)(2,1)}, u32[]{:S(2)}, u32[]{:S(2)}) collective-permute-start(bf16[3,256,512]{2,1,0:T(8,128)(2,1)} %get-tuple-element.34), channel_id=1, source_target_pairs={{0,8},{2,10},{4,12},{6,14},{8,0},{10,2},{12,4},{14,6},{16,24},{18,... | collective-permute-start | bytes 2359304 | tf_op jit(solution)/shard_map/ppermute | solution.py:201
  98.5 1.3 copy-start.1
  99.8 98.7 %all-gather.15.cloned.1.call-start = ((), (), s32[]{:S(2)}) async-start(), calls=%async_computation.2 | async-start | bytes 5898240 | tf_op jit(solution)/shard_map/all_gather | solution.py:268
  101.8 2.5 collective-permute-start.6
  101.8 48.3 %collective-permute-start.5 = (bf16[512,2048]{1,0:T(8,128)(2,1)}, bf16[512,2048]{1,0:T(8,128)(2,1)S(1)}, u32[]{:S(2)}, u32[]{:S(2)}) collective-permute-start(bf16[512,2048]{1,0:T(8,128)(2,1)} %collective-permute-done.4.refs_3_.refs_7_), channel_id=1, source_target_pairs={{0,1},{1,0},{2,3},{3,2},{4,5},{5,4},{6,7},{7,6},{8,9},{9,8},{10,11... | collective-permute-start | bytes 6291464 | tf_op jit(solution)/shard_map/ppermute | solution.py:205
  104.3 5.9 %copy-start.9 = (bf16[144,2048]{1,0:T(8,128)(2,1)}, bf16[144,2048]{1,0:T(8,128)(2,1)S(1)}, u32[]{:S(2)}) copy-start(bf16[144,2048]{1,0:T(8,128)(2,1)S(1)} %collective-permute-done.6) | copy-start | bytes 1769476
  105.6 29.4 %collective-permute-start.7 = (bf16[144,2048]{1,0:T(8,128)(2,1)S(1)}, bf16[144,2048]{1,0:T(8,128)(2,1)S(1)}, u32[]{:S(2)}, u32[]{:S(2)}) collective-permute-start(bf16[144,2048]{1,0:T(8,128)(2,1)S(1)} %broadcast_select_fusion.3), channel_id=1, source_target_pairs={{0,4},{2,6},{4,8},{6,10},{8,12},{10,14},{12,16},{14,18},{16,20},{1... | collective-permute-start | bytes 1769480 | tf_op jit(solution)/shard_map/ppermute | solution.py:213
  110.2 2.6 copy-start.15
  110.2 37.4 %collective-permute-start.11 = (bf16[2,3,256,256]{3,2,1,0:T(8,128)(2,1)}, bf16[2,3,256,256]{3,2,1,0:T(8,128)(2,1)S(1)}, u32[]{:S(2)}, u32[]{:S(2)}) collective-permute-start(bf16[2,3,256,256]{3,2,1,0:T(8,128)(2,1)} %shard_map.66), channel_id=1, source_target_pairs={{0,16},{2,18},{4,20},{6,22},{8,24},{10,26},{12,28},{14,30},{16,0},... | collective-permute-start | bytes 2359304 | tf_op jit(solution)/shard_map/ppermute | solution.py:201
  112.7 36.0 %collective-permute-start.12 = (bf16[3,256,512]{2,1,0:T(8,128)(2,1)S(1)}, bf16[3,256,512]{2,1,0:T(8,128)(2,1)S(1)}, u32[]{:S(2)}, u32[]{:S(2)}) collective-permute-start(bf16[3,256,512]{2,1,0:T(8,128)(2,1)S(1)} %copy-done.15), channel_id=1, source_target_pairs={{0,8},{2,10},{4,12},{6,14},{8,0},{10,2},{12,4},{14,6},{16,24},{18,... | collective-permute-start | bytes 2359304 | tf_op jit(solution)/shard_map/ppermute | solution.py:201
  148.8 1.3 copy-start.7
  150.1 1.4 copy-start
  151.5 1.1 copy-start.2
  151.5 2.6 copy-start.8
  151.5 2.7 copy-start.11
  151.5 94.4 %all-gather.17.cloned.1.call-start = ((), (), s32[]{:S(2)}) async-start(), calls=%async_computation.3 | async-start | bytes 5898240 | tf_op jit(solution)/shard_map/all_gather | solution.py:268
  152.5 26.2 %collective-permute-start.9 = (bf16[144,2048]{1,0:T(8,128)(2,1)S(1)}, bf16[144,2048]{1,0:T(8,128)(2,1)S(1)}, u32[]{:S(2)}, u32[]{:S(2)}) collective-permute-start(bf16[144,2048]{1,0:T(8,128)(2,1)S(1)} %copy-done.2), channel_id=1, source_target_pairs={{0,8},{2,10},{4,12},{6,14},{8,0},{10,2},{12,4},{14,6},{16,24},{18,... | collective-permute-start | bytes 1769480 | tf_op jit(solution)/shard_map/ppermute | solution.py:201
  155.2 36.9 %collective-permute-start.13 = (bf16[2,3,256,256]{3,2,1,0:T(8,128)(2,1)}, bf16[2,3,256,256]{3,2,1,0:T(8,128)(2,1)S(1)}, u32[]{:S(2)}, u32[]{:S(2)}) collective-permute-start(bf16[2,3,256,256]{3,2,1,0:T(8,128)(2,1)} %shard_map.69), channel_id=1, source_target_pairs={{0,16},{2,18},{4,20},{6,22},{8,24},{10,26},{12,28},{14,30},{16,0},... | collective-permute-start | bytes 2359304 | tf_op jit(solution)/shard_map/ppermute | solution.py:201
  157.7 35.5 %collective-permute-start.8 = (bf16[144,2048]{1,0:T(8,128)(2,1)S(1)}, bf16[144,2048]{1,0:T(8,128)(2,1)S(1)}, u32[]{:S(2)}, u32[]{:S(2)}) collective-permute-start(bf16[144,2048]{1,0:T(8,128)(2,1)S(1)} %copy-done.2), channel_id=1, source_target_pairs={{0,1},{1,0},{2,3},{3,2},{4,5},{5,4},{6,7},{7,6},{8,9},{9,8},{10,11... | collective-permute-start | bytes 1769480 | tf_op jit(solution)/shard_map/ppermute | solution.py:205
  178.8 19.8 %copy-start.5 = (bf16[144,2048]{1,0:T(8,128)(2,1)}, bf16[144,2048]{1,0:T(8,128)(2,1)S(1)}, u32[]{:S(2)}) copy-start(bf16[144,2048]{1,0:T(8,128)(2,1)S(1)} %collective-permute-done.9.refs_11_) | copy-start | bytes 1769476
  178.8 14.5 %collective-permute-start.10 = (bf16[144,2048]{1,0:T(8,128)(2,1)S(1)}, bf16[144,2048]{1,0:T(8,128)(2,1)S(1)}, u32[]{:S(2)}, u32[]{:S(2)}) collective-permute-start(bf16[144,2048]{1,0:T(8,128)(2,1)S(1)} %collective-permute-done.9.refs_11_), channel_id=1, source_target_pairs={{0,1},{1,0},{2,3},{3,2},{4,5},{5,4},{6,7},{7,6},{8,9},{9,8},{10,11... | collective-permute-start | bytes 1769480 | tf_op jit(solution)/shard_map/ppermute | solution.py:205
  193.3 5.2 %copy-start.3 = (bf16[144,2048]{1,0:T(8,128)(2,1)}, bf16[144,2048]{1,0:T(8,128)(2,1)S(1)}, u32[]{:S(2)}) copy-start(bf16[144,2048]{1,0:T(8,128)(2,1)S(1)} %collective-permute-done.8.refs_10_.refs_2_) | copy-start | bytes 1769476
  193.3 5.2 %copy-start.4 = (bf16[144,2048]{1,0:T(8,128)(2,1)}, bf16[144,2048]{1,0:T(8,128)(2,1)S(1)}, u32[]{:S(2)}) copy-start(bf16[144,2048]{1,0:T(8,128)(2,1)S(1)} %collective-permute-done.10.refs_12_.refs_3_) | copy-start | bytes 1769476
  198.5 1.0 copy-start.10
  198.5 87.4 %all-gather.19.cloned.1.call-start = ((), (), s32[]{:S(2)}) async-start(), calls=%async_computation.4 | async-start | bytes 5898240 | tf_op jit(solution)/shard_map/all_gather | solution.py:268
  200.5 3.1 copy-start.16
  200.5 3.7 %copy-start.14 = (f32[3,7,1024]{2,1,0:T(8,128)S(1)}, f32[3,7,1024]{2,1,0:T(8,128)}, u32[]{:S(2)}) copy-start(f32[3,7,1024]{2,1,0:T(8,128)} %convert_bitcast_fusion.refs_5_) | copy-start | bytes 258052
  200.5 44.2 %collective-permute-start.14 = (bf16[2,3,256,256]{3,2,1,0:T(8,128)(2,1)}, bf16[2,3,256,256]{3,2,1,0:T(8,128)(2,1)S(1)}, u32[]{:S(2)}, u32[]{:S(2)}) collective-permute-start(bf16[2,3,256,256]{3,2,1,0:T(8,128)(2,1)} %shard_map.72), channel_id=1, source_target_pairs={{0,16},{2,18},{4,20},{6,22},{8,24},{10,26},{12,28},{14,30},{16,0},... | collective-permute-start | bytes 2359304 | tf_op jit(solution)/shard_map/ppermute | solution.py:201
  245.9 1.0 copy-start.22
  245.9 2.4 copy-start.13
  245.9 2.4 copy-start.21
  245.9 10.2 %copy-start.12 = (bf16[512,256]{1,0:T(8,128)(2,1)S(1)}, bf16[512,256]{1,0:T(8,128)(2,1)}, u32[]{:S(2)}) copy-start(bf16[512,256]{1,0:T(8,128)(2,1)} %get-tuple-element.14.refs_3_) | copy-start | bytes 786436
  246.8 9.2 %collective-permute-start.15 = (bf16[512,256]{1,0:T(8,128)(2,1)S(1)}, bf16[512,256]{1,0:T(8,128)(2,1)S(1)}, u32[]{:S(2)}, u32[]{:S(2)}) collective-permute-start(bf16[512,256]{1,0:T(8,128)(2,1)S(1)} %copy-done.22), channel_id=1, source_target_pairs={{0,8},{2,10},{4,12},{6,14},{8,0},{10,2},{12,4},{14,6},{16,24},{18,... | collective-permute-start | bytes 786440 | tf_op jit(solution)/shard_map/ppermute | solution.py:201
  248.3 29.8 %collective-permute-start.16 = (bf16[512,256]{1,0:T(8,128)(2,1)S(1)}, bf16[512,256]{1,0:T(8,128)(2,1)S(1)}, u32[]{:S(2)}, u32[]{:S(2)}) collective-permute-start(bf16[512,256]{1,0:T(8,128)(2,1)S(1)} %copy-done.21), channel_id=1, source_target_pairs={{0,8},{2,10},{4,12},{6,14},{8,0},{10,2},{12,4},{14,6},{16,24},{18,... | collective-permute-start | bytes 786440 | tf_op jit(solution)/shard_map/ppermute | solution.py:201
  276.4 31.0 %collective-permute-start.17 = (bf16[512,256]{1,0:T(8,128)(2,1)}, bf16[512,256]{1,0:T(8,128)(2,1)S(1)}, u32[]{:S(2)}, u32[]{:S(2)}) collective-permute-start(bf16[512,256]{1,0:T(8,128)(2,1)} %get-tuple-element.19), channel_id=1, source_target_pairs={{0,8},{2,10},{4,12},{6,14},{8,0},{10,2},{12,4},{14,6},{16,24},{18,... | collective-permute-start | bytes 786440 | tf_op jit(solution)/shard_map/ppermute | solution.py:201
  285.9 21.4 %copy-start.17 = (bf16[512,256]{1,0:T(8,128)(2,1)S(1)}, bf16[512,256]{1,0:T(8,128)(2,1)}, u32[]{:S(2)}) copy-start(bf16[512,256]{1,0:T(8,128)(2,1)} %get-tuple-element.15) | copy-start | bytes 786436
  305.8 8.7 %collective-permute-start.18 = (bf16[512,256]{1,0:T(8,128)(2,1)}, bf16[512,256]{1,0:T(8,128)(2,1)S(1)}, u32[]{:S(2)}, u32[]{:S(2)}) collective-permute-start(bf16[512,256]{1,0:T(8,128)(2,1)} %get-tuple-element.20), channel_id=1, source_target_pairs={{0,8},{2,10},{4,12},{6,14},{8,0},{10,2},{12,4},{14,6},{16,24},{18,... | collective-permute-start | bytes 786440 | tf_op jit(solution)/shard_map/ppermute | solution.py:201
Sparse Core Ops, SparseCore 0:
  10.9 49.0 all-gather.10
  99.9 46.7 all-gather.12
  151.6 46.8 all-gather.14
  199.9 40.0 all-gather.16
  246.0 39.8 all-gather.18
